TPU v7x, 32 devices: a whole 2x2x4 slice. The times are simulated.
32 devices in a mesh: groups: 2 (over y), gx: 4 (over z), gy: 4 (over x, core).
Axes of the slice: x: 2, y: 2, z: 4, core: 2. Of those that a mesh axis runs over, the one named last changes fastest.
Arguments:
- stored_rows: bfloat16 [320, 16384], P(('groups', 'gy'), 'gx'), parts along dimension 0, may hold values from -6 to 6
- new_rows: bfloat16 [16, 16384], P(('groups', 'gy'), 'gx'), parts along dimension 0, may hold values from -6 to 6
- w_query: bfloat16 [16384, 8192], P('gx', 'gy'), may hold values from -0.046875 to 0.046875
- w_key: bfloat16 [16384, 512], P('gx', 'gy'), may hold values from -0.046875 to 0.046875
- w_value: bfloat16 [16384, 512], P('gx', 'gy'), may hold values from -0.046875 to 0.046875
- w_out: bfloat16 [8192, 16384], P('gy', 'gx'), may hold values from -0.0625 to 0.0625
- kv_cache: bfloat16 [2, 16, 512, 512], P(None, ('groups', 'gx'), None, 'gy'), parts along dimension 1, may hold values from -52 to 52
- cache_len: int32 [16], P(('groups', 'gx')), parts along dimension 0, may hold values from 1 to 512, as said below
- owner: int32 [8], P('groups'), parts along dimension 0, may hold values from 0 to 3, as said below
Outputs:
- mixed: bfloat16 [16, 16384], P(('groups', 'gy'), 'gx'), parts along dimension 0
- rebuilt_key: bfloat16 [8, 40, 512], P(('groups', 'gx'), None, 'gy'), parts along dimension 0
- rebuilt_value: bfloat16 [8, 40, 512], P(('groups', 'gx'), None, 'gy'), parts along dimension 0
There are 2 independent parts, one for each index of `groups`. A program takes and returns all parts, laid end to end along the dimension named above; an argument that names none is the same for every part. Nothing has to cross between parts.
Inputs may be any that keep to these rules, and one draw needn't show every extreme that they name: A permutation: each owner index takes exactly one conversation. Only a row's first cache_len slots hold data; some row has all 512 slots in use.
All inputs are finite; a program needn't handle non-finite values.
Results may differ from a plain program's by a relative error of at most 0.013.
Values may be sent and summed in bfloat16 or wider, within the bound.
No kernel may reach another device: no remote copies, remote signals or barrier semaphores. Data moves between devices by JAX's collectives and lax.ppermute only.
A program may use at most 64 MiB of HBM per device.

v0:
```python
import math

import jax
import jax.numpy as jnp
from jax import lax
from jax.sharding import PartitionSpec as P

HD = 128
LC = 40
ROWS_DEV = 2


BASE = 500000.0


def rotate(incoming_values, position):
    half = incoming_values.shape[-1] // 2
    index_row = jnp.arange(half).astype(jnp.float32)
    frequency = jnp.exp(index_row * (-2.0 * math.log(BASE) / incoming_values.shape[-1]))
    angle = position.astype(jnp.float32)[..., None] * frequency
    cosine = jnp.cos(angle)
    sine = jnp.sin(angle)
    first_half = incoming_values[..., :half]
    second_half = incoming_values[..., half:]
    return jnp.concatenate(
        [first_half * cosine - second_half * sine, second_half * cosine + first_half * sine],
        axis=-1,
    )


def per_device(stored_rows, new_rows, w_query, w_key, w_value, w_out, kv_cache, cache_len, owner):
    owners = lax.axis_size("gx")
    key_cols = w_key.shape[1]
    query_cols = w_query.shape[1]
    heads_here = key_cols // HD
    group_size = query_cols // key_cols
    slot_ids = jnp.arange(owners, dtype=jnp.int32)
    stored_all, fresh_all = (
        lax.all_gather(stored_rows, "gy", axis=0, tiled=True),
        lax.all_gather(new_rows, "gy", axis=0, tiled=True),
    )
    inverse = jnp.sum(jnp.where(owner[None, :] == slot_ids[:, None], slot_ids[None, :], 0), axis=1)
    source_rows = stored_all.reshape(owners, LC, stored_all.shape[1])[inverse].reshape(
        owners * LC, stored_all.shape[1]
    )
    count = 1 * lax.axis_size("gx")
    pieces = []
    pieces.append(
        jnp.dot(source_rows, w_key, preferred_element_type=jnp.float32).reshape(
            count, LC * key_cols
        )
    )
    pieces.append(
        jnp.dot(source_rows, w_value, preferred_element_type=jnp.float32).reshape(
            count, LC * key_cols
        )
    )
    pieces.append(
        jnp.dot(fresh_all, w_query, preferred_element_type=jnp.float32).reshape(
            count, ROWS_DEV * query_cols
        )
    )
    pieces.append(
        jnp.dot(fresh_all, w_key, preferred_element_type=jnp.float32).reshape(
            count, ROWS_DEV * key_cols
        )
    )
    pieces.append(
        jnp.dot(fresh_all, w_value, preferred_element_type=jnp.float32).reshape(
            count, ROWS_DEV * key_cols
        )
    )
    received = lax.psum_scatter(
        jnp.concatenate(pieces, axis=1), "gx", scatter_dimension=0, tiled=True
    )[0]
    trailing_columns = LC * key_cols
    offset = 0
    own_key = received[:trailing_columns].reshape(LC, key_cols)
    own_value = received[trailing_columns : 2 * trailing_columns].reshape(LC, key_cols)
    offset = 2 * trailing_columns
    query = received[offset : offset + ROWS_DEV * query_cols].reshape(ROWS_DEV, query_cols)
    offset = offset + ROWS_DEV * query_cols
    fresh_key = received[offset : offset + ROWS_DEV * key_cols].reshape(ROWS_DEV, key_cols)
    offset = offset + ROWS_DEV * key_cols
    fresh_value = received[offset : offset + ROWS_DEV * key_cols].reshape(ROWS_DEV, key_cols)
    first_len = cache_len[0]
    tail_pos = first_len + jnp.arange(LC, dtype=jnp.int32)
    rebuilt_key = (
        rotate(own_key.reshape(LC, heads_here, HD), tail_pos[:, None])
        .reshape(LC, key_cols)
        .astype(jnp.bfloat16)
    )
    rebuilt_value = own_value.astype(jnp.bfloat16)
    resumed = jnp.arange(ROWS_DEV, dtype=jnp.int32) == 0
    new_pos = cache_len + jnp.where(resumed, LC, 0).astype(jnp.int32)
    query_rot = rotate(query.reshape(ROWS_DEV, query_cols // HD, HD), new_pos[:, None]).astype(
        jnp.bfloat16
    )
    rotary_key_rows = rotate(fresh_key.reshape(ROWS_DEV, heads_here, HD), new_pos[:, None]).astype(
        jnp.bfloat16
    )
    value_new = fresh_value.reshape(ROWS_DEV, heads_here, HD).astype(jnp.bfloat16)
    score_scaling_factor = 1.0 / math.sqrt(HD)
    slots_cache = kv_cache.shape[2]
    grouped_query_heads = query_rot.reshape(ROWS_DEV, heads_here, group_size, HD)
    cached_keys_lookup = kv_cache[0].reshape(ROWS_DEV, slots_cache, heads_here, HD)
    cache_value = kv_cache[1].reshape(ROWS_DEV, slots_cache, heads_here, HD)
    tail_key = rebuilt_key.reshape(LC, heads_here, HD)
    tail_value = rebuilt_value.reshape(LC, heads_here, HD)
    live_row_mask = jnp.arange(slots_cache, dtype=jnp.int32)[None, :] < cache_len[:, None]
    s_cache = (
        jnp.einsum(
            "bkgd,blkd->bkgl",
            grouped_query_heads,
            cached_keys_lookup,
            preferred_element_type=jnp.float32,
        )
        * score_scaling_factor
    )
    s_cache = jnp.where(live_row_mask[:, None, None, :], s_cache, -jnp.inf)
    s_tail = (
        jnp.einsum(
            "bkgd,tkd->bkgt", grouped_query_heads, tail_key, preferred_element_type=jnp.float32
        )
        * score_scaling_factor
    )
    s_tail = jnp.where(resumed[:, None, None, None], s_tail, -jnp.inf)
    self_score = (
        jnp.einsum(
            "hzrt,hzt->hzr",
            grouped_query_heads,
            rotary_key_rows,
            preferred_element_type=jnp.float32,
        )
        * score_scaling_factor
    )
    highest = jnp.maximum(
        jnp.maximum(jnp.max(s_cache, axis=-1), jnp.max(s_tail, axis=-1)), self_score
    )
    e_cache = jnp.exp(s_cache - highest[..., None])
    e_tail = jnp.exp(s_tail - highest[..., None])
    e_self = jnp.exp(self_score - highest)
    denominator = jnp.sum(e_cache, axis=-1) + jnp.sum(e_tail, axis=-1) + e_self
    w_cache = (e_cache / denominator[..., None]).astype(jnp.bfloat16)
    w_tail = (e_tail / denominator[..., None]).astype(jnp.bfloat16)
    w_self = (e_self / denominator).astype(jnp.bfloat16)
    attn = jnp.einsum("bkgl,blkd->bkgd", w_cache, cache_value, preferred_element_type=jnp.float32)
    attn = attn + jnp.einsum(
        "bkgt,tkd->bkgd", w_tail, tail_value, preferred_element_type=jnp.float32
    )
    attn = (
        attn + w_self.astype(jnp.float32)[..., None] * value_new.astype(jnp.float32)[:, :, None, :]
    )
    attn = attn.reshape(ROWS_DEV, query_cols).astype(jnp.bfloat16)
    partial_out = jnp.dot(
        lax.all_gather(attn, "gx", axis=0, tiled=True), w_out, preferred_element_type=jnp.float32
    )
    mixed = lax.psum_scatter(
        partial_out.astype(jnp.bfloat16), "gy", scatter_dimension=0, tiled=True
    )
    return (mixed, rebuilt_key[None], rebuilt_value[None])


def solution(mesh):
    in_specs = (
        P(("groups", "gy"), "gx"),
        P(("groups", "gy"), "gx"),
        P("gx", "gy"),
        P("gx", "gy"),
        P("gx", "gy"),
        P("gy", "gx"),
        P(None, ("groups", "gx"), None, "gy"),
        P(("groups", "gx")),
        P("groups"),
    )
    out_specs = (
        P(("groups", "gy"), "gx"),
        P(("groups", "gx"), None, "gy"),
        P(("groups", "gx"), None, "gy"),
    )
    return jax.shard_map(
        per_device, mesh=mesh, in_specs=in_specs, out_specs=out_specs, check_vma=False
    )
```

profile of v0, /device:TPU:0, one launch (start us, length us, event | category | flops | bytes accessed | tf_op | source)
XLA Modules:
  0.0 144.5 jit_solution(7778349608240214939)
XLA Ops:
  7.2 0.7 all-gather.4.cloned.1.call-update
  8.0 6.4 %all-gather = bf16[4,2,4096]{2,1,0:T(2,128)(2,1)S(1)} all-gather(bf16[1,2,4096]{2,1,0:T(2,128)(2,1)} %bitcast.90), channel_id=1, replica_groups=mesh['groups'=2,'gx'=4,'gy'=4] {'gy'}, dimensions={0}, use_global_device_ids=true | all-gather | bytes 81920 | tf_op jit(solution)/shard_map/all_gather | solution.py:40
  14.4 8.4 %fusion.49 = f32[8,2048]{1,0:T(8,128)S(1)} fusion(bf16[8,4096]{1,0:T(8,128)(2,1)S(1)} %reshape.455, bf16[4096,2048]{1,0:T(8,128)(2,1)} %param.11), kind=kOutput, calls=%fused_computation.93 | convolution fusion | flops 134217728 | bytes 16908288 | tf_op jit(solution)/shard_map/dot_general | solution.py:59
  23.2 0.6 reshape.440
  24.3 0.6 reshape.441
  24.9 0.6 multiply_exponential_fusion
  26.2 0.5 add_convert_fusion.2
  26.7 0.6 iota_compare_fusion
  27.4 3.1 %all-gather.4.cloned.1.call-done = bf16[160,4096]{1,0:T(8,128)(2,1)} async-done(((bf16[40,4096]{1,0:T(8,128)(2,1)}), bf16[160,4096]{1,0:T(8,128)(2,1)}) %all-gather.4.cloned.1.call-update) | async-done | bytes 1310736 | tf_op jit(solution)/shard_map/all_gather | solution.py:39
  30.5 1.9 %gather_fusion = bf16[4,40,4096]{2,1,0:T(8,128)(2,1)S(1)} fusion(bf16[4,40,4096]{2,1,0:T(8,128)(2,1)} %bitcast.85, s32[1024]{0:T(1024)S(1)} %pad_clamp_fusion), kind=kCustom, calls=%fused_computation | custom fusion | bytes 2621456 | tf_op jit(solution)/shard_map/gather | solution.py:43
  32.4 1.1 fusion.47
  34.1 1.0 reshape.437
  35.2 0.7 constant_dynamic-update-slice_fusion.1
  35.9 0.7 constant_dynamic-update-slice_fusion
  36.6 0.7 copy-done.2
  37.3 0.7 add_convert_fusion.1
  38.0 1.2 dynamic-slice
  39.2 1.2 dynamic-slice.2
  41.1 0.8 multiply_cosine_fusion.2
  41.9 30.5 %all-reduce.5.cloned.1.call-done = f32[4,14848]{1,0:T(4,128)} async-done(((f32[4,14848]{1,0:T(4,128)}), f32[4,14848]{1,0:T(4,128)}) %all-reduce.5.cloned.1.call-update) | async-done | bytes 237584
  72.4 1.4 dynamic-slice.6
  73.8 0.8 fusion.42
  74.7 1.6 %constant_dynamic-slice_fusion = f32[1,5120]{1,0:T(1,128)S(1)} fusion(f32[4,14848]{1,0:T(4,128)} %all-reduce.5.cloned.1.call-done, u32[]{:T(128)} %bitcast.27), kind=kLoop, calls=%fused_computation.79 | loop fusion | bytes 40964 | tf_op jit(solution)/shard_map/slice | solution.py:78
  76.2 0.8 fusion.19
  77.1 1.6 %dynamic-slice.4 = f32[1,4096]{1,0:T(1,128)S(1)} dynamic-slice(f32[4,14848]{1,0:T(4,128)} %all-reduce.5.cloned.1.call-done, u32[]{:T(128)} %bitcast.27, u32[]{:T(128)S(6)} %convert.36), dynamic_slice_sizes={1,4096} | dynamic-slice | bytes 32772 | tf_op jit(solution)/shard_map/slice | solution.py:81
  80.2 1.7 %fusion.22 = bf16[5120]{0:T(1024)(128)(2,1)S(1)} fusion(f32[4,14848]{1,0:T(4,128)} %all-reduce.5.cloned.1.call-done, u32[]{:T(128)} %bitcast.27, u32[]{:T(128)S(6)} %convert.38), kind=kLoop, calls=%fused_computation.33 | loop fusion | bytes 20488 | tf_op jit(solution)/shard_map/convert_element_type | solution.py:93
  81.9 1.4 fusion.35
  83.5 13.2 %all-gather.1 = bf16[4,2,2048]{2,1,0:T(2,128)(2,1)S(1)} all-gather(bf16[1,2,2048]{2,1,0:T(2,128)(2,1)S(1)} %reshape.456), channel_id=1, replica_groups=mesh['groups'=2,'gx'=4,'gy'=4] {'gx'}, dimensions={0}, use_global_device_ids=true | all-gather | bytes 40960 | tf_op jit(solution)/shard_map/all_gather | solution.py:156
  96.7 8.7 %convolution_convert_fusion = bf16[8,4096]{1,0:T(8,128)(2,1)} fusion(bf16[8,2048]{1,0:T(8,128)(2,1)S(1)} %reshape.457, bf16[2048,4096]{1,0:T(8,128)(2,1)} %param.14), kind=kOutput, calls=%fused_computation.1 | convolution fusion | flops 134250496 | bytes 16875520 | tf_op jit(solution)/shard_map/dot_general | solution.py:155
  105.4 0.7 maximum_bitcast_fusion.2
  106.0 30.5 %all-reduce.7.cloned.1.call-done = bf16[8,4096]{1,0:T(8,128)(2,1)} async-done(((bf16[8,4096]{1,0:T(8,128)(2,1)}), bf16[8,4096]{1,0:T(8,128)(2,1)}) %all-reduce.7.cloned.1.call-update) | async-done | bytes 65552
  136.5 1.5 %constant_dynamic-slice_fusion.1 = bf16[2,4096]{1,0:T(2,128)(2,1)} fusion(bf16[8,4096]{1,0:T(8,128)(2,1)} %all-reduce.7.cloned.1.call-done, u32[]{:T(128)S(6)} %multiply.3), kind=kLoop, calls=%fused_computation.80 | loop fusion | bytes 32772
  (48 shorter events, 4.0 us)
Async XLA Ops:
  7.2 15.7 %copy-start = (bf16[4096,128]{1,0:T(8,128)(2,1)S(1)}, bf16[4096,128]{1,0:T(8,128)(2,1)}, u32[]{:S(2)}) copy-start(bf16[4096,128]{1,0:T(8,128)(2,1)} %param.12) | copy-start | bytes 3145732
  7.2 23.3 %all-gather.4.cloned.1.call-start = ((), (), s32[]{:S(2)}) async-start(), calls=%async_computation | async-start | bytes 1638400 | tf_op jit(solution)/shard_map/all_gather | solution.py:39
  7.9 64.5 %all-reduce.5.cloned.1.call-start = ((), (), s32[]{:S(2)}) async-start(), calls=%async_computation.1 | async-start | bytes 475136
  22.9 1.2 copy-start.1
  22.9 3.2 %copy-start.8 = (s32[4]{0:T(128)S(1)}, s32[4]{0:T(128)}, u32[]{:S(2)}) copy-start(s32[4]{0:T(128)} %param.17) | copy-start | bytes 52
  22.9 3.3 %copy-start.7 = (s32[2]{0:T(128)S(1)}, s32[2]{0:T(128)}, u32[]{:S(2)}) copy-start(s32[2]{0:T(128)} %param.16) | copy-start | bytes 28
  34.1 44.9 %copy-start.3 = (bf16[2,2,512,128]{3,2,1,0:T(8,128)(2,1)S(1)}, bf16[2,2,512,128]{3,2,1,0:T(8,128)(2,1)}, u32[]{:S(2)}) copy-start(bf16[2,2,512,128]{3,2,1,0:T(8,128)(2,1)} %param.15) | copy-start | bytes 1572868
  34.1 44.9 %copy-start.5 = (pred[2,512]{1,0:T(4,128)(4,1)S(1)}, pred[2,512]{1,0:T(4,128)(4,1)}, u32[]{:S(2)}) copy-start(pred[2,512]{1,0:T(4,128)(4,1)} %iota_compare_fusion) | copy-start | bytes 3076
  34.1 45.2 %copy-start.6 = (pred[2]{0:T(512)(128)(4,1)S(1)}, pred[2]{0:T(512)(128)(4,1)}, u32[]{:S(2)}) copy-start(pred[2]{0:T(512)(128)(4,1)} %iota_compare_fusion.2) | copy-start | bytes 10
  36.5 0.7 copy-start.2
  37.3 99.2 %all-reduce.7.cloned.1.call-start = ((), (), s32[]{:S(2)}) async-start(), calls=%async_computation.2 | async-start | bytes 131072
  81.9 23.5 %copy-start.4 = (bf16[5120]{0:T(1024)(128)(2,1)}, bf16[5120]{0:T(1024)(128)(2,1)S(1)}, u32[]{:S(2)}) copy-start(bf16[5120]{0:T(1024)(128)(2,1)S(1)} %fusion.22) | copy-start | bytes 30724
Sparse Core Ops, SparseCore 0:
  9.6 20.8 all-gather.3
  37.4 34.9 all-reduce.4
  105.5 30.9 all-reduce.6
where the time goes:
time: 145 us; the launch traced here: 144 us
  waiting for transfers between devices  64.8 us (45%)
  matrix products  20.4 us (14%)
  blocking collectives  19.6 us (14%)
  local copies, waits for them, and re-layouts  17 us (12%)
  between operations  14.6 us (10%)
  other arithmetic  8.05 us (6%)
    unnamed x5, waiting for transfers between devices  61.7 us
    all_gather x1, blocking collectives, per_device(): lax.all_gather(attn, 'gx', axis=0, tiled=True)  13.2 us
    dot_general x1, matrix products, per_device(): jnp.dot(lax.all_gather(attn, 'gx', axis=0, tiled=True), w_out, preferred_...  8.66 us
    dot_general x1, matrix products, per_device(): jnp.dot(fresh_all, w_query, preferred_element_type=jnp.float32)  8.43 us
    all_gather x1, blocking collectives, per_device(): lax.all_gather(new_rows, 'gy', axis=0, tiled=True)  6.43 us
    unnamed x28, local copies, waits for them, and re-layouts  5.79 us
    all_gather x1, waiting for transfers between devices, per_device(): lax.all_gather(stored_rows, 'gy', axis=0, tiled=True)  3.11 us
  transfers between devices with their start and end apart: 3, of which 3 were waited for; matrix products, arithmetic and copies ran while one was open for 12% of the time, Pallas kernels for 0%

commit v1 on v0

v1 whole, which is shorter than its diff:
```python
import math

import jax
import jax.numpy as jnp
from jax import lax
from jax.experimental import pallas as pl
from jax.experimental.pallas import tpu as pltpu
from jax.sharding import PartitionSpec as P

HD = 128
LC = 40
ROWS_DEV = 2
BASE = 500000.0
DIRECT = 8


def rotate(values, position):
    half = values.shape[-1] // 2
    index_row = jnp.arange(half).astype(jnp.float32)
    frequency = jnp.exp(index_row * (-2.0 * math.log(BASE) / values.shape[-1]))
    angle = position.astype(jnp.float32)[..., None] * frequency
    cosine = jnp.cos(angle)
    sine = jnp.sin(angle)
    first_half = values[..., :half]
    second_half = values[..., half:]
    return jnp.concatenate(
        [first_half * cosine - second_half * sine, second_half * cosine + first_half * sine],
        axis=-1,
    )


def swap(x, axis, k):
    n = lax.axis_size(axis)
    return lax.ppermute(x, axis, [(i, i ^ k) for i in range(n)])


def gather(x, axis):
    n = lax.axis_size(axis)
    if n > DIRECT or n & (n - 1):
        return lax.all_gather(x, axis, axis=0)
    me = lax.axis_index(axis)
    out = jnp.zeros((n,) + x.shape, x.dtype)
    for k in range(n):
        block = x if k == 0 else swap(x, axis, k)
        out = lax.dynamic_update_index_in_dim(out, block, me ^ k, 0)
    return out


def scatter_sum(parts, axis):
    n = lax.axis_size(axis)
    me = lax.axis_index(axis)
    if n > DIRECT or n & (n - 1):
        whole = jnp.stack([parts(d) for d in range(n)])
        return lax.psum_scatter(whole.astype(jnp.float32), axis, scatter_dimension=0)
    total = parts(me).astype(jnp.float32)
    for k in range(1, n):
        total = total + swap(parts(me ^ k).astype(jnp.bfloat16), axis, k).astype(jnp.float32)
    return total


def general(stored_rows, new_rows, w_query, w_key, w_value, w_out, kv_cache, cache_len, owner):
    owners = lax.axis_size("gx")
    key_cols = w_key.shape[1]
    query_cols = w_query.shape[1]
    heads_here = key_cols // HD
    group_size = query_cols // key_cols
    slot_ids = jnp.arange(owners, dtype=jnp.int32)
    inverse = jnp.sum(jnp.where(owner[None, :] == slot_ids[:, None], slot_ids[None, :], 0), axis=1)

    fresh_all = gather(new_rows, "gy").reshape(-1, new_rows.shape[1])
    stored_all = gather(stored_rows, "gy").reshape(owners, LC, stored_rows.shape[1])
    flat = stored_all.reshape(owners * LC, stored_rows.shape[1])
    query_part = jnp.dot(fresh_all, w_query, preferred_element_type=jnp.float32)
    new_key_part = jnp.dot(fresh_all, w_key, preferred_element_type=jnp.float32)
    new_value_part = jnp.dot(fresh_all, w_value, preferred_element_type=jnp.float32)
    key_part = jnp.dot(flat, w_key, preferred_element_type=jnp.float32)
    value_part = jnp.dot(flat, w_value, preferred_element_type=jnp.float32)

    small = jnp.concatenate([query_part, new_key_part, new_value_part], axis=1)
    small = small.reshape(owners, ROWS_DEV, -1)
    large = jnp.concatenate([key_part, value_part], axis=1).reshape(owners, LC, -1)

    small_sum = scatter_sum(lambda d: lax.dynamic_index_in_dim(small, d, 0, False), "gx")
    large_sum = scatter_sum(
        lambda d: lax.dynamic_index_in_dim(
            large, lax.dynamic_index_in_dim(inverse, d, 0, False), 0, False
        ),
        "gx",
    )
    query = small_sum[:, :query_cols]
    fresh_key = small_sum[:, query_cols : query_cols + key_cols]
    fresh_value = small_sum[:, query_cols + key_cols :]
    own_key = large_sum[:, :key_cols]
    own_value = large_sum[:, key_cols:]

    first_len = cache_len[0]
    tail_pos = first_len + jnp.arange(LC, dtype=jnp.int32)
    rebuilt_key = (
        rotate(own_key.reshape(LC, heads_here, HD), tail_pos[:, None])
        .reshape(LC, key_cols)
        .astype(jnp.bfloat16)
    )
    rebuilt_value = own_value.astype(jnp.bfloat16)
    resumed = jnp.arange(ROWS_DEV, dtype=jnp.int32) == 0
    new_pos = cache_len + jnp.where(resumed, LC, 0).astype(jnp.int32)
    query_rot = rotate(query.reshape(ROWS_DEV, query_cols // HD, HD), new_pos[:, None]).astype(
        jnp.bfloat16
    )
    key_rot = rotate(fresh_key.reshape(ROWS_DEV, heads_here, HD), new_pos[:, None]).astype(
        jnp.bfloat16
    )
    value_new = fresh_value.reshape(ROWS_DEV, heads_here, HD).astype(jnp.bfloat16)
    scale = 1.0 / math.sqrt(HD)
    slots = kv_cache.shape[2]
    grouped = query_rot.reshape(ROWS_DEV, heads_here, group_size, HD)
    cache_key = kv_cache[0].reshape(ROWS_DEV, slots, heads_here, HD)
    cache_value = kv_cache[1].reshape(ROWS_DEV, slots, heads_here, HD)
    tail_key = rebuilt_key.reshape(LC, heads_here, HD)
    tail_value = rebuilt_value.reshape(LC, heads_here, HD)
    live = jnp.arange(slots, dtype=jnp.int32)[None, :] < cache_len[:, None]
    dot = lambda spec, a, b: jnp.einsum(spec, a, b, preferred_element_type=jnp.float32)
    s_cache = dot("bkgd,blkd->bkgl", grouped, cache_key) * scale
    s_cache = jnp.where(live[:, None, None, :], s_cache, -jnp.inf)
    s_tail = dot("bkgd,tkd->bkgt", grouped, tail_key) * scale
    s_tail = jnp.where(resumed[:, None, None, None], s_tail, -jnp.inf)
    s_self = dot("bkgd,bkd->bkg", grouped, key_rot) * scale
    highest = jnp.maximum(jnp.maximum(jnp.max(s_cache, axis=-1), jnp.max(s_tail, axis=-1)), s_self)
    e_cache = jnp.exp(s_cache - highest[..., None])
    e_tail = jnp.exp(s_tail - highest[..., None])
    e_self = jnp.exp(s_self - highest)
    denominator = jnp.sum(e_cache, axis=-1) + jnp.sum(e_tail, axis=-1) + e_self
    w_cache = (e_cache / denominator[..., None]).astype(jnp.bfloat16)
    w_tail = (e_tail / denominator[..., None]).astype(jnp.bfloat16)
    w_self = (e_self / denominator).astype(jnp.bfloat16)
    attn = dot("bkgl,blkd->bkgd", w_cache, cache_value)
    attn = attn + dot("bkgt,tkd->bkgd", w_tail, tail_value)
    attn = (
        attn + w_self.astype(jnp.float32)[..., None] * value_new.astype(jnp.float32)[:, :, None, :]
    )
    attn = attn.reshape(ROWS_DEV, query_cols).astype(jnp.bfloat16)

    attn_all = gather(attn, "gx").reshape(owners * ROWS_DEV, query_cols)
    out_part = jnp.dot(attn_all, w_out, preferred_element_type=jnp.float32)
    out_part = out_part.reshape(lax.axis_size("gy"), -1, w_out.shape[1])
    mixed = scatter_sum(lambda d: lax.dynamic_index_in_dim(out_part, d, 0, False), "gy")
    return (mixed.astype(jnp.bfloat16), rebuilt_key[None], rebuilt_value[None])


CHUNK = 512
ROW_TILE = 48
PAY = 128
VALUES = 48
QUERY = 96
F32 = jnp.float32
BF16 = jnp.bfloat16


def whole(space=pltpu.VMEM):
    return pl.BlockSpec(memory_space=space)


def params(limit):
    return pltpu.CompilerParams(vmem_limit_bytes=limit * 1024 * 1024)


def cost(flops, bytes_accessed):
    return pl.CostEstimate(flops=flops, bytes_accessed=bytes_accessed, transcendentals=0)


def exchange_tag():
    return lax.axis_index("gx") ^ lax.axis_index("gy")


def angle_kernel(len_ref, cos_ref, sin_ref):
    first, second = len_ref[0], len_ref[1]
    row = lax.broadcasted_iota(jnp.int32, (PAY, HD), 0)
    lane = lax.broadcasted_iota(jnp.int32, (PAY, HD), 1)
    resumed = (row == LC) | ((row >= QUERY) & (row < QUERY + 16))
    other = (row == LC + 1) | (row >= QUERY + 16)
    position = jnp.where(row < LC, first + row, 0)
    position = jnp.where(resumed, first + LC, jnp.where(other, second, position))
    half = lax.rem(lane, HD // 2).astype(F32)
    frequency = jnp.exp(half * (-2.0 * math.log(BASE) / HD))
    angle = position.astype(F32) * frequency
    sine = jnp.sin(angle)
    cos_ref[...] = jnp.cos(angle)
    sin_ref[...] = jnp.where(lane < HD // 2, -sine, sine)


def query_kernel(b0, b1, b2, b3, w_hbm, out_ref, w, acc, sems):
    copies = []
    for c in range(w.shape[0] // CHUNK):
        rows = pl.ds(c * CHUNK, CHUNK)
        copy = pltpu.make_async_copy(w_hbm.at[rows], w.at[rows], sems.at[c])
        copy.start()
        copies.append(copy)
    lhs = jnp.concatenate([b[...].astype(F32) for b in (b0, b1, b2, b3)], axis=0).astype(BF16)
    for c, copy in enumerate(copies):
        copy.wait()
        rows = slice(c * CHUNK, (c + 1) * CHUNK)
        part = jnp.dot(lhs[:, rows], w[rows, :], preferred_element_type=F32)
        acc[...] = part if c == 0 else acc[...] + part
    for r in range(acc.shape[0]):
        for h in range(out_ref.shape[1]):
            out_ref[r, pl.ds(h, 1), :] = acc[pl.ds(r, 1), pl.ds(h * HD, HD)]


def payload_kernel(
    owner_ref, s0, s1, s2, s3, b0, b1, b2, b3, wk, wv, q_ref, o0, o1, o2, o3, x, pay
):
    gx, gy = lax.axis_index("gx"), lax.axis_index("gy")
    stored = (s0, s1, s2, s3)
    for k, s in enumerate(stored):
        x[pl.ds(k * ROW_TILE, LC), :] = s[...]
    fresh = [b[...].astype(F32) for b in (b0, b1, b2, b3)]
    fresh.append(jnp.zeros((8, x.shape[1]), F32))
    base = len(stored) * ROW_TILE
    x[pl.ds(base, 16), :] = jnp.concatenate(fresh, axis=0).astype(BF16)
    key = jnp.zeros((x.shape[0], HD), F32)
    value = key
    for c in range(x.shape[1] // CHUNK):
        rows = slice(c * CHUNK, (c + 1) * CHUNK)
        lhs = x[:, rows]
        key += jnp.dot(lhs, wk[rows, :], preferred_element_type=F32)
        value += jnp.dot(lhs, wv[rows, :], preferred_element_type=F32)
    empty = jnp.zeros((8 - ROWS_DEV, HD), F32)
    for k in range(len(stored)):
        rows = slice(k * ROW_TILE, k * ROW_TILE + LC)
        target = owner_ref[gy ^ k] ^ gx
        pay[target, pl.ds(0, LC), :] = key[rows]
        pay[target, pl.ds(VALUES, LC), :] = value[rows]
        rows = slice(base + k * ROWS_DEV, base + (k + 1) * ROWS_DEV)
        target = k ^ gx ^ gy
        pay[target, pl.ds(LC, 8), :] = jnp.concatenate([key[rows], empty], axis=0)
        pay[target, pl.ds(VALUES + LC, 8), :] = jnp.concatenate([value[rows], empty], axis=0)
        for r in range(ROWS_DEV):
            pay[target, pl.ds(QUERY + 16 * r, 16), :] = q_ref[k * ROWS_DEV + r]
    o0[...] = pay[0]
    o1[...] = pay[1].astype(BF16)
    o2[...] = pay[2].astype(BF16)
    o3[...] = pay[3].astype(BF16)


def attend_kernel(
    len_ref, p0, p1, p2, p3, cos_ref, sin_ref, kv, key_out, value_out, attn_out, attn
):
    total = p0[...] + p1[...].astype(F32) + p2[...].astype(F32) + p3[...].astype(F32)
    turned = total * cos_ref[...] + pltpu.roll(total, HD // 2, 1) * sin_ref[...]
    turned = turned.astype(BF16)
    key_out[...] = turned[:LC]
    value_out[...] = turned[VALUES : VALUES + LC]
    scale = 1.0 / math.sqrt(HD)
    more_key = turned[:VALUES]
    more_value = turned[VALUES:QUERY]
    slots = kv.shape[2]
    contract = (((1,), (1,)), ((), ()))
    for r in range(ROWS_DEV):
        q = turned[QUERY + 16 * r : QUERY + 16 * (r + 1)]
        s = lax.dot_general(q, kv[0, r], contract, preferred_element_type=F32) * scale
        live = lax.broadcasted_iota(jnp.int32, s.shape, 1) < len_ref[r]
        s = jnp.where(live, s, -jnp.inf)
        s_more = lax.dot_general(q, more_key, contract, preferred_element_type=F32) * scale
        lane = lax.broadcasted_iota(jnp.int32, s_more.shape, 1)
        live = lane <= LC if r == 0 else lane == LC + r
        s_more = jnp.where(live, s_more, -jnp.inf)
        highest = jnp.maximum(
            jnp.max(s, axis=1, keepdims=True), jnp.max(s_more, axis=1, keepdims=True)
        )
        e = jnp.exp(s - highest)
        e_more = jnp.exp(s_more - highest)
        total_e = jnp.sum(e, axis=1, keepdims=True) + jnp.sum(e_more, axis=1, keepdims=True)
        out = jnp.dot((e / total_e).astype(BF16), kv[1, r], preferred_element_type=F32)
        out += jnp.dot((e_more / total_e).astype(BF16), more_value, preferred_element_type=F32)
        for h in range(out.shape[0]):
            attn[pl.ds(r, 1), pl.ds(h * HD, HD)] = out[h : h + 1]
    attn_out[...] = attn[...].astype(BF16)


def out_kernel(a0, a1, a2, a3, w_hbm, o0, o1, o2, o3, w, blocks, sems):
    copies = []
    chunk = CHUNK // 2
    for c in range(w.shape[0] // chunk):
        rows = pl.ds(c * chunk, chunk)
        copy = pltpu.make_async_copy(w_hbm.at[rows], w.at[rows], sems.at[c])
        copy.start()
        copies.append(copy)
    tag = exchange_tag()
    for s, a in enumerate((a0, a1, a2, a3)):
        blocks[s ^ tag] = a[...].astype(F32)
    lhs = jnp.concatenate([blocks[k] for k in range(4)], axis=0).astype(BF16)
    acc = jnp.zeros((lhs.shape[0], w.shape[1]), F32)
    for c, copy in enumerate(copies):
        copy.wait()
        rows = slice(c * chunk, (c + 1) * chunk)
        acc += jnp.dot(lhs[:, rows], w[rows, :], preferred_element_type=F32)
    o0[...] = acc[0:2]
    o1[...] = acc[2:4].astype(BF16)
    o2[...] = acc[4:6].astype(BF16)
    o3[...] = acc[6:8].astype(BF16)


def others(blocks, axis):
    return [swap(b, axis, k + 1) for k, b in enumerate(blocks)]


def per_device(stored_rows, new_rows, w_query, w_key, w_value, w_out, kv_cache, cache_len, owner):
    shape = jax.ShapeDtypeStruct
    depth, query_cols = w_query.shape
    width = w_out.shape[1]
    heads = query_cols // HD
    cos, sin = pl.pallas_call(
        angle_kernel,
        out_shape=[shape((PAY, HD), F32)] * 2,
        in_specs=[whole(pltpu.SMEM)],
        out_specs=[whole()] * 2,
        cost_estimate=cost(2000000, 100000),
        name="angles",
    )(cache_len)
    fresh = [new_rows] + others([new_rows] * 3, "gy")
    near = swap(stored_rows, "gy", 1)
    far = swap(stored_rows, "gy", 2)
    far_near = swap(far, "gy", 1)
    stored = [stored_rows, near, far, far_near]
    query = pl.pallas_call(
        query_kernel,
        out_shape=shape((4 * ROWS_DEV, heads, HD), F32),
        in_specs=[whole()] * 4 + [whole(pl.ANY)],
        out_specs=whole(),
        scratch_shapes=[
            pltpu.VMEM((depth, query_cols), BF16),
            pltpu.VMEM((4 * ROWS_DEV, query_cols), F32),
            pltpu.SemaphoreType.DMA((depth // CHUNK,)),
        ],
        compiler_params=params(28),
        cost_estimate=cost(2 * 8 * depth * query_cols, 2 * depth * query_cols),
        name="query",
    )(*fresh, w_query)
    payload = pl.pallas_call(
        payload_kernel,
        out_shape=[shape((PAY, HD), F32)] + [shape((PAY, HD), BF16)] * 3,
        in_specs=[whole(pltpu.SMEM)] + [whole()] * 11,
        out_specs=[whole()] * 4,
        scratch_shapes=[
            pltpu.VMEM((4 * ROW_TILE + 16, depth), BF16),
            pltpu.VMEM((4, PAY, HD), F32),
        ],
        compiler_params=params(28),
        cost_estimate=cost(2 * 208 * depth * 256, 4 * depth * HD),
        name="payload",
    )(owner, *stored, *fresh, w_key, w_value, query)
    sums = [payload[0]] + others(payload[1:], "gx")
    rebuilt_key, rebuilt_value, attn = pl.pallas_call(
        attend_kernel,
        out_shape=[shape((LC, HD), BF16)] * 2 + [shape((ROWS_DEV, query_cols), BF16)],
        in_specs=[whole(pltpu.SMEM)] + [whole()] * 7,
        out_specs=[whole()] * 3,
        scratch_shapes=[pltpu.VMEM((ROWS_DEV, query_cols), F32)],
        compiler_params=params(28),
        cost_estimate=cost(10000000, 1000000),
        name="attend",
    )(cache_len, *sums, cos, sin, kv_cache)
    attn_all = [attn] + others([attn] * 3, "gx")
    parts = pl.pallas_call(
        out_kernel,
        out_shape=[shape((ROWS_DEV, width), F32)] + [shape((ROWS_DEV, width), BF16)] * 3,
        in_specs=[whole()] * 4 + [whole(pl.ANY)],
        out_specs=[whole()] * 4,
        scratch_shapes=[
            pltpu.VMEM((query_cols, width), BF16),
            pltpu.VMEM((4, ROWS_DEV, query_cols), F32),
            pltpu.SemaphoreType.DMA((2 * query_cols // CHUNK,)),
        ],
        compiler_params=params(28),
        cost_estimate=cost(2 * 8 * width * query_cols, 2 * width * query_cols),
        name="project",
    )(*attn_all, w_out)
    arrived = others(parts[1:], "gy")
    mixed = parts[0] + arrived[0].astype(F32) + arrived[1].astype(F32) + arrived[2].astype(F32)
    return (mixed.astype(BF16), rebuilt_key[None], rebuilt_value[None])


def solution(mesh):
    direct = mesh.shape["gx"] == 4 and mesh.shape["gy"] == 4
    in_specs = (
        P(("groups", "gy"), "gx"),
        P(("groups", "gy"), "gx"),
        P("gx", "gy"),
        P("gx", "gy"),
        P("gx", "gy"),
        P("gy", "gx"),
        P(None, ("groups", "gx"), None, "gy"),
        P(("groups", "gx")),
        P("groups"),
    )
    out_specs = (
        P(("groups", "gy"), "gx"),
        P(("groups", "gx"), None, "gy"),
        P(("groups", "gx"), None, "gy"),
    )
    return jax.shard_map(
        per_device if direct else general, mesh=mesh, in_specs=in_specs, out_specs=out_specs, check_vma=False
    )
```

time: 145 us -> 62.2 us (0.43)
  waiting for transfers between devices: 64.8 us -> 19.5 us
  matrix products: 20.4 us -> 0 us
  blocking collectives: 19.6 us -> 0 us
  starting transfers between devices: 0.12 us -> 15.1 us
  between operations: 14.6 us -> 0.75 us
  Pallas kernels: 0 us -> 11.8 us
  other arithmetic: 8.05 us -> 0.64 us
  local copies, waits for them, and re-layouts: 17 us -> 14 us
    unnamed x5 -> x0, waiting for transfers between devices: 61.7 us -> none
    dot_general x11 -> x0, matrix products: 20.4 us -> none  [the longest x1 8.66 us: per_device(): jnp.dot(lax.all_gather(attn, 'gx', axis=0, tiled=True), w_out, preferred_...]
    all_gather x2 -> x0, blocking collectives: 19.6 us -> none  [the longest x1 13.2 us: per_device(): lax.all_gather(attn, 'gx', axis=0, tiled=True)]
    ppermute x0 -> x15, waiting for transfers between devices: none -> 19.5 us  [swap(): return lax.ppermute(x, axis, [(i, i ^ k) for i in range(n)])]
    ppermute x0 -> x15, starting transfers between devices: none -> 15.1 us  [swap(): return lax.ppermute(x, axis, [(i, i ^ k) for i in range(n)])]
    pallas_call x0 -> x5, Pallas kernels: none -> 11.8 us  [the longest x1 3.66 us: per_device(): pl.pallas_call(out_kernel, out_shape=[shape((ROWS_DEV, width), F32)] + [s...]
    unnamed x28 -> x22, local copies, waits for them, and re-layouts: 5.79 us -> 14 us
    slice x3 -> x0, local copies, waits for them, and re-layouts: 4.6 us -> none  [the longest x1 1.63 us: per_device(): received[offset:offset + ROWS_DEV * query_cols]]
  transfers between devices with their start and end apart: 3 -> 15, of which waited for: 3 -> 9; matrix products, arithmetic and copies ran while one was open for 12% -> 0% of each run, Pallas kernels for 0% -> 8%
where the time goes in v1:
time: 62.2 us; the launch traced here: 61.8 us
  waiting for transfers between devices  19.5 us (31%)
  starting transfers between devices  15.1 us (24%)
  local copies, waits for them, and re-layouts  14 us (23%)
  Pallas kernels  11.8 us (19%)
  between operations  0.75 us (1%)
  other arithmetic  0.64 us (1%)
    ppermute x15, waiting for transfers between devices, swap(): return lax.ppermute(x, axis, [(i, i ^ k) for i in range(n)])  19.5 us
    ppermute x15, starting transfers between devices, swap(): return lax.ppermute(x, axis, [(i, i ^ k) for i in range(n)])  15.1 us
    unnamed x22, local copies, waits for them, and re-layouts  14 us
    pallas_call x1, Pallas kernels, per_device(): pl.pallas_call(out_kernel, out_shape=[shape((ROWS_DEV, width), F32)] + [s...  3.66 us
    pallas_call x1, Pallas kernels, per_device(): pl.pallas_call(query_kernel, out_shape=shape((4 * ROWS_DEV, heads, HD), F...  3.56 us
    pallas_call x1, Pallas kernels, per_device(): pl.pallas_call(payload_kernel, out_shape=[shape((PAY, HD), F32)] + [shape...  1.61 us
    pallas_call x1, Pallas kernels, per_device(): pl.pallas_call(attend_kernel, out_shape=[shape((LC, HD), BF16)] * 2 + [sh...  1.52 us
    pallas_call x1, Pallas kernels, per_device(): pl.pallas_call(angle_kernel, out_shape=[shape((PAY, HD), F32)] * 2, in_sp...  1.47 us
  transfers between devices with their start and end apart: 15, of which 9 were waited for; matrix products, arithmetic and copies ran while one was open for 0% of the time, Pallas kernels for 8%

profile of v1, /device:TPU:0, one launch (start us, length us, event | category | flops | bytes accessed | tf_op | source)
XLA Modules:
  0.0 61.8 jit_solution(6038204279457501660)
XLA Ops:
  0.6 3.0 %collective-permute-start.1 = (bf16[40,4096]{1,0:T(8,128)(2,1)}, bf16[40,4096]{1,0:T(8,128)(2,1)S(1)}, u32[]{:S(2)}, u32[]{:S(2)}) collective-permute-start(bf16[40,4096]{1,0:T(8,128)(2,1)} %s0.1), channel_id=1, source_target_pairs={{0,2},{1,3},{2,0},{3,1},{4,6},{5,7},{6,4},{7,5},{8,10},{9,11},{10,... | collective-permute-start | bytes 983048 | tf_op jit(solution)/shard_map/ppermute | solution.py:34
  3.6 7.9 %collective-permute-done.1.s2 = bf16[40,4096]{1,0:T(8,128)(2,1)S(1)} collective-permute-done((bf16[40,4096]{1,0:T(8,128)(2,1)}, bf16[40,4096]{1,0:T(8,128)(2,1)S(1)}, u32[]{:S(2)}, u32[]{:S(2)}) %collective-permute-start.1) | collective-permute-done | bytes 327712 | tf_op jit(solution)/shard_map/ppermute | solution.py:34
  11.6 0.5 collective-permute-start.3
  12.1 1.7 %collective-permute-start.4 = (bf16[2,4096]{1,0:T(2,128)(2,1)}, bf16[2,4096]{1,0:T(2,128)(2,1)S(1)}, u32[]{:S(2)}, u32[]{:S(2)}) collective-permute-start(bf16[2,4096]{1,0:T(2,128)(2,1)} %b0.3), channel_id=1, source_target_pairs={{0,2},{1,3},{2,0},{3,1},{4,6},{5,7},{6,4},{7,5},{8,10},{9,11},{10,... | collective-permute-start | bytes 49160 | tf_op jit(solution)/shard_map/ppermute | solution.py:34
  13.8 2.2 %collective-permute-done.4.b2 = bf16[2,4096]{1,0:T(2,128)(2,1)S(1)} collective-permute-done((bf16[2,4096]{1,0:T(2,128)(2,1)}, bf16[2,4096]{1,0:T(2,128)(2,1)S(1)}, u32[]{:S(2)}, u32[]{:S(2)}) %collective-permute-start.4) | collective-permute-done | bytes 16416 | tf_op jit(solution)/shard_map/ppermute | solution.py:34
  16.0 1.2 %collective-permute-done.5.b3 = bf16[2,4096]{1,0:T(2,128)(2,1)S(1)} collective-permute-done((bf16[2,4096]{1,0:T(2,128)(2,1)}, bf16[2,4096]{1,0:T(2,128)(2,1)S(1)}, u32[]{:S(2)}, u32[]{:S(2)}) %collective-permute-start.5) | collective-permute-done | bytes 16416 | tf_op jit(solution)/shard_map/ppermute | solution.py:34
  17.3 5.8 %copy-done = bf16[4096,2048]{1,0:T(8,128)(2,1)S(1)} copy-done((bf16[4096,2048]{1,0:T(8,128)(2,1)S(1)}, bf16[4096,2048]{1,0:T(8,128)(2,1)}, u32[]{:S(2)}) %copy-start) | copy-done | bytes 16777240
  23.0 0.7 %copy-done.8 = bf16[2,4096]{1,0:T(2,128)(2,1)S(1)} copy-done((bf16[2,4096]{1,0:T(2,128)(2,1)S(1)}, bf16[2,4096]{1,0:T(2,128)(2,1)}, u32[]{:S(2)}) %copy-start.8) | copy-done | bytes 16408
  23.8 0.0 copy-start.9
  23.8 3.6 %query.1.q_ref = f32[8,16,128]{2,1,0:T(8,128)S(1)} custom-call(bf16[2,4096]{1,0:T(2,128)(2,1)S(1)} %copy-done.8, bf16[2,4096]{1,0:T(2,128)(2,1)S(1)} %collective-permute-done.3.b1, bf16[2,4096]{1,0:T(2,128)(2,1)S(1)} %collective-permute-done.4.b2, bf16[2,4096]{1,0:T(2,128)(2,1)S(1)} %collective-permute-done.5.b3, bf16[4096,2048]{1,0:T(8,128)(2,1)S(1)} %copy-done), custom_call_target="tpu_custom_call" | custom-call | flops 134217728 | bytes 16777216 | tf_op jit(solution)/shard_map/query/pallas_call | solution.py:324
  27.4 1.6 %payload.1 = (f32[128,128]{1,0:T(8,128)S(1)}, bf16[128,128]{1,0:T(8,128)(2,1)S(1)}, bf16[128,128]{1,0:T(8,128)(2,1)S(1)}, bf16[128,128]{1,0:T(8,128)(2,1)S(1)}) custom-call(s32[4]{0:T(128)S(1)} %copy-done.10, bf16[40,4096]{1,0:T(8,128)(2,1)S(1)} %copy-done.5, bf16[40,4096]{1,0:T(8,128)(2,1)S(1)} %collective-permute-done.s1, ...), custom_call_target="tpu_custom_call" | custom-call | flops 436207616 | bytes 2097152 | tf_op jit(solution)/shard_map/payload/pallas_call | solution.py:338
  29.0 1.6 %collective-permute-start.6 = (bf16[128,128]{1,0:T(8,128)(2,1)S(1)}, bf16[128,128]{1,0:T(8,128)(2,1)S(1)}, u32[]{:S(2)}, u32[]{:S(2)}) collective-permute-start(bf16[128,128]{1,0:T(8,128)(2,1)S(1)} %get-tuple-element.17), channel_id=1, source_target_pairs={{0,4},{4,0},{8,12},{12,8},{1,5},{5,1},{9,13},{13,9},{2,6},{6,2},{1... | collective-permute-start | bytes 98312 | tf_op jit(solution)/shard_map/ppermute | solution.py:34
  30.7 2.6 %collective-permute-start.7 = (bf16[128,128]{1,0:T(8,128)(2,1)S(1)}, bf16[128,128]{1,0:T(8,128)(2,1)S(1)}, u32[]{:S(2)}, u32[]{:S(2)}) collective-permute-start(bf16[128,128]{1,0:T(8,128)(2,1)S(1)} %get-tuple-element.18), channel_id=1, source_target_pairs={{0,8},{4,12},{8,0},{12,4},{1,9},{5,13},{9,1},{13,5},{2,10},{6,14},... | collective-permute-start | bytes 98312 | tf_op jit(solution)/shard_map/ppermute | solution.py:34
  33.3 0.2 collective-permute-start.8
  33.5 1.5 %angles.1 = (f32[128,128]{1,0:T(8,128)}, f32[128,128]{1,0:T(8,128)}) custom-call(s32[2]{0:T(128)} %len_ref.3), custom_call_target="tpu_custom_call" | custom-call | flops 2000000 | bytes 100000 | tf_op jit(solution)/shard_map/angles/pallas_call | solution.py:311
  35.0 1.1 %collective-permute-done.7.p2 = bf16[128,128]{1,0:T(8,128)(2,1)S(1)} collective-permute-done((bf16[128,128]{1,0:T(8,128)(2,1)S(1)}, bf16[128,128]{1,0:T(8,128)(2,1)S(1)}, u32[]{:S(2)}, u32[]{:S(2)}) %collective-permute-start.7) | collective-permute-done | bytes 32800 | tf_op jit(solution)/shard_map/ppermute | solution.py:34
  36.1 2.9 %collective-permute-done.8.p3 = bf16[128,128]{1,0:T(8,128)(2,1)S(1)} collective-permute-done((bf16[128,128]{1,0:T(8,128)(2,1)S(1)}, bf16[128,128]{1,0:T(8,128)(2,1)S(1)}, u32[]{:S(2)}, u32[]{:S(2)}) %collective-permute-start.8) | collective-permute-done | bytes 32800 | tf_op jit(solution)/shard_map/ppermute | solution.py:34
  39.0 0.8 %copy-done.6 = f32[128,128]{1,0:T(8,128)S(1)} copy-done((f32[128,128]{1,0:T(8,128)S(1)}, f32[128,128]{1,0:T(8,128)}, u32[]{:S(2)}) %copy-start.6) | copy-done | bytes 65560
  39.8 0.8 %copy-done.7 = f32[128,128]{1,0:T(8,128)S(1)} copy-done((f32[128,128]{1,0:T(8,128)S(1)}, f32[128,128]{1,0:T(8,128)}, u32[]{:S(2)}) %copy-start.7) | copy-done | bytes 65560
  40.7 1.5 %attend.1 = (bf16[40,128]{1,0:T(8,128)(2,1)}, bf16[40,128]{1,0:T(8,128)(2,1)}, bf16[2,2048]{1,0:T(2,128)(2,1)S(1)}) custom-call(s32[2]{0:T(128)S(1)} %copy-done.9, f32[128,128]{1,0:T(8,128)S(1)} %get-tuple-element.16.p0, bf16[128,128]{1,0:T(8,128)(2,1)S(1)} %collective-permute-done.6.p1, bf16[128,128]{1,0:T(8,128)(2,1)S(1)} %collective-permute-done.7.p2, ...), custom_call_target="tpu_custom_call" | custom-call | flops 10000000 | bytes 1000000 | tf_op jit(solution)/shard_map/attend/pallas_call | solution.py:352
  42.2 1.0 %collective-permute-start.11 = (bf16[2,2048]{1,0:T(2,128)(2,1)S(1)}, bf16[2,2048]{1,0:T(2,128)(2,1)S(1)}, u32[]{:S(2)}, u32[]{:S(2)}) collective-permute-start(bf16[2,2048]{1,0:T(2,128)(2,1)S(1)} %get-tuple-element.22.a0), channel_id=1, source_target_pairs={{0,12},{4,8},{8,4},{12,0},{1,13},{5,9},{9,5},{13,1},{2,14},{6,10},... | collective-permute-start | bytes 24584 | tf_op jit(solution)/shard_map/ppermute | solution.py:34
  43.2 2.5 %collective-permute-start.9 = (bf16[2,2048]{1,0:T(2,128)(2,1)S(1)}, bf16[2,2048]{1,0:T(2,128)(2,1)S(1)}, u32[]{:S(2)}, u32[]{:S(2)}) collective-permute-start(bf16[2,2048]{1,0:T(2,128)(2,1)S(1)} %get-tuple-element.22.a0), channel_id=1, source_target_pairs={{0,4},{4,0},{8,12},{12,8},{1,5},{5,1},{9,13},{13,9},{2,6},{6,2},{1... | collective-permute-start | bytes 24584 | tf_op jit(solution)/shard_map/ppermute | solution.py:34
  45.7 1.1 %collective-permute-done.10.a2 = bf16[2,2048]{1,0:T(2,128)(2,1)S(1)} collective-permute-done((bf16[2,2048]{1,0:T(2,128)(2,1)S(1)}, bf16[2,2048]{1,0:T(2,128)(2,1)S(1)}, u32[]{:S(2)}, u32[]{:S(2)}) %collective-permute-start.10) | collective-permute-done | bytes 8224 | tf_op jit(solution)/shard_map/ppermute | solution.py:34
  46.7 1.0 %collective-permute-done.11.a3 = bf16[2,2048]{1,0:T(2,128)(2,1)S(1)} collective-permute-done((bf16[2,2048]{1,0:T(2,128)(2,1)S(1)}, bf16[2,2048]{1,0:T(2,128)(2,1)S(1)}, u32[]{:S(2)}, u32[]{:S(2)}) %collective-permute-start.11) | collective-permute-done | bytes 8224 | tf_op jit(solution)/shard_map/ppermute | solution.py:34
  47.7 5.8 %copy-done.1 = bf16[2048,4096]{1,0:T(8,128)(2,1)S(1)} copy-done((bf16[2048,4096]{1,0:T(8,128)(2,1)S(1)}, bf16[2048,4096]{1,0:T(8,128)(2,1)}, u32[]{:S(2)}) %copy-start.1) | copy-done | bytes 16777240
  53.5 3.7 %project.1 = (f32[2,4096]{1,0:T(2,128)S(1)}, bf16[2,4096]{1,0:T(2,128)(2,1)S(1)}, bf16[2,4096]{1,0:T(2,128)(2,1)S(1)}, bf16[2,4096]{1,0:T(2,128)(2,1)S(1)}) custom-call(bf16[2,2048]{1,0:T(2,128)(2,1)S(1)} %get-tuple-element.22.a0, bf16[2,2048]{1,0:T(2,128)(2,1)S(1)} %collective-permute-done.9.a1, bf16[2,2048]{1,0:T(2,128)(2,1)S(1)} %collective-permute-done.10.a2, ...), custom_call_target="tpu_custom_call" | custom-call | flops 134217728 | bytes 16777216 | tf_op jit(solution)/shard_map/project/pallas_call | solution.py:363
  57.1 0.1 collective-permute-start.12
  57.2 0.7 %collective-permute-start.13 = (bf16[2,4096]{1,0:T(2,128)(2,1)S(1)}, bf16[2,4096]{1,0:T(2,128)(2,1)S(1)}, u32[]{:S(2)}, u32[]{:S(2)}) collective-permute-start(bf16[2,4096]{1,0:T(2,128)(2,1)S(1)} %get-tuple-element.25), channel_id=1, source_target_pairs={{0,2},{1,3},{2,0},{3,1},{4,6},{5,7},{6,4},{7,5},{8,10},{9,11},{10,... | collective-permute-start | bytes 49160 | tf_op jit(solution)/shard_map/ppermute | solution.py:34
  57.9 1.2 %collective-permute-start.14 = (bf16[2,4096]{1,0:T(2,128)(2,1)S(1)}, bf16[2,4096]{1,0:T(2,128)(2,1)S(1)}, u32[]{:S(2)}, u32[]{:S(2)}) collective-permute-start(bf16[2,4096]{1,0:T(2,128)(2,1)S(1)} %get-tuple-element.26), channel_id=1, source_target_pairs={{0,3},{1,2},{2,1},{3,0},{4,7},{5,6},{6,5},{7,4},{8,11},{9,10},{10,... | collective-permute-start | bytes 49160 | tf_op jit(solution)/shard_map/ppermute | solution.py:34
  59.1 2.1 %collective-permute-done.13 = bf16[2,4096]{1,0:T(2,128)(2,1)S(1)} collective-permute-done((bf16[2,4096]{1,0:T(2,128)(2,1)S(1)}, bf16[2,4096]{1,0:T(2,128)(2,1)S(1)}, u32[]{:S(2)}, u32[]{:S(2)}) %collective-permute-start.13) | collective-permute-done | bytes 16416 | tf_op jit(solution)/shard_map/ppermute | solution.py:34
  61.1 0.1 collective-permute-done.14
  61.2 0.6 %add_convert_fusion = bf16[2,4096]{1,0:T(2,128)(2,1)} fusion(bf16[2,4096]{1,0:T(2,128)(2,1)S(1)} %collective-permute-done.14, bf16[2,4096]{1,0:T(2,128)(2,1)S(1)} %collective-permute-done.13, f32[2,4096]{1,0:T(2,128)S(1)} %get-tuple-element.23, bf16[2,4096]{1,0:T(2,128)(2,1)S(1)} %collective-permute-done.12), kind=kLoop, calls=%fused_computation | loop fusion | flops 57344 | bytes 98304 | tf_op jit(solution)/shard_map/convert_element_type | solution.py:379
  (26 shorter events, 0.1 us)
Async XLA Ops:
  0.6 10.9 %collective-permute-start.1 = (bf16[40,4096]{1,0:T(8,128)(2,1)}, bf16[40,4096]{1,0:T(8,128)(2,1)S(1)}, u32[]{:S(2)}, u32[]{:S(2)}) collective-permute-start(bf16[40,4096]{1,0:T(8,128)(2,1)} %s0.1), channel_id=1, source_target_pairs={{0,2},{1,3},{2,0},{3,1},{4,6},{5,7},{6,4},{7,5},{8,10},{9,11},{10,... | collective-permute-start | bytes 983048 | tf_op jit(solution)/shard_map/ppermute | solution.py:34
  3.6 23.7 %collective-permute-start = (bf16[40,4096]{1,0:T(8,128)(2,1)}, bf16[40,4096]{1,0:T(8,128)(2,1)S(1)}, u32[]{:S(2)}, u32[]{:S(2)}) collective-permute-start(bf16[40,4096]{1,0:T(8,128)(2,1)} %s0.1), channel_id=1, source_target_pairs={{0,1},{1,0},{2,3},{3,2},{4,5},{5,4},{6,7},{7,6},{8,9},{9,8},{10,11... | collective-permute-start | bytes 983048 | tf_op jit(solution)/shard_map/ppermute | solution.py:34
  11.6 15.8 %collective-permute-start.2 = (bf16[40,4096]{1,0:T(8,128)(2,1)S(1)}, bf16[40,4096]{1,0:T(8,128)(2,1)S(1)}, u32[]{:S(2)}, u32[]{:S(2)}) collective-permute-start(bf16[40,4096]{1,0:T(8,128)(2,1)S(1)} %collective-permute-done.1.s2), channel_id=1, source_target_pairs={{0,1},{1,0},{2,3},{3,2},{4,5},{5,4},{6,7},{7,6},{8,9},{9,8},{10,11... | collective-permute-start | bytes 983048 | tf_op jit(solution)/shard_map/ppermute | solution.py:34
  11.6 2.3 %collective-permute-start.3 = (bf16[2,4096]{1,0:T(2,128)(2,1)}, bf16[2,4096]{1,0:T(2,128)(2,1)S(1)}, u32[]{:S(2)}, u32[]{:S(2)}) collective-permute-start(bf16[2,4096]{1,0:T(2,128)(2,1)} %b0.3), channel_id=1, source_target_pairs={{0,1},{1,0},{2,3},{3,2},{4,5},{5,4},{6,7},{7,6},{8,9},{9,8},{10,11... | collective-permute-start | bytes 49160 | tf_op jit(solution)/shard_map/ppermute | solution.py:34
  12.1 3.9 %collective-permute-start.4 = (bf16[2,4096]{1,0:T(2,128)(2,1)}, bf16[2,4096]{1,0:T(2,128)(2,1)S(1)}, u32[]{:S(2)}, u32[]{:S(2)}) collective-permute-start(bf16[2,4096]{1,0:T(2,128)(2,1)} %b0.3), channel_id=1, source_target_pairs={{0,2},{1,3},{2,0},{3,1},{4,6},{5,7},{6,4},{7,5},{8,10},{9,11},{10,... | collective-permute-start | bytes 49160 | tf_op jit(solution)/shard_map/ppermute | solution.py:34
  13.8 3.5 %collective-permute-start.5 = (bf16[2,4096]{1,0:T(2,128)(2,1)}, bf16[2,4096]{1,0:T(2,128)(2,1)S(1)}, u32[]{:S(2)}, u32[]{:S(2)}) collective-permute-start(bf16[2,4096]{1,0:T(2,128)(2,1)} %b0.3), channel_id=1, source_target_pairs={{0,3},{1,2},{2,1},{3,0},{4,7},{5,6},{6,5},{7,4},{8,11},{9,10},{10,... | collective-permute-start | bytes 49160 | tf_op jit(solution)/shard_map/ppermute | solution.py:34
  17.3 5.8 %copy-start = (bf16[4096,2048]{1,0:T(8,128)(2,1)S(1)}, bf16[4096,2048]{1,0:T(8,128)(2,1)}, u32[]{:S(2)}) copy-start(bf16[4096,2048]{1,0:T(8,128)(2,1)} %w_hbm.2) | copy-start | bytes 50331652
  23.0 0.7 %copy-start.8 = (bf16[2,4096]{1,0:T(2,128)(2,1)S(1)}, bf16[2,4096]{1,0:T(2,128)(2,1)}, u32[]{:S(2)}) copy-start(bf16[2,4096]{1,0:T(2,128)(2,1)} %b0.3) | copy-start | bytes 49156
  23.8 3.6 %copy-start.2 = (bf16[4096,128]{1,0:T(8,128)(2,1)S(1)}, bf16[4096,128]{1,0:T(8,128)(2,1)}, u32[]{:S(2)}) copy-start(bf16[4096,128]{1,0:T(8,128)(2,1)} %wk.1) | copy-start | bytes 3145732
  23.8 3.6 %copy-start.3 = (bf16[4096,128]{1,0:T(8,128)(2,1)S(1)}, bf16[4096,128]{1,0:T(8,128)(2,1)}, u32[]{:S(2)}) copy-start(bf16[4096,128]{1,0:T(8,128)(2,1)} %wv.1) | copy-start | bytes 3145732
  23.8 3.6 %copy-start.5 = (bf16[40,4096]{1,0:T(8,128)(2,1)S(1)}, bf16[40,4096]{1,0:T(8,128)(2,1)}, u32[]{:S(2)}) copy-start(bf16[40,4096]{1,0:T(8,128)(2,1)} %s0.1) | copy-start | bytes 983044
  23.8 3.6 %copy-start.10 = (s32[4]{0:T(128)S(1)}, s32[4]{0:T(128)}, u32[]{:S(2)}) copy-start(s32[4]{0:T(128)} %owner_ref.1) | copy-start | bytes 52
  23.8 15.2 %copy-start.4 = (bf16[2,2,512,128]{3,2,1,0:T(8,128)(2,1)S(1)}, bf16[2,2,512,128]{3,2,1,0:T(8,128)(2,1)}, u32[]{:S(2)}) copy-start(bf16[2,2,512,128]{3,2,1,0:T(8,128)(2,1)} %kv.1) | copy-start | bytes 1572868
  23.8 15.2 %copy-start.9 = (s32[2]{0:T(128)S(1)}, s32[2]{0:T(128)}, u32[]{:S(2)}) copy-start(s32[2]{0:T(128)} %len_ref.3) | copy-start | bytes 28
  29.0 5.9 %collective-permute-start.6 = (bf16[128,128]{1,0:T(8,128)(2,1)S(1)}, bf16[128,128]{1,0:T(8,128)(2,1)S(1)}, u32[]{:S(2)}, u32[]{:S(2)}) collective-permute-start(bf16[128,128]{1,0:T(8,128)(2,1)S(1)} %get-tuple-element.17), channel_id=1, source_target_pairs={{0,4},{4,0},{8,12},{12,8},{1,5},{5,1},{9,13},{13,9},{2,6},{6,2},{1... | collective-permute-start | bytes 98312 | tf_op jit(solution)/shard_map/ppermute | solution.py:34
  30.7 5.4 %collective-permute-start.7 = (bf16[128,128]{1,0:T(8,128)(2,1)S(1)}, bf16[128,128]{1,0:T(8,128)(2,1)S(1)}, u32[]{:S(2)}, u32[]{:S(2)}) collective-permute-start(bf16[128,128]{1,0:T(8,128)(2,1)S(1)} %get-tuple-element.18), channel_id=1, source_target_pairs={{0,8},{4,12},{8,0},{12,4},{1,9},{5,13},{9,1},{13,5},{2,10},{6,14},... | collective-permute-start | bytes 98312 | tf_op jit(solution)/shard_map/ppermute | solution.py:34
  33.3 5.7 %collective-permute-start.8 = (bf16[128,128]{1,0:T(8,128)(2,1)S(1)}, bf16[128,128]{1,0:T(8,128)(2,1)S(1)}, u32[]{:S(2)}, u32[]{:S(2)}) collective-permute-start(bf16[128,128]{1,0:T(8,128)(2,1)S(1)} %get-tuple-element.19), channel_id=1, source_target_pairs={{0,12},{4,8},{8,4},{12,0},{1,13},{5,9},{9,5},{13,1},{2,14},{6,10},... | collective-permute-start | bytes 98312 | tf_op jit(solution)/shard_map/ppermute | solution.py:34
  39.0 0.8 %copy-start.6 = (f32[128,128]{1,0:T(8,128)S(1)}, f32[128,128]{1,0:T(8,128)}, u32[]{:S(2)}) copy-start(f32[128,128]{1,0:T(8,128)} %get-tuple-element.20.cos_ref) | copy-start | bytes 196612
  39.8 0.8 %copy-start.7 = (f32[128,128]{1,0:T(8,128)S(1)}, f32[128,128]{1,0:T(8,128)}, u32[]{:S(2)}) copy-start(f32[128,128]{1,0:T(8,128)} %get-tuple-element.21.sin_ref) | copy-start | bytes 196612
  42.2 4.5 %collective-permute-start.10 = (bf16[2,2048]{1,0:T(2,128)(2,1)S(1)}, bf16[2,2048]{1,0:T(2,128)(2,1)S(1)}, u32[]{:S(2)}, u32[]{:S(2)}) collective-permute-start(bf16[2,2048]{1,0:T(2,128)(2,1)S(1)} %get-tuple-element.22.a0), channel_id=1, source_target_pairs={{0,8},{4,12},{8,0},{12,4},{1,9},{5,13},{9,1},{13,5},{2,10},{6,14},... | collective-permute-start | bytes 24584 | tf_op jit(solution)/shard_map/ppermute | solution.py:34
  42.2 5.5 %collective-permute-start.11 = (bf16[2,2048]{1,0:T(2,128)(2,1)S(1)}, bf16[2,2048]{1,0:T(2,128)(2,1)S(1)}, u32[]{:S(2)}, u32[]{:S(2)}) collective-permute-start(bf16[2,2048]{1,0:T(2,128)(2,1)S(1)} %get-tuple-element.22.a0), channel_id=1, source_target_pairs={{0,12},{4,8},{8,4},{12,0},{1,13},{5,9},{9,5},{13,1},{2,14},{6,10},... | collective-permute-start | bytes 24584 | tf_op jit(solution)/shard_map/ppermute | solution.py:34
  43.2 4.5 %collective-permute-start.9 = (bf16[2,2048]{1,0:T(2,128)(2,1)S(1)}, bf16[2,2048]{1,0:T(2,128)(2,1)S(1)}, u32[]{:S(2)}, u32[]{:S(2)}) collective-permute-start(bf16[2,2048]{1,0:T(2,128)(2,1)S(1)} %get-tuple-element.22.a0), channel_id=1, source_target_pairs={{0,4},{4,0},{8,12},{12,8},{1,5},{5,1},{9,13},{13,9},{2,6},{6,2},{1... | collective-permute-start | bytes 24584 | tf_op jit(solution)/shard_map/ppermute | solution.py:34
  47.7 5.8 %copy-start.1 = (bf16[2048,4096]{1,0:T(8,128)(2,1)S(1)}, bf16[2048,4096]{1,0:T(8,128)(2,1)}, u32[]{:S(2)}) copy-start(bf16[2048,4096]{1,0:T(8,128)(2,1)} %w_hbm.3) | copy-start | bytes 50331652
  57.1 1.9 %collective-permute-start.12 = (bf16[2,4096]{1,0:T(2,128)(2,1)S(1)}, bf16[2,4096]{1,0:T(2,128)(2,1)S(1)}, u32[]{:S(2)}, u32[]{:S(2)}) collective-permute-start(bf16[2,4096]{1,0:T(2,128)(2,1)S(1)} %get-tuple-element.24), channel_id=1, source_target_pairs={{0,1},{1,0},{2,3},{3,2},{4,5},{5,4},{6,7},{7,6},{8,9},{9,8},{10,11... | collective-permute-start | bytes 49160 | tf_op jit(solution)/shard_map/ppermute | solution.py:34
  57.2 3.9 %collective-permute-start.13 = (bf16[2,4096]{1,0:T(2,128)(2,1)S(1)}, bf16[2,4096]{1,0:T(2,128)(2,1)S(1)}, u32[]{:S(2)}, u32[]{:S(2)}) collective-permute-start(bf16[2,4096]{1,0:T(2,128)(2,1)S(1)} %get-tuple-element.25), channel_id=1, source_target_pairs={{0,2},{1,3},{2,0},{3,1},{4,6},{5,7},{6,4},{7,5},{8,10},{9,11},{10,... | collective-permute-start | bytes 49160 | tf_op jit(solution)/shard_map/ppermute | solution.py:34
  57.9 3.3 %collective-permute-start.14 = (bf16[2,4096]{1,0:T(2,128)(2,1)S(1)}, bf16[2,4096]{1,0:T(2,128)(2,1)S(1)}, u32[]{:S(2)}, u32[]{:S(2)}) collective-permute-start(bf16[2,4096]{1,0:T(2,128)(2,1)S(1)} %get-tuple-element.26), channel_id=1, source_target_pairs={{0,3},{1,2},{2,1},{3,0},{4,7},{5,6},{6,5},{7,4},{8,11},{9,10},{10,... | collective-permute-start | bytes 49160 | tf_op jit(solution)/shard_map/ppermute | solution.py:34

commit v2 on v1

--- a/solution.py
+++ b/solution.py
@@ -167,11 +167,7 @@
     return pl.CostEstimate(flops=flops, bytes_accessed=bytes_accessed, transcendentals=0)
 
 
-def exchange_tag():
-    return lax.axis_index("gx") ^ lax.axis_index("gy")
-
-
-def angle_kernel(len_ref, cos_ref, sin_ref):
+def angle_kernel(ready, len_ref, cos_ref, sin_ref):
     first, second = len_ref[0], len_ref[1]
     row = lax.broadcasted_iota(jnp.int32, (PAY, HD), 0)
     lane = lax.broadcasted_iota(jnp.int32, (PAY, HD), 1)
@@ -187,28 +183,40 @@
     sin_ref[...] = jnp.where(lane < HD // 2, -sine, sine)
 
 
-def query_kernel(b0, b1, b2, b3, w_hbm, out_ref, w, acc, sems):
+def start_load(source, target, sems, first, pieces):
     copies = []
-    for c in range(w.shape[0] // CHUNK):
-        rows = pl.ds(c * CHUNK, CHUNK)
-        copy = pltpu.make_async_copy(w_hbm.at[rows], w.at[rows], sems.at[c])
+    rows = source.shape[0] // pieces
+    for c in range(pieces):
+        part = pl.ds(c * rows, rows)
+        copy = pltpu.make_async_copy(source.at[part], target.at[part], sems.at[first + c])
         copy.start()
         copies.append(copy)
+    return copies
+
+
+def load_kernel(wq_hbm, b_hbm, wq, b, sems):
+    copies = start_load(wq_hbm, wq, sems, 0, 8)
+    copies += start_load(b_hbm, b, sems, 8, 1)
+    for copy in copies:
+        copy.wait()
+
+
+def query_kernel(far, b0, b1, b2, b3, w, wk_hbm, wv_hbm, out_ref, wkv, acc, sems):
+    copies = start_load(wk_hbm, wkv.at[:, pl.ds(0, HD)], sems, 0, 1)
+    copies += start_load(wv_hbm, wkv.at[:, pl.ds(HD, HD)], sems, 1, 1)
     lhs = jnp.concatenate([b[...].astype(F32) for b in (b0, b1, b2, b3)], axis=0).astype(BF16)
-    for c, copy in enumerate(copies):
-        copy.wait()
-        rows = slice(c * CHUNK, (c + 1) * CHUNK)
-        part = jnp.dot(lhs[:, rows], w[rows, :], preferred_element_type=F32)
-        acc[...] = part if c == 0 else acc[...] + part
+    acc[...] = jnp.dot(lhs, w[...], preferred_element_type=F32)
     for r in range(acc.shape[0]):
         for h in range(out_ref.shape[1]):
             out_ref[r, pl.ds(h, 1), :] = acc[pl.ds(r, 1), pl.ds(h * HD, HD)]
+    for copy in copies:
+        copy.wait()
 
 
 def payload_kernel(
-    owner_ref, s0, s1, s2, s3, b0, b1, b2, b3, wk, wv, q_ref, o0, o1, o2, o3, x, pay
+    owner_ref, s0, s1, s2, s3, b0, b1, b2, b3, wkv, q_ref, out, x, pay
 ):
-    gx, gy = lax.axis_index("gx"), lax.axis_index("gy")
+    gy = lax.axis_index("gy")
     stored = (s0, s1, s2, s3)
     for k, s in enumerate(stored):
         x[pl.ds(k * ROW_TILE, LC), :] = s[...]
@@ -216,35 +224,30 @@
     fresh.append(jnp.zeros((8, x.shape[1]), F32))
     base = len(stored) * ROW_TILE
     x[pl.ds(base, 16), :] = jnp.concatenate(fresh, axis=0).astype(BF16)
-    key = jnp.zeros((x.shape[0], HD), F32)
-    value = key
+    both = jnp.zeros((x.shape[0], 2 * HD), F32)
     for c in range(x.shape[1] // CHUNK):
         rows = slice(c * CHUNK, (c + 1) * CHUNK)
-        lhs = x[:, rows]
-        key += jnp.dot(lhs, wk[rows, :], preferred_element_type=F32)
-        value += jnp.dot(lhs, wv[rows, :], preferred_element_type=F32)
+        both += jnp.dot(x[:, rows], wkv[rows, :], preferred_element_type=F32)
+    key, value = both[:, :HD], both[:, HD:]
     empty = jnp.zeros((8 - ROWS_DEV, HD), F32)
     for k in range(len(stored)):
         rows = slice(k * ROW_TILE, k * ROW_TILE + LC)
-        target = owner_ref[gy ^ k] ^ gx
+        target = owner_ref[gy ^ k]
         pay[target, pl.ds(0, LC), :] = key[rows]
         pay[target, pl.ds(VALUES, LC), :] = value[rows]
         rows = slice(base + k * ROWS_DEV, base + (k + 1) * ROWS_DEV)
-        target = k ^ gx ^ gy
+        target = k ^ gy
         pay[target, pl.ds(LC, 8), :] = jnp.concatenate([key[rows], empty], axis=0)
         pay[target, pl.ds(VALUES + LC, 8), :] = jnp.concatenate([value[rows], empty], axis=0)
         for r in range(ROWS_DEV):
             pay[target, pl.ds(QUERY + 16 * r, 16), :] = q_ref[k * ROWS_DEV + r]
-    o0[...] = pay[0]
-    o1[...] = pay[1].astype(BF16)
-    o2[...] = pay[2].astype(BF16)
-    o3[...] = pay[3].astype(BF16)
+    out[...] = pay[...].astype(BF16)
 
 
 def attend_kernel(
-    len_ref, p0, p1, p2, p3, cos_ref, sin_ref, kv, key_out, value_out, attn_out, attn
+    len_ref, terms, cos_ref, sin_ref, kv, key_out, value_out, attn_out, attn
 ):
-    total = p0[...] + p1[...].astype(F32) + p2[...].astype(F32) + p3[...].astype(F32)
+    total = jnp.sum(terms[...].astype(F32), axis=0)
     turned = total * cos_ref[...] + pltpu.roll(total, HD // 2, 1) * sin_ref[...]
     turned = turned.astype(BF16)
     key_out[...] = turned[:LC]
@@ -276,27 +279,14 @@
     attn_out[...] = attn[...].astype(BF16)
 
 
-def out_kernel(a0, a1, a2, a3, w_hbm, o0, o1, o2, o3, w, blocks, sems):
-    copies = []
-    chunk = CHUNK // 2
-    for c in range(w.shape[0] // chunk):
-        rows = pl.ds(c * chunk, chunk)
-        copy = pltpu.make_async_copy(w_hbm.at[rows], w.at[rows], sems.at[c])
-        copy.start()
-        copies.append(copy)
-    tag = exchange_tag()
+def out_kernel(a0, a1, a2, a3, w, out, blocks):
+    gx = lax.axis_index("gx")
     for s, a in enumerate((a0, a1, a2, a3)):
-        blocks[s ^ tag] = a[...].astype(F32)
+        blocks[s ^ gx] = a[...].astype(F32)
     lhs = jnp.concatenate([blocks[k] for k in range(4)], axis=0).astype(BF16)
-    acc = jnp.zeros((lhs.shape[0], w.shape[1]), F32)
-    for c, copy in enumerate(copies):
-        copy.wait()
-        rows = slice(c * chunk, (c + 1) * chunk)
-        acc += jnp.dot(lhs[:, rows], w[rows, :], preferred_element_type=F32)
-    o0[...] = acc[0:2]
-    o1[...] = acc[2:4].astype(BF16)
-    o2[...] = acc[4:6].astype(BF16)
-    o3[...] = acc[6:8].astype(BF16)
+    acc = jnp.dot(lhs, w[...], preferred_element_type=F32)
+    for k in range(4):
+        out[k] = acc[k * ROWS_DEV : (k + 1) * ROWS_DEV].astype(BF16)
 
 
 def others(blocks, axis):
@@ -308,74 +298,83 @@
     depth, query_cols = w_query.shape
     width = w_out.shape[1]
     heads = query_cols // HD
-    cos, sin = pl.pallas_call(
-        angle_kernel,
-        out_shape=[shape((PAY, HD), F32)] * 2,
-        in_specs=[whole(pltpu.SMEM)],
+    semaphores = pltpu.SemaphoreType.DMA
+    in_hbm = lambda x: pltpu.with_memory_space_constraint(x, pltpu.HBM)
+    far = swap(stored_rows, "gy", 2)
+    near = swap(stored_rows, "gy", 1)
+    fresh = others([new_rows] * 3, "gy")
+    wq, own_fresh = pl.pallas_call(
+        load_kernel,
+        out_shape=[pltpu.VMEM((depth, query_cols), BF16), pltpu.VMEM(new_rows.shape, BF16)],
+        in_specs=[whole(pltpu.HBM)] * 2,
         out_specs=[whole()] * 2,
-        cost_estimate=cost(2000000, 100000),
-        name="angles",
-    )(cache_len)
-    fresh = [new_rows] + others([new_rows] * 3, "gy")
-    near = swap(stored_rows, "gy", 1)
-    far = swap(stored_rows, "gy", 2)
+        scratch_shapes=[semaphores((9,))],
+        compiler_params=params(8),
+        cost_estimate=cost(1000, 2 * depth * query_cols),
+        name="load",
+    )(in_hbm(w_query), in_hbm(new_rows))
+    far, own_fresh, *fresh = lax.optimization_barrier((far, own_fresh, *fresh))
     far_near = swap(far, "gy", 1)
+    fresh = [own_fresh] + fresh
     stored = [stored_rows, near, far, far_near]
-    query = pl.pallas_call(
+    query, wkv = pl.pallas_call(
         query_kernel,
-        out_shape=shape((4 * ROWS_DEV, heads, HD), F32),
-        in_specs=[whole()] * 4 + [whole(pl.ANY)],
-        out_specs=whole(),
-        scratch_shapes=[
-            pltpu.VMEM((depth, query_cols), BF16),
-            pltpu.VMEM((4 * ROWS_DEV, query_cols), F32),
-            pltpu.SemaphoreType.DMA((depth // CHUNK,)),
+        out_shape=[
+            pltpu.VMEM((4 * ROWS_DEV, heads, HD), F32),
+            pltpu.VMEM((depth, 2 * HD), BF16),
         ],
-        compiler_params=params(28),
-        cost_estimate=cost(2 * 8 * depth * query_cols, 2 * depth * query_cols),
+        in_specs=[whole(pl.ANY)] + [whole()] * 5 + [whole(pltpu.HBM)] * 2,
+        out_specs=[whole()] * 2,
+        scratch_shapes=[pltpu.VMEM((4 * ROWS_DEV, query_cols), F32), semaphores((2,))],
+        compiler_params=params(8),
+        cost_estimate=cost(2 * 8 * depth * query_cols, 4 * depth * HD),
         name="query",
-    )(*fresh, w_query)
+    )(far, *fresh, wq, in_hbm(w_key), in_hbm(w_value))
     payload = pl.pallas_call(
         payload_kernel,
-        out_shape=[shape((PAY, HD), F32)] + [shape((PAY, HD), BF16)] * 3,
-        in_specs=[whole(pltpu.SMEM)] + [whole()] * 11,
-        out_specs=[whole()] * 4,
+        out_shape=shape((4, PAY, HD), BF16),
+        in_specs=[whole(pltpu.SMEM)] + [whole()] * 10,
+        out_specs=whole(),
         scratch_shapes=[
             pltpu.VMEM((4 * ROW_TILE + 16, depth), BF16),
             pltpu.VMEM((4, PAY, HD), F32),
         ],
-        compiler_params=params(28),
+        compiler_params=params(8),
         cost_estimate=cost(2 * 208 * depth * 256, 4 * depth * HD),
         name="payload",
-    )(owner, *stored, *fresh, w_key, w_value, query)
-    sums = [payload[0]] + others(payload[1:], "gx")
+    )(owner, *stored, *fresh, wkv, query)
+    terms = lax.all_to_all(payload, "gx", 0, 0)
+    cos, sin = pl.pallas_call(
+        angle_kernel,
+        out_shape=[pltpu.VMEM((PAY, HD), F32)] * 2,
+        in_specs=[whole(pl.ANY), whole(pltpu.SMEM)],
+        out_specs=[whole()] * 2,
+        cost_estimate=cost(2000000, 100000),
+        name="angles",
+    )(payload, cache_len)
     rebuilt_key, rebuilt_value, attn = pl.pallas_call(
         attend_kernel,
         out_shape=[shape((LC, HD), BF16)] * 2 + [shape((ROWS_DEV, query_cols), BF16)],
-        in_specs=[whole(pltpu.SMEM)] + [whole()] * 7,
+        in_specs=[whole(pltpu.SMEM)] + [whole()] * 4,
         out_specs=[whole()] * 3,
         scratch_shapes=[pltpu.VMEM((ROWS_DEV, query_cols), F32)],
-        compiler_params=params(28),
+        compiler_params=params(8),
         cost_estimate=cost(10000000, 1000000),
         name="attend",
-    )(cache_len, *sums, cos, sin, kv_cache)
+    )(cache_len, terms, cos, sin, kv_cache)
     attn_all = [attn] + others([attn] * 3, "gx")
     parts = pl.pallas_call(
         out_kernel,
-        out_shape=[shape((ROWS_DEV, width), F32)] + [shape((ROWS_DEV, width), BF16)] * 3,
-        in_specs=[whole()] * 4 + [whole(pl.ANY)],
-        out_specs=[whole()] * 4,
-        scratch_shapes=[
-            pltpu.VMEM((query_cols, width), BF16),
-            pltpu.VMEM((4, ROWS_DEV, query_cols), F32),
-            pltpu.SemaphoreType.DMA((2 * query_cols // CHUNK,)),
-        ],
-        compiler_params=params(28),
+        out_shape=shape((4, ROWS_DEV, width), BF16),
+        in_specs=[whole()] * 5,
+        out_specs=whole(),
+        scratch_shapes=[pltpu.VMEM((4, ROWS_DEV, query_cols), F32)],
+        compiler_params=params(8),
         cost_estimate=cost(2 * 8 * width * query_cols, 2 * width * query_cols),
         name="project",
-    )(*attn_all, w_out)
-    arrived = others(parts[1:], "gy")
-    mixed = parts[0] + arrived[0].astype(F32) + arrived[1].astype(F32) + arrived[2].astype(F32)
+    )(*attn_all, pltpu.with_memory_space_constraint(w_out, pltpu.VMEM))
+    arrived = lax.all_to_all(parts, "gy", 0, 0)
+    mixed = jnp.sum(arrived.astype(F32), axis=0)
     return (mixed.astype(BF16), rebuilt_key[None], rebuilt_value[None])
 
 

time: 62.2 us -> 52.9 us (0.85)
  waiting for transfers between devices: 19.5 us -> 9.28 us
  local copies, waits for them, and re-layouts: 14 us -> 5.79 us
  blocking collectives: 0 us -> 6.68 us
  Pallas kernels: 11.8 us -> 14.7 us
    ppermute x15 -> x9, waiting for transfers between devices: 19.5 us -> 3.68 us  [swap(): return lax.ppermute(x, axis, [(i, i ^ k) for i in range(n)])]
    unnamed x22 -> x10, local copies, waits for them, and re-layouts: 14 us -> 5.79 us
    all_to_all x0 -> x1, blocking collectives: none -> 6.68 us  [per_device(): arrived = lax.all_to_all(parts, 'gy', 0, 0)]
    all_to_all x0 -> x1, waiting for transfers between devices: none -> 5.6 us  [per_device(): terms = lax.all_to_all(payload, 'gx', 0, 0)]
    ppermute x15 -> x9, starting transfers between devices: 15.1 us -> 9.65 us  [swap(): return lax.ppermute(x, axis, [(i, i ^ k) for i in range(n)])]
    all_to_all x0 -> x1, starting transfers between devices: none -> 5.12 us  [per_device(): terms = lax.all_to_all(payload, 'gx', 0, 0)]
    pallas_call x4 -> x5, Pallas kernels: 10.3 us -> 13.2 us  [the longest x1 5.93 us: per_device(): pl.pallas_call(load_kernel, out_shape=[pltpu.VMEM((depth, query_cols), BF...]
    reduce_sum x0 -> x1, other arithmetic: none -> 0.67 us  [per_device(): mixed = jnp.sum(arrived.astype(F32), axis=0)]
  transfers between devices with their start and end apart: 15 -> 10, of which waited for: 9 -> 4; matrix products, arithmetic and copies ran while one was open for 0% -> 0% of each run, Pallas kernels for 8% -> 17%
where the time goes in v2:
time: 52.9 us; the launch traced here: 52.6 us
  starting transfers between devices  14.8 us (28%)
  Pallas kernels  14.7 us (28%)
  waiting for transfers between devices  9.28 us (18%)
  blocking collectives  6.68 us (13%)
  local copies, waits for them, and re-layouts  5.79 us (11%)
  between operations  0.74 us (1%)
  other arithmetic  0.67 us (1%)
    ppermute x9, starting transfers between devices, swap(): return lax.ppermute(x, axis, [(i, i ^ k) for i in range(n)])  9.65 us
    all_to_all x1, blocking collectives, per_device(): arrived = lax.all_to_all(parts, 'gy', 0, 0)  6.68 us
    pallas_call x1, Pallas kernels, per_device(): pl.pallas_call(load_kernel, out_shape=[pltpu.VMEM((depth, query_cols), BF...  5.93 us
    unnamed x10, local copies, waits for them, and re-layouts  5.79 us
    all_to_all x1, waiting for transfers between devices, per_device(): terms = lax.all_to_all(payload, 'gx', 0, 0)  5.6 us
    all_to_all x1, starting transfers between devices, per_device(): terms = lax.all_to_all(payload, 'gx', 0, 0)  5.12 us
    ppermute x9, waiting for transfers between devices, swap(): return lax.ppermute(x, axis, [(i, i ^ k) for i in range(n)])  3.68 us
    pallas_call x1, Pallas kernels, per_device(): pl.pallas_call(query_kernel, out_shape=[pltpu.VMEM((4 * ROWS_DEV, heads,...  2.32 us
  transfers between devices with their start and end apart: 10, of which 4 were waited for; matrix products, arithmetic and copies ran while one was open for 0% of the time, Pallas kernels for 17%

profile of v2, /device:TPU:0, one launch (start us, length us, event | category | flops | bytes accessed | tf_op | source)
XLA Modules:
  0.0 52.6 jit_solution(11083603120966978665)
XLA Ops:
  0.6 0.0 copy-start.2
  0.7 0.0 copy-start.3
  0.7 0.0 copy-start.1
  0.7 3.0 %collective-permute-start.1 = (bf16[40,4096]{1,0:T(8,128)(2,1)}, bf16[40,4096]{1,0:T(8,128)(2,1)S(1)}, u32[]{:S(2)}, u32[]{:S(2)}) collective-permute-start(bf16[40,4096]{1,0:T(8,128)(2,1)} %s0.1), channel_id=1, source_target_pairs={{0,2},{1,3},{2,0},{3,1},{4,6},{5,7},{6,4},{7,5},{8,10},{9,11},{10,... | collective-permute-start | bytes 983048 | tf_op jit(solution)/shard_map/ppermute | solution.py:34
  3.7 0.0 collective-permute-start.2
  3.7 0.2 collective-permute-start.3
  3.8 1.7 %collective-permute-start.4 = (bf16[2,4096]{1,0:T(2,128)(2,1)}, bf16[2,4096]{1,0:T(2,128)(2,1)S(1)}, u32[]{:S(2)}, u32[]{:S(2)}) collective-permute-start(bf16[2,4096]{1,0:T(2,128)(2,1)} %b_hbm.1), channel_id=1, source_target_pairs={{0,3},{1,2},{2,1},{3,0},{4,7},{5,6},{6,5},{7,4},{8,11},{9,10},{10,... | collective-permute-start | bytes 49160 | tf_op jit(solution)/shard_map/ppermute | solution.py:34
  5.5 0.3 collective-permute-start
  5.8 5.9 %load.1 = (bf16[4096,2048]{1,0:T(8,128)(2,1)S(1)}, bf16[2,4096]{1,0:T(2,128)(2,1)S(1)}) custom-call(bf16[4096,2048]{1,0:T(8,128)(2,1)} %wq_hbm.1, bf16[2,4096]{1,0:T(2,128)(2,1)} %b_hbm.1), custom_call_target="tpu_custom_call" | custom-call | flops 1000 | bytes 16777216 | tf_op jit(solution)/shard_map/load/pallas_call | solution.py:306
  11.8 0.0 collective-permute-done.2.b1
  11.8 0.3 collective-permute-done.3.b2
  12.1 0.0 collective-permute-done.4.b3
  12.1 0.0 collective-permute-done.1.far.s2
  12.1 0.1 collective-permute-start.5
  12.2 2.3 %query.1 = (f32[8,16,128]{2,1,0:T(8,128)S(1)}, bf16[4096,256]{1,0:T(8,128)(2,1)S(1)}) custom-call(bf16[40,4096]{1,0:T(8,128)(2,1)S(1)} %collective-permute-done.1.far.s2, bf16[2,4096]{1,0:T(2,128)(2,1)S(1)} %get-tuple-element.19.b0, bf16[2,4096]{1,0:T(2,128)(2,1)S(1)} %collective-permute-done.2.b1, bf16[2,4096]{1,0:T(2,128)(2,1)S(1)} %collective-permute-done.3.b2, ...), custom_call_target="tpu_custom_call" | custom-call | flops 134217728 | bytes 2097152 | tf_op jit(solution)/shard_map/query/pallas_call | solution.py:320
  14.6 0.0 collective-permute-done.s1
  14.6 0.0 collective-permute-done.5.s3
  14.6 1.8 %payload.1.ready = bf16[4,128,128]{2,1,0:T(8,128)(2,1)} custom-call(s32[4]{0:T(128)S(1)} %copy-done.4, bf16[40,4096]{1,0:T(8,128)(2,1)S(1)} %copy-done.2, bf16[40,4096]{1,0:T(8,128)(2,1)S(1)} %collective-permute-done.s1, bf16[40,4096]{1,0:T(8,128)(2,1)S(1)} %collective-permute-done.1.far.s2, bf16[40,4096]{1,0:T(8,128)(2,1)S(1)} %collective-permute-done.5.s3, ...), custom_call_target="tpu_custom_call" | custom-call | flops 436207616 | bytes 2097152 | tf_op jit(solution)/shard_map/payload/pallas_call | solution.py:333
  16.5 5.1 %all-to-all-start = ((bf16[4,128,128]{2,1,0:T(8,128)(2,1)}), bf16[4,128,128]{2,1,0:T(8,128)(2,1)S(1)}, u32[]{:S(2)}, u32[]{:S(2)}) async-start(bf16[4,128,128]{2,1,0:T(8,128)(2,1)} %payload.1.ready), calls=%async_computation | async-start | bytes 262144 | tf_op jit(solution)/shard_map/all_to_all | solution.py:346
  21.6 0.8 %angles.1 = (f32[128,128]{1,0:T(8,128)S(1)}, f32[128,128]{1,0:T(8,128)S(1)}) custom-call(bf16[4,128,128]{2,1,0:T(8,128)(2,1)} %payload.1.ready, s32[2]{0:T(128)} %len_ref.3), custom_call_target="tpu_custom_call" | custom-call | flops 2000000 | bytes 100000 | tf_op jit(solution)/shard_map/angles/pallas_call | solution.py:347
  22.4 5.6 %all-to-all-done.terms = bf16[4,128,128]{2,1,0:T(8,128)(2,1)S(1)} async-done(((bf16[4,128,128]{2,1,0:T(8,128)(2,1)}), bf16[4,128,128]{2,1,0:T(8,128)(2,1)S(1)}, u32[]{:S(2)}, u32[]{:S(2)}) %all-to-all-start) | async-done | bytes 131104 | tf_op jit(solution)/shard_map/all_to_all | solution.py:346
  28.0 1.5 %attend.1 = (bf16[40,128]{1,0:T(8,128)(2,1)}, bf16[40,128]{1,0:T(8,128)(2,1)}, bf16[2,2048]{1,0:T(2,128)(2,1)S(1)}) custom-call(s32[2]{0:T(128)S(1)} %copy-done.3, bf16[4,128,128]{2,1,0:T(8,128)(2,1)S(1)} %all-to-all-done.terms, f32[128,128]{1,0:T(8,128)S(1)} %get-tuple-element.26.cos_ref, f32[128,128]{1,0:T(8,128)S(1)} %get-tuple-element.27.sin_ref, ...), custom_call_target="tpu_custom_call" | custom-call | flops 10000000 | bytes 1000000 | tf_op jit(solution)/shard_map/attend/pallas_call | solution.py:355
  29.5 1.0 %collective-permute-start.6 = (bf16[2,2048]{1,0:T(2,128)(2,1)S(1)}, bf16[2,2048]{1,0:T(2,128)(2,1)S(1)}, u32[]{:S(2)}, u32[]{:S(2)}) collective-permute-start(bf16[2,2048]{1,0:T(2,128)(2,1)S(1)} %get-tuple-element.28.a0), channel_id=1, source_target_pairs={{0,4},{4,0},{8,12},{12,8},{1,5},{5,1},{9,13},{13,9},{2,6},{6,2},{1... | collective-permute-start | bytes 24584 | tf_op jit(solution)/shard_map/ppermute | solution.py:34
  30.5 1.3 %collective-permute-start.7 = (bf16[2,2048]{1,0:T(2,128)(2,1)S(1)}, bf16[2,2048]{1,0:T(2,128)(2,1)S(1)}, u32[]{:S(2)}, u32[]{:S(2)}) collective-permute-start(bf16[2,2048]{1,0:T(2,128)(2,1)S(1)} %get-tuple-element.28.a0), channel_id=1, source_target_pairs={{0,8},{4,12},{8,0},{12,4},{1,9},{5,13},{9,1},{13,5},{2,10},{6,14},... | collective-permute-start | bytes 24584 | tf_op jit(solution)/shard_map/ppermute | solution.py:34
  31.8 2.1 %collective-permute-start.8 = (bf16[2,2048]{1,0:T(2,128)(2,1)S(1)}, bf16[2,2048]{1,0:T(2,128)(2,1)S(1)}, u32[]{:S(2)}, u32[]{:S(2)}) collective-permute-start(bf16[2,2048]{1,0:T(2,128)(2,1)S(1)} %get-tuple-element.28.a0), channel_id=1, source_target_pairs={{0,12},{4,8},{8,4},{12,0},{1,13},{5,9},{9,5},{13,1},{2,14},{6,10},... | collective-permute-start | bytes 24584 | tf_op jit(solution)/shard_map/ppermute | solution.py:34
  33.9 0.0 collective-permute-done.6.a1
  33.9 1.2 %collective-permute-done.7.a2 = bf16[2,2048]{1,0:T(2,128)(2,1)S(1)} collective-permute-done((bf16[2,2048]{1,0:T(2,128)(2,1)S(1)}, bf16[2,2048]{1,0:T(2,128)(2,1)S(1)}, u32[]{:S(2)}, u32[]{:S(2)}) %collective-permute-start.7) | collective-permute-done | bytes 8224 | tf_op jit(solution)/shard_map/ppermute | solution.py:34
  35.1 2.2 %collective-permute-done.8.a3 = bf16[2,2048]{1,0:T(2,128)(2,1)S(1)} collective-permute-done((bf16[2,2048]{1,0:T(2,128)(2,1)S(1)}, bf16[2,2048]{1,0:T(2,128)(2,1)S(1)}, u32[]{:S(2)}, u32[]{:S(2)}) %collective-permute-start.8) | collective-permute-done | bytes 8224 | tf_op jit(solution)/shard_map/ppermute | solution.py:34
  37.2 5.8 %copy-done = bf16[2048,4096]{1,0:T(8,128)(2,1)S(1)} copy-done((bf16[2048,4096]{1,0:T(8,128)(2,1)S(1)}, bf16[2048,4096]{1,0:T(8,128)(2,1)}, u32[]{:S(2)}) %copy-start) | copy-done | bytes 16777240
  43.0 2.3 %project.1 = bf16[4,2,4096]{2,1,0:T(2,128)(2,1)S(1)} custom-call(bf16[2,2048]{1,0:T(2,128)(2,1)S(1)} %get-tuple-element.28.a0, bf16[2,2048]{1,0:T(2,128)(2,1)S(1)} %collective-permute-done.6.a1, bf16[2,2048]{1,0:T(2,128)(2,1)S(1)} %collective-permute-done.7.a2, bf16[2,2048]{1,0:T(2,128)(2,1)S(1)} %collective-permute-done.8.a3, bf16[2048,4096]{1,0:T(8,128)(2,1)S(1)} %copy-done), custom_call_target="tpu_custom_call" | custom-call | flops 134217728 | bytes 16777216 | tf_op jit(solution)/shard_map/project/pallas_call | solution.py:366
  45.3 6.7 %all_to_all.10 = bf16[4,2,4096]{2,1,0:T(2,128)(2,1)S(1)} all-to-all(bf16[4,2,4096]{2,1,0:T(2,128)(2,1)S(1)} %project.1), channel_id=1, replica_groups=mesh['groups'=2,'gx'=4,'gy'=4] {'gy'}, dimensions={0} | all-to-all | bytes 131072 | tf_op jit(solution)/shard_map/all_to_all | solution.py:376
  52.0 0.7 %reduce_sum.12 = bf16[2,4096]{1,0:T(2,128)(2,1)} reduce(bf16[4,2,4096]{2,1,0:T(2,128)(2,1)S(1)} %all_to_all.10, bf16[]{:T(256)} %constant.2.clone.1), dimensions={0}, to_apply=%region_0.0 | reduce | flops 24576 | bytes 81922 | tf_op jit(solution)/shard_map/reduce_sum | solution.py:377
  (6 shorter events, 0.0 us)
Async XLA Ops:
  0.6 14.0 %copy-start.2 = (bf16[40,4096]{1,0:T(8,128)(2,1)S(1)}, bf16[40,4096]{1,0:T(8,128)(2,1)}, u32[]{:S(2)}) copy-start(bf16[40,4096]{1,0:T(8,128)(2,1)} %s0.1) | copy-start | bytes 983044
  0.6 14.0 %copy-start.4 = (s32[4]{0:T(128)S(1)}, s32[4]{0:T(128)}, u32[]{:S(2)}) copy-start(s32[4]{0:T(128)} %owner_ref.1) | copy-start | bytes 52
  0.7 27.3 %copy-start.3 = (s32[2]{0:T(128)S(1)}, s32[2]{0:T(128)}, u32[]{:S(2)}) copy-start(s32[2]{0:T(128)} %len_ref.3) | copy-start | bytes 28
  0.7 27.3 %copy-start.1 = (bf16[2,2,512,128]{3,2,1,0:T(8,128)(2,1)S(1)}, bf16[2,2,512,128]{3,2,1,0:T(8,128)(2,1)}, u32[]{:S(2)}) copy-start(bf16[2,2,512,128]{3,2,1,0:T(8,128)(2,1)} %kv.1) | copy-start | bytes 1572868
  0.7 11.5 %collective-permute-start.1 = (bf16[40,4096]{1,0:T(8,128)(2,1)}, bf16[40,4096]{1,0:T(8,128)(2,1)S(1)}, u32[]{:S(2)}, u32[]{:S(2)}) collective-permute-start(bf16[40,4096]{1,0:T(8,128)(2,1)} %s0.1), channel_id=1, source_target_pairs={{0,2},{1,3},{2,0},{3,1},{4,6},{5,7},{6,4},{7,5},{8,10},{9,11},{10,... | collective-permute-start | bytes 983048 | tf_op jit(solution)/shard_map/ppermute | solution.py:34
  3.7 8.1 %collective-permute-start.2 = (bf16[2,4096]{1,0:T(2,128)(2,1)}, bf16[2,4096]{1,0:T(2,128)(2,1)S(1)}, u32[]{:S(2)}, u32[]{:S(2)}) collective-permute-start(bf16[2,4096]{1,0:T(2,128)(2,1)} %b_hbm.1), channel_id=1, source_target_pairs={{0,1},{1,0},{2,3},{3,2},{4,5},{5,4},{6,7},{7,6},{8,9},{9,8},{10,11... | collective-permute-start | bytes 49160 | tf_op jit(solution)/shard_map/ppermute | solution.py:34
  3.7 8.4 %collective-permute-start.3 = (bf16[2,4096]{1,0:T(2,128)(2,1)}, bf16[2,4096]{1,0:T(2,128)(2,1)S(1)}, u32[]{:S(2)}, u32[]{:S(2)}) collective-permute-start(bf16[2,4096]{1,0:T(2,128)(2,1)} %b_hbm.1), channel_id=1, source_target_pairs={{0,2},{1,3},{2,0},{3,1},{4,6},{5,7},{6,4},{7,5},{8,10},{9,11},{10,... | collective-permute-start | bytes 49160 | tf_op jit(solution)/shard_map/ppermute | solution.py:34
  3.8 8.3 %collective-permute-start.4 = (bf16[2,4096]{1,0:T(2,128)(2,1)}, bf16[2,4096]{1,0:T(2,128)(2,1)S(1)}, u32[]{:S(2)}, u32[]{:S(2)}) collective-permute-start(bf16[2,4096]{1,0:T(2,128)(2,1)} %b_hbm.1), channel_id=1, source_target_pairs={{0,3},{1,2},{2,1},{3,0},{4,7},{5,6},{6,5},{7,4},{8,11},{9,10},{10,... | collective-permute-start | bytes 49160 | tf_op jit(solution)/shard_map/ppermute | solution.py:34
  5.5 9.0 %collective-permute-start = (bf16[40,4096]{1,0:T(8,128)(2,1)}, bf16[40,4096]{1,0:T(8,128)(2,1)S(1)}, u32[]{:S(2)}, u32[]{:S(2)}) collective-permute-start(bf16[40,4096]{1,0:T(8,128)(2,1)} %s0.1), channel_id=1, source_target_pairs={{0,1},{1,0},{2,3},{3,2},{4,5},{5,4},{6,7},{7,6},{8,9},{9,8},{10,11... | collective-permute-start | bytes 983048 | tf_op jit(solution)/shard_map/ppermute | solution.py:34
  12.1 2.5 %collective-permute-start.5 = (bf16[40,4096]{1,0:T(8,128)(2,1)S(1)}, bf16[40,4096]{1,0:T(8,128)(2,1)S(1)}, u32[]{:S(2)}, u32[]{:S(2)}) collective-permute-start(bf16[40,4096]{1,0:T(8,128)(2,1)S(1)} %collective-permute-done.1.far.s2), channel_id=1, source_target_pairs={{0,1},{1,0},{2,3},{3,2},{4,5},{5,4},{6,7},{7,6},{8,9},{9,8},{10,11... | collective-permute-start | bytes 983048 | tf_op jit(solution)/shard_map/ppermute | solution.py:34
  16.5 11.5 %all-to-all-start = ((bf16[4,128,128]{2,1,0:T(8,128)(2,1)}), bf16[4,128,128]{2,1,0:T(8,128)(2,1)S(1)}, u32[]{:S(2)}, u32[]{:S(2)}) async-start(bf16[4,128,128]{2,1,0:T(8,128)(2,1)} %payload.1.ready), calls=%async_computation | async-start | bytes 262144 | tf_op jit(solution)/shard_map/all_to_all | solution.py:346
  29.5 4.4 %collective-permute-start.6 = (bf16[2,2048]{1,0:T(2,128)(2,1)S(1)}, bf16[2,2048]{1,0:T(2,128)(2,1)S(1)}, u32[]{:S(2)}, u32[]{:S(2)}) collective-permute-start(bf16[2,2048]{1,0:T(2,128)(2,1)S(1)} %get-tuple-element.28.a0), channel_id=1, source_target_pairs={{0,4},{4,0},{8,12},{12,8},{1,5},{5,1},{9,13},{13,9},{2,6},{6,2},{1... | collective-permute-start | bytes 24584 | tf_op jit(solution)/shard_map/ppermute | solution.py:34
  30.5 4.5 %collective-permute-start.7 = (bf16[2,2048]{1,0:T(2,128)(2,1)S(1)}, bf16[2,2048]{1,0:T(2,128)(2,1)S(1)}, u32[]{:S(2)}, u32[]{:S(2)}) collective-permute-start(bf16[2,2048]{1,0:T(2,128)(2,1)S(1)} %get-tuple-element.28.a0), channel_id=1, source_target_pairs={{0,8},{4,12},{8,0},{12,4},{1,9},{5,13},{9,1},{13,5},{2,10},{6,14},... | collective-permute-start | bytes 24584 | tf_op jit(solution)/shard_map/ppermute | solution.py:34
  31.8 5.4 %collective-permute-start.8 = (bf16[2,2048]{1,0:T(2,128)(2,1)S(1)}, bf16[2,2048]{1,0:T(2,128)(2,1)S(1)}, u32[]{:S(2)}, u32[]{:S(2)}) collective-permute-start(bf16[2,2048]{1,0:T(2,128)(2,1)S(1)} %get-tuple-element.28.a0), channel_id=1, source_target_pairs={{0,12},{4,8},{8,4},{12,0},{1,13},{5,9},{9,5},{13,1},{2,14},{6,10},... | collective-permute-start | bytes 24584 | tf_op jit(solution)/shard_map/ppermute | solution.py:34
  37.2 5.8 %copy-start = (bf16[2048,4096]{1,0:T(8,128)(2,1)S(1)}, bf16[2048,4096]{1,0:T(8,128)(2,1)}, u32[]{:S(2)}) copy-start(bf16[2048,4096]{1,0:T(8,128)(2,1)} %w.1) | copy-start | bytes 50331652

commit v3 on v2

--- a/solution.py
+++ b/solution.py
@@ -167,7 +167,7 @@
     return pl.CostEstimate(flops=flops, bytes_accessed=bytes_accessed, transcendentals=0)
 
 
-def angle_kernel(ready, len_ref, cos_ref, sin_ref):
+def angles(len_ref, cos_ref, sin_ref):
     first, second = len_ref[0], len_ref[1]
     row = lax.broadcasted_iota(jnp.int32, (PAY, HD), 0)
     lane = lax.broadcasted_iota(jnp.int32, (PAY, HD), 1)
@@ -194,16 +194,18 @@
     return copies
 
 
-def load_kernel(wq_hbm, b_hbm, wq, b, sems):
-    copies = start_load(wq_hbm, wq, sems, 0, 8)
-    copies += start_load(b_hbm, b, sems, 8, 1)
+def load_kernel(wo_hbm, wk_hbm, wv_hbm, b_hbm, wo, wkv, b, sems):
+    copies = start_load(b_hbm, b, sems, 0, 1)
+    copies += start_load(wk_hbm, wkv.at[:, pl.ds(0, HD)], sems, 1, 1)
+    copies += start_load(wv_hbm, wkv.at[:, pl.ds(HD, HD)], sems, 2, 1)
+    copies += start_load(wo_hbm.at[pl.ds(0, wo.shape[0])], wo, sems, 3, 2)
     for copy in copies:
         copy.wait()
 
 
-def query_kernel(far, b0, b1, b2, b3, w, wk_hbm, wv_hbm, out_ref, wkv, acc, sems):
-    copies = start_load(wk_hbm, wkv.at[:, pl.ds(0, HD)], sems, 0, 1)
-    copies += start_load(wv_hbm, wkv.at[:, pl.ds(HD, HD)], sems, 1, 1)
+def query_kernel(far, b0, b1, b2, b3, w, wo_hbm, out_ref, wo, acc, sems):
+    rows = wo.shape[0]
+    copies = start_load(wo_hbm.at[pl.ds(rows, rows)], wo, sems, 0, 2)
     lhs = jnp.concatenate([b[...].astype(F32) for b in (b0, b1, b2, b3)], axis=0).astype(BF16)
     acc[...] = jnp.dot(lhs, w[...], preferred_element_type=F32)
     for r in range(acc.shape[0]):
@@ -213,10 +215,18 @@
         copy.wait()
 
 
+def rest_kernel(ready, len_ref, wo_hbm, cos_ref, sin_ref, wo, sems):
+    rows = wo.shape[0]
+    copies = start_load(wo_hbm.at[pl.ds(wo_hbm.shape[0] - rows, rows)], wo, sems, 0, 4)
+    angles(len_ref, cos_ref, sin_ref)
+    for copy in copies:
+        copy.wait()
+
+
 def payload_kernel(
-    owner_ref, s0, s1, s2, s3, b0, b1, b2, b3, wkv, q_ref, out, x, pay
+    owner_ref, s0, s1, s2, s3, b0, b1, b2, b3, wkv, q_ref, o0, o1, o2, o3, x, pay
 ):
-    gy = lax.axis_index("gy")
+    gx, gy = lax.axis_index("gx"), lax.axis_index("gy")
     stored = (s0, s1, s2, s3)
     for k, s in enumerate(stored):
         x[pl.ds(k * ROW_TILE, LC), :] = s[...]
@@ -232,22 +242,25 @@
     empty = jnp.zeros((8 - ROWS_DEV, HD), F32)
     for k in range(len(stored)):
         rows = slice(k * ROW_TILE, k * ROW_TILE + LC)
-        target = owner_ref[gy ^ k]
+        target = owner_ref[gy ^ k] ^ gx
         pay[target, pl.ds(0, LC), :] = key[rows]
         pay[target, pl.ds(VALUES, LC), :] = value[rows]
         rows = slice(base + k * ROWS_DEV, base + (k + 1) * ROWS_DEV)
-        target = k ^ gy
+        target = k ^ gx ^ gy
         pay[target, pl.ds(LC, 8), :] = jnp.concatenate([key[rows], empty], axis=0)
         pay[target, pl.ds(VALUES + LC, 8), :] = jnp.concatenate([value[rows], empty], axis=0)
         for r in range(ROWS_DEV):
             pay[target, pl.ds(QUERY + 16 * r, 16), :] = q_ref[k * ROWS_DEV + r]
-    out[...] = pay[...].astype(BF16)
+    o0[...] = pay[0]
+    o1[...] = pay[1].astype(BF16)
+    o2[...] = pay[2].astype(BF16)
+    o3[...] = pay[3].astype(BF16)
 
 
 def attend_kernel(
-    len_ref, terms, cos_ref, sin_ref, kv, key_out, value_out, attn_out, attn
+    len_ref, ready, p0, p1, p2, p3, cos_ref, sin_ref, kv, key_out, value_out, attn_out, attn
 ):
-    total = jnp.sum(terms[...].astype(F32), axis=0)
+    total = p0[...] + p1[...].astype(F32) + p2[...].astype(F32) + p3[...].astype(F32)
     turned = total * cos_ref[...] + pltpu.roll(total, HD // 2, 1) * sin_ref[...]
     turned = turned.astype(BF16)
     key_out[...] = turned[:LC]
@@ -279,14 +292,21 @@
     attn_out[...] = attn[...].astype(BF16)
 
 
-def out_kernel(a0, a1, a2, a3, w, out, blocks):
-    gx = lax.axis_index("gx")
+def out_kernel(a0, a1, a2, a3, w0, w1, w2, o0, o1, o2, o3, blocks):
+    tag = lax.axis_index("gx") ^ lax.axis_index("gy")
     for s, a in enumerate((a0, a1, a2, a3)):
-        blocks[s ^ gx] = a[...].astype(F32)
+        blocks[s ^ tag] = a[...].astype(F32)
     lhs = jnp.concatenate([blocks[k] for k in range(4)], axis=0).astype(BF16)
-    acc = jnp.dot(lhs, w[...], preferred_element_type=F32)
-    for k in range(4):
-        out[k] = acc[k * ROWS_DEV : (k + 1) * ROWS_DEV].astype(BF16)
+    first = 0
+    acc = jnp.zeros((lhs.shape[0], w0.shape[1]), F32)
+    for w in (w0, w1, w2):
+        last = first + w.shape[0]
+        acc += jnp.dot(lhs[:, first:last], w[...], preferred_element_type=F32)
+        first = last
+    o0[...] = acc[0:2]
+    o1[...] = acc[2:4].astype(BF16)
+    o2[...] = acc[4:6].astype(BF16)
+    o3[...] = acc[6:8].astype(BF16)
 
 
 def others(blocks, axis):
@@ -298,43 +318,49 @@
     depth, query_cols = w_query.shape
     width = w_out.shape[1]
     heads = query_cols // HD
+    cut = query_cols * 5 // 16
     semaphores = pltpu.SemaphoreType.DMA
+    in_vmem = lambda x: pltpu.with_memory_space_constraint(x, pltpu.VMEM)
     in_hbm = lambda x: pltpu.with_memory_space_constraint(x, pltpu.HBM)
     far = swap(stored_rows, "gy", 2)
     near = swap(stored_rows, "gy", 1)
     fresh = others([new_rows] * 3, "gy")
-    wq, own_fresh = pl.pallas_call(
+    wo_first, wkv, own_fresh = pl.pallas_call(
         load_kernel,
-        out_shape=[pltpu.VMEM((depth, query_cols), BF16), pltpu.VMEM(new_rows.shape, BF16)],
-        in_specs=[whole(pltpu.HBM)] * 2,
-        out_specs=[whole()] * 2,
-        scratch_shapes=[semaphores((9,))],
-        compiler_params=params(8),
+        out_shape=[
+            pltpu.VMEM((cut, width), BF16),
+            pltpu.VMEM((depth, 2 * HD), BF16),
+            pltpu.VMEM(new_rows.shape, BF16),
+        ],
+        in_specs=[whole(pltpu.HBM)] * 4,
+        out_specs=[whole()] * 3,
+        scratch_shapes=[semaphores((5,))],
+        compiler_params=params(4),
         cost_estimate=cost(1000, 2 * depth * query_cols),
         name="load",
-    )(in_hbm(w_query), in_hbm(new_rows))
+    )(in_hbm(w_out), in_hbm(w_key), in_hbm(w_value), in_hbm(new_rows))
     far, own_fresh, *fresh = lax.optimization_barrier((far, own_fresh, *fresh))
     far_near = swap(far, "gy", 1)
     fresh = [own_fresh] + fresh
     stored = [stored_rows, near, far, far_near]
-    query, wkv = pl.pallas_call(
+    query, wo_second = pl.pallas_call(
         query_kernel,
         out_shape=[
             pltpu.VMEM((4 * ROWS_DEV, heads, HD), F32),
-            pltpu.VMEM((depth, 2 * HD), BF16),
+            pltpu.VMEM((cut, width), BF16),
         ],
-        in_specs=[whole(pl.ANY)] + [whole()] * 5 + [whole(pltpu.HBM)] * 2,
+        in_specs=[whole(pl.ANY)] + [whole()] * 5 + [whole(pltpu.HBM)],
         out_specs=[whole()] * 2,
         scratch_shapes=[pltpu.VMEM((4 * ROWS_DEV, query_cols), F32), semaphores((2,))],
-        compiler_params=params(8),
+        compiler_params=params(4),
         cost_estimate=cost(2 * 8 * depth * query_cols, 4 * depth * HD),
         name="query",
-    )(far, *fresh, wq, in_hbm(w_key), in_hbm(w_value))
+    )(far, *fresh, in_vmem(w_query), in_hbm(w_out))
     payload = pl.pallas_call(
         payload_kernel,
-        out_shape=shape((4, PAY, HD), BF16),
+        out_shape=[shape((PAY, HD), F32)] + [shape((PAY, HD), BF16)] * 3,
         in_specs=[whole(pltpu.SMEM)] + [whole()] * 10,
-        out_specs=whole(),
+        out_specs=[whole()] * 4,
         scratch_shapes=[
             pltpu.VMEM((4 * ROW_TILE + 16, depth), BF16),
             pltpu.VMEM((4, PAY, HD), F32),
@@ -343,38 +369,41 @@
         cost_estimate=cost(2 * 208 * depth * 256, 4 * depth * HD),
         name="payload",
     )(owner, *stored, *fresh, wkv, query)
-    terms = lax.all_to_all(payload, "gx", 0, 0)
-    cos, sin = pl.pallas_call(
-        angle_kernel,
-        out_shape=[pltpu.VMEM((PAY, HD), F32)] * 2,
-        in_specs=[whole(pl.ANY), whole(pltpu.SMEM)],
-        out_specs=[whole()] * 2,
-        cost_estimate=cost(2000000, 100000),
-        name="angles",
-    )(payload, cache_len)
+    sums = [payload[0]] + others(payload[1:], "gx")
+    cos, sin, wo_third = pl.pallas_call(
+        rest_kernel,
+        out_shape=[pltpu.VMEM((PAY, HD), F32)] * 2
+        + [pltpu.VMEM((query_cols - 2 * cut, width), BF16)],
+        in_specs=[whole(pl.ANY), whole(pltpu.SMEM), whole(pltpu.HBM)],
+        out_specs=[whole()] * 3,
+        scratch_shapes=[semaphores((4,))],
+        compiler_params=params(4),
+        cost_estimate=cost(2000000, 2 * (query_cols - 2 * cut) * width),
+        name="rest",
+    )(payload[0], cache_len, in_hbm(w_out))
     rebuilt_key, rebuilt_value, attn = pl.pallas_call(
         attend_kernel,
         out_shape=[shape((LC, HD), BF16)] * 2 + [shape((ROWS_DEV, query_cols), BF16)],
-        in_specs=[whole(pltpu.SMEM)] + [whole()] * 4,
+        in_specs=[whole(pltpu.SMEM), whole(pl.ANY)] + [whole()] * 7,
         out_specs=[whole()] * 3,
         scratch_shapes=[pltpu.VMEM((ROWS_DEV, query_cols), F32)],
-        compiler_params=params(8),
+        compiler_params=params(4),
         cost_estimate=cost(10000000, 1000000),
         name="attend",
-    )(cache_len, terms, cos, sin, kv_cache)
+    )(cache_len, wo_third, *sums, cos, sin, kv_cache)
     attn_all = [attn] + others([attn] * 3, "gx")
     parts = pl.pallas_call(
         out_kernel,
-        out_shape=shape((4, ROWS_DEV, width), BF16),
-        in_specs=[whole()] * 5,
-        out_specs=whole(),
+        out_shape=[shape((ROWS_DEV, width), F32)] + [shape((ROWS_DEV, width), BF16)] * 3,
+        in_specs=[whole()] * 7,
+        out_specs=[whole()] * 4,
         scratch_shapes=[pltpu.VMEM((4, ROWS_DEV, query_cols), F32)],
-        compiler_params=params(8),
+        compiler_params=params(4),
         cost_estimate=cost(2 * 8 * width * query_cols, 2 * width * query_cols),
         name="project",
-    )(*attn_all, pltpu.with_memory_space_constraint(w_out, pltpu.VMEM))
-    arrived = lax.all_to_all(parts, "gy", 0, 0)
-    mixed = jnp.sum(arrived.astype(F32), axis=0)
+    )(*attn_all, wo_first, wo_second, wo_third)
+    arrived = others(parts[1:], "gy")
+    mixed = parts[0] + arrived[0].astype(F32) + arrived[1].astype(F32) + arrived[2].astype(F32)
     return (mixed.astype(BF16), rebuilt_key[None], rebuilt_value[None])
 
 

time: 52.9 us -> 41.8 us (0.79)
  blocking collectives: 6.68 us -> 0 us
  local copies, waits for them, and re-layouts: 5.79 us -> 0.02 us
  starting transfers between devices: 14.8 us -> 16 us
  waiting for transfers between devices: 9.28 us -> 10.1 us
    all_to_all x1 -> x0, blocking collectives: 6.68 us -> none  [per_device(): arrived = lax.all_to_all(parts, 'gy', 0, 0)]
    ppermute x9 -> x15, waiting for transfers between devices: 3.68 us -> 10.1 us  [swap(): return lax.ppermute(x, axis, [(i, i ^ k) for i in range(n)])]
    ppermute x9 -> x15, starting transfers between devices: 9.65 us -> 16 us  [swap(): return lax.ppermute(x, axis, [(i, i ^ k) for i in range(n)])]
    unnamed x10, local copies, waits for them, and re-layouts: 5.79 us -> 0.02 us
    all_to_all x1 -> x0, waiting for transfers between devices: 5.6 us -> none  [per_device(): terms = lax.all_to_all(payload, 'gx', 0, 0)]
    all_to_all x1 -> x0, starting transfers between devices: 5.12 us -> none  [per_device(): terms = lax.all_to_all(payload, 'gx', 0, 0)]
    pallas_call x4, Pallas kernels: 10.9 us -> 10.1 us  [the longest x1 3.41 us: per_device(): pl.pallas_call(rest_kernel, out_shape=[pltpu.VMEM((PAY, HD), F32)] * 2 +...]
    reduce_sum x1 -> x0, other arithmetic: 0.67 us -> none  [per_device(): mixed = jnp.sum(arrived.astype(F32), axis=0)]
  transfers between devices with their start and end apart: 10 -> 15, of which waited for: 4 -> 7; matrix products, arithmetic and copies ran while one was open for 0% -> 0% of each run, Pallas kernels for 17% -> 22%
where the time goes in v3:
time: 41.8 us; the launch traced here: 41.7 us
  starting transfers between devices  16 us (38%)
  Pallas kernels  14.2 us (34%)
  waiting for transfers between devices  10.1 us (24%)
  between operations  0.76 us (2%)
  other arithmetic  0.64 us (2%)
    ppermute x15, starting transfers between devices, swap(): return lax.ppermute(x, axis, [(i, i ^ k) for i in range(n)])  16 us
    ppermute x15, waiting for transfers between devices, swap(): return lax.ppermute(x, axis, [(i, i ^ k) for i in range(n)])  10.1 us
    pallas_call x1, Pallas kernels, per_device(): pl.pallas_call(rest_kernel, out_shape=[pltpu.VMEM((PAY, HD), F32)] * 2 +...  3.41 us
    pallas_call x1, Pallas kernels, per_device(): pl.pallas_call(load_kernel, out_shape=[pltpu.VMEM((cut, width), BF16), pl...  3.24 us
    pallas_call x1, Pallas kernels, per_device(): pl.pallas_call(query_kernel, out_shape=[pltpu.VMEM((4 * ROWS_DEV, heads,...  2.58 us
    pallas_call x1, Pallas kernels, per_device(): pl.pallas_call(out_kernel, out_shape=[shape((ROWS_DEV, width), F32)] + [s...  2.28 us
    pallas_call x1, Pallas kernels, per_device(): pl.pallas_call(attend_kernel, out_shape=[shape((LC, HD), BF16)] * 2 + [sh...  1.53 us
    pallas_call x1, Pallas kernels, per_device(): pl.pallas_call(payload_kernel, out_shape=[shape((PAY, HD), F32)] + [shape...  1.19 us
  transfers between devices with their start and end apart: 15, of which 7 were waited for; matrix products, arithmetic and copies ran while one was open for 0% of the time, Pallas kernels for 22%

profile of v3, /device:TPU:0, one launch (start us, length us, event | category | flops | bytes accessed | tf_op | source)
XLA Modules:
  0.0 41.7 jit_solution(7721707605439929747)
XLA Ops:
  0.6 3.0 %collective-permute-start.1 = (bf16[40,4096]{1,0:T(8,128)(2,1)}, bf16[40,4096]{1,0:T(8,128)(2,1)S(1)}, u32[]{:S(2)}, u32[]{:S(2)}) collective-permute-start(bf16[40,4096]{1,0:T(8,128)(2,1)} %s0.1), channel_id=1, source_target_pairs={{0,2},{1,3},{2,0},{3,1},{4,6},{5,7},{6,4},{7,5},{8,10},{9,11},{10,... | collective-permute-start | bytes 983048 | tf_op jit(solution)/shard_map/ppermute | solution.py:34
  3.6 0.0 collective-permute-start.2
  3.6 0.2 collective-permute-start.4
  3.9 1.9 %collective-permute-start.3 = (bf16[2,4096]{1,0:T(2,128)(2,1)}, bf16[2,4096]{1,0:T(2,128)(2,1)S(1)}, u32[]{:S(2)}, u32[]{:S(2)}) collective-permute-start(bf16[2,4096]{1,0:T(2,128)(2,1)} %b_hbm.1), channel_id=1, source_target_pairs={{0,2},{1,3},{2,0},{3,1},{4,6},{5,7},{6,4},{7,5},{8,10},{9,11},{10,... | collective-permute-start | bytes 49160 | tf_op jit(solution)/shard_map/ppermute | solution.py:34
  5.8 0.0 collective-permute-start
  5.8 3.2 %load.1 = (bf16[640,4096]{1,0:T(8,128)(2,1)S(1)}, bf16[4096,256]{1,0:T(8,128)(2,1)S(1)}, bf16[2,4096]{1,0:T(2,128)(2,1)S(1)}) custom-call(bf16[2048,4096]{1,0:T(8,128)(2,1)} %wo_hbm.5, bf16[4096,128]{1,0:T(8,128)(2,1)} %wk_hbm.1, bf16[4096,128]{1,0:T(8,128)(2,1)} %wv_hbm.1, bf16[2,4096]{1,0:T(2,128)(2,1)} %b_hbm.1), custom_call_target="tpu_custom_call" | custom-call | flops 1000 | bytes 16777216 | tf_op jit(solution)/shard_map/load/pallas_call | solution.py:328
  9.0 2.3 %collective-permute-done.4.b3 = bf16[2,4096]{1,0:T(2,128)(2,1)S(1)} collective-permute-done((bf16[2,4096]{1,0:T(2,128)(2,1)}, bf16[2,4096]{1,0:T(2,128)(2,1)S(1)}, u32[]{:S(2)}, u32[]{:S(2)}) %collective-permute-start.4) | collective-permute-done | bytes 16416 | tf_op jit(solution)/shard_map/ppermute | solution.py:34
  11.4 0.9 %collective-permute-done.3.b2 = bf16[2,4096]{1,0:T(2,128)(2,1)S(1)} collective-permute-done((bf16[2,4096]{1,0:T(2,128)(2,1)}, bf16[2,4096]{1,0:T(2,128)(2,1)S(1)}, u32[]{:S(2)}, u32[]{:S(2)}) %collective-permute-start.3) | collective-permute-done | bytes 16416 | tf_op jit(solution)/shard_map/ppermute | solution.py:34
  12.3 0.0 collective-permute-done.1.far.s2
  12.3 0.1 collective-permute-start.5
  12.4 0.0 copy-done
  12.4 2.6 %query.1 = (f32[8,16,128]{2,1,0:T(8,128)S(1)}, bf16[640,4096]{1,0:T(8,128)(2,1)S(1)}) custom-call(bf16[40,4096]{1,0:T(8,128)(2,1)S(1)} %collective-permute-done.1.far.s2, bf16[2,4096]{1,0:T(2,128)(2,1)S(1)} %get-tuple-element.29.b0, bf16[2,4096]{1,0:T(2,128)(2,1)S(1)} %collective-permute-done.2.b1, bf16[2,4096]{1,0:T(2,128)(2,1)S(1)} %collective-permute-done.3.b2, ...), custom_call_target="tpu_custom_call" | custom-call | flops 134217728 | bytes 2097152 | tf_op jit(solution)/shard_map/query/pallas_call | solution.py:346
  15.0 0.0 collective-permute-done.s1
  15.0 1.2 %payload.1 = (f32[128,128]{1,0:T(8,128)S(1)}, bf16[128,128]{1,0:T(8,128)(2,1)S(1)}, bf16[128,128]{1,0:T(8,128)(2,1)S(1)}, bf16[128,128]{1,0:T(8,128)(2,1)S(1)}) custom-call(s32[4]{0:T(128)S(1)} %copy-done.4, bf16[40,4096]{1,0:T(8,128)(2,1)S(1)} %copy-done.2, bf16[40,4096]{1,0:T(8,128)(2,1)S(1)} %collective-permute-done.s1, ...), custom_call_target="tpu_custom_call" | custom-call | flops 436207616 | bytes 2097152 | tf_op jit(solution)/shard_map/payload/pallas_call | solution.py:359
  16.2 1.9 %collective-permute-start.6 = (bf16[128,128]{1,0:T(8,128)(2,1)S(1)}, bf16[128,128]{1,0:T(8,128)(2,1)S(1)}, u32[]{:S(2)}, u32[]{:S(2)}) collective-permute-start(bf16[128,128]{1,0:T(8,128)(2,1)S(1)} %get-tuple-element.37), channel_id=1, source_target_pairs={{0,4},{4,0},{8,12},{12,8},{1,5},{5,1},{9,13},{13,9},{2,6},{6,2},{1... | collective-permute-start | bytes 98312 | tf_op jit(solution)/shard_map/ppermute | solution.py:34
  18.1 2.6 %collective-permute-start.7 = (bf16[128,128]{1,0:T(8,128)(2,1)S(1)}, bf16[128,128]{1,0:T(8,128)(2,1)S(1)}, u32[]{:S(2)}, u32[]{:S(2)}) collective-permute-start(bf16[128,128]{1,0:T(8,128)(2,1)S(1)} %get-tuple-element.38), channel_id=1, source_target_pairs={{0,8},{4,12},{8,0},{12,4},{1,9},{5,13},{9,1},{13,5},{2,10},{6,14},... | collective-permute-start | bytes 98312 | tf_op jit(solution)/shard_map/ppermute | solution.py:34
  20.7 0.0 collective-permute-start.8
  20.7 3.4 %rest.1 = (f32[128,128]{1,0:T(8,128)S(1)}, f32[128,128]{1,0:T(8,128)S(1)}, bf16[768,4096]{1,0:T(8,128)(2,1)S(1)}) custom-call(f32[128,128]{1,0:T(8,128)S(1)} %get-tuple-element.35.ready.p0, s32[2]{0:T(128)S(1)} %copy-done.3, bf16[2048,4096]{1,0:T(8,128)(2,1)} %wo_hbm.5), custom_call_target="tpu_custom_call" | custom-call | flops 2000000 | bytes 6291456 | tf_op jit(solution)/shard_map/rest/pallas_call | solution.py:373
  24.1 0.0 collective-permute-done.7.p2
  24.1 2.3 %collective-permute-done.8.p3 = bf16[128,128]{1,0:T(8,128)(2,1)S(1)} collective-permute-done((bf16[128,128]{1,0:T(8,128)(2,1)S(1)}, bf16[128,128]{1,0:T(8,128)(2,1)S(1)}, u32[]{:S(2)}, u32[]{:S(2)}) %collective-permute-start.8) | collective-permute-done | bytes 32800 | tf_op jit(solution)/shard_map/ppermute | solution.py:34
  26.4 1.5 %attend.1 = (bf16[40,128]{1,0:T(8,128)(2,1)}, bf16[40,128]{1,0:T(8,128)(2,1)}, bf16[2,2048]{1,0:T(2,128)(2,1)S(1)}) custom-call(s32[2]{0:T(128)S(1)} %copy-done.3, bf16[768,4096]{1,0:T(8,128)(2,1)S(1)} %get-tuple-element.36.ready.w2, f32[128,128]{1,0:T(8,128)S(1)} %get-tuple-element.35.ready.p0, bf16[128,128]{1,0:T(8,128)(2,1)S(1)} %collective-permute-done.6.p1, ...), custom_call_target="tpu_custom_call" | custom-call | flops 10000000 | bytes 1000000 | tf_op jit(solution)/shard_map/attend/pallas_call | solution.py:384
  27.9 1.6 %collective-permute-start.11 = (bf16[2,2048]{1,0:T(2,128)(2,1)S(1)}, bf16[2,2048]{1,0:T(2,128)(2,1)S(1)}, u32[]{:S(2)}, u32[]{:S(2)}) collective-permute-start(bf16[2,2048]{1,0:T(2,128)(2,1)S(1)} %get-tuple-element.42.a0), channel_id=1, source_target_pairs={{0,12},{4,8},{8,4},{12,0},{1,13},{5,9},{9,5},{13,1},{2,14},{6,10},... | collective-permute-start | bytes 24584 | tf_op jit(solution)/shard_map/ppermute | solution.py:34
  29.5 2.8 %collective-permute-start.9 = (bf16[2,2048]{1,0:T(2,128)(2,1)S(1)}, bf16[2,2048]{1,0:T(2,128)(2,1)S(1)}, u32[]{:S(2)}, u32[]{:S(2)}) collective-permute-start(bf16[2,2048]{1,0:T(2,128)(2,1)S(1)} %get-tuple-element.42.a0), channel_id=1, source_target_pairs={{0,4},{4,0},{8,12},{12,8},{1,5},{5,1},{9,13},{13,9},{2,6},{6,2},{1... | collective-permute-start | bytes 24584 | tf_op jit(solution)/shard_map/ppermute | solution.py:34
  32.3 1.1 %collective-permute-done.11.a3 = bf16[2,2048]{1,0:T(2,128)(2,1)S(1)} collective-permute-done((bf16[2,2048]{1,0:T(2,128)(2,1)S(1)}, bf16[2,2048]{1,0:T(2,128)(2,1)S(1)}, u32[]{:S(2)}, u32[]{:S(2)}) %collective-permute-start.11) | collective-permute-done | bytes 8224 | tf_op jit(solution)/shard_map/ppermute | solution.py:34
  33.4 0.7 %collective-permute-done.10.a2 = bf16[2,2048]{1,0:T(2,128)(2,1)S(1)} collective-permute-done((bf16[2,2048]{1,0:T(2,128)(2,1)S(1)}, bf16[2,2048]{1,0:T(2,128)(2,1)S(1)}, u32[]{:S(2)}, u32[]{:S(2)}) %collective-permute-start.10) | collective-permute-done | bytes 8224 | tf_op jit(solution)/shard_map/ppermute | solution.py:34
  34.1 0.0 collective-permute-done.9.a1
  34.1 2.3 %project.1 = (f32[2,4096]{1,0:T(2,128)S(1)}, bf16[2,4096]{1,0:T(2,128)(2,1)S(1)}, bf16[2,4096]{1,0:T(2,128)(2,1)S(1)}, bf16[2,4096]{1,0:T(2,128)(2,1)S(1)}) custom-call(bf16[2,2048]{1,0:T(2,128)(2,1)S(1)} %get-tuple-element.42.a0, bf16[2,2048]{1,0:T(2,128)(2,1)S(1)} %collective-permute-done.9.a1, bf16[2,2048]{1,0:T(2,128)(2,1)S(1)} %collective-permute-done.10.a2, ...), custom_call_target="tpu_custom_call" | custom-call | flops 134217728 | bytes 16777216 | tf_op jit(solution)/shard_map/project/pallas_call | solution.py:395
  36.3 1.6 %collective-permute-start.13 = (bf16[2,4096]{1,0:T(2,128)(2,1)S(1)}, bf16[2,4096]{1,0:T(2,128)(2,1)S(1)}, u32[]{:S(2)}, u32[]{:S(2)}) collective-permute-start(bf16[2,4096]{1,0:T(2,128)(2,1)S(1)} %get-tuple-element.47), channel_id=1, source_target_pairs={{0,2},{1,3},{2,0},{3,1},{4,6},{5,7},{6,4},{7,5},{8,10},{9,11},{10,... | collective-permute-start | bytes 49160 | tf_op jit(solution)/shard_map/ppermute | solution.py:34
  37.9 0.3 collective-permute-start.14
  38.2 1.9 %collective-permute-done.13 = bf16[2,4096]{1,0:T(2,128)(2,1)S(1)} collective-permute-done((bf16[2,4096]{1,0:T(2,128)(2,1)S(1)}, bf16[2,4096]{1,0:T(2,128)(2,1)S(1)}, u32[]{:S(2)}, u32[]{:S(2)}) %collective-permute-start.13) | collective-permute-done | bytes 16416 | tf_op jit(solution)/shard_map/ppermute | solution.py:34
  40.1 0.9 %collective-permute-done.14 = bf16[2,4096]{1,0:T(2,128)(2,1)S(1)} collective-permute-done((bf16[2,4096]{1,0:T(2,128)(2,1)S(1)}, bf16[2,4096]{1,0:T(2,128)(2,1)S(1)}, u32[]{:S(2)}, u32[]{:S(2)}) %collective-permute-start.14) | collective-permute-done | bytes 16416 | tf_op jit(solution)/shard_map/ppermute | solution.py:34
  41.1 0.6 %add_convert_fusion = bf16[2,4096]{1,0:T(2,128)(2,1)} fusion(bf16[2,4096]{1,0:T(2,128)(2,1)S(1)} %collective-permute-done.14, bf16[2,4096]{1,0:T(2,128)(2,1)S(1)} %collective-permute-done.13, f32[2,4096]{1,0:T(2,128)S(1)} %get-tuple-element.45, bf16[2,4096]{1,0:T(2,128)(2,1)S(1)} %collective-permute-done.12), kind=kLoop, calls=%fused_computation | loop fusion | flops 57344 | bytes 98304 | tf_op jit(solution)/shard_map/convert_element_type | solution.py:407
  (15 shorter events, 0.0 us)
Async XLA Ops:
  0.6 11.7 %copy-start = (bf16[4096,2048]{1,0:T(8,128)(2,1)S(1)}, bf16[4096,2048]{1,0:T(8,128)(2,1)}, u32[]{:S(2)}) copy-start(bf16[4096,2048]{1,0:T(8,128)(2,1)} %w.1) | copy-start | bytes 50331652
  0.6 11.6 %collective-permute-start.1 = (bf16[40,4096]{1,0:T(8,128)(2,1)}, bf16[40,4096]{1,0:T(8,128)(2,1)S(1)}, u32[]{:S(2)}, u32[]{:S(2)}) collective-permute-start(bf16[40,4096]{1,0:T(8,128)(2,1)} %s0.1), channel_id=1, source_target_pairs={{0,2},{1,3},{2,0},{3,1},{4,6},{5,7},{6,4},{7,5},{8,10},{9,11},{10,... | collective-permute-start | bytes 983048 | tf_op jit(solution)/shard_map/ppermute | solution.py:34
  3.6 5.4 %collective-permute-start.2 = (bf16[2,4096]{1,0:T(2,128)(2,1)}, bf16[2,4096]{1,0:T(2,128)(2,1)S(1)}, u32[]{:S(2)}, u32[]{:S(2)}) collective-permute-start(bf16[2,4096]{1,0:T(2,128)(2,1)} %b_hbm.1), channel_id=1, source_target_pairs={{0,1},{1,0},{2,3},{3,2},{4,5},{5,4},{6,7},{7,6},{8,9},{9,8},{10,11... | collective-permute-start | bytes 49160 | tf_op jit(solution)/shard_map/ppermute | solution.py:34
  3.6 7.7 %collective-permute-start.4 = (bf16[2,4096]{1,0:T(2,128)(2,1)}, bf16[2,4096]{1,0:T(2,128)(2,1)S(1)}, u32[]{:S(2)}, u32[]{:S(2)}) collective-permute-start(bf16[2,4096]{1,0:T(2,128)(2,1)} %b_hbm.1), channel_id=1, source_target_pairs={{0,3},{1,2},{2,1},{3,0},{4,7},{5,6},{6,5},{7,4},{8,11},{9,10},{10,... | collective-permute-start | bytes 49160 | tf_op jit(solution)/shard_map/ppermute | solution.py:34
  3.9 8.4 %collective-permute-start.3 = (bf16[2,4096]{1,0:T(2,128)(2,1)}, bf16[2,4096]{1,0:T(2,128)(2,1)S(1)}, u32[]{:S(2)}, u32[]{:S(2)}) collective-permute-start(bf16[2,4096]{1,0:T(2,128)(2,1)} %b_hbm.1), channel_id=1, source_target_pairs={{0,2},{1,3},{2,0},{3,1},{4,6},{5,7},{6,4},{7,5},{8,10},{9,11},{10,... | collective-permute-start | bytes 49160 | tf_op jit(solution)/shard_map/ppermute | solution.py:34
  5.8 9.2 %collective-permute-start = (bf16[40,4096]{1,0:T(8,128)(2,1)}, bf16[40,4096]{1,0:T(8,128)(2,1)S(1)}, u32[]{:S(2)}, u32[]{:S(2)}) collective-permute-start(bf16[40,4096]{1,0:T(8,128)(2,1)} %s0.1), channel_id=1, source_target_pairs={{0,1},{1,0},{2,3},{3,2},{4,5},{5,4},{6,7},{7,6},{8,9},{9,8},{10,11... | collective-permute-start | bytes 983048 | tf_op jit(solution)/shard_map/ppermute | solution.py:34
  12.3 2.7 %copy-start.2 = (bf16[40,4096]{1,0:T(8,128)(2,1)S(1)}, bf16[40,4096]{1,0:T(8,128)(2,1)}, u32[]{:S(2)}) copy-start(bf16[40,4096]{1,0:T(8,128)(2,1)} %s0.1) | copy-start | bytes 983044
  12.3 2.7 %copy-start.4 = (s32[4]{0:T(128)S(1)}, s32[4]{0:T(128)}, u32[]{:S(2)}) copy-start(s32[4]{0:T(128)} %owner_ref.1) | copy-start | bytes 52
  12.3 8.4 %copy-start.3 = (s32[2]{0:T(128)S(1)}, s32[2]{0:T(128)}, u32[]{:S(2)}) copy-start(s32[2]{0:T(128)} %len_ref.3) | copy-start | bytes 28
  12.3 2.7 %collective-permute-start.5 = (bf16[40,4096]{1,0:T(8,128)(2,1)S(1)}, bf16[40,4096]{1,0:T(8,128)(2,1)S(1)}, u32[]{:S(2)}, u32[]{:S(2)}) collective-permute-start(bf16[40,4096]{1,0:T(8,128)(2,1)S(1)} %collective-permute-done.1.far.s2), channel_id=1, source_target_pairs={{0,1},{1,0},{2,3},{3,2},{4,5},{5,4},{6,7},{7,6},{8,9},{9,8},{10,11... | collective-permute-start | bytes 983048 | tf_op jit(solution)/shard_map/ppermute | solution.py:34
  16.2 7.9 %collective-permute-start.6 = (bf16[128,128]{1,0:T(8,128)(2,1)S(1)}, bf16[128,128]{1,0:T(8,128)(2,1)S(1)}, u32[]{:S(2)}, u32[]{:S(2)}) collective-permute-start(bf16[128,128]{1,0:T(8,128)(2,1)S(1)} %get-tuple-element.37), channel_id=1, source_target_pairs={{0,4},{4,0},{8,12},{12,8},{1,5},{5,1},{9,13},{13,9},{2,6},{6,2},{1... | collective-permute-start | bytes 98312 | tf_op jit(solution)/shard_map/ppermute | solution.py:34
  18.1 6.0 %collective-permute-start.7 = (bf16[128,128]{1,0:T(8,128)(2,1)S(1)}, bf16[128,128]{1,0:T(8,128)(2,1)S(1)}, u32[]{:S(2)}, u32[]{:S(2)}) collective-permute-start(bf16[128,128]{1,0:T(8,128)(2,1)S(1)} %get-tuple-element.38), channel_id=1, source_target_pairs={{0,8},{4,12},{8,0},{12,4},{1,9},{5,13},{9,1},{13,5},{2,10},{6,14},... | collective-permute-start | bytes 98312 | tf_op jit(solution)/shard_map/ppermute | solution.py:34
  20.7 5.7 %collective-permute-start.8 = (bf16[128,128]{1,0:T(8,128)(2,1)S(1)}, bf16[128,128]{1,0:T(8,128)(2,1)S(1)}, u32[]{:S(2)}, u32[]{:S(2)}) collective-permute-start(bf16[128,128]{1,0:T(8,128)(2,1)S(1)} %get-tuple-element.39), channel_id=1, source_target_pairs={{0,12},{4,8},{8,4},{12,0},{1,13},{5,9},{9,5},{13,1},{2,14},{6,10},... | collective-permute-start | bytes 98312 | tf_op jit(solution)/shard_map/ppermute | solution.py:34
  20.7 5.7 %copy-start.1 = (bf16[2,2,512,128]{3,2,1,0:T(8,128)(2,1)S(1)}, bf16[2,2,512,128]{3,2,1,0:T(8,128)(2,1)}, u32[]{:S(2)}) copy-start(bf16[2,2,512,128]{3,2,1,0:T(8,128)(2,1)} %kv.1) | copy-start | bytes 1572868
  27.9 5.4 %collective-permute-start.11 = (bf16[2,2048]{1,0:T(2,128)(2,1)S(1)}, bf16[2,2048]{1,0:T(2,128)(2,1)S(1)}, u32[]{:S(2)}, u32[]{:S(2)}) collective-permute-start(bf16[2,2048]{1,0:T(2,128)(2,1)S(1)} %get-tuple-element.42.a0), channel_id=1, source_target_pairs={{0,12},{4,8},{8,4},{12,0},{1,13},{5,9},{9,5},{13,1},{2,14},{6,10},... | collective-permute-start | bytes 24584 | tf_op jit(solution)/shard_map/ppermute | solution.py:34
  29.5 4.5 %collective-permute-start.10 = (bf16[2,2048]{1,0:T(2,128)(2,1)S(1)}, bf16[2,2048]{1,0:T(2,128)(2,1)S(1)}, u32[]{:S(2)}, u32[]{:S(2)}) collective-permute-start(bf16[2,2048]{1,0:T(2,128)(2,1)S(1)} %get-tuple-element.42.a0), channel_id=1, source_target_pairs={{0,8},{4,12},{8,0},{12,4},{1,9},{5,13},{9,1},{13,5},{2,10},{6,14},... | collective-permute-start | bytes 24584 | tf_op jit(solution)/shard_map/ppermute | solution.py:34
  29.5 4.5 %collective-permute-start.9 = (bf16[2,2048]{1,0:T(2,128)(2,1)S(1)}, bf16[2,2048]{1,0:T(2,128)(2,1)S(1)}, u32[]{:S(2)}, u32[]{:S(2)}) collective-permute-start(bf16[2,2048]{1,0:T(2,128)(2,1)S(1)} %get-tuple-element.42.a0), channel_id=1, source_target_pairs={{0,4},{4,0},{8,12},{12,8},{1,5},{5,1},{9,13},{13,9},{2,6},{6,2},{1... | collective-permute-start | bytes 24584 | tf_op jit(solution)/shard_map/ppermute | solution.py:34
  36.3 1.9 %collective-permute-start.12 = (bf16[2,4096]{1,0:T(2,128)(2,1)S(1)}, bf16[2,4096]{1,0:T(2,128)(2,1)S(1)}, u32[]{:S(2)}, u32[]{:S(2)}) collective-permute-start(bf16[2,4096]{1,0:T(2,128)(2,1)S(1)} %get-tuple-element.46), channel_id=1, source_target_pairs={{0,1},{1,0},{2,3},{3,2},{4,5},{5,4},{6,7},{7,6},{8,9},{9,8},{10,11... | collective-permute-start | bytes 49160 | tf_op jit(solution)/shard_map/ppermute | solution.py:34
  36.3 3.8 %collective-permute-start.13 = (bf16[2,4096]{1,0:T(2,128)(2,1)S(1)}, bf16[2,4096]{1,0:T(2,128)(2,1)S(1)}, u32[]{:S(2)}, u32[]{:S(2)}) collective-permute-start(bf16[2,4096]{1,0:T(2,128)(2,1)S(1)} %get-tuple-element.47), channel_id=1, source_target_pairs={{0,2},{1,3},{2,0},{3,1},{4,6},{5,7},{6,4},{7,5},{8,10},{9,11},{10,... | collective-permute-start | bytes 49160 | tf_op jit(solution)/shard_map/ppermute | solution.py:34
  37.9 3.2 %collective-permute-start.14 = (bf16[2,4096]{1,0:T(2,128)(2,1)S(1)}, bf16[2,4096]{1,0:T(2,128)(2,1)S(1)}, u32[]{:S(2)}, u32[]{:S(2)}) collective-permute-start(bf16[2,4096]{1,0:T(2,128)(2,1)S(1)} %get-tuple-element.48), channel_id=1, source_target_pairs={{0,3},{1,2},{2,1},{3,0},{4,7},{5,6},{6,5},{7,4},{8,11},{9,10},{10,... | collective-permute-start | bytes 49160 | tf_op jit(solution)/shard_map/ppermute | solution.py:34

commit v4 on v3

--- a/solution.py
+++ b/solution.py
@@ -155,6 +155,10 @@
 BF16 = jnp.bfloat16
 
 
+def ring(step):
+    return lax.rem(step + 8, 4)
+
+
 def whole(space=pltpu.VMEM):
     return pl.BlockSpec(memory_space=space)
 
@@ -205,7 +209,7 @@
 
 def query_kernel(far, b0, b1, b2, b3, w, wo_hbm, out_ref, wo, acc, sems):
     rows = wo.shape[0]
-    copies = start_load(wo_hbm.at[pl.ds(rows, rows)], wo, sems, 0, 2)
+    copies = start_load(wo_hbm.at[pl.ds(2 * rows, rows)], wo, sems, 0, 2)
     lhs = jnp.concatenate([b[...].astype(F32) for b in (b0, b1, b2, b3)], axis=0).astype(BF16)
     acc[...] = jnp.dot(lhs, w[...], preferred_element_type=F32)
     for r in range(acc.shape[0]):
@@ -242,11 +246,11 @@
     empty = jnp.zeros((8 - ROWS_DEV, HD), F32)
     for k in range(len(stored)):
         rows = slice(k * ROW_TILE, k * ROW_TILE + LC)
-        target = owner_ref[gy ^ k] ^ gx
+        target = ring(owner_ref[gy ^ k] - gx)
         pay[target, pl.ds(0, LC), :] = key[rows]
         pay[target, pl.ds(VALUES, LC), :] = value[rows]
         rows = slice(base + k * ROWS_DEV, base + (k + 1) * ROWS_DEV)
-        target = k ^ gx ^ gy
+        target = ring((gy ^ k) - gx)
         pay[target, pl.ds(LC, 8), :] = jnp.concatenate([key[rows], empty], axis=0)
         pay[target, pl.ds(VALUES + LC, 8), :] = jnp.concatenate([value[rows], empty], axis=0)
         for r in range(ROWS_DEV):
@@ -293,9 +297,9 @@
 
 
 def out_kernel(a0, a1, a2, a3, w0, w1, w2, o0, o1, o2, o3, blocks):
-    tag = lax.axis_index("gx") ^ lax.axis_index("gy")
+    tag = lax.axis_index("gx") - lax.axis_index("gy")
     for s, a in enumerate((a0, a1, a2, a3)):
-        blocks[s ^ tag] = a[...].astype(F32)
+        blocks[ring(tag - s)] = a[...].astype(F32)
     lhs = jnp.concatenate([blocks[k] for k in range(4)], axis=0).astype(BF16)
     first = 0
     acc = jnp.zeros((lhs.shape[0], w0.shape[1]), F32)
@@ -313,12 +317,20 @@
     return [swap(b, axis, k + 1) for k, b in enumerate(blocks)]
 
 
+def rotated(blocks, axis):
+    n = lax.axis_size(axis)
+    return [
+        lax.ppermute(b, axis, [(i, (i + k + 1) % n) for i in range(n)])
+        for k, b in enumerate(blocks)
+    ]
+
+
 def per_device(stored_rows, new_rows, w_query, w_key, w_value, w_out, kv_cache, cache_len, owner):
     shape = jax.ShapeDtypeStruct
     depth, query_cols = w_query.shape
     width = w_out.shape[1]
     heads = query_cols // HD
-    cut = query_cols * 5 // 16
+    half, quarter = query_cols // 2, query_cols // 4
     semaphores = pltpu.SemaphoreType.DMA
     in_vmem = lambda x: pltpu.with_memory_space_constraint(x, pltpu.VMEM)
     in_hbm = lambda x: pltpu.with_memory_space_constraint(x, pltpu.HBM)
@@ -328,7 +340,7 @@
     wo_first, wkv, own_fresh = pl.pallas_call(
         load_kernel,
         out_shape=[
-            pltpu.VMEM((cut, width), BF16),
+            pltpu.VMEM((half, width), BF16),
             pltpu.VMEM((depth, 2 * HD), BF16),
             pltpu.VMEM(new_rows.shape, BF16),
         ],
@@ -347,7 +359,7 @@
         query_kernel,
         out_shape=[
             pltpu.VMEM((4 * ROWS_DEV, heads, HD), F32),
-            pltpu.VMEM((cut, width), BF16),
+            pltpu.VMEM((quarter, width), BF16),
         ],
         in_specs=[whole(pl.ANY)] + [whole()] * 5 + [whole(pltpu.HBM)],
         out_specs=[whole()] * 2,
@@ -369,16 +381,16 @@
         cost_estimate=cost(2 * 208 * depth * 256, 4 * depth * HD),
         name="payload",
     )(owner, *stored, *fresh, wkv, query)
-    sums = [payload[0]] + others(payload[1:], "gx")
+    sums = [payload[0]] + rotated(payload[1:], "gx")
     cos, sin, wo_third = pl.pallas_call(
         rest_kernel,
         out_shape=[pltpu.VMEM((PAY, HD), F32)] * 2
-        + [pltpu.VMEM((query_cols - 2 * cut, width), BF16)],
+        + [pltpu.VMEM((quarter, width), BF16)],
         in_specs=[whole(pl.ANY), whole(pltpu.SMEM), whole(pltpu.HBM)],
         out_specs=[whole()] * 3,
         scratch_shapes=[semaphores((4,))],
         compiler_params=params(4),
-        cost_estimate=cost(2000000, 2 * (query_cols - 2 * cut) * width),
+        cost_estimate=cost(2000000, 2 * quarter * width),
         name="rest",
     )(payload[0], cache_len, in_hbm(w_out))
     rebuilt_key, rebuilt_value, attn = pl.pallas_call(
@@ -391,7 +403,7 @@
         cost_estimate=cost(10000000, 1000000),
         name="attend",
     )(cache_len, wo_third, *sums, cos, sin, kv_cache)
-    attn_all = [attn] + others([attn] * 3, "gx")
+    attn_all = [attn] + rotated([attn] * 3, "gx")
     parts = pl.pallas_call(
         out_kernel,
         out_shape=[shape((ROWS_DEV, width), F32)] + [shape((ROWS_DEV, width), BF16)] * 3,
@@ -402,7 +414,7 @@
         cost_estimate=cost(2 * 8 * width * query_cols, 2 * width * query_cols),
         name="project",
     )(*attn_all, wo_first, wo_second, wo_third)
-    arrived = others(parts[1:], "gy")
+    arrived = rotated(parts[1:], "gy")
     mixed = parts[0] + arrived[0].astype(F32) + arrived[1].astype(F32) + arrived[2].astype(F32)
     return (mixed.astype(BF16), rebuilt_key[None], rebuilt_value[None])
 

time: 41.8 us -> 42.1 us (level)
  starting transfers between devices: 16 us -> 17.5 us
  waiting for transfers between devices: 10.1 us -> 8.66 us
    ppermute x0 -> x9, starting transfers between devices: none -> 12.3 us  [rotated(): lax.ppermute(b, axis, [(i, (i + k + 1) % n) for i in range(n)])]
    ppermute x15 -> x6, starting transfers between devices: 16 us -> 5.22 us  [swap(): return lax.ppermute(x, axis, [(i, i ^ k) for i in range(n)])]
    ppermute x15 -> x6, waiting for transfers between devices: 10.1 us -> 2.37 us  [swap(): return lax.ppermute(x, axis, [(i, i ^ k) for i in range(n)])]
    ppermute x0 -> x9, waiting for transfers between devices: none -> 6.29 us  [rotated(): lax.ppermute(b, axis, [(i, (i + k + 1) % n) for i in range(n)])]
    pallas_call x1, Pallas kernels: 3.24 us -> 4.11 us  [per_device(): pl.pallas_call(load_kernel, out_shape=[pltpu.VMEM((half, width), BF16), p...]
    pallas_call x1, Pallas kernels: 3.41 us -> 2.75 us  [per_device(): pl.pallas_call(rest_kernel, out_shape=[pltpu.VMEM((PAY, HD), F32)] * 2 +...]
  transfers between devices with their start and end apart: 15 -> 15, of which waited for: 7 -> 8; matrix products, arithmetic and copies ran while one was open for 0% -> 0% of each run, Pallas kernels for 22% -> 22%
where the time goes in v4:
time: 42.1 us; the launch traced here: 41.8 us
  starting transfers between devices  17.5 us (42%)
  Pallas kernels  14.2 us (34%)
  waiting for transfers between devices  8.66 us (21%)
  between operations  0.78 us (2%)
  other arithmetic  0.64 us (2%)
    ppermute x9, starting transfers between devices, rotated(): lax.ppermute(b, axis, [(i, (i + k + 1) % n) for i in range(n)])  12.3 us
    ppermute x9, waiting for transfers between devices, rotated(): lax.ppermute(b, axis, [(i, (i + k + 1) % n) for i in range(n)])  6.29 us
    ppermute x6, starting transfers between devices, swap(): return lax.ppermute(x, axis, [(i, i ^ k) for i in range(n)])  5.22 us
    pallas_call x1, Pallas kernels, per_device(): pl.pallas_call(load_kernel, out_shape=[pltpu.VMEM((half, width), BF16), p...  4.11 us
    pallas_call x1, Pallas kernels, per_device(): pl.pallas_call(rest_kernel, out_shape=[pltpu.VMEM((PAY, HD), F32)] * 2 +...  2.75 us
    ppermute x6, waiting for transfers between devices, swap(): return lax.ppermute(x, axis, [(i, i ^ k) for i in range(n)])  2.37 us
    pallas_call x1, Pallas kernels, per_device(): pl.pallas_call(query_kernel, out_shape=[pltpu.VMEM((4 * ROWS_DEV, heads,...  2.33 us
    pallas_call x1, Pallas kernels, per_device(): pl.pallas_call(out_kernel, out_shape=[shape((ROWS_DEV, width), F32)] + [s...  2.28 us
  transfers between devices with their start and end apart: 15, of which 8 were waited for; matrix products, arithmetic and copies ran while one was open for 0% of the time, Pallas kernels for 22%

profile of v4, /device:TPU:0, one launch (start us, length us, event | category | flops | bytes accessed | tf_op | source)
XLA Modules:
  0.0 41.8 jit_solution(10586804048154345447)
XLA Ops:
  0.6 3.0 %collective-permute-start.1 = (bf16[40,4096]{1,0:T(8,128)(2,1)}, bf16[40,4096]{1,0:T(8,128)(2,1)S(1)}, u32[]{:S(2)}, u32[]{:S(2)}) collective-permute-start(bf16[40,4096]{1,0:T(8,128)(2,1)} %s0.1), channel_id=1, source_target_pairs={{0,2},{1,3},{2,0},{3,1},{4,6},{5,7},{6,4},{7,5},{8,10},{9,11},{10,... | collective-permute-start | bytes 983048 | tf_op jit(solution)/shard_map/ppermute | solution.py:34
  3.6 0.0 collective-permute-start.2
  3.6 0.2 collective-permute-start.4
  3.9 1.9 %collective-permute-start.3 = (bf16[2,4096]{1,0:T(2,128)(2,1)}, bf16[2,4096]{1,0:T(2,128)(2,1)S(1)}, u32[]{:S(2)}, u32[]{:S(2)}) collective-permute-start(bf16[2,4096]{1,0:T(2,128)(2,1)} %b_hbm.1), channel_id=1, source_target_pairs={{0,2},{1,3},{2,0},{3,1},{4,6},{5,7},{6,4},{7,5},{8,10},{9,11},{10,... | collective-permute-start | bytes 49160 | tf_op jit(solution)/shard_map/ppermute | solution.py:34
  5.8 0.0 collective-permute-start
  5.8 4.1 %load.1 = (bf16[1024,4096]{1,0:T(8,128)(2,1)S(1)}, bf16[4096,256]{1,0:T(8,128)(2,1)S(1)}, bf16[2,4096]{1,0:T(2,128)(2,1)S(1)}) custom-call(bf16[2048,4096]{1,0:T(8,128)(2,1)} %wo_hbm.5, bf16[4096,128]{1,0:T(8,128)(2,1)} %wk_hbm.1, bf16[4096,128]{1,0:T(8,128)(2,1)} %wv_hbm.1, bf16[2,4096]{1,0:T(2,128)(2,1)} %b_hbm.1), custom_call_target="tpu_custom_call" | custom-call | flops 1000 | bytes 16777216 | tf_op jit(solution)/shard_map/load/pallas_call | solution.py:340
  9.9 0.0 collective-permute-done.2.b1
  9.9 1.4 %collective-permute-done.4.b3 = bf16[2,4096]{1,0:T(2,128)(2,1)S(1)} collective-permute-done((bf16[2,4096]{1,0:T(2,128)(2,1)}, bf16[2,4096]{1,0:T(2,128)(2,1)S(1)}, u32[]{:S(2)}, u32[]{:S(2)}) %collective-permute-start.4) | collective-permute-done | bytes 16416 | tf_op jit(solution)/shard_map/ppermute | solution.py:34
  11.4 0.9 %collective-permute-done.3.b2 = bf16[2,4096]{1,0:T(2,128)(2,1)S(1)} collective-permute-done((bf16[2,4096]{1,0:T(2,128)(2,1)}, bf16[2,4096]{1,0:T(2,128)(2,1)S(1)}, u32[]{:S(2)}, u32[]{:S(2)}) %collective-permute-start.3) | collective-permute-done | bytes 16416 | tf_op jit(solution)/shard_map/ppermute | solution.py:34
  12.3 0.1 collective-permute-start.5
  12.4 0.0 copy-done
  12.4 2.3 %query.1 = (f32[8,16,128]{2,1,0:T(8,128)S(1)}, bf16[512,4096]{1,0:T(8,128)(2,1)S(1)}) custom-call(bf16[40,4096]{1,0:T(8,128)(2,1)S(1)} %collective-permute-done.1.far.s2, bf16[2,4096]{1,0:T(2,128)(2,1)S(1)} %get-tuple-element.29.b0, bf16[2,4096]{1,0:T(2,128)(2,1)S(1)} %collective-permute-done.2.b1, bf16[2,4096]{1,0:T(2,128)(2,1)S(1)} %collective-permute-done.3.b2, ...), custom_call_target="tpu_custom_call" | custom-call | flops 134217728 | bytes 2097152 | tf_op jit(solution)/shard_map/query/pallas_call | solution.py:358
  14.7 1.2 %payload.1 = (f32[128,128]{1,0:T(8,128)S(1)}, bf16[128,128]{1,0:T(8,128)(2,1)S(1)}, bf16[128,128]{1,0:T(8,128)(2,1)S(1)}, bf16[128,128]{1,0:T(8,128)(2,1)S(1)}) custom-call(s32[4]{0:T(128)S(1)} %copy-done.4, bf16[40,4096]{1,0:T(8,128)(2,1)S(1)} %copy-done.2, bf16[40,4096]{1,0:T(8,128)(2,1)S(1)} %collective-permute-done.s1, ...), custom_call_target="tpu_custom_call" | custom-call | flops 436207616 | bytes 2097152 | tf_op jit(solution)/shard_map/payload/pallas_call | solution.py:371
  15.9 1.9 %collective-permute-start.6 = (bf16[128,128]{1,0:T(8,128)(2,1)S(1)}, bf16[128,128]{1,0:T(8,128)(2,1)S(1)}, u32[]{:S(2)}, u32[]{:S(2)}) collective-permute-start(bf16[128,128]{1,0:T(8,128)(2,1)S(1)} %get-tuple-element.37), channel_id=1, source_target_pairs={{0,4},{4,8},{8,12},{12,0},{1,5},{5,9},{9,13},{13,1},{2,6},{6,10},{... | collective-permute-start | bytes 98312 | tf_op jit(solution)/shard_map/ppermute | solution.py:323
  17.8 2.6 %collective-permute-start.7 = (bf16[128,128]{1,0:T(8,128)(2,1)S(1)}, bf16[128,128]{1,0:T(8,128)(2,1)S(1)}, u32[]{:S(2)}, u32[]{:S(2)}) collective-permute-start(bf16[128,128]{1,0:T(8,128)(2,1)S(1)} %get-tuple-element.38), channel_id=1, source_target_pairs={{0,8},{4,12},{8,0},{12,4},{1,9},{5,13},{9,1},{13,5},{2,10},{6,14},... | collective-permute-start | bytes 98312 | tf_op jit(solution)/shard_map/ppermute | solution.py:323
  20.4 1.3 %collective-permute-start.8 = (bf16[128,128]{1,0:T(8,128)(2,1)S(1)}, bf16[128,128]{1,0:T(8,128)(2,1)S(1)}, u32[]{:S(2)}, u32[]{:S(2)}) collective-permute-start(bf16[128,128]{1,0:T(8,128)(2,1)S(1)} %get-tuple-element.39), channel_id=1, source_target_pairs={{0,12},{4,0},{8,4},{12,8},{1,13},{5,1},{9,5},{13,9},{2,14},{6,2},{... | collective-permute-start | bytes 98312 | tf_op jit(solution)/shard_map/ppermute | solution.py:323
  21.8 2.7 %rest.1 = (f32[128,128]{1,0:T(8,128)S(1)}, f32[128,128]{1,0:T(8,128)S(1)}, bf16[512,4096]{1,0:T(8,128)(2,1)S(1)}) custom-call(f32[128,128]{1,0:T(8,128)S(1)} %get-tuple-element.35.ready.p0, s32[2]{0:T(128)S(1)} %copy-done.3, bf16[2048,4096]{1,0:T(8,128)(2,1)} %wo_hbm.5), custom_call_target="tpu_custom_call" | custom-call | flops 2000000 | bytes 4194304 | tf_op jit(solution)/shard_map/rest/pallas_call | solution.py:385
  24.5 0.0 collective-permute-done.7.p2
  24.5 0.0 collective-permute-done.8.p3
  24.6 1.5 %attend.1 = (bf16[40,128]{1,0:T(8,128)(2,1)}, bf16[40,128]{1,0:T(8,128)(2,1)}, bf16[2,2048]{1,0:T(2,128)(2,1)S(1)}) custom-call(s32[2]{0:T(128)S(1)} %copy-done.3, bf16[512,4096]{1,0:T(8,128)(2,1)S(1)} %get-tuple-element.36.ready.w2, f32[128,128]{1,0:T(8,128)S(1)} %get-tuple-element.35.ready.p0, bf16[128,128]{1,0:T(8,128)(2,1)S(1)} %collective-permute-done.6.p1, ...), custom_call_target="tpu_custom_call" | custom-call | flops 10000000 | bytes 1000000 | tf_op jit(solution)/shard_map/attend/pallas_call | solution.py:396
  26.1 2.9 %collective-permute-start.11 = (bf16[2,2048]{1,0:T(2,128)(2,1)S(1)}, bf16[2,2048]{1,0:T(2,128)(2,1)S(1)}, u32[]{:S(2)}, u32[]{:S(2)}) collective-permute-start(bf16[2,2048]{1,0:T(2,128)(2,1)S(1)} %get-tuple-element.42.a0), channel_id=1, source_target_pairs={{0,12},{4,0},{8,4},{12,8},{1,13},{5,1},{9,5},{13,9},{2,14},{6,2},{... | collective-permute-start | bytes 24584 | tf_op jit(solution)/shard_map/ppermute | solution.py:323
  29.0 0.6 %collective-permute-start.9 = (bf16[2,2048]{1,0:T(2,128)(2,1)S(1)}, bf16[2,2048]{1,0:T(2,128)(2,1)S(1)}, u32[]{:S(2)}, u32[]{:S(2)}) collective-permute-start(bf16[2,2048]{1,0:T(2,128)(2,1)S(1)} %get-tuple-element.42.a0), channel_id=1, source_target_pairs={{0,4},{4,8},{8,12},{12,0},{1,5},{5,9},{9,13},{13,1},{2,6},{6,10},{... | collective-permute-start | bytes 24584 | tf_op jit(solution)/shard_map/ppermute | solution.py:323
  29.6 0.8 %collective-permute-done.11.a3 = bf16[2,2048]{1,0:T(2,128)(2,1)S(1)} collective-permute-done((bf16[2,2048]{1,0:T(2,128)(2,1)S(1)}, bf16[2,2048]{1,0:T(2,128)(2,1)S(1)}, u32[]{:S(2)}, u32[]{:S(2)}) %collective-permute-start.11) | collective-permute-done | bytes 8224 | tf_op jit(solution)/shard_map/ppermute | solution.py:323
  30.4 3.2 %collective-permute-done.10.a2 = bf16[2,2048]{1,0:T(2,128)(2,1)S(1)} collective-permute-done((bf16[2,2048]{1,0:T(2,128)(2,1)S(1)}, bf16[2,2048]{1,0:T(2,128)(2,1)S(1)}, u32[]{:S(2)}, u32[]{:S(2)}) %collective-permute-start.10) | collective-permute-done | bytes 8224 | tf_op jit(solution)/shard_map/ppermute | solution.py:323
  33.5 0.9 %collective-permute-done.9.a1 = bf16[2,2048]{1,0:T(2,128)(2,1)S(1)} collective-permute-done((bf16[2,2048]{1,0:T(2,128)(2,1)S(1)}, bf16[2,2048]{1,0:T(2,128)(2,1)S(1)}, u32[]{:S(2)}, u32[]{:S(2)}) %collective-permute-start.9) | collective-permute-done | bytes 8224 | tf_op jit(solution)/shard_map/ppermute | solution.py:323
  34.5 2.3 %project.1 = (f32[2,4096]{1,0:T(2,128)S(1)}, bf16[2,4096]{1,0:T(2,128)(2,1)S(1)}, bf16[2,4096]{1,0:T(2,128)(2,1)S(1)}, bf16[2,4096]{1,0:T(2,128)(2,1)S(1)}) custom-call(bf16[2,2048]{1,0:T(2,128)(2,1)S(1)} %get-tuple-element.42.a0, bf16[2,2048]{1,0:T(2,128)(2,1)S(1)} %collective-permute-done.9.a1, bf16[2,2048]{1,0:T(2,128)(2,1)S(1)} %collective-permute-done.10.a2, ...), custom_call_target="tpu_custom_call" | custom-call | flops 134217728 | bytes 16777216 | tf_op jit(solution)/shard_map/project/pallas_call | solution.py:407
  36.7 1.6 %collective-permute-start.13 = (bf16[2,4096]{1,0:T(2,128)(2,1)S(1)}, bf16[2,4096]{1,0:T(2,128)(2,1)S(1)}, u32[]{:S(2)}, u32[]{:S(2)}) collective-permute-start(bf16[2,4096]{1,0:T(2,128)(2,1)S(1)} %get-tuple-element.47), channel_id=1, source_target_pairs={{0,2},{1,3},{2,0},{3,1},{4,6},{5,7},{6,4},{7,5},{8,10},{9,11},{10,... | collective-permute-start | bytes 49160 | tf_op jit(solution)/shard_map/ppermute | solution.py:323
  38.3 1.4 %collective-permute-start.14 = (bf16[2,4096]{1,0:T(2,128)(2,1)S(1)}, bf16[2,4096]{1,0:T(2,128)(2,1)S(1)}, u32[]{:S(2)}, u32[]{:S(2)}) collective-permute-start(bf16[2,4096]{1,0:T(2,128)(2,1)S(1)} %get-tuple-element.48), channel_id=1, source_target_pairs={{0,3},{1,0},{2,1},{3,2},{4,7},{5,4},{6,5},{7,6},{8,11},{9,8},{10,9... | collective-permute-start | bytes 49160 | tf_op jit(solution)/shard_map/ppermute | solution.py:323
  39.7 0.2 collective-permute-done.12
  39.9 0.6 %collective-permute-done.13 = bf16[2,4096]{1,0:T(2,128)(2,1)S(1)} collective-permute-done((bf16[2,4096]{1,0:T(2,128)(2,1)S(1)}, bf16[2,4096]{1,0:T(2,128)(2,1)S(1)}, u32[]{:S(2)}, u32[]{:S(2)}) %collective-permute-start.13) | collective-permute-done | bytes 16416 | tf_op jit(solution)/shard_map/ppermute | solution.py:323
  40.5 0.6 %collective-permute-done.14 = bf16[2,4096]{1,0:T(2,128)(2,1)S(1)} collective-permute-done((bf16[2,4096]{1,0:T(2,128)(2,1)S(1)}, bf16[2,4096]{1,0:T(2,128)(2,1)S(1)}, u32[]{:S(2)}, u32[]{:S(2)}) %collective-permute-start.14) | collective-permute-done | bytes 16416 | tf_op jit(solution)/shard_map/ppermute | solution.py:323
  41.1 0.6 %add_convert_fusion = bf16[2,4096]{1,0:T(2,128)(2,1)} fusion(bf16[2,4096]{1,0:T(2,128)(2,1)S(1)} %collective-permute-done.14, bf16[2,4096]{1,0:T(2,128)(2,1)S(1)} %collective-permute-done.13, f32[2,4096]{1,0:T(2,128)S(1)} %get-tuple-element.45, bf16[2,4096]{1,0:T(2,128)(2,1)S(1)} %collective-permute-done.12), kind=kLoop, calls=%fused_computation | loop fusion | flops 57344 | bytes 98304 | tf_op jit(solution)/shard_map/convert_element_type | solution.py:419
  (15 shorter events, 0.0 us)
Async XLA Ops:
  0.6 11.7 %copy-start = (bf16[4096,2048]{1,0:T(8,128)(2,1)S(1)}, bf16[4096,2048]{1,0:T(8,128)(2,1)}, u32[]{:S(2)}) copy-start(bf16[4096,2048]{1,0:T(8,128)(2,1)} %w.1) | copy-start | bytes 50331652
  0.6 11.6 %collective-permute-start.1 = (bf16[40,4096]{1,0:T(8,128)(2,1)}, bf16[40,4096]{1,0:T(8,128)(2,1)S(1)}, u32[]{:S(2)}, u32[]{:S(2)}) collective-permute-start(bf16[40,4096]{1,0:T(8,128)(2,1)} %s0.1), channel_id=1, source_target_pairs={{0,2},{1,3},{2,0},{3,1},{4,6},{5,7},{6,4},{7,5},{8,10},{9,11},{10,... | collective-permute-start | bytes 983048 | tf_op jit(solution)/shard_map/ppermute | solution.py:34
  3.6 6.3 %collective-permute-start.2 = (bf16[2,4096]{1,0:T(2,128)(2,1)}, bf16[2,4096]{1,0:T(2,128)(2,1)S(1)}, u32[]{:S(2)}, u32[]{:S(2)}) collective-permute-start(bf16[2,4096]{1,0:T(2,128)(2,1)} %b_hbm.1), channel_id=1, source_target_pairs={{0,1},{1,0},{2,3},{3,2},{4,5},{5,4},{6,7},{7,6},{8,9},{9,8},{10,11... | collective-permute-start | bytes 49160 | tf_op jit(solution)/shard_map/ppermute | solution.py:34
  3.6 7.7 %collective-permute-start.4 = (bf16[2,4096]{1,0:T(2,128)(2,1)}, bf16[2,4096]{1,0:T(2,128)(2,1)S(1)}, u32[]{:S(2)}, u32[]{:S(2)}) collective-permute-start(bf16[2,4096]{1,0:T(2,128)(2,1)} %b_hbm.1), channel_id=1, source_target_pairs={{0,3},{1,2},{2,1},{3,0},{4,7},{5,6},{6,5},{7,4},{8,11},{9,10},{10,... | collective-permute-start | bytes 49160 | tf_op jit(solution)/shard_map/ppermute | solution.py:34
  3.9 8.4 %collective-permute-start.3 = (bf16[2,4096]{1,0:T(2,128)(2,1)}, bf16[2,4096]{1,0:T(2,128)(2,1)S(1)}, u32[]{:S(2)}, u32[]{:S(2)}) collective-permute-start(bf16[2,4096]{1,0:T(2,128)(2,1)} %b_hbm.1), channel_id=1, source_target_pairs={{0,2},{1,3},{2,0},{3,1},{4,6},{5,7},{6,4},{7,5},{8,10},{9,11},{10,... | collective-permute-start | bytes 49160 | tf_op jit(solution)/shard_map/ppermute | solution.py:34
  5.8 8.9 %collective-permute-start = (bf16[40,4096]{1,0:T(8,128)(2,1)}, bf16[40,4096]{1,0:T(8,128)(2,1)S(1)}, u32[]{:S(2)}, u32[]{:S(2)}) collective-permute-start(bf16[40,4096]{1,0:T(8,128)(2,1)} %s0.1), channel_id=1, source_target_pairs={{0,1},{1,0},{2,3},{3,2},{4,5},{5,4},{6,7},{7,6},{8,9},{9,8},{10,11... | collective-permute-start | bytes 983048 | tf_op jit(solution)/shard_map/ppermute | solution.py:34
  12.3 2.5 %copy-start.2 = (bf16[40,4096]{1,0:T(8,128)(2,1)S(1)}, bf16[40,4096]{1,0:T(8,128)(2,1)}, u32[]{:S(2)}) copy-start(bf16[40,4096]{1,0:T(8,128)(2,1)} %s0.1) | copy-start | bytes 983044
  12.3 2.5 %copy-start.4 = (s32[4]{0:T(128)S(1)}, s32[4]{0:T(128)}, u32[]{:S(2)}) copy-start(s32[4]{0:T(128)} %owner_ref.1) | copy-start | bytes 52
  12.3 9.5 %copy-start.3 = (s32[2]{0:T(128)S(1)}, s32[2]{0:T(128)}, u32[]{:S(2)}) copy-start(s32[2]{0:T(128)} %len_ref.3) | copy-start | bytes 28
  12.3 2.4 %collective-permute-start.5 = (bf16[40,4096]{1,0:T(8,128)(2,1)S(1)}, bf16[40,4096]{1,0:T(8,128)(2,1)S(1)}, u32[]{:S(2)}, u32[]{:S(2)}) collective-permute-start(bf16[40,4096]{1,0:T(8,128)(2,1)S(1)} %collective-permute-done.1.far.s2), channel_id=1, source_target_pairs={{0,1},{1,0},{2,3},{3,2},{4,5},{5,4},{6,7},{7,6},{8,9},{9,8},{10,11... | collective-permute-start | bytes 983048 | tf_op jit(solution)/shard_map/ppermute | solution.py:34
  15.9 8.6 %collective-permute-start.6 = (bf16[128,128]{1,0:T(8,128)(2,1)S(1)}, bf16[128,128]{1,0:T(8,128)(2,1)S(1)}, u32[]{:S(2)}, u32[]{:S(2)}) collective-permute-start(bf16[128,128]{1,0:T(8,128)(2,1)S(1)} %get-tuple-element.37), channel_id=1, source_target_pairs={{0,4},{4,8},{8,12},{12,0},{1,5},{5,9},{9,13},{13,1},{2,6},{6,10},{... | collective-permute-start | bytes 98312 | tf_op jit(solution)/shard_map/ppermute | solution.py:323
  17.8 6.7 %collective-permute-start.7 = (bf16[128,128]{1,0:T(8,128)(2,1)S(1)}, bf16[128,128]{1,0:T(8,128)(2,1)S(1)}, u32[]{:S(2)}, u32[]{:S(2)}) collective-permute-start(bf16[128,128]{1,0:T(8,128)(2,1)S(1)} %get-tuple-element.38), channel_id=1, source_target_pairs={{0,8},{4,12},{8,0},{12,4},{1,9},{5,13},{9,1},{13,5},{2,10},{6,14},... | collective-permute-start | bytes 98312 | tf_op jit(solution)/shard_map/ppermute | solution.py:323
  20.4 4.1 %collective-permute-start.8 = (bf16[128,128]{1,0:T(8,128)(2,1)S(1)}, bf16[128,128]{1,0:T(8,128)(2,1)S(1)}, u32[]{:S(2)}, u32[]{:S(2)}) collective-permute-start(bf16[128,128]{1,0:T(8,128)(2,1)S(1)} %get-tuple-element.39), channel_id=1, source_target_pairs={{0,12},{4,0},{8,4},{12,8},{1,13},{5,1},{9,5},{13,9},{2,14},{6,2},{... | collective-permute-start | bytes 98312 | tf_op jit(solution)/shard_map/ppermute | solution.py:323
  21.8 2.8 %copy-start.1 = (bf16[2,2,512,128]{3,2,1,0:T(8,128)(2,1)S(1)}, bf16[2,2,512,128]{3,2,1,0:T(8,128)(2,1)}, u32[]{:S(2)}) copy-start(bf16[2,2,512,128]{3,2,1,0:T(8,128)(2,1)} %kv.1) | copy-start | bytes 1572868
  26.1 4.3 %collective-permute-start.11 = (bf16[2,2048]{1,0:T(2,128)(2,1)S(1)}, bf16[2,2048]{1,0:T(2,128)(2,1)S(1)}, u32[]{:S(2)}, u32[]{:S(2)}) collective-permute-start(bf16[2,2048]{1,0:T(2,128)(2,1)S(1)} %get-tuple-element.42.a0), channel_id=1, source_target_pairs={{0,12},{4,0},{8,4},{12,8},{1,13},{5,1},{9,5},{13,9},{2,14},{6,2},{... | collective-permute-start | bytes 24584 | tf_op jit(solution)/shard_map/ppermute | solution.py:323
  29.0 4.5 %collective-permute-start.10 = (bf16[2,2048]{1,0:T(2,128)(2,1)S(1)}, bf16[2,2048]{1,0:T(2,128)(2,1)S(1)}, u32[]{:S(2)}, u32[]{:S(2)}) collective-permute-start(bf16[2,2048]{1,0:T(2,128)(2,1)S(1)} %get-tuple-element.42.a0), channel_id=1, source_target_pairs={{0,8},{4,12},{8,0},{12,4},{1,9},{5,13},{9,1},{13,5},{2,10},{6,14},... | collective-permute-start | bytes 24584 | tf_op jit(solution)/shard_map/ppermute | solution.py:323
  29.0 5.4 %collective-permute-start.9 = (bf16[2,2048]{1,0:T(2,128)(2,1)S(1)}, bf16[2,2048]{1,0:T(2,128)(2,1)S(1)}, u32[]{:S(2)}, u32[]{:S(2)}) collective-permute-start(bf16[2,2048]{1,0:T(2,128)(2,1)S(1)} %get-tuple-element.42.a0), channel_id=1, source_target_pairs={{0,4},{4,8},{8,12},{12,0},{1,5},{5,9},{9,13},{13,1},{2,6},{6,10},{... | collective-permute-start | bytes 24584 | tf_op jit(solution)/shard_map/ppermute | solution.py:323
  36.7 3.2 %collective-permute-start.12 = (bf16[2,4096]{1,0:T(2,128)(2,1)S(1)}, bf16[2,4096]{1,0:T(2,128)(2,1)S(1)}, u32[]{:S(2)}, u32[]{:S(2)}) collective-permute-start(bf16[2,4096]{1,0:T(2,128)(2,1)S(1)} %get-tuple-element.46), channel_id=1, source_target_pairs={{0,1},{1,2},{2,3},{3,0},{4,5},{5,6},{6,7},{7,4},{8,9},{9,10},{10,1... | collective-permute-start | bytes 49160 | tf_op jit(solution)/shard_map/ppermute | solution.py:323
  36.7 3.8 %collective-permute-start.13 = (bf16[2,4096]{1,0:T(2,128)(2,1)S(1)}, bf16[2,4096]{1,0:T(2,128)(2,1)S(1)}, u32[]{:S(2)}, u32[]{:S(2)}) collective-permute-start(bf16[2,4096]{1,0:T(2,128)(2,1)S(1)} %get-tuple-element.47), channel_id=1, source_target_pairs={{0,2},{1,3},{2,0},{3,1},{4,6},{5,7},{6,4},{7,5},{8,10},{9,11},{10,... | collective-permute-start | bytes 49160 | tf_op jit(solution)/shard_map/ppermute | solution.py:323
  38.3 2.8 %collective-permute-start.14 = (bf16[2,4096]{1,0:T(2,128)(2,1)S(1)}, bf16[2,4096]{1,0:T(2,128)(2,1)S(1)}, u32[]{:S(2)}, u32[]{:S(2)}) collective-permute-start(bf16[2,4096]{1,0:T(2,128)(2,1)S(1)} %get-tuple-element.48), channel_id=1, source_target_pairs={{0,3},{1,0},{2,1},{3,2},{4,7},{5,4},{6,5},{7,6},{8,11},{9,8},{10,9... | collective-permute-start | bytes 49160 | tf_op jit(solution)/shard_map/ppermute | solution.py:323

commit v5 on v3

--- a/solution.py
+++ b/solution.py
@@ -194,20 +194,29 @@
     return copies
 
 
-def load_kernel(wo_hbm, wk_hbm, wv_hbm, b_hbm, wo, wkv, b, sems):
+def load_kernel(
+    len_ref, wo_hbm, wk_hbm, wv_hbm, b_hbm, cos_ref, sin_ref, wo, wkv, b, sems
+):
     copies = start_load(b_hbm, b, sems, 0, 1)
     copies += start_load(wk_hbm, wkv.at[:, pl.ds(0, HD)], sems, 1, 1)
     copies += start_load(wv_hbm, wkv.at[:, pl.ds(HD, HD)], sems, 2, 1)
-    copies += start_load(wo_hbm.at[pl.ds(0, wo.shape[0])], wo, sems, 3, 2)
+    copies += start_load(wo_hbm.at[pl.ds(0, wo.shape[0])], wo, sems, 3, 6)
+    angles(len_ref, cos_ref, sin_ref)
     for copy in copies:
         copy.wait()
 
 
 def query_kernel(far, b0, b1, b2, b3, w, wo_hbm, out_ref, wo, acc, sems):
     rows = wo.shape[0]
-    copies = start_load(wo_hbm.at[pl.ds(rows, rows)], wo, sems, 0, 2)
+    copies = start_load(wo_hbm.at[pl.ds(wo_hbm.shape[0] - rows, rows)], wo, sems, 0, 2)
     lhs = jnp.concatenate([b[...].astype(F32) for b in (b0, b1, b2, b3)], axis=0).astype(BF16)
-    acc[...] = jnp.dot(lhs, w[...], preferred_element_type=F32)
+    left = jnp.zeros((lhs.shape[0], w.shape[1] // 2), F32)
+    right = left
+    for c in range(w.shape[0] // 256):
+        rows = slice(c * 256, (c + 1) * 256)
+        left += jnp.dot(lhs[:, rows], w[rows, : left.shape[1]], preferred_element_type=F32)
+        right += jnp.dot(lhs[:, rows], w[rows, left.shape[1] :], preferred_element_type=F32)
+    acc[...] = jnp.concatenate([left, right], axis=1)
     for r in range(acc.shape[0]):
         for h in range(out_ref.shape[1]):
             out_ref[r, pl.ds(h, 1), :] = acc[pl.ds(r, 1), pl.ds(h * HD, HD)]
@@ -215,16 +224,8 @@
         copy.wait()
 
 
-def rest_kernel(ready, len_ref, wo_hbm, cos_ref, sin_ref, wo, sems):
-    rows = wo.shape[0]
-    copies = start_load(wo_hbm.at[pl.ds(wo_hbm.shape[0] - rows, rows)], wo, sems, 0, 4)
-    angles(len_ref, cos_ref, sin_ref)
-    for copy in copies:
-        copy.wait()
-
-
 def payload_kernel(
-    owner_ref, s0, s1, s2, s3, b0, b1, b2, b3, wkv, q_ref, o0, o1, o2, o3, x, pay
+    owner_ref, s0, s1, s2, s3, b0, b1, b2, b3, wkv, q_ref, o0, o3, o2, o1, x, pay
 ):
     gx, gy = lax.axis_index("gx"), lax.axis_index("gy")
     stored = (s0, s1, s2, s3)
@@ -252,13 +253,13 @@
         for r in range(ROWS_DEV):
             pay[target, pl.ds(QUERY + 16 * r, 16), :] = q_ref[k * ROWS_DEV + r]
     o0[...] = pay[0]
+    o3[...] = pay[3].astype(BF16)
+    o2[...] = pay[2].astype(BF16)
     o1[...] = pay[1].astype(BF16)
-    o2[...] = pay[2].astype(BF16)
-    o3[...] = pay[3].astype(BF16)
 
 
 def attend_kernel(
-    len_ref, ready, p0, p1, p2, p3, cos_ref, sin_ref, kv, key_out, value_out, attn_out, attn
+    len_ref, p0, p1, p2, p3, cos_ref, sin_ref, kv, key_out, value_out, attn_out, attn
 ):
     total = p0[...] + p1[...].astype(F32) + p2[...].astype(F32) + p3[...].astype(F32)
     turned = total * cos_ref[...] + pltpu.roll(total, HD // 2, 1) * sin_ref[...]
@@ -292,14 +293,14 @@
     attn_out[...] = attn[...].astype(BF16)
 
 
-def out_kernel(a0, a1, a2, a3, w0, w1, w2, o0, o1, o2, o3, blocks):
+def out_kernel(a0, a1, a2, a3, w0, w1, o0, o3, o2, o1, blocks):
     tag = lax.axis_index("gx") ^ lax.axis_index("gy")
     for s, a in enumerate((a0, a1, a2, a3)):
         blocks[s ^ tag] = a[...].astype(F32)
     lhs = jnp.concatenate([blocks[k] for k in range(4)], axis=0).astype(BF16)
     first = 0
     acc = jnp.zeros((lhs.shape[0], w0.shape[1]), F32)
-    for w in (w0, w1, w2):
+    for w in (w0, w1):
         last = first + w.shape[0]
         acc += jnp.dot(lhs[:, first:last], w[...], preferred_element_type=F32)
         first = last
@@ -310,7 +311,7 @@
 
 
 def others(blocks, axis):
-    return [swap(b, axis, k + 1) for k, b in enumerate(blocks)]
+    return [swap(b, axis, 3 - k) for k, b in enumerate(blocks)]
 
 
 def per_device(stored_rows, new_rows, w_query, w_key, w_value, w_out, kv_cache, cache_len, owner):
@@ -318,27 +319,28 @@
     depth, query_cols = w_query.shape
     width = w_out.shape[1]
     heads = query_cols // HD
-    cut = query_cols * 5 // 16
+    quarter = query_cols // 4
     semaphores = pltpu.SemaphoreType.DMA
     in_vmem = lambda x: pltpu.with_memory_space_constraint(x, pltpu.VMEM)
     in_hbm = lambda x: pltpu.with_memory_space_constraint(x, pltpu.HBM)
     far = swap(stored_rows, "gy", 2)
     near = swap(stored_rows, "gy", 1)
-    fresh = others([new_rows] * 3, "gy")
-    wo_first, wkv, own_fresh = pl.pallas_call(
+    fresh = [swap(new_rows, "gy", k) for k in (1, 2, 3)]
+    cos, sin, wo_first, wkv, own_fresh = pl.pallas_call(
         load_kernel,
-        out_shape=[
-            pltpu.VMEM((cut, width), BF16),
+        out_shape=[pltpu.VMEM((PAY, HD), F32)] * 2
+        + [
+            pltpu.VMEM((query_cols - quarter, width), BF16),
             pltpu.VMEM((depth, 2 * HD), BF16),
             pltpu.VMEM(new_rows.shape, BF16),
         ],
-        in_specs=[whole(pltpu.HBM)] * 4,
-        out_specs=[whole()] * 3,
-        scratch_shapes=[semaphores((5,))],
+        in_specs=[whole(pltpu.SMEM)] + [whole(pltpu.HBM)] * 4,
+        out_specs=[whole()] * 5,
+        scratch_shapes=[semaphores((9,))],
         compiler_params=params(4),
         cost_estimate=cost(1000, 2 * depth * query_cols),
         name="load",
-    )(in_hbm(w_out), in_hbm(w_key), in_hbm(w_value), in_hbm(new_rows))
+    )(cache_len, in_hbm(w_out), in_hbm(w_key), in_hbm(w_value), in_hbm(new_rows))
     far, own_fresh, *fresh = lax.optimization_barrier((far, own_fresh, *fresh))
     far_near = swap(far, "gy", 1)
     fresh = [own_fresh] + fresh
@@ -347,7 +349,7 @@
         query_kernel,
         out_shape=[
             pltpu.VMEM((4 * ROWS_DEV, heads, HD), F32),
-            pltpu.VMEM((cut, width), BF16),
+            pltpu.VMEM((quarter, width), BF16),
         ],
         in_specs=[whole(pl.ANY)] + [whole()] * 5 + [whole(pltpu.HBM)],
         out_specs=[whole()] * 2,
@@ -370,38 +372,27 @@
         name="payload",
     )(owner, *stored, *fresh, wkv, query)
     sums = [payload[0]] + others(payload[1:], "gx")
-    cos, sin, wo_third = pl.pallas_call(
-        rest_kernel,
-        out_shape=[pltpu.VMEM((PAY, HD), F32)] * 2
-        + [pltpu.VMEM((query_cols - 2 * cut, width), BF16)],
-        in_specs=[whole(pl.ANY), whole(pltpu.SMEM), whole(pltpu.HBM)],
-        out_specs=[whole()] * 3,
-        scratch_shapes=[semaphores((4,))],
-        compiler_params=params(4),
-        cost_estimate=cost(2000000, 2 * (query_cols - 2 * cut) * width),
-        name="rest",
-    )(payload[0], cache_len, in_hbm(w_out))
     rebuilt_key, rebuilt_value, attn = pl.pallas_call(
         attend_kernel,
         out_shape=[shape((LC, HD), BF16)] * 2 + [shape((ROWS_DEV, query_cols), BF16)],
-        in_specs=[whole(pltpu.SMEM), whole(pl.ANY)] + [whole()] * 7,
+        in_specs=[whole(pltpu.SMEM)] + [whole()] * 7,
         out_specs=[whole()] * 3,
         scratch_shapes=[pltpu.VMEM((ROWS_DEV, query_cols), F32)],
         compiler_params=params(4),
         cost_estimate=cost(10000000, 1000000),
         name="attend",
-    )(cache_len, wo_third, *sums, cos, sin, kv_cache)
-    attn_all = [attn] + others([attn] * 3, "gx")
+    )(cache_len, *sums, cos, sin, kv_cache)
+    attn_all = [attn] + [swap(attn, "gx", k) for k in (1, 2, 3)]
     parts = pl.pallas_call(
         out_kernel,
         out_shape=[shape((ROWS_DEV, width), F32)] + [shape((ROWS_DEV, width), BF16)] * 3,
-        in_specs=[whole()] * 7,
+        in_specs=[whole()] * 6,
         out_specs=[whole()] * 4,
         scratch_shapes=[pltpu.VMEM((4, ROWS_DEV, query_cols), F32)],
         compiler_params=params(4),
         cost_estimate=cost(2 * 8 * width * query_cols, 2 * width * query_cols),
         name="project",
-    )(*attn_all, wo_first, wo_second, wo_third)
+    )(*attn_all, wo_first, wo_second)
     arrived = others(parts[1:], "gy")
     mixed = parts[0] + arrived[0].astype(F32) + arrived[1].astype(F32) + arrived[2].astype(F32)
     return (mixed.astype(BF16), rebuilt_key[None], rebuilt_value[None])

time: 41.8 us -> 41.7 us (level)
  waiting for transfers between devices: 10.1 us -> 7.98 us
  starting transfers between devices: 16 us -> 16.7 us
  local copies, waits for them, and re-layouts: 0.02 us -> 0.68 us
  Pallas kernels: 14.2 us -> 14.7 us
    ppermute x15, waiting for transfers between devices: 10.1 us -> 7.98 us  [swap(): return lax.ppermute(x, axis, [(i, i ^ k) for i in range(n)])]
    pallas_call x1, Pallas kernels: 2.58 us -> 3.75 us  [per_device(): pl.pallas_call(query_kernel, out_shape=[pltpu.VMEM((4 * ROWS_DEV, heads,...]
    pallas_call x2 -> x1, Pallas kernels: 6.64 us -> 5.9 us  [per_device(): pl.pallas_call(load_kernel, out_shape=[pltpu.VMEM((PAY, HD), F32)] * 2 +...]
    ppermute x15, starting transfers between devices: 16 us -> 16.7 us  [swap(): return lax.ppermute(x, axis, [(i, i ^ k) for i in range(n)])]
    unnamed x10 -> x12, local copies, waits for them, and re-layouts: 0.02 us -> 0.68 us
  transfers between devices with their start and end apart: 15 -> 15, of which waited for: 7 -> 6; matrix products, arithmetic and copies ran while one was open for 0% -> 0% of each run, Pallas kernels for 22% -> 23%
where the time goes in v5:
time: 41.7 us; the launch traced here: 41.4 us
  starting transfers between devices  16.7 us (40%)
  Pallas kernels  14.7 us (35%)
  waiting for transfers between devices  7.98 us (19%)
  between operations  0.78 us (2%)
  local copies, waits for them, and re-layouts  0.68 us (2%)
  other arithmetic  0.64 us (2%)
    ppermute x15, starting transfers between devices, swap(): return lax.ppermute(x, axis, [(i, i ^ k) for i in range(n)])  16.7 us
    ppermute x15, waiting for transfers between devices, swap(): return lax.ppermute(x, axis, [(i, i ^ k) for i in range(n)])  7.98 us
    pallas_call x1, Pallas kernels, per_device(): pl.pallas_call(load_kernel, out_shape=[pltpu.VMEM((PAY, HD), F32)] * 2 +...  5.9 us
    pallas_call x1, Pallas kernels, per_device(): pl.pallas_call(query_kernel, out_shape=[pltpu.VMEM((4 * ROWS_DEV, heads,...  3.75 us
    pallas_call x1, Pallas kernels, per_device(): pl.pallas_call(out_kernel, out_shape=[shape((ROWS_DEV, width), F32)] + [s...  2.28 us
    pallas_call x1, Pallas kernels, per_device(): pl.pallas_call(attend_kernel, out_shape=[shape((LC, HD), BF16)] * 2 + [sh...  1.52 us
    pallas_call x1, Pallas kernels, per_device(): pl.pallas_call(payload_kernel, out_shape=[shape((PAY, HD), F32)] + [shape...  1.2 us
  transfers between devices with their start and end apart: 15, of which 6 were waited for; matrix products, arithmetic and copies ran while one was open for 0% of the time, Pallas kernels for 23%

profile of v5, /device:TPU:0, one launch (start us, length us, event | category | flops | bytes accessed | tf_op | source)
XLA Modules:
  0.0 41.4 jit_solution(1463359728553295182)
XLA Ops:
  0.6 3.0 %collective-permute-start.1 = (bf16[40,4096]{1,0:T(8,128)(2,1)}, bf16[40,4096]{1,0:T(8,128)(2,1)S(1)}, u32[]{:S(2)}, u32[]{:S(2)}) collective-permute-start(bf16[40,4096]{1,0:T(8,128)(2,1)} %s0.1), channel_id=1, source_target_pairs={{0,2},{1,3},{2,0},{3,1},{4,6},{5,7},{6,4},{7,5},{8,10},{9,11},{10,... | collective-permute-start | bytes 983048 | tf_op jit(solution)/shard_map/ppermute | solution.py:34
  3.6 0.2 collective-permute-start.4
  3.9 1.9 %collective-permute-start.3 = (bf16[2,4096]{1,0:T(2,128)(2,1)}, bf16[2,4096]{1,0:T(2,128)(2,1)S(1)}, u32[]{:S(2)}, u32[]{:S(2)}) collective-permute-start(bf16[2,4096]{1,0:T(2,128)(2,1)} %b_hbm.1), channel_id=1, source_target_pairs={{0,2},{1,3},{2,0},{3,1},{4,6},{5,7},{6,4},{7,5},{8,10},{9,11},{10,... | collective-permute-start | bytes 49160 | tf_op jit(solution)/shard_map/ppermute | solution.py:34
  5.8 0.0 collective-permute-start
  5.8 0.7 %copy-done.3 = s32[2]{0:T(128)S(1)} copy-done((s32[2]{0:T(128)S(1)}, s32[2]{0:T(128)}, u32[]{:S(2)}) %copy-start.3) | copy-done | bytes 32
  6.4 5.9 %load.1 = (f32[128,128]{1,0:T(8,128)S(1)}, f32[128,128]{1,0:T(8,128)S(1)}, bf16[1536,4096]{1,0:T(8,128)(2,1)S(1)}, bf16[4096,256]{1,0:T(8,128)(2,1)S(1)}, bf16[2,4096]{1,0:T(2,128)(2,1)S(1)}) custom-call(s32[2]{0:T(128)S(1)} %copy-done.3, bf16[2048,4096]{1,0:T(8,128)(2,1)} %wo_hbm.3, bf16[4096,128]{1,0:T(8,128)(2,1)} %wk_hbm.1, bf16[4096,128]{1,0:T(8,128)(2,1)} %wv_hbm.1, ...), custom_call_target="tpu_custom_call" | custom-call | flops 1000 | bytes 16777216 | tf_op jit(solution)/shard_map/load/pallas_call | solution.py:329
  12.4 0.0 collective-permute-done.2.b1
  12.4 0.0 collective-permute-done.4.b3
  12.4 0.0 collective-permute-done.1.far.s2
  12.4 0.0 copy-start.2
  12.4 0.0 copy-start.5
  12.4 0.0 copy-start.1
  12.4 0.0 copy-start.4
  12.4 0.6 %collective-permute-start.5 = (bf16[40,4096]{1,0:T(8,128)(2,1)S(1)}, bf16[40,4096]{1,0:T(8,128)(2,1)S(1)}, u32[]{:S(2)}, u32[]{:S(2)}) collective-permute-start(bf16[40,4096]{1,0:T(8,128)(2,1)S(1)} %collective-permute-done.1.far.s2), channel_id=1, source_target_pairs={{0,1},{1,0},{2,3},{3,2},{4,5},{5,4},{6,7},{7,6},{8,9},{9,8},{10,11... | collective-permute-start | bytes 983048 | tf_op jit(solution)/shard_map/ppermute | solution.py:34
  13.0 3.7 %query.1 = (f32[8,16,128]{2,1,0:T(8,128)S(1)}, bf16[512,4096]{1,0:T(8,128)(2,1)S(1)}) custom-call(bf16[40,4096]{1,0:T(8,128)(2,1)S(1)} %collective-permute-done.1.far.s2, bf16[2,4096]{1,0:T(2,128)(2,1)S(1)} %get-tuple-element.28.b0, bf16[2,4096]{1,0:T(2,128)(2,1)S(1)} %collective-permute-done.2.b1, bf16[2,4096]{1,0:T(2,128)(2,1)S(1)} %collective-permute-done.3.b2, ...), custom_call_target="tpu_custom_call" | custom-call | flops 134217728 | bytes 2097152 | tf_op jit(solution)/shard_map/query/pallas_call | solution.py:348
  16.8 1.2 %payload.1 = (f32[128,128]{1,0:T(8,128)S(1)}, bf16[128,128]{1,0:T(8,128)(2,1)S(1)}, bf16[128,128]{1,0:T(8,128)(2,1)S(1)}, bf16[128,128]{1,0:T(8,128)(2,1)S(1)}) custom-call(s32[4]{0:T(128)S(1)} %copy-done.5, bf16[40,4096]{1,0:T(8,128)(2,1)S(1)} %copy-done.2, bf16[40,4096]{1,0:T(8,128)(2,1)S(1)} %collective-permute-done.s1, ...), custom_call_target="tpu_custom_call" | custom-call | flops 436207616 | bytes 2097152 | tf_op jit(solution)/shard_map/payload/pallas_call | solution.py:361
  18.0 4.1 %collective-permute-start.6 = (bf16[128,128]{1,0:T(8,128)(2,1)S(1)}, bf16[128,128]{1,0:T(8,128)(2,1)S(1)}, u32[]{:S(2)}, u32[]{:S(2)}) collective-permute-start(bf16[128,128]{1,0:T(8,128)(2,1)S(1)} %get-tuple-element.35), channel_id=1, source_target_pairs={{0,12},{4,8},{8,4},{12,0},{1,13},{5,9},{9,5},{13,1},{2,14},{6,10},... | collective-permute-start | bytes 98312 | tf_op jit(solution)/shard_map/ppermute | solution.py:34
  22.1 0.6 %collective-permute-start.8 = (bf16[128,128]{1,0:T(8,128)(2,1)S(1)}, bf16[128,128]{1,0:T(8,128)(2,1)S(1)}, u32[]{:S(2)}, u32[]{:S(2)}) collective-permute-start(bf16[128,128]{1,0:T(8,128)(2,1)S(1)} %get-tuple-element.37), channel_id=1, source_target_pairs={{0,4},{4,0},{8,12},{12,8},{1,5},{5,1},{9,13},{13,9},{2,6},{6,2},{1... | collective-permute-start | bytes 98312 | tf_op jit(solution)/shard_map/ppermute | solution.py:34
  22.7 1.4 %collective-permute-done.6.p1 = bf16[128,128]{1,0:T(8,128)(2,1)S(1)} collective-permute-done((bf16[128,128]{1,0:T(8,128)(2,1)S(1)}, bf16[128,128]{1,0:T(8,128)(2,1)S(1)}, u32[]{:S(2)}, u32[]{:S(2)}) %collective-permute-start.6) | collective-permute-done | bytes 32800 | tf_op jit(solution)/shard_map/ppermute | solution.py:34
  24.1 2.8 %collective-permute-done.7.p2 = bf16[128,128]{1,0:T(8,128)(2,1)S(1)} collective-permute-done((bf16[128,128]{1,0:T(8,128)(2,1)S(1)}, bf16[128,128]{1,0:T(8,128)(2,1)S(1)}, u32[]{:S(2)}, u32[]{:S(2)}) %collective-permute-start.7) | collective-permute-done | bytes 32800 | tf_op jit(solution)/shard_map/ppermute | solution.py:34
  26.9 1.5 %attend.1 = (bf16[40,128]{1,0:T(8,128)(2,1)}, bf16[40,128]{1,0:T(8,128)(2,1)}, bf16[2,2048]{1,0:T(2,128)(2,1)S(1)}) custom-call(s32[2]{0:T(128)S(1)} %copy-done.4, f32[128,128]{1,0:T(8,128)S(1)} %get-tuple-element.34.p0, bf16[128,128]{1,0:T(8,128)(2,1)S(1)} %collective-permute-done.6.p1, bf16[128,128]{1,0:T(8,128)(2,1)S(1)} %collective-permute-done.7.p2, ...), custom_call_target="tpu_custom_call" | custom-call | flops 10000000 | bytes 1000000 | tf_op jit(solution)/shard_map/attend/pallas_call | solution.py:375
  28.5 1.5 %collective-permute-start.11 = (bf16[2,2048]{1,0:T(2,128)(2,1)S(1)}, bf16[2,2048]{1,0:T(2,128)(2,1)S(1)}, u32[]{:S(2)}, u32[]{:S(2)}) collective-permute-start(bf16[2,2048]{1,0:T(2,128)(2,1)S(1)} %get-tuple-element.40.a0), channel_id=1, source_target_pairs={{0,12},{4,8},{8,4},{12,0},{1,13},{5,9},{9,5},{13,1},{2,14},{6,10},... | collective-permute-start | bytes 24584 | tf_op jit(solution)/shard_map/ppermute | solution.py:34
  29.9 0.6 %collective-permute-start.10 = (bf16[2,2048]{1,0:T(2,128)(2,1)S(1)}, bf16[2,2048]{1,0:T(2,128)(2,1)S(1)}, u32[]{:S(2)}, u32[]{:S(2)}) collective-permute-start(bf16[2,2048]{1,0:T(2,128)(2,1)S(1)} %get-tuple-element.40.a0), channel_id=1, source_target_pairs={{0,8},{4,12},{8,0},{12,4},{1,9},{5,13},{9,1},{13,5},{2,10},{6,14},... | collective-permute-start | bytes 24584 | tf_op jit(solution)/shard_map/ppermute | solution.py:34
  30.5 2.3 %collective-permute-start.9 = (bf16[2,2048]{1,0:T(2,128)(2,1)S(1)}, bf16[2,2048]{1,0:T(2,128)(2,1)S(1)}, u32[]{:S(2)}, u32[]{:S(2)}) collective-permute-start(bf16[2,2048]{1,0:T(2,128)(2,1)S(1)} %get-tuple-element.40.a0), channel_id=1, source_target_pairs={{0,4},{4,0},{8,12},{12,8},{1,5},{5,1},{9,13},{13,9},{2,6},{6,2},{1... | collective-permute-start | bytes 24584 | tf_op jit(solution)/shard_map/ppermute | solution.py:34
  32.8 1.1 %collective-permute-done.11.a3 = bf16[2,2048]{1,0:T(2,128)(2,1)S(1)} collective-permute-done((bf16[2,2048]{1,0:T(2,128)(2,1)S(1)}, bf16[2,2048]{1,0:T(2,128)(2,1)S(1)}, u32[]{:S(2)}, u32[]{:S(2)}) %collective-permute-start.11) | collective-permute-done | bytes 8224 | tf_op jit(solution)/shard_map/ppermute | solution.py:34
  34.0 0.6 %collective-permute-done.10.a2 = bf16[2,2048]{1,0:T(2,128)(2,1)S(1)} collective-permute-done((bf16[2,2048]{1,0:T(2,128)(2,1)S(1)}, bf16[2,2048]{1,0:T(2,128)(2,1)S(1)}, u32[]{:S(2)}, u32[]{:S(2)}) %collective-permute-start.10) | collective-permute-done | bytes 8224 | tf_op jit(solution)/shard_map/ppermute | solution.py:34
  34.6 2.3 %project.1 = (f32[2,4096]{1,0:T(2,128)S(1)}, bf16[2,4096]{1,0:T(2,128)(2,1)S(1)}, bf16[2,4096]{1,0:T(2,128)(2,1)S(1)}, bf16[2,4096]{1,0:T(2,128)(2,1)S(1)}) custom-call(bf16[2,2048]{1,0:T(2,128)(2,1)S(1)} %get-tuple-element.40.a0, bf16[2,2048]{1,0:T(2,128)(2,1)S(1)} %collective-permute-done.9.a1, bf16[2,2048]{1,0:T(2,128)(2,1)S(1)} %collective-permute-done.10.a2, ...), custom_call_target="tpu_custom_call" | custom-call | flops 134217728 | bytes 16777216 | tf_op jit(solution)/shard_map/project/pallas_call | solution.py:386
  36.8 0.9 %collective-permute-start.13 = (bf16[2,4096]{1,0:T(2,128)(2,1)S(1)}, bf16[2,4096]{1,0:T(2,128)(2,1)S(1)}, u32[]{:S(2)}, u32[]{:S(2)}) collective-permute-start(bf16[2,4096]{1,0:T(2,128)(2,1)S(1)} %get-tuple-element.45), channel_id=1, source_target_pairs={{0,2},{1,3},{2,0},{3,1},{4,6},{5,7},{6,4},{7,5},{8,10},{9,11},{10,... | collective-permute-start | bytes 49160 | tf_op jit(solution)/shard_map/ppermute | solution.py:34
  37.8 0.9 %collective-permute-start.14 = (bf16[2,4096]{1,0:T(2,128)(2,1)S(1)}, bf16[2,4096]{1,0:T(2,128)(2,1)S(1)}, u32[]{:S(2)}, u32[]{:S(2)}) collective-permute-start(bf16[2,4096]{1,0:T(2,128)(2,1)S(1)} %get-tuple-element.46), channel_id=1, source_target_pairs={{0,1},{1,0},{2,3},{3,2},{4,5},{5,4},{6,7},{7,6},{8,9},{9,8},{10,11... | collective-permute-start | bytes 49160 | tf_op jit(solution)/shard_map/ppermute | solution.py:34
  38.7 1.3 %collective-permute-done.12 = bf16[2,4096]{1,0:T(2,128)(2,1)S(1)} collective-permute-done((bf16[2,4096]{1,0:T(2,128)(2,1)S(1)}, bf16[2,4096]{1,0:T(2,128)(2,1)S(1)}, u32[]{:S(2)}, u32[]{:S(2)}) %collective-permute-start.12) | collective-permute-done | bytes 16416 | tf_op jit(solution)/shard_map/ppermute | solution.py:34
  40.0 0.8 %collective-permute-done.13 = bf16[2,4096]{1,0:T(2,128)(2,1)S(1)} collective-permute-done((bf16[2,4096]{1,0:T(2,128)(2,1)S(1)}, bf16[2,4096]{1,0:T(2,128)(2,1)S(1)}, u32[]{:S(2)}, u32[]{:S(2)}) %collective-permute-start.13) | collective-permute-done | bytes 16416 | tf_op jit(solution)/shard_map/ppermute | solution.py:34
  40.8 0.6 %add_convert_fusion = bf16[2,4096]{1,0:T(2,128)(2,1)} fusion(bf16[2,4096]{1,0:T(2,128)(2,1)S(1)} %collective-permute-done.14, bf16[2,4096]{1,0:T(2,128)(2,1)S(1)} %collective-permute-done.13, f32[2,4096]{1,0:T(2,128)S(1)} %get-tuple-element.43, bf16[2,4096]{1,0:T(2,128)(2,1)S(1)} %collective-permute-done.12), kind=kLoop, calls=%fused_computation | loop fusion | flops 57344 | bytes 98304 | tf_op jit(solution)/shard_map/convert_element_type | solution.py:398
  (16 shorter events, 0.0 us)
Async XLA Ops:
  0.6 12.4 %copy-start = (bf16[4096,2048]{1,0:T(8,128)(2,1)S(1)}, bf16[4096,2048]{1,0:T(8,128)(2,1)}, u32[]{:S(2)}) copy-start(bf16[4096,2048]{1,0:T(8,128)(2,1)} %w.1) | copy-start | bytes 50331652
  0.6 11.7 %collective-permute-start.1 = (bf16[40,4096]{1,0:T(8,128)(2,1)}, bf16[40,4096]{1,0:T(8,128)(2,1)S(1)}, u32[]{:S(2)}, u32[]{:S(2)}) collective-permute-start(bf16[40,4096]{1,0:T(8,128)(2,1)} %s0.1), channel_id=1, source_target_pairs={{0,2},{1,3},{2,0},{3,1},{4,6},{5,7},{6,4},{7,5},{8,10},{9,11},{10,... | collective-permute-start | bytes 983048 | tf_op jit(solution)/shard_map/ppermute | solution.py:34
  3.6 8.7 %collective-permute-start.2 = (bf16[2,4096]{1,0:T(2,128)(2,1)}, bf16[2,4096]{1,0:T(2,128)(2,1)S(1)}, u32[]{:S(2)}, u32[]{:S(2)}) collective-permute-start(bf16[2,4096]{1,0:T(2,128)(2,1)} %b_hbm.1), channel_id=1, source_target_pairs={{0,1},{1,0},{2,3},{3,2},{4,5},{5,4},{6,7},{7,6},{8,9},{9,8},{10,11... | collective-permute-start | bytes 49160 | tf_op jit(solution)/shard_map/ppermute | solution.py:34
  3.6 8.7 %collective-permute-start.4 = (bf16[2,4096]{1,0:T(2,128)(2,1)}, bf16[2,4096]{1,0:T(2,128)(2,1)S(1)}, u32[]{:S(2)}, u32[]{:S(2)}) collective-permute-start(bf16[2,4096]{1,0:T(2,128)(2,1)} %b_hbm.1), channel_id=1, source_target_pairs={{0,3},{1,2},{2,1},{3,0},{4,7},{5,6},{6,5},{7,4},{8,11},{9,10},{10,... | collective-permute-start | bytes 49160 | tf_op jit(solution)/shard_map/ppermute | solution.py:34
  3.9 8.5 %collective-permute-start.3 = (bf16[2,4096]{1,0:T(2,128)(2,1)}, bf16[2,4096]{1,0:T(2,128)(2,1)S(1)}, u32[]{:S(2)}, u32[]{:S(2)}) collective-permute-start(bf16[2,4096]{1,0:T(2,128)(2,1)} %b_hbm.1), channel_id=1, source_target_pairs={{0,2},{1,3},{2,0},{3,1},{4,6},{5,7},{6,4},{7,5},{8,10},{9,11},{10,... | collective-permute-start | bytes 49160 | tf_op jit(solution)/shard_map/ppermute | solution.py:34
  5.8 11.0 %collective-permute-start = (bf16[40,4096]{1,0:T(8,128)(2,1)}, bf16[40,4096]{1,0:T(8,128)(2,1)S(1)}, u32[]{:S(2)}, u32[]{:S(2)}) collective-permute-start(bf16[40,4096]{1,0:T(8,128)(2,1)} %s0.1), channel_id=1, source_target_pairs={{0,1},{1,0},{2,3},{3,2},{4,5},{5,4},{6,7},{7,6},{8,9},{9,8},{10,11... | collective-permute-start | bytes 983048 | tf_op jit(solution)/shard_map/ppermute | solution.py:34
  5.8 0.7 %copy-start.3 = (s32[2]{0:T(128)S(1)}, s32[2]{0:T(128)}, u32[]{:S(2)}) copy-start(s32[2]{0:T(128)} %len_ref.3) | copy-start | bytes 28
  12.4 4.4 %copy-start.2 = (bf16[40,4096]{1,0:T(8,128)(2,1)S(1)}, bf16[40,4096]{1,0:T(8,128)(2,1)}, u32[]{:S(2)}) copy-start(bf16[40,4096]{1,0:T(8,128)(2,1)} %s0.1) | copy-start | bytes 983044
  12.4 4.4 %copy-start.5 = (s32[4]{0:T(128)S(1)}, s32[4]{0:T(128)}, u32[]{:S(2)}) copy-start(s32[4]{0:T(128)} %owner_ref.1) | copy-start | bytes 52
  12.4 14.5 %copy-start.1 = (bf16[2,2,512,128]{3,2,1,0:T(8,128)(2,1)S(1)}, bf16[2,2,512,128]{3,2,1,0:T(8,128)(2,1)}, u32[]{:S(2)}) copy-start(bf16[2,2,512,128]{3,2,1,0:T(8,128)(2,1)} %kv.1) | copy-start | bytes 1572868
  12.4 14.5 %copy-start.4 = (s32[2]{0:T(128)S(1)}, s32[2]{0:T(128)}, u32[]{:S(2)}) copy-start(s32[2]{0:T(128)} %len_ref.3) | copy-start | bytes 28
  12.4 4.3 %collective-permute-start.5 = (bf16[40,4096]{1,0:T(8,128)(2,1)S(1)}, bf16[40,4096]{1,0:T(8,128)(2,1)S(1)}, u32[]{:S(2)}, u32[]{:S(2)}) collective-permute-start(bf16[40,4096]{1,0:T(8,128)(2,1)S(1)} %collective-permute-done.1.far.s2), channel_id=1, source_target_pairs={{0,1},{1,0},{2,3},{3,2},{4,5},{5,4},{6,7},{7,6},{8,9},{9,8},{10,11... | collective-permute-start | bytes 983048 | tf_op jit(solution)/shard_map/ppermute | solution.py:34
  18.0 6.1 %collective-permute-start.6 = (bf16[128,128]{1,0:T(8,128)(2,1)S(1)}, bf16[128,128]{1,0:T(8,128)(2,1)S(1)}, u32[]{:S(2)}, u32[]{:S(2)}) collective-permute-start(bf16[128,128]{1,0:T(8,128)(2,1)S(1)} %get-tuple-element.35), channel_id=1, source_target_pairs={{0,12},{4,8},{8,4},{12,0},{1,13},{5,9},{9,5},{13,1},{2,14},{6,10},... | collective-permute-start | bytes 98312 | tf_op jit(solution)/shard_map/ppermute | solution.py:34
  22.1 4.8 %collective-permute-start.7 = (bf16[128,128]{1,0:T(8,128)(2,1)S(1)}, bf16[128,128]{1,0:T(8,128)(2,1)S(1)}, u32[]{:S(2)}, u32[]{:S(2)}) collective-permute-start(bf16[128,128]{1,0:T(8,128)(2,1)S(1)} %get-tuple-element.36), channel_id=1, source_target_pairs={{0,8},{4,12},{8,0},{12,4},{1,9},{5,13},{9,1},{13,5},{2,10},{6,14},... | collective-permute-start | bytes 98312 | tf_op jit(solution)/shard_map/ppermute | solution.py:34
  22.1 4.8 %collective-permute-start.8 = (bf16[128,128]{1,0:T(8,128)(2,1)S(1)}, bf16[128,128]{1,0:T(8,128)(2,1)S(1)}, u32[]{:S(2)}, u32[]{:S(2)}) collective-permute-start(bf16[128,128]{1,0:T(8,128)(2,1)S(1)} %get-tuple-element.37), channel_id=1, source_target_pairs={{0,4},{4,0},{8,12},{12,8},{1,5},{5,1},{9,13},{13,9},{2,6},{6,2},{1... | collective-permute-start | bytes 98312 | tf_op jit(solution)/shard_map/ppermute | solution.py:34
  28.5 5.5 %collective-permute-start.11 = (bf16[2,2048]{1,0:T(2,128)(2,1)S(1)}, bf16[2,2048]{1,0:T(2,128)(2,1)S(1)}, u32[]{:S(2)}, u32[]{:S(2)}) collective-permute-start(bf16[2,2048]{1,0:T(2,128)(2,1)S(1)} %get-tuple-element.40.a0), channel_id=1, source_target_pairs={{0,12},{4,8},{8,4},{12,0},{1,13},{5,9},{9,5},{13,1},{2,14},{6,10},... | collective-permute-start | bytes 24584 | tf_op jit(solution)/shard_map/ppermute | solution.py:34
  29.9 4.6 %collective-permute-start.10 = (bf16[2,2048]{1,0:T(2,128)(2,1)S(1)}, bf16[2,2048]{1,0:T(2,128)(2,1)S(1)}, u32[]{:S(2)}, u32[]{:S(2)}) collective-permute-start(bf16[2,2048]{1,0:T(2,128)(2,1)S(1)} %get-tuple-element.40.a0), channel_id=1, source_target_pairs={{0,8},{4,12},{8,0},{12,4},{1,9},{5,13},{9,1},{13,5},{2,10},{6,14},... | collective-permute-start | bytes 24584 | tf_op jit(solution)/shard_map/ppermute | solution.py:34
  30.5 4.0 %collective-permute-start.9 = (bf16[2,2048]{1,0:T(2,128)(2,1)S(1)}, bf16[2,2048]{1,0:T(2,128)(2,1)S(1)}, u32[]{:S(2)}, u32[]{:S(2)}) collective-permute-start(bf16[2,2048]{1,0:T(2,128)(2,1)S(1)} %get-tuple-element.40.a0), channel_id=1, source_target_pairs={{0,4},{4,0},{8,12},{12,8},{1,5},{5,1},{9,13},{13,9},{2,6},{6,2},{1... | collective-permute-start | bytes 24584 | tf_op jit(solution)/shard_map/ppermute | solution.py:34
  36.8 3.2 %collective-permute-start.12 = (bf16[2,4096]{1,0:T(2,128)(2,1)S(1)}, bf16[2,4096]{1,0:T(2,128)(2,1)S(1)}, u32[]{:S(2)}, u32[]{:S(2)}) collective-permute-start(bf16[2,4096]{1,0:T(2,128)(2,1)S(1)} %get-tuple-element.44), channel_id=1, source_target_pairs={{0,3},{1,2},{2,1},{3,0},{4,7},{5,6},{6,5},{7,4},{8,11},{9,10},{10,... | collective-permute-start | bytes 49160 | tf_op jit(solution)/shard_map/ppermute | solution.py:34
  36.8 3.9 %collective-permute-start.13 = (bf16[2,4096]{1,0:T(2,128)(2,1)S(1)}, bf16[2,4096]{1,0:T(2,128)(2,1)S(1)}, u32[]{:S(2)}, u32[]{:S(2)}) collective-permute-start(bf16[2,4096]{1,0:T(2,128)(2,1)S(1)} %get-tuple-element.45), channel_id=1, source_target_pairs={{0,2},{1,3},{2,0},{3,1},{4,6},{5,7},{6,4},{7,5},{8,10},{9,11},{10,... | collective-permute-start | bytes 49160 | tf_op jit(solution)/shard_map/ppermute | solution.py:34
  37.8 3.0 %collective-permute-start.14 = (bf16[2,4096]{1,0:T(2,128)(2,1)S(1)}, bf16[2,4096]{1,0:T(2,128)(2,1)S(1)}, u32[]{:S(2)}, u32[]{:S(2)}) collective-permute-start(bf16[2,4096]{1,0:T(2,128)(2,1)S(1)} %get-tuple-element.46), channel_id=1, source_target_pairs={{0,1},{1,0},{2,3},{3,2},{4,5},{5,4},{6,7},{7,6},{8,9},{9,8},{10,11... | collective-permute-start | bytes 49160 | tf_op jit(solution)/shard_map/ppermute | solution.py:34

commit v6 on v5

--- a/solution.py
+++ b/solution.py
@@ -1,3 +1,4 @@
+import functools
 import math
 
 import jax
@@ -195,28 +196,31 @@
 
 
 def load_kernel(
-    len_ref, wo_hbm, wk_hbm, wv_hbm, b_hbm, cos_ref, sin_ref, wo, wkv, b, sems
+    len_hbm, wo_hbm, wk_hbm, wv_hbm, b_hbm, cos_ref, sin_ref, wo, wkv, b, len_ref, sems
 ):
+    lengths = pltpu.make_async_copy(len_hbm, len_ref, sems.at[9])
+    lengths.start()
     copies = start_load(b_hbm, b, sems, 0, 1)
     copies += start_load(wk_hbm, wkv.at[:, pl.ds(0, HD)], sems, 1, 1)
     copies += start_load(wv_hbm, wkv.at[:, pl.ds(HD, HD)], sems, 2, 1)
-    copies += start_load(wo_hbm.at[pl.ds(0, wo.shape[0])], wo, sems, 3, 6)
+    copies += start_load(wo_hbm.at[pl.ds(0, wo.shape[0])], wo, sems, 3, 5)
+    lengths.wait()
     angles(len_ref, cos_ref, sin_ref)
     for copy in copies:
         copy.wait()
 
 
-def query_kernel(far, b0, b1, b2, b3, w, wo_hbm, out_ref, wo, acc, sems):
+def rest_kernel(ready, wo_hbm, wo, sems):
     rows = wo.shape[0]
-    copies = start_load(wo_hbm.at[pl.ds(wo_hbm.shape[0] - rows, rows)], wo, sems, 0, 2)
+    for copy in start_load(wo_hbm.at[pl.ds(wo_hbm.shape[0] - rows, rows)], wo, sems, 0, 2):
+        copy.wait()
+
+
+def query_kernel(first, far, b0, b1, b2, b3, w, wo_hbm, out_ref, wo, acc, sems):
+    rows = wo.shape[0]
+    copies = start_load(wo_hbm.at[pl.ds(first, rows)], wo, sems, 0, 2)
     lhs = jnp.concatenate([b[...].astype(F32) for b in (b0, b1, b2, b3)], axis=0).astype(BF16)
-    left = jnp.zeros((lhs.shape[0], w.shape[1] // 2), F32)
-    right = left
-    for c in range(w.shape[0] // 256):
-        rows = slice(c * 256, (c + 1) * 256)
-        left += jnp.dot(lhs[:, rows], w[rows, : left.shape[1]], preferred_element_type=F32)
-        right += jnp.dot(lhs[:, rows], w[rows, left.shape[1] :], preferred_element_type=F32)
-    acc[...] = jnp.concatenate([left, right], axis=1)
+    acc[...] = jnp.dot(lhs, w[...], preferred_element_type=F32)
     for r in range(acc.shape[0]):
         for h in range(out_ref.shape[1]):
             out_ref[r, pl.ds(h, 1), :] = acc[pl.ds(r, 1), pl.ds(h * HD, HD)]
@@ -259,7 +263,7 @@
 
 
 def attend_kernel(
-    len_ref, p0, p1, p2, p3, cos_ref, sin_ref, kv, key_out, value_out, attn_out, attn
+    len_ref, ready, p0, p1, p2, p3, cos_ref, sin_ref, kv, key_out, value_out, attn_out, attn
 ):
     total = p0[...] + p1[...].astype(F32) + p2[...].astype(F32) + p3[...].astype(F32)
     turned = total * cos_ref[...] + pltpu.roll(total, HD // 2, 1) * sin_ref[...]
@@ -293,14 +297,14 @@
     attn_out[...] = attn[...].astype(BF16)
 
 
-def out_kernel(a0, a1, a2, a3, w0, w1, o0, o3, o2, o1, blocks):
+def out_kernel(a0, a1, a2, a3, w0, w1, w2, o0, o3, o2, o1, blocks):
     tag = lax.axis_index("gx") ^ lax.axis_index("gy")
     for s, a in enumerate((a0, a1, a2, a3)):
         blocks[s ^ tag] = a[...].astype(F32)
     lhs = jnp.concatenate([blocks[k] for k in range(4)], axis=0).astype(BF16)
     first = 0
     acc = jnp.zeros((lhs.shape[0], w0.shape[1]), F32)
-    for w in (w0, w1):
+    for w in (w0, w1, w2):
         last = first + w.shape[0]
         acc += jnp.dot(lhs[:, first:last], w[...], preferred_element_type=F32)
         first = last
@@ -319,7 +323,7 @@
     depth, query_cols = w_query.shape
     width = w_out.shape[1]
     heads = query_cols // HD
-    quarter = query_cols // 4
+    last, quarter = query_cols // 8, query_cols // 4
     semaphores = pltpu.SemaphoreType.DMA
     in_vmem = lambda x: pltpu.with_memory_space_constraint(x, pltpu.VMEM)
     in_hbm = lambda x: pltpu.with_memory_space_constraint(x, pltpu.HBM)
@@ -330,23 +334,23 @@
         load_kernel,
         out_shape=[pltpu.VMEM((PAY, HD), F32)] * 2
         + [
-            pltpu.VMEM((query_cols - quarter, width), BF16),
+            pltpu.VMEM((query_cols - quarter - last, width), BF16),
             pltpu.VMEM((depth, 2 * HD), BF16),
             pltpu.VMEM(new_rows.shape, BF16),
         ],
-        in_specs=[whole(pltpu.SMEM)] + [whole(pltpu.HBM)] * 4,
+        in_specs=[whole(pltpu.HBM)] * 5,
         out_specs=[whole()] * 5,
-        scratch_shapes=[semaphores((9,))],
+        scratch_shapes=[pltpu.SMEM(cache_len.shape, jnp.int32), semaphores((10,))],
         compiler_params=params(4),
         cost_estimate=cost(1000, 2 * depth * query_cols),
         name="load",
-    )(cache_len, in_hbm(w_out), in_hbm(w_key), in_hbm(w_value), in_hbm(new_rows))
+    )(in_hbm(cache_len), in_hbm(w_out), in_hbm(w_key), in_hbm(w_value), in_hbm(new_rows))
     far, own_fresh, *fresh = lax.optimization_barrier((far, own_fresh, *fresh))
     far_near = swap(far, "gy", 1)
     fresh = [own_fresh] + fresh
     stored = [stored_rows, near, far, far_near]
     query, wo_second = pl.pallas_call(
-        query_kernel,
+        functools.partial(query_kernel, query_cols - quarter - last),
         out_shape=[
             pltpu.VMEM((4 * ROWS_DEV, heads, HD), F32),
             pltpu.VMEM((quarter, width), BF16),
@@ -372,27 +376,37 @@
         name="payload",
     )(owner, *stored, *fresh, wkv, query)
     sums = [payload[0]] + others(payload[1:], "gx")
+    wo_third = pl.pallas_call(
+        rest_kernel,
+        out_shape=pltpu.VMEM((last, width), BF16),
+        in_specs=[whole(pl.ANY), whole(pltpu.HBM)],
+        out_specs=whole(),
+        scratch_shapes=[semaphores((2,))],
+        compiler_params=params(4),
+        cost_estimate=cost(1000, 2 * last * width),
+        name="rest",
+    )(payload[0], in_hbm(w_out))
     rebuilt_key, rebuilt_value, attn = pl.pallas_call(
         attend_kernel,
         out_shape=[shape((LC, HD), BF16)] * 2 + [shape((ROWS_DEV, query_cols), BF16)],
-        in_specs=[whole(pltpu.SMEM)] + [whole()] * 7,
+        in_specs=[whole(pltpu.SMEM), whole(pl.ANY)] + [whole()] * 7,
         out_specs=[whole()] * 3,
         scratch_shapes=[pltpu.VMEM((ROWS_DEV, query_cols), F32)],
         compiler_params=params(4),
         cost_estimate=cost(10000000, 1000000),
         name="attend",
-    )(cache_len, *sums, cos, sin, kv_cache)
+    )(cache_len, wo_third, *sums, cos, sin, kv_cache)
     attn_all = [attn] + [swap(attn, "gx", k) for k in (1, 2, 3)]
     parts = pl.pallas_call(
         out_kernel,
         out_shape=[shape((ROWS_DEV, width), F32)] + [shape((ROWS_DEV, width), BF16)] * 3,
-        in_specs=[whole()] * 6,
+        in_specs=[whole()] * 7,
         out_specs=[whole()] * 4,
         scratch_shapes=[pltpu.VMEM((4, ROWS_DEV, query_cols), F32)],
         compiler_params=params(4),
         cost_estimate=cost(2 * 8 * width * query_cols, 2 * width * query_cols),
         name="project",
-    )(*attn_all, wo_first, wo_second)
+    )(*attn_all, wo_first, wo_second, wo_third)
     arrived = others(parts[1:], "gy")
     mixed = parts[0] + arrived[0].astype(F32) + arrived[1].astype(F32) + arrived[2].astype(F32)
     return (mixed.astype(BF16), rebuilt_key[None], rebuilt_value[None])

time: 41.7 us -> 39.3 us (0.942)
  Pallas kernels: 14.7 us -> 13.7 us
  local copies, waits for them, and re-layouts: 0.68 us -> 0.02 us
  starting transfers between devices: 16.7 us -> 16.1 us
    pallas_call x1, Pallas kernels: 5.9 us -> 4.77 us  [per_device(): pl.pallas_call(load_kernel, out_shape=[pltpu.VMEM((PAY, HD), F32)] * 2 +...]
    unnamed x12 -> x10, local copies, waits for them, and re-layouts: 0.68 us -> 0.02 us
    ppermute x15, starting transfers between devices: 16.7 us -> 16.1 us  [swap(): return lax.ppermute(x, axis, [(i, i ^ k) for i in range(n)])]
    pallas_call x1 -> x2, Pallas kernels: 3.75 us -> 3.88 us  [the longest x1 2.33 us: per_device(): pl.pallas_call(functools.partial(query_kernel, query_cols - quarter - las...]
  transfers between devices with their start and end apart: 15 -> 15, of which waited for: 6 -> 7; matrix products, arithmetic and copies ran while one was open for 0% -> 0% of each run, Pallas kernels for 23% -> 22%
where the time goes in v6:
time: 39.3 us; the launch traced here: 39.1 us
  starting transfers between devices  16.1 us (41%)
  Pallas kernels  13.7 us (35%)
  waiting for transfers between devices  7.97 us (20%)
  between operations  0.78 us (2%)
  other arithmetic  0.64 us (2%)
    ppermute x15, starting transfers between devices, swap(): return lax.ppermute(x, axis, [(i, i ^ k) for i in range(n)])  16.1 us
    ppermute x15, waiting for transfers between devices, swap(): return lax.ppermute(x, axis, [(i, i ^ k) for i in range(n)])  7.97 us
    pallas_call x1, Pallas kernels, per_device(): pl.pallas_call(load_kernel, out_shape=[pltpu.VMEM((PAY, HD), F32)] * 2 +...  4.77 us
    pallas_call x1, Pallas kernels, per_device(): pl.pallas_call(functools.partial(query_kernel, query_cols - quarter - las...  2.33 us
    pallas_call x1, Pallas kernels, per_device(): pl.pallas_call(out_kernel, out_shape=[shape((ROWS_DEV, width), F32)] + [s...  2.27 us
    pallas_call x1, Pallas kernels, per_device(): pl.pallas_call(rest_kernel, out_shape=pltpu.VMEM((last, width), BF16), in...  1.56 us
    pallas_call x1, Pallas kernels, per_device(): pl.pallas_call(attend_kernel, out_shape=[shape((LC, HD), BF16)] * 2 + [sh...  1.52 us
    pallas_call x1, Pallas kernels, per_device(): pl.pallas_call(payload_kernel, out_shape=[shape((PAY, HD), F32)] + [shape...  1.2 us
  transfers between devices with their start and end apart: 15, of which 7 were waited for; matrix products, arithmetic and copies ran while one was open for 0% of the time, Pallas kernels for 22%

profile of v6, /device:TPU:0, one launch (start us, length us, event | category | flops | bytes accessed | tf_op | source)
XLA Modules:
  0.0 39.1 jit_solution(17510774830187102759)
XLA Ops:
  0.6 3.0 %collective-permute-start.1 = (bf16[40,4096]{1,0:T(8,128)(2,1)}, bf16[40,4096]{1,0:T(8,128)(2,1)S(1)}, u32[]{:S(2)}, u32[]{:S(2)}) collective-permute-start(bf16[40,4096]{1,0:T(8,128)(2,1)} %s0.1), channel_id=1, source_target_pairs={{0,2},{1,3},{2,0},{3,1},{4,6},{5,7},{6,4},{7,5},{8,10},{9,11},{10,... | collective-permute-start | bytes 983048 | tf_op jit(solution)/shard_map/ppermute | solution.py:35
  3.6 0.0 collective-permute-start.2
  3.6 0.2 collective-permute-start.4
  3.9 1.9 %collective-permute-start.3 = (bf16[2,4096]{1,0:T(2,128)(2,1)}, bf16[2,4096]{1,0:T(2,128)(2,1)S(1)}, u32[]{:S(2)}, u32[]{:S(2)}) collective-permute-start(bf16[2,4096]{1,0:T(2,128)(2,1)} %b_hbm.1), channel_id=1, source_target_pairs={{0,2},{1,3},{2,0},{3,1},{4,6},{5,7},{6,4},{7,5},{8,10},{9,11},{10,... | collective-permute-start | bytes 49160 | tf_op jit(solution)/shard_map/ppermute | solution.py:35
  5.8 0.0 collective-permute-start
  5.8 4.8 %load.1 = (f32[128,128]{1,0:T(8,128)S(1)}, f32[128,128]{1,0:T(8,128)S(1)}, bf16[1280,4096]{1,0:T(8,128)(2,1)S(1)}, bf16[4096,256]{1,0:T(8,128)(2,1)S(1)}, bf16[2,4096]{1,0:T(2,128)(2,1)S(1)}) custom-call(s32[2]{0:T(128)} %len_ref.1, bf16[2048,4096]{1,0:T(8,128)(2,1)} %wo_hbm.5, bf16[4096,128]{1,0:T(8,128)(2,1)} %wk_hbm.1, bf16[4096,128]{1,0:T(8,128)(2,1)} %wv_hbm.1, ...), custom_call_target="tpu_custom_call" | custom-call | flops 1000 | bytes 16777216 | tf_op jit(solution)/shard_map/load/pallas_call | solution.py:333
  10.6 0.8 %collective-permute-done.4.b3 = bf16[2,4096]{1,0:T(2,128)(2,1)S(1)} collective-permute-done((bf16[2,4096]{1,0:T(2,128)(2,1)}, bf16[2,4096]{1,0:T(2,128)(2,1)S(1)}, u32[]{:S(2)}, u32[]{:S(2)}) %collective-permute-start.4) | collective-permute-done | bytes 16416 | tf_op jit(solution)/shard_map/ppermute | solution.py:35
  11.4 0.9 %collective-permute-done.3.b2 = bf16[2,4096]{1,0:T(2,128)(2,1)S(1)} collective-permute-done((bf16[2,4096]{1,0:T(2,128)(2,1)}, bf16[2,4096]{1,0:T(2,128)(2,1)S(1)}, u32[]{:S(2)}, u32[]{:S(2)}) %collective-permute-start.3) | collective-permute-done | bytes 16416 | tf_op jit(solution)/shard_map/ppermute | solution.py:35
  12.3 0.0 collective-permute-done.1.far.s2
  12.3 0.1 collective-permute-start.5
  12.4 0.0 copy-done
  12.4 2.3 %query.1 = (f32[8,16,128]{2,1,0:T(8,128)S(1)}, bf16[512,4096]{1,0:T(8,128)(2,1)S(1)}) custom-call(bf16[40,4096]{1,0:T(8,128)(2,1)S(1)} %collective-permute-done.1.far.s2, bf16[2,4096]{1,0:T(2,128)(2,1)S(1)} %get-tuple-element.28.b0, bf16[2,4096]{1,0:T(2,128)(2,1)S(1)} %collective-permute-done.2.b1, bf16[2,4096]{1,0:T(2,128)(2,1)S(1)} %collective-permute-done.3.b2, ...), custom_call_target="tpu_custom_call" | custom-call | flops 134217728 | bytes 2097152 | tf_op jit(solution)/shard_map/query/pallas_call | solution.py:352
  14.7 0.0 copy-start.1
  14.7 0.0 copy-start.3
  14.8 1.2 %payload.1 = (f32[128,128]{1,0:T(8,128)S(1)}, bf16[128,128]{1,0:T(8,128)(2,1)S(1)}, bf16[128,128]{1,0:T(8,128)(2,1)S(1)}, bf16[128,128]{1,0:T(8,128)(2,1)S(1)}) custom-call(s32[4]{0:T(128)S(1)} %copy-done.4, bf16[40,4096]{1,0:T(8,128)(2,1)S(1)} %copy-done.2, bf16[40,4096]{1,0:T(8,128)(2,1)S(1)} %collective-permute-done.s1, ...), custom_call_target="tpu_custom_call" | custom-call | flops 436207616 | bytes 2097152 | tf_op jit(solution)/shard_map/payload/pallas_call | solution.py:365
  16.0 3.9 %collective-permute-start.6 = (bf16[128,128]{1,0:T(8,128)(2,1)S(1)}, bf16[128,128]{1,0:T(8,128)(2,1)S(1)}, u32[]{:S(2)}, u32[]{:S(2)}) collective-permute-start(bf16[128,128]{1,0:T(8,128)(2,1)S(1)} %get-tuple-element.35), channel_id=1, source_target_pairs={{0,12},{4,8},{8,4},{12,0},{1,13},{5,9},{9,5},{13,1},{2,14},{6,10},... | collective-permute-start | bytes 98312 | tf_op jit(solution)/shard_map/ppermute | solution.py:35
  19.9 0.6 %collective-permute-start.8 = (bf16[128,128]{1,0:T(8,128)(2,1)S(1)}, bf16[128,128]{1,0:T(8,128)(2,1)S(1)}, u32[]{:S(2)}, u32[]{:S(2)}) collective-permute-start(bf16[128,128]{1,0:T(8,128)(2,1)S(1)} %get-tuple-element.37), channel_id=1, source_target_pairs={{0,4},{4,0},{8,12},{12,8},{1,5},{5,1},{9,13},{13,9},{2,6},{6,2},{1... | collective-permute-start | bytes 98312 | tf_op jit(solution)/shard_map/ppermute | solution.py:35
  20.5 1.6 %rest.1.ready.w2 = bf16[256,4096]{1,0:T(8,128)(2,1)S(1)} custom-call(f32[128,128]{1,0:T(8,128)S(1)} %get-tuple-element.34.ready.p0, bf16[2048,4096]{1,0:T(8,128)(2,1)} %wo_hbm.5), custom_call_target="tpu_custom_call" | custom-call | flops 1000 | bytes 2097152 | tf_op jit(solution)/shard_map/rest/pallas_call | solution.py:379
  22.1 2.6 %collective-permute-done.7.p2 = bf16[128,128]{1,0:T(8,128)(2,1)S(1)} collective-permute-done((bf16[128,128]{1,0:T(8,128)(2,1)S(1)}, bf16[128,128]{1,0:T(8,128)(2,1)S(1)}, u32[]{:S(2)}, u32[]{:S(2)}) %collective-permute-start.7) | collective-permute-done | bytes 32800 | tf_op jit(solution)/shard_map/ppermute | solution.py:35
  24.7 1.5 %attend.1 = (bf16[40,128]{1,0:T(8,128)(2,1)}, bf16[40,128]{1,0:T(8,128)(2,1)}, bf16[2,2048]{1,0:T(2,128)(2,1)S(1)}) custom-call(s32[2]{0:T(128)S(1)} %copy-done.3, bf16[256,4096]{1,0:T(8,128)(2,1)S(1)} %rest.1.ready.w2, f32[128,128]{1,0:T(8,128)S(1)} %get-tuple-element.34.ready.p0, bf16[128,128]{1,0:T(8,128)(2,1)S(1)} %collective-permute-done.6.p1, ...), custom_call_target="tpu_custom_call" | custom-call | flops 10000000 | bytes 1000000 | tf_op jit(solution)/shard_map/attend/pallas_call | solution.py:389
  26.2 1.5 %collective-permute-start.11 = (bf16[2,2048]{1,0:T(2,128)(2,1)S(1)}, bf16[2,2048]{1,0:T(2,128)(2,1)S(1)}, u32[]{:S(2)}, u32[]{:S(2)}) collective-permute-start(bf16[2,2048]{1,0:T(2,128)(2,1)S(1)} %get-tuple-element.40.a0), channel_id=1, source_target_pairs={{0,12},{4,8},{8,4},{12,0},{1,13},{5,9},{9,5},{13,1},{2,14},{6,10},... | collective-permute-start | bytes 24584 | tf_op jit(solution)/shard_map/ppermute | solution.py:35
  27.7 0.6 %collective-permute-start.10 = (bf16[2,2048]{1,0:T(2,128)(2,1)S(1)}, bf16[2,2048]{1,0:T(2,128)(2,1)S(1)}, u32[]{:S(2)}, u32[]{:S(2)}) collective-permute-start(bf16[2,2048]{1,0:T(2,128)(2,1)S(1)} %get-tuple-element.40.a0), channel_id=1, source_target_pairs={{0,8},{4,12},{8,0},{12,4},{1,9},{5,13},{9,1},{13,5},{2,10},{6,14},... | collective-permute-start | bytes 24584 | tf_op jit(solution)/shard_map/ppermute | solution.py:35
  28.3 2.3 %collective-permute-start.9 = (bf16[2,2048]{1,0:T(2,128)(2,1)S(1)}, bf16[2,2048]{1,0:T(2,128)(2,1)S(1)}, u32[]{:S(2)}, u32[]{:S(2)}) collective-permute-start(bf16[2,2048]{1,0:T(2,128)(2,1)S(1)} %get-tuple-element.40.a0), channel_id=1, source_target_pairs={{0,4},{4,0},{8,12},{12,8},{1,5},{5,1},{9,13},{13,9},{2,6},{6,2},{1... | collective-permute-start | bytes 24584 | tf_op jit(solution)/shard_map/ppermute | solution.py:35
  30.6 1.1 %collective-permute-done.11.a3 = bf16[2,2048]{1,0:T(2,128)(2,1)S(1)} collective-permute-done((bf16[2,2048]{1,0:T(2,128)(2,1)S(1)}, bf16[2,2048]{1,0:T(2,128)(2,1)S(1)}, u32[]{:S(2)}, u32[]{:S(2)}) %collective-permute-start.11) | collective-permute-done | bytes 8224 | tf_op jit(solution)/shard_map/ppermute | solution.py:35
  31.7 0.7 %collective-permute-done.10.a2 = bf16[2,2048]{1,0:T(2,128)(2,1)S(1)} collective-permute-done((bf16[2,2048]{1,0:T(2,128)(2,1)S(1)}, bf16[2,2048]{1,0:T(2,128)(2,1)S(1)}, u32[]{:S(2)}, u32[]{:S(2)}) %collective-permute-start.10) | collective-permute-done | bytes 8224 | tf_op jit(solution)/shard_map/ppermute | solution.py:35
  32.3 2.3 %project.1 = (f32[2,4096]{1,0:T(2,128)S(1)}, bf16[2,4096]{1,0:T(2,128)(2,1)S(1)}, bf16[2,4096]{1,0:T(2,128)(2,1)S(1)}, bf16[2,4096]{1,0:T(2,128)(2,1)S(1)}) custom-call(bf16[2,2048]{1,0:T(2,128)(2,1)S(1)} %get-tuple-element.40.a0, bf16[2,2048]{1,0:T(2,128)(2,1)S(1)} %collective-permute-done.9.a1, bf16[2,2048]{1,0:T(2,128)(2,1)S(1)} %collective-permute-done.10.a2, ...), custom_call_target="tpu_custom_call" | custom-call | flops 134217728 | bytes 16777216 | tf_op jit(solution)/shard_map/project/pallas_call | solution.py:400
  34.6 0.1 collective-permute-start.12
  34.7 1.6 %collective-permute-start.13 = (bf16[2,4096]{1,0:T(2,128)(2,1)S(1)}, bf16[2,4096]{1,0:T(2,128)(2,1)S(1)}, u32[]{:S(2)}, u32[]{:S(2)}) collective-permute-start(bf16[2,4096]{1,0:T(2,128)(2,1)S(1)} %get-tuple-element.45), channel_id=1, source_target_pairs={{0,2},{1,3},{2,0},{3,1},{4,6},{5,7},{6,4},{7,5},{8,10},{9,11},{10,... | collective-permute-start | bytes 49160 | tf_op jit(solution)/shard_map/ppermute | solution.py:35
  36.3 0.2 collective-permute-start.14
  36.5 1.4 %collective-permute-done.12 = bf16[2,4096]{1,0:T(2,128)(2,1)S(1)} collective-permute-done((bf16[2,4096]{1,0:T(2,128)(2,1)S(1)}, bf16[2,4096]{1,0:T(2,128)(2,1)S(1)}, u32[]{:S(2)}, u32[]{:S(2)}) %collective-permute-start.12) | collective-permute-done | bytes 16416 | tf_op jit(solution)/shard_map/ppermute | solution.py:35
  37.9 0.6 %collective-permute-done.13 = bf16[2,4096]{1,0:T(2,128)(2,1)S(1)} collective-permute-done((bf16[2,4096]{1,0:T(2,128)(2,1)S(1)}, bf16[2,4096]{1,0:T(2,128)(2,1)S(1)}, u32[]{:S(2)}, u32[]{:S(2)}) %collective-permute-start.13) | collective-permute-done | bytes 16416 | tf_op jit(solution)/shard_map/ppermute | solution.py:35
  38.5 0.6 %add_convert_fusion = bf16[2,4096]{1,0:T(2,128)(2,1)} fusion(bf16[2,4096]{1,0:T(2,128)(2,1)S(1)} %collective-permute-done.14, bf16[2,4096]{1,0:T(2,128)(2,1)S(1)} %collective-permute-done.13, f32[2,4096]{1,0:T(2,128)S(1)} %get-tuple-element.43, bf16[2,4096]{1,0:T(2,128)(2,1)S(1)} %collective-permute-done.12), kind=kLoop, calls=%fused_computation | loop fusion | flops 57344 | bytes 98304 | tf_op jit(solution)/shard_map/convert_element_type | solution.py:412
  (15 shorter events, 0.0 us)
Async XLA Ops:
  0.6 11.7 %copy-start = (bf16[4096,2048]{1,0:T(8,128)(2,1)S(1)}, bf16[4096,2048]{1,0:T(8,128)(2,1)}, u32[]{:S(2)}) copy-start(bf16[4096,2048]{1,0:T(8,128)(2,1)} %w.1) | copy-start | bytes 50331652
  0.6 11.6 %collective-permute-start.1 = (bf16[40,4096]{1,0:T(8,128)(2,1)}, bf16[40,4096]{1,0:T(8,128)(2,1)S(1)}, u32[]{:S(2)}, u32[]{:S(2)}) collective-permute-start(bf16[40,4096]{1,0:T(8,128)(2,1)} %s0.1), channel_id=1, source_target_pairs={{0,2},{1,3},{2,0},{3,1},{4,6},{5,7},{6,4},{7,5},{8,10},{9,11},{10,... | collective-permute-start | bytes 983048 | tf_op jit(solution)/shard_map/ppermute | solution.py:35
  3.6 6.9 %collective-permute-start.2 = (bf16[2,4096]{1,0:T(2,128)(2,1)}, bf16[2,4096]{1,0:T(2,128)(2,1)S(1)}, u32[]{:S(2)}, u32[]{:S(2)}) collective-permute-start(bf16[2,4096]{1,0:T(2,128)(2,1)} %b_hbm.1), channel_id=1, source_target_pairs={{0,1},{1,0},{2,3},{3,2},{4,5},{5,4},{6,7},{7,6},{8,9},{9,8},{10,11... | collective-permute-start | bytes 49160 | tf_op jit(solution)/shard_map/ppermute | solution.py:35
  3.6 7.7 %collective-permute-start.4 = (bf16[2,4096]{1,0:T(2,128)(2,1)}, bf16[2,4096]{1,0:T(2,128)(2,1)S(1)}, u32[]{:S(2)}, u32[]{:S(2)}) collective-permute-start(bf16[2,4096]{1,0:T(2,128)(2,1)} %b_hbm.1), channel_id=1, source_target_pairs={{0,3},{1,2},{2,1},{3,0},{4,7},{5,6},{6,5},{7,4},{8,11},{9,10},{10,... | collective-permute-start | bytes 49160 | tf_op jit(solution)/shard_map/ppermute | solution.py:35
  3.9 8.4 %collective-permute-start.3 = (bf16[2,4096]{1,0:T(2,128)(2,1)}, bf16[2,4096]{1,0:T(2,128)(2,1)S(1)}, u32[]{:S(2)}, u32[]{:S(2)}) collective-permute-start(bf16[2,4096]{1,0:T(2,128)(2,1)} %b_hbm.1), channel_id=1, source_target_pairs={{0,2},{1,3},{2,0},{3,1},{4,6},{5,7},{6,4},{7,5},{8,10},{9,11},{10,... | collective-permute-start | bytes 49160 | tf_op jit(solution)/shard_map/ppermute | solution.py:35
  5.8 8.9 %collective-permute-start = (bf16[40,4096]{1,0:T(8,128)(2,1)}, bf16[40,4096]{1,0:T(8,128)(2,1)S(1)}, u32[]{:S(2)}, u32[]{:S(2)}) collective-permute-start(bf16[40,4096]{1,0:T(8,128)(2,1)} %s0.1), channel_id=1, source_target_pairs={{0,1},{1,0},{2,3},{3,2},{4,5},{5,4},{6,7},{7,6},{8,9},{9,8},{10,11... | collective-permute-start | bytes 983048 | tf_op jit(solution)/shard_map/ppermute | solution.py:35
  12.3 2.4 %copy-start.2 = (bf16[40,4096]{1,0:T(8,128)(2,1)S(1)}, bf16[40,4096]{1,0:T(8,128)(2,1)}, u32[]{:S(2)}) copy-start(bf16[40,4096]{1,0:T(8,128)(2,1)} %s0.1) | copy-start | bytes 983044
  12.3 2.5 %copy-start.4 = (s32[4]{0:T(128)S(1)}, s32[4]{0:T(128)}, u32[]{:S(2)}) copy-start(s32[4]{0:T(128)} %owner_ref.1) | copy-start | bytes 52
  12.3 2.4 %collective-permute-start.5 = (bf16[40,4096]{1,0:T(8,128)(2,1)S(1)}, bf16[40,4096]{1,0:T(8,128)(2,1)S(1)}, u32[]{:S(2)}, u32[]{:S(2)}) collective-permute-start(bf16[40,4096]{1,0:T(8,128)(2,1)S(1)} %collective-permute-done.1.far.s2), channel_id=1, source_target_pairs={{0,1},{1,0},{2,3},{3,2},{4,5},{5,4},{6,7},{7,6},{8,9},{9,8},{10,11... | collective-permute-start | bytes 983048 | tf_op jit(solution)/shard_map/ppermute | solution.py:35
  14.7 10.0 %copy-start.1 = (bf16[2,2,512,128]{3,2,1,0:T(8,128)(2,1)S(1)}, bf16[2,2,512,128]{3,2,1,0:T(8,128)(2,1)}, u32[]{:S(2)}) copy-start(bf16[2,2,512,128]{3,2,1,0:T(8,128)(2,1)} %kv.1) | copy-start | bytes 1572868
  14.7 10.0 %copy-start.3 = (s32[2]{0:T(128)S(1)}, s32[2]{0:T(128)}, u32[]{:S(2)}) copy-start(s32[2]{0:T(128)} %len_ref.1) | copy-start | bytes 28
  16.0 6.1 %collective-permute-start.6 = (bf16[128,128]{1,0:T(8,128)(2,1)S(1)}, bf16[128,128]{1,0:T(8,128)(2,1)S(1)}, u32[]{:S(2)}, u32[]{:S(2)}) collective-permute-start(bf16[128,128]{1,0:T(8,128)(2,1)S(1)} %get-tuple-element.35), channel_id=1, source_target_pairs={{0,12},{4,8},{8,4},{12,0},{1,13},{5,9},{9,5},{13,1},{2,14},{6,10},... | collective-permute-start | bytes 98312 | tf_op jit(solution)/shard_map/ppermute | solution.py:35
  19.9 4.8 %collective-permute-start.7 = (bf16[128,128]{1,0:T(8,128)(2,1)S(1)}, bf16[128,128]{1,0:T(8,128)(2,1)S(1)}, u32[]{:S(2)}, u32[]{:S(2)}) collective-permute-start(bf16[128,128]{1,0:T(8,128)(2,1)S(1)} %get-tuple-element.36), channel_id=1, source_target_pairs={{0,8},{4,12},{8,0},{12,4},{1,9},{5,13},{9,1},{13,5},{2,10},{6,14},... | collective-permute-start | bytes 98312 | tf_op jit(solution)/shard_map/ppermute | solution.py:35
  19.9 4.8 %collective-permute-start.8 = (bf16[128,128]{1,0:T(8,128)(2,1)S(1)}, bf16[128,128]{1,0:T(8,128)(2,1)S(1)}, u32[]{:S(2)}, u32[]{:S(2)}) collective-permute-start(bf16[128,128]{1,0:T(8,128)(2,1)S(1)} %get-tuple-element.37), channel_id=1, source_target_pairs={{0,4},{4,0},{8,12},{12,8},{1,5},{5,1},{9,13},{13,9},{2,6},{6,2},{1... | collective-permute-start | bytes 98312 | tf_op jit(solution)/shard_map/ppermute | solution.py:35
  26.2 5.4 %collective-permute-start.11 = (bf16[2,2048]{1,0:T(2,128)(2,1)S(1)}, bf16[2,2048]{1,0:T(2,128)(2,1)S(1)}, u32[]{:S(2)}, u32[]{:S(2)}) collective-permute-start(bf16[2,2048]{1,0:T(2,128)(2,1)S(1)} %get-tuple-element.40.a0), channel_id=1, source_target_pairs={{0,12},{4,8},{8,4},{12,0},{1,13},{5,9},{9,5},{13,1},{2,14},{6,10},... | collective-permute-start | bytes 24584 | tf_op jit(solution)/shard_map/ppermute | solution.py:35
  27.7 4.6 %collective-permute-start.10 = (bf16[2,2048]{1,0:T(2,128)(2,1)S(1)}, bf16[2,2048]{1,0:T(2,128)(2,1)S(1)}, u32[]{:S(2)}, u32[]{:S(2)}) collective-permute-start(bf16[2,2048]{1,0:T(2,128)(2,1)S(1)} %get-tuple-element.40.a0), channel_id=1, source_target_pairs={{0,8},{4,12},{8,0},{12,4},{1,9},{5,13},{9,1},{13,5},{2,10},{6,14},... | collective-permute-start | bytes 24584 | tf_op jit(solution)/shard_map/ppermute | solution.py:35
  28.3 4.0 %collective-permute-start.9 = (bf16[2,2048]{1,0:T(2,128)(2,1)S(1)}, bf16[2,2048]{1,0:T(2,128)(2,1)S(1)}, u32[]{:S(2)}, u32[]{:S(2)}) collective-permute-start(bf16[2,2048]{1,0:T(2,128)(2,1)S(1)} %get-tuple-element.40.a0), channel_id=1, source_target_pairs={{0,4},{4,0},{8,12},{12,8},{1,5},{5,1},{9,13},{13,9},{2,6},{6,2},{1... | collective-permute-start | bytes 24584 | tf_op jit(solution)/shard_map/ppermute | solution.py:35
  34.6 3.3 %collective-permute-start.12 = (bf16[2,4096]{1,0:T(2,128)(2,1)S(1)}, bf16[2,4096]{1,0:T(2,128)(2,1)S(1)}, u32[]{:S(2)}, u32[]{:S(2)}) collective-permute-start(bf16[2,4096]{1,0:T(2,128)(2,1)S(1)} %get-tuple-element.44), channel_id=1, source_target_pairs={{0,3},{1,2},{2,1},{3,0},{4,7},{5,6},{6,5},{7,4},{8,11},{9,10},{10,... | collective-permute-start | bytes 49160 | tf_op jit(solution)/shard_map/ppermute | solution.py:35
  34.7 3.8 %collective-permute-start.13 = (bf16[2,4096]{1,0:T(2,128)(2,1)S(1)}, bf16[2,4096]{1,0:T(2,128)(2,1)S(1)}, u32[]{:S(2)}, u32[]{:S(2)}) collective-permute-start(bf16[2,4096]{1,0:T(2,128)(2,1)S(1)} %get-tuple-element.45), channel_id=1, source_target_pairs={{0,2},{1,3},{2,0},{3,1},{4,6},{5,7},{6,4},{7,5},{8,10},{9,11},{10,... | collective-permute-start | bytes 49160 | tf_op jit(solution)/shard_map/ppermute | solution.py:35
  36.3 2.2 %collective-permute-start.14 = (bf16[2,4096]{1,0:T(2,128)(2,1)S(1)}, bf16[2,4096]{1,0:T(2,128)(2,1)S(1)}, u32[]{:S(2)}, u32[]{:S(2)}) collective-permute-start(bf16[2,4096]{1,0:T(2,128)(2,1)S(1)} %get-tuple-element.46), channel_id=1, source_target_pairs={{0,1},{1,0},{2,3},{3,2},{4,5},{5,4},{6,7},{7,6},{8,9},{9,8},{10,11... | collective-permute-start | bytes 49160 | tf_op jit(solution)/shard_map/ppermute | solution.py:35

commit v7 on v5

--- a/solution.py
+++ b/solution.py
@@ -1,3 +1,4 @@
+import functools
 import math
 
 import jax
@@ -194,29 +195,37 @@
     return copies
 
 
+def project_rows(x, wkv):
+    both = jnp.zeros((x.shape[0], wkv.shape[1]), F32)
+    for c in range(x.shape[1] // CHUNK):
+        part = slice(c * CHUNK, (c + 1) * CHUNK)
+        both += jnp.dot(x[:, part], wkv[part, :], preferred_element_type=F32)
+    return both
+
+
 def load_kernel(
-    len_ref, wo_hbm, wk_hbm, wv_hbm, b_hbm, cos_ref, sin_ref, wo, wkv, b, sems
+    len_hbm, wo_hbm, wk_hbm, wv_hbm, cos_ref, sin_ref, wo, wkv, len_ref, sems
 ):
-    copies = start_load(b_hbm, b, sems, 0, 1)
-    copies += start_load(wk_hbm, wkv.at[:, pl.ds(0, HD)], sems, 1, 1)
+    lengths = pltpu.make_async_copy(len_hbm, len_ref, sems.at[0])
+    lengths.start()
+    copies = start_load(wk_hbm, wkv.at[:, pl.ds(0, HD)], sems, 1, 1)
     copies += start_load(wv_hbm, wkv.at[:, pl.ds(HD, HD)], sems, 2, 1)
     copies += start_load(wo_hbm.at[pl.ds(0, wo.shape[0])], wo, sems, 3, 6)
+    lengths.wait()
     angles(len_ref, cos_ref, sin_ref)
     for copy in copies:
         copy.wait()
 
 
-def query_kernel(far, b0, b1, b2, b3, w, wo_hbm, out_ref, wo, acc, sems):
+def own_kernel(s, wkv, out):
+    out[...] = project_rows(s, wkv)
+
+
+def query_kernel(first, far, b0, b1, b2, b3, w, wo_hbm, out_ref, wo, acc, sems):
     rows = wo.shape[0]
-    copies = start_load(wo_hbm.at[pl.ds(wo_hbm.shape[0] - rows, rows)], wo, sems, 0, 2)
+    copies = start_load(wo_hbm.at[pl.ds(first, rows)], wo, sems, 0, 2)
     lhs = jnp.concatenate([b[...].astype(F32) for b in (b0, b1, b2, b3)], axis=0).astype(BF16)
-    left = jnp.zeros((lhs.shape[0], w.shape[1] // 2), F32)
-    right = left
-    for c in range(w.shape[0] // 256):
-        rows = slice(c * 256, (c + 1) * 256)
-        left += jnp.dot(lhs[:, rows], w[rows, : left.shape[1]], preferred_element_type=F32)
-        right += jnp.dot(lhs[:, rows], w[rows, left.shape[1] :], preferred_element_type=F32)
-    acc[...] = jnp.concatenate([left, right], axis=1)
+    acc[...] = jnp.dot(lhs, w[...], preferred_element_type=F32)
     for r in range(acc.shape[0]):
         for h in range(out_ref.shape[1]):
             out_ref[r, pl.ds(h, 1), :] = acc[pl.ds(r, 1), pl.ds(h * HD, HD)]
@@ -225,31 +234,26 @@
 
 
 def payload_kernel(
-    owner_ref, s0, s1, s2, s3, b0, b1, b2, b3, wkv, q_ref, o0, o3, o2, o1, x, pay
+    owner_ref, own, s1, s2, s3, b0, b1, b2, b3, wkv, q_ref, o0, o3, o2, o1, x, pay
 ):
     gx, gy = lax.axis_index("gx"), lax.axis_index("gy")
-    stored = (s0, s1, s2, s3)
-    for k, s in enumerate(stored):
+    for k, s in enumerate((s1, s2, s3)):
         x[pl.ds(k * ROW_TILE, LC), :] = s[...]
     fresh = [b[...].astype(F32) for b in (b0, b1, b2, b3)]
     fresh.append(jnp.zeros((8, x.shape[1]), F32))
-    base = len(stored) * ROW_TILE
+    base = 3 * ROW_TILE
     x[pl.ds(base, 16), :] = jnp.concatenate(fresh, axis=0).astype(BF16)
-    both = jnp.zeros((x.shape[0], 2 * HD), F32)
-    for c in range(x.shape[1] // CHUNK):
-        rows = slice(c * CHUNK, (c + 1) * CHUNK)
-        both += jnp.dot(x[:, rows], wkv[rows, :], preferred_element_type=F32)
-    key, value = both[:, :HD], both[:, HD:]
+    late = project_rows(x, wkv)
     empty = jnp.zeros((8 - ROWS_DEV, HD), F32)
-    for k in range(len(stored)):
-        rows = slice(k * ROW_TILE, k * ROW_TILE + LC)
+    for k in range(4):
         target = owner_ref[gy ^ k] ^ gx
-        pay[target, pl.ds(0, LC), :] = key[rows]
-        pay[target, pl.ds(VALUES, LC), :] = value[rows]
-        rows = slice(base + k * ROWS_DEV, base + (k + 1) * ROWS_DEV)
+        both = late[(k - 1) * ROW_TILE : (k - 1) * ROW_TILE + LC] if k else own[...]
+        pay[target, pl.ds(0, LC), :] = both[:, :HD]
+        pay[target, pl.ds(VALUES, LC), :] = both[:, HD:]
+        both = late[base + k * ROWS_DEV : base + (k + 1) * ROWS_DEV]
         target = k ^ gx ^ gy
-        pay[target, pl.ds(LC, 8), :] = jnp.concatenate([key[rows], empty], axis=0)
-        pay[target, pl.ds(VALUES + LC, 8), :] = jnp.concatenate([value[rows], empty], axis=0)
+        pay[target, pl.ds(LC, 8), :] = jnp.concatenate([both[:, :HD], empty], axis=0)
+        pay[target, pl.ds(VALUES + LC, 8), :] = jnp.concatenate([both[:, HD:], empty], axis=0)
         for r in range(ROWS_DEV):
             pay[target, pl.ds(QUERY + 16 * r, 16), :] = q_ref[k * ROWS_DEV + r]
     o0[...] = pay[0]
@@ -326,27 +330,36 @@
     far = swap(stored_rows, "gy", 2)
     near = swap(stored_rows, "gy", 1)
     fresh = [swap(new_rows, "gy", k) for k in (1, 2, 3)]
-    cos, sin, wo_first, wkv, own_fresh = pl.pallas_call(
+    cos, sin, wo_first, wkv = pl.pallas_call(
         load_kernel,
         out_shape=[pltpu.VMEM((PAY, HD), F32)] * 2
         + [
             pltpu.VMEM((query_cols - quarter, width), BF16),
             pltpu.VMEM((depth, 2 * HD), BF16),
-            pltpu.VMEM(new_rows.shape, BF16),
         ],
-        in_specs=[whole(pltpu.SMEM)] + [whole(pltpu.HBM)] * 4,
-        out_specs=[whole()] * 5,
-        scratch_shapes=[semaphores((9,))],
+        in_specs=[whole(pltpu.HBM)] * 4,
+        out_specs=[whole()] * 4,
+        scratch_shapes=[pltpu.SMEM(cache_len.shape, jnp.int32), semaphores((9,))],
         compiler_params=params(4),
         cost_estimate=cost(1000, 2 * depth * query_cols),
         name="load",
-    )(cache_len, in_hbm(w_out), in_hbm(w_key), in_hbm(w_value), in_hbm(new_rows))
-    far, own_fresh, *fresh = lax.optimization_barrier((far, own_fresh, *fresh))
+    )(
+        in_hbm(cache_len), in_hbm(w_out), in_hbm(w_key), in_hbm(w_value)
+    )
+    own = pl.pallas_call(
+        own_kernel,
+        out_shape=pltpu.VMEM((LC, 2 * HD), F32),
+        in_specs=[whole()] * 2,
+        out_specs=whole(),
+        compiler_params=params(4),
+        cost_estimate=cost(2 * LC * depth * 256, 4 * depth * HD),
+        name="own",
+    )(stored_rows, wkv)
+    far, own, *fresh = lax.optimization_barrier((far, own, *fresh))
     far_near = swap(far, "gy", 1)
-    fresh = [own_fresh] + fresh
-    stored = [stored_rows, near, far, far_near]
+    fresh = [new_rows] + fresh
     query, wo_second = pl.pallas_call(
-        query_kernel,
+        functools.partial(query_kernel, query_cols - quarter),
         out_shape=[
             pltpu.VMEM((4 * ROWS_DEV, heads, HD), F32),
             pltpu.VMEM((quarter, width), BF16),
@@ -364,17 +377,17 @@
         in_specs=[whole(pltpu.SMEM)] + [whole()] * 10,
         out_specs=[whole()] * 4,
         scratch_shapes=[
-            pltpu.VMEM((4 * ROW_TILE + 16, depth), BF16),
+            pltpu.VMEM((3 * ROW_TILE + 16, depth), BF16),
             pltpu.VMEM((4, PAY, HD), F32),
         ],
         compiler_params=params(8),
         cost_estimate=cost(2 * 208 * depth * 256, 4 * depth * HD),
         name="payload",
-    )(owner, *stored, *fresh, wkv, query)
+    )(owner, own, near, far, far_near, *fresh, wkv, query)
     sums = [payload[0]] + others(payload[1:], "gx")
     rebuilt_key, rebuilt_value, attn = pl.pallas_call(
         attend_kernel,
-        out_shape=[shape((LC, HD), BF16)] * 2 + [shape((ROWS_DEV, query_cols), BF16)],
+        out_shape=[pltpu.VMEM((LC, HD), BF16)] * 2 + [pltpu.VMEM((ROWS_DEV, query_cols), BF16)],
         in_specs=[whole(pltpu.SMEM)] + [whole()] * 7,
         out_specs=[whole()] * 3,
         scratch_shapes=[pltpu.VMEM((ROWS_DEV, query_cols), F32)],

time: 41.7 us -> 39.2 us (0.940)
  Pallas kernels: 14.7 us -> 13 us
  starting transfers between devices: 16.7 us -> 16 us
  local copies, waits for them, and re-layouts: 0.68 us -> 1.23 us
  waiting for transfers between devices: 7.98 us -> 7.49 us
    pallas_call x2 -> x3, Pallas kernels: 5.27 us -> 4.24 us  [the longest x1 2.33 us: per_device(): pl.pallas_call(functools.partial(query_kernel, query_cols - quarter), out...]
    ppermute x15, starting transfers between devices: 16.7 us -> 16 us  [swap(): return lax.ppermute(x, axis, [(i, i ^ k) for i in range(n)])]
    pallas_call x1, Pallas kernels: 5.9 us -> 5.35 us  [per_device(): pl.pallas_call(load_kernel, out_shape=[pltpu.VMEM((PAY, HD), F32)] * 2 +...]
    unnamed x12 -> x14, local copies, waits for them, and re-layouts: 0.68 us -> 1.23 us
    ppermute x15, waiting for transfers between devices: 7.98 us -> 7.49 us  [swap(): return lax.ppermute(x, axis, [(i, i ^ k) for i in range(n)])]
  transfers between devices with their start and end apart: 15 -> 15, of which waited for: 6 -> 7; matrix products, arithmetic and copies ran while one was open for 0% -> 3% of each run, Pallas kernels for 23% -> 21%
where the time goes in v7:
time: 39.2 us; the launch traced here: 39.1 us
  starting transfers between devices  16 us (41%)
  Pallas kernels  13 us (33%)
  waiting for transfers between devices  7.49 us (19%)
  local copies, waits for them, and re-layouts  1.23 us (3%)
  between operations  0.8 us (2%)
  other arithmetic  0.64 us (2%)
    ppermute x15, starting transfers between devices, swap(): return lax.ppermute(x, axis, [(i, i ^ k) for i in range(n)])  16 us
    ppermute x15, waiting for transfers between devices, swap(): return lax.ppermute(x, axis, [(i, i ^ k) for i in range(n)])  7.49 us
    pallas_call x1, Pallas kernels, per_device(): pl.pallas_call(load_kernel, out_shape=[pltpu.VMEM((PAY, HD), F32)] * 2 +...  5.35 us
    pallas_call x1, Pallas kernels, per_device(): pl.pallas_call(functools.partial(query_kernel, query_cols - quarter), out...  2.33 us
    pallas_call x1, Pallas kernels, per_device(): pl.pallas_call(out_kernel, out_shape=[shape((ROWS_DEV, width), F32)] + [s...  2.28 us
    pallas_call x1, Pallas kernels, per_device(): pl.pallas_call(attend_kernel, out_shape=[pltpu.VMEM((LC, HD), BF16)] * 2...  1.43 us
    unnamed x14, local copies, waits for them, and re-layouts  1.23 us
    pallas_call x1, Pallas kernels, per_device(): pl.pallas_call(payload_kernel, out_shape=[shape((PAY, HD), F32)] + [shape...  1.11 us
  transfers between devices with their start and end apart: 15, of which 7 were waited for; matrix products, arithmetic and copies ran while one was open for 3% of the time, Pallas kernels for 21%

profile of v7, /device:TPU:0, one launch (start us, length us, event | category | flops | bytes accessed | tf_op | source)
XLA Modules:
  0.0 39.1 jit_solution(10840957683148501302)
XLA Ops:
  0.7 3.0 %collective-permute-start = (bf16[40,4096]{1,0:T(8,128)(2,1)}, bf16[40,4096]{1,0:T(8,128)(2,1)S(1)}, u32[]{:S(2)}, u32[]{:S(2)}) collective-permute-start(bf16[40,4096]{1,0:T(8,128)(2,1)} %s.1), channel_id=1, source_target_pairs={{0,2},{1,3},{2,0},{3,1},{4,6},{5,7},{6,4},{7,5},{8,10},{9,11},{10,... | collective-permute-start | bytes 983048 | tf_op jit(solution)/shard_map/ppermute | solution.py:35
  3.7 1.2 %collective-permute-start.2 = (bf16[2,4096]{1,0:T(2,128)(2,1)}, bf16[2,4096]{1,0:T(2,128)(2,1)S(1)}, u32[]{:S(2)}, u32[]{:S(2)}) collective-permute-start(bf16[2,4096]{1,0:T(2,128)(2,1)} %b0.3), channel_id=1, source_target_pairs={{0,2},{1,3},{2,0},{3,1},{4,6},{5,7},{6,4},{7,5},{8,10},{9,11},{10,... | collective-permute-start | bytes 49160 | tf_op jit(solution)/shard_map/ppermute | solution.py:35
  4.9 0.7 %collective-permute-start.1 = (bf16[2,4096]{1,0:T(2,128)(2,1)}, bf16[2,4096]{1,0:T(2,128)(2,1)S(1)}, u32[]{:S(2)}, u32[]{:S(2)}) collective-permute-start(bf16[2,4096]{1,0:T(2,128)(2,1)} %b0.3), channel_id=1, source_target_pairs={{0,1},{1,0},{2,3},{3,2},{4,5},{5,4},{6,7},{7,6},{8,9},{9,8},{10,11... | collective-permute-start | bytes 49160 | tf_op jit(solution)/shard_map/ppermute | solution.py:35
  5.5 0.0 collective-permute-start.4
  5.5 5.3 %load.1 = (f32[128,128]{1,0:T(8,128)S(1)}, f32[128,128]{1,0:T(8,128)S(1)}, bf16[1536,4096]{1,0:T(8,128)(2,1)S(1)}, bf16[4096,256]{1,0:T(8,128)(2,1)S(1)}) custom-call(s32[2]{0:T(128)} %len_ref.1, bf16[2048,4096]{1,0:T(8,128)(2,1)} %wo_hbm.3, bf16[4096,128]{1,0:T(8,128)(2,1)} %wk_hbm.1, bf16[4096,128]{1,0:T(8,128)(2,1)} %wv_hbm.1), custom_call_target="tpu_custom_call" | custom-call | flops 1000 | bytes 16777216 | tf_op jit(solution)/shard_map/load/pallas_call | solution.py:333
  10.9 0.5 %own.1 = f32[40,256]{1,0:T(8,128)S(1)} custom-call(bf16[40,4096]{1,0:T(8,128)(2,1)S(1)} %copy-done.2, bf16[4096,256]{1,0:T(8,128)(2,1)S(1)} %get-tuple-element.25.wkv), custom_call_target="tpu_custom_call" | custom-call | flops 83886080 | bytes 2097152 | tf_op jit(solution)/shard_map/own/pallas_call | solution.py:349
  11.4 0.0 copy-start.5
  11.4 0.0 copy-start.1
  11.4 0.0 copy-start.4
  11.4 0.0 collective-permute-done.3.b3
  11.4 0.9 %collective-permute-done.2.b2 = bf16[2,4096]{1,0:T(2,128)(2,1)S(1)} collective-permute-done((bf16[2,4096]{1,0:T(2,128)(2,1)}, bf16[2,4096]{1,0:T(2,128)(2,1)S(1)}, u32[]{:S(2)}, u32[]{:S(2)}) %collective-permute-start.2) | collective-permute-done | bytes 16416 | tf_op jit(solution)/shard_map/ppermute | solution.py:35
  12.3 0.0 collective-permute-done.1.b1
  12.3 2.3 %query.1 = (f32[8,16,128]{2,1,0:T(8,128)S(1)}, bf16[512,4096]{1,0:T(8,128)(2,1)S(1)}) custom-call(bf16[40,4096]{1,0:T(8,128)(2,1)S(1)} %collective-permute-done.far.s2, bf16[2,4096]{1,0:T(2,128)(2,1)S(1)} %copy-done.3, bf16[2,4096]{1,0:T(2,128)(2,1)S(1)} %collective-permute-done.1.b1, bf16[2,4096]{1,0:T(2,128)(2,1)S(1)} %collective-permute-done.2.b2, ...), custom_call_target="tpu_custom_call" | custom-call | flops 134217728 | bytes 2097152 | tf_op jit(solution)/shard_map/query/pallas_call | solution.py:361
  14.7 1.1 %payload.1 = (f32[128,128]{1,0:T(8,128)S(1)}, bf16[128,128]{1,0:T(8,128)(2,1)S(1)}, bf16[128,128]{1,0:T(8,128)(2,1)S(1)}, bf16[128,128]{1,0:T(8,128)(2,1)S(1)}) custom-call(s32[4]{0:T(128)S(1)} %copy-done.5, f32[40,256]{1,0:T(8,128)S(1)} %own.1, bf16[40,4096]{1,0:T(8,128)(2,1)S(1)} %collective-permute-done.4.s1, ...), custom_call_target="tpu_custom_call" | custom-call | flops 436207616 | bytes 2097152 | tf_op jit(solution)/shard_map/payload/pallas_call | solution.py:374
  15.8 4.1 %collective-permute-start.6 = (bf16[128,128]{1,0:T(8,128)(2,1)S(1)}, bf16[128,128]{1,0:T(8,128)(2,1)S(1)}, u32[]{:S(2)}, u32[]{:S(2)}) collective-permute-start(bf16[128,128]{1,0:T(8,128)(2,1)S(1)} %get-tuple-element.33), channel_id=1, source_target_pairs={{0,12},{4,8},{8,4},{12,0},{1,13},{5,9},{9,5},{13,1},{2,14},{6,10},... | collective-permute-start | bytes 98312 | tf_op jit(solution)/shard_map/ppermute | solution.py:35
  19.9 0.6 %collective-permute-start.8 = (bf16[128,128]{1,0:T(8,128)(2,1)S(1)}, bf16[128,128]{1,0:T(8,128)(2,1)S(1)}, u32[]{:S(2)}, u32[]{:S(2)}) collective-permute-start(bf16[128,128]{1,0:T(8,128)(2,1)S(1)} %get-tuple-element.35), channel_id=1, source_target_pairs={{0,4},{4,0},{8,12},{12,8},{1,5},{5,1},{9,13},{13,9},{2,6},{6,2},{1... | collective-permute-start | bytes 98312 | tf_op jit(solution)/shard_map/ppermute | solution.py:35
  20.6 1.3 %collective-permute-done.6.p1 = bf16[128,128]{1,0:T(8,128)(2,1)S(1)} collective-permute-done((bf16[128,128]{1,0:T(8,128)(2,1)S(1)}, bf16[128,128]{1,0:T(8,128)(2,1)S(1)}, u32[]{:S(2)}, u32[]{:S(2)}) %collective-permute-start.6) | collective-permute-done | bytes 32800 | tf_op jit(solution)/shard_map/ppermute | solution.py:35
  21.9 2.9 %collective-permute-done.7.p2 = bf16[128,128]{1,0:T(8,128)(2,1)S(1)} collective-permute-done((bf16[128,128]{1,0:T(8,128)(2,1)S(1)}, bf16[128,128]{1,0:T(8,128)(2,1)S(1)}, u32[]{:S(2)}, u32[]{:S(2)}) %collective-permute-start.7) | collective-permute-done | bytes 32800 | tf_op jit(solution)/shard_map/ppermute | solution.py:35
  24.8 1.4 %attend.1 = (bf16[40,128]{1,0:T(8,128)(2,1)S(1)}, bf16[40,128]{1,0:T(8,128)(2,1)S(1)}, bf16[2,2048]{1,0:T(2,128)(2,1)S(1)}) custom-call(s32[2]{0:T(128)S(1)} %copy-done.4, f32[128,128]{1,0:T(8,128)S(1)} %get-tuple-element.32.p0, bf16[128,128]{1,0:T(8,128)(2,1)S(1)} %collective-permute-done.6.p1, bf16[128,128]{1,0:T(8,128)(2,1)S(1)} %collective-permute-done.7.p2, ...), custom_call_target="tpu_custom_call" | custom-call | flops 10000000 | bytes 1000000 | tf_op jit(solution)/shard_map/attend/pallas_call | solution.py:388
  26.2 1.6 %collective-permute-start.11 = (bf16[2,2048]{1,0:T(2,128)(2,1)S(1)}, bf16[2,2048]{1,0:T(2,128)(2,1)S(1)}, u32[]{:S(2)}, u32[]{:S(2)}) collective-permute-start(bf16[2,2048]{1,0:T(2,128)(2,1)S(1)} %get-tuple-element.38.a0), channel_id=1, source_target_pairs={{0,12},{4,8},{8,4},{12,0},{1,13},{5,9},{9,5},{13,1},{2,14},{6,10},... | collective-permute-start | bytes 24584 | tf_op jit(solution)/shard_map/ppermute | solution.py:35
  27.8 0.6 %collective-permute-start.10 = (bf16[2,2048]{1,0:T(2,128)(2,1)S(1)}, bf16[2,2048]{1,0:T(2,128)(2,1)S(1)}, u32[]{:S(2)}, u32[]{:S(2)}) collective-permute-start(bf16[2,2048]{1,0:T(2,128)(2,1)S(1)} %get-tuple-element.38.a0), channel_id=1, source_target_pairs={{0,8},{4,12},{8,0},{12,4},{1,9},{5,13},{9,1},{13,5},{2,10},{6,14},... | collective-permute-start | bytes 24584 | tf_op jit(solution)/shard_map/ppermute | solution.py:35
  28.4 2.3 %collective-permute-start.9 = (bf16[2,2048]{1,0:T(2,128)(2,1)S(1)}, bf16[2,2048]{1,0:T(2,128)(2,1)S(1)}, u32[]{:S(2)}, u32[]{:S(2)}) collective-permute-start(bf16[2,2048]{1,0:T(2,128)(2,1)S(1)} %get-tuple-element.38.a0), channel_id=1, source_target_pairs={{0,4},{4,0},{8,12},{12,8},{1,5},{5,1},{9,13},{13,9},{2,6},{6,2},{1... | collective-permute-start | bytes 24584 | tf_op jit(solution)/shard_map/ppermute | solution.py:35
  30.6 1.1 %collective-permute-done.11.a3 = bf16[2,2048]{1,0:T(2,128)(2,1)S(1)} collective-permute-done((bf16[2,2048]{1,0:T(2,128)(2,1)S(1)}, bf16[2,2048]{1,0:T(2,128)(2,1)S(1)}, u32[]{:S(2)}, u32[]{:S(2)}) %collective-permute-start.11) | collective-permute-done | bytes 8224 | tf_op jit(solution)/shard_map/ppermute | solution.py:35
  31.7 0.7 %collective-permute-done.10.a2 = bf16[2,2048]{1,0:T(2,128)(2,1)S(1)} collective-permute-done((bf16[2,2048]{1,0:T(2,128)(2,1)S(1)}, bf16[2,2048]{1,0:T(2,128)(2,1)S(1)}, u32[]{:S(2)}, u32[]{:S(2)}) %collective-permute-start.10) | collective-permute-done | bytes 8224 | tf_op jit(solution)/shard_map/ppermute | solution.py:35
  32.4 2.3 %project.1 = (f32[2,4096]{1,0:T(2,128)S(1)}, bf16[2,4096]{1,0:T(2,128)(2,1)S(1)}, bf16[2,4096]{1,0:T(2,128)(2,1)S(1)}, bf16[2,4096]{1,0:T(2,128)(2,1)S(1)}) custom-call(bf16[2,2048]{1,0:T(2,128)(2,1)S(1)} %get-tuple-element.38.a0, bf16[2,2048]{1,0:T(2,128)(2,1)S(1)} %collective-permute-done.9.a1, bf16[2,2048]{1,0:T(2,128)(2,1)S(1)} %collective-permute-done.10.a2, ...), custom_call_target="tpu_custom_call" | custom-call | flops 134217728 | bytes 16777216 | tf_op jit(solution)/shard_map/project/pallas_call | solution.py:399
  34.7 1.4 %collective-permute-start.13 = (bf16[2,4096]{1,0:T(2,128)(2,1)S(1)}, bf16[2,4096]{1,0:T(2,128)(2,1)S(1)}, u32[]{:S(2)}, u32[]{:S(2)}) collective-permute-start(bf16[2,4096]{1,0:T(2,128)(2,1)S(1)} %get-tuple-element.43), channel_id=1, source_target_pairs={{0,2},{1,3},{2,0},{3,1},{4,6},{5,7},{6,4},{7,5},{8,10},{9,11},{10,... | collective-permute-start | bytes 49160 | tf_op jit(solution)/shard_map/ppermute | solution.py:35
  36.1 0.5 %collective-permute-start.14 = (bf16[2,4096]{1,0:T(2,128)(2,1)S(1)}, bf16[2,4096]{1,0:T(2,128)(2,1)S(1)}, u32[]{:S(2)}, u32[]{:S(2)}) collective-permute-start(bf16[2,4096]{1,0:T(2,128)(2,1)S(1)} %get-tuple-element.44), channel_id=1, source_target_pairs={{0,1},{1,0},{2,3},{3,2},{4,5},{5,4},{6,7},{7,6},{8,9},{9,8},{10,11... | collective-permute-start | bytes 49160 | tf_op jit(solution)/shard_map/ppermute | solution.py:35
  36.5 0.6 %copy.12 = bf16[1,40,128]{2,1,0:T(8,128)(2,1)} copy(bf16[1,40,128]{2,1,0:T(8,128)(2,1)S(1)} %bitcast.3) | data formatting | bytes 20480
  37.1 0.6 %copy.13 = bf16[1,40,128]{2,1,0:T(8,128)(2,1)} copy(bf16[1,40,128]{2,1,0:T(8,128)(2,1)S(1)} %bitcast.2) | data formatting | bytes 20480
  37.7 0.2 collective-permute-done.12
  37.9 0.5 %collective-permute-done.13 = bf16[2,4096]{1,0:T(2,128)(2,1)S(1)} collective-permute-done((bf16[2,4096]{1,0:T(2,128)(2,1)S(1)}, bf16[2,4096]{1,0:T(2,128)(2,1)S(1)}, u32[]{:S(2)}, u32[]{:S(2)}) %collective-permute-start.13) | collective-permute-done | bytes 16416 | tf_op jit(solution)/shard_map/ppermute | solution.py:35
  38.5 0.6 %add_convert_fusion = bf16[2,4096]{1,0:T(2,128)(2,1)} fusion(bf16[2,4096]{1,0:T(2,128)(2,1)S(1)} %collective-permute-done.14, bf16[2,4096]{1,0:T(2,128)(2,1)S(1)} %collective-permute-done.13, f32[2,4096]{1,0:T(2,128)S(1)} %get-tuple-element.41, bf16[2,4096]{1,0:T(2,128)(2,1)S(1)} %collective-permute-done.12), kind=kLoop, calls=%fused_computation | loop fusion | flops 57344 | bytes 98304 | tf_op jit(solution)/shard_map/convert_element_type | solution.py:411
  (19 shorter events, 0.0 us)
Async XLA Ops:
  0.6 10.3 %copy-start.2 = (bf16[40,4096]{1,0:T(8,128)(2,1)S(1)}, bf16[40,4096]{1,0:T(8,128)(2,1)}, u32[]{:S(2)}) copy-start(bf16[40,4096]{1,0:T(8,128)(2,1)} %s.1) | copy-start | bytes 983044
  0.6 11.7 %copy-start.3 = (bf16[2,4096]{1,0:T(2,128)(2,1)S(1)}, bf16[2,4096]{1,0:T(2,128)(2,1)}, u32[]{:S(2)}) copy-start(bf16[2,4096]{1,0:T(2,128)(2,1)} %b0.3) | copy-start | bytes 49156
  0.7 11.7 %copy-start = (bf16[4096,2048]{1,0:T(8,128)(2,1)S(1)}, bf16[4096,2048]{1,0:T(8,128)(2,1)}, u32[]{:S(2)}) copy-start(bf16[4096,2048]{1,0:T(8,128)(2,1)} %w.1) | copy-start | bytes 50331652
  0.7 11.6 %collective-permute-start = (bf16[40,4096]{1,0:T(8,128)(2,1)}, bf16[40,4096]{1,0:T(8,128)(2,1)S(1)}, u32[]{:S(2)}, u32[]{:S(2)}) collective-permute-start(bf16[40,4096]{1,0:T(8,128)(2,1)} %s.1), channel_id=1, source_target_pairs={{0,2},{1,3},{2,0},{3,1},{4,6},{5,7},{6,4},{7,5},{8,10},{9,11},{10,... | collective-permute-start | bytes 983048 | tf_op jit(solution)/shard_map/ppermute | solution.py:35
  3.7 7.8 %collective-permute-start.3 = (bf16[2,4096]{1,0:T(2,128)(2,1)}, bf16[2,4096]{1,0:T(2,128)(2,1)S(1)}, u32[]{:S(2)}, u32[]{:S(2)}) collective-permute-start(bf16[2,4096]{1,0:T(2,128)(2,1)} %b0.3), channel_id=1, source_target_pairs={{0,3},{1,2},{2,1},{3,0},{4,7},{5,6},{6,5},{7,4},{8,11},{9,10},{10,... | collective-permute-start | bytes 49160 | tf_op jit(solution)/shard_map/ppermute | solution.py:35
  3.7 8.6 %collective-permute-start.2 = (bf16[2,4096]{1,0:T(2,128)(2,1)}, bf16[2,4096]{1,0:T(2,128)(2,1)S(1)}, u32[]{:S(2)}, u32[]{:S(2)}) collective-permute-start(bf16[2,4096]{1,0:T(2,128)(2,1)} %b0.3), channel_id=1, source_target_pairs={{0,2},{1,3},{2,0},{3,1},{4,6},{5,7},{6,4},{7,5},{8,10},{9,11},{10,... | collective-permute-start | bytes 49160 | tf_op jit(solution)/shard_map/ppermute | solution.py:35
  4.9 7.4 %collective-permute-start.1 = (bf16[2,4096]{1,0:T(2,128)(2,1)}, bf16[2,4096]{1,0:T(2,128)(2,1)S(1)}, u32[]{:S(2)}, u32[]{:S(2)}) collective-permute-start(bf16[2,4096]{1,0:T(2,128)(2,1)} %b0.3), channel_id=1, source_target_pairs={{0,1},{1,0},{2,3},{3,2},{4,5},{5,4},{6,7},{7,6},{8,9},{9,8},{10,11... | collective-permute-start | bytes 49160 | tf_op jit(solution)/shard_map/ppermute | solution.py:35
  5.5 9.1 %collective-permute-start.4 = (bf16[40,4096]{1,0:T(8,128)(2,1)}, bf16[40,4096]{1,0:T(8,128)(2,1)S(1)}, u32[]{:S(2)}, u32[]{:S(2)}) collective-permute-start(bf16[40,4096]{1,0:T(8,128)(2,1)} %s.1), channel_id=1, source_target_pairs={{0,1},{1,0},{2,3},{3,2},{4,5},{5,4},{6,7},{7,6},{8,9},{9,8},{10,11... | collective-permute-start | bytes 983048 | tf_op jit(solution)/shard_map/ppermute | solution.py:35
  11.4 3.3 %copy-start.5 = (s32[4]{0:T(128)S(1)}, s32[4]{0:T(128)}, u32[]{:S(2)}) copy-start(s32[4]{0:T(128)} %owner_ref.1) | copy-start | bytes 52
  11.4 13.4 %copy-start.1 = (bf16[2,2,512,128]{3,2,1,0:T(8,128)(2,1)S(1)}, bf16[2,2,512,128]{3,2,1,0:T(8,128)(2,1)}, u32[]{:S(2)}) copy-start(bf16[2,2,512,128]{3,2,1,0:T(8,128)(2,1)} %kv.1) | copy-start | bytes 1572868
  11.4 13.3 %copy-start.4 = (s32[2]{0:T(128)S(1)}, s32[2]{0:T(128)}, u32[]{:S(2)}) copy-start(s32[2]{0:T(128)} %len_ref.1) | copy-start | bytes 28
  12.3 2.4 %collective-permute-start.5 = (bf16[40,4096]{1,0:T(8,128)(2,1)S(1)}, bf16[40,4096]{1,0:T(8,128)(2,1)S(1)}, u32[]{:S(2)}, u32[]{:S(2)}) collective-permute-start(bf16[40,4096]{1,0:T(8,128)(2,1)S(1)} %collective-permute-done.far.s2), channel_id=1, source_target_pairs={{0,1},{1,0},{2,3},{3,2},{4,5},{5,4},{6,7},{7,6},{8,9},{9,8},{10,11... | collective-permute-start | bytes 983048 | tf_op jit(solution)/shard_map/ppermute | solution.py:35
  15.8 6.1 %collective-permute-start.6 = (bf16[128,128]{1,0:T(8,128)(2,1)S(1)}, bf16[128,128]{1,0:T(8,128)(2,1)S(1)}, u32[]{:S(2)}, u32[]{:S(2)}) collective-permute-start(bf16[128,128]{1,0:T(8,128)(2,1)S(1)} %get-tuple-element.33), channel_id=1, source_target_pairs={{0,12},{4,8},{8,4},{12,0},{1,13},{5,9},{9,5},{13,1},{2,14},{6,10},... | collective-permute-start | bytes 98312 | tf_op jit(solution)/shard_map/ppermute | solution.py:35
  19.9 4.8 %collective-permute-start.7 = (bf16[128,128]{1,0:T(8,128)(2,1)S(1)}, bf16[128,128]{1,0:T(8,128)(2,1)S(1)}, u32[]{:S(2)}, u32[]{:S(2)}) collective-permute-start(bf16[128,128]{1,0:T(8,128)(2,1)S(1)} %get-tuple-element.34), channel_id=1, source_target_pairs={{0,8},{4,12},{8,0},{12,4},{1,9},{5,13},{9,1},{13,5},{2,10},{6,14},... | collective-permute-start | bytes 98312 | tf_op jit(solution)/shard_map/ppermute | solution.py:35
  19.9 4.8 %collective-permute-start.8 = (bf16[128,128]{1,0:T(8,128)(2,1)S(1)}, bf16[128,128]{1,0:T(8,128)(2,1)S(1)}, u32[]{:S(2)}, u32[]{:S(2)}) collective-permute-start(bf16[128,128]{1,0:T(8,128)(2,1)S(1)} %get-tuple-element.35), channel_id=1, source_target_pairs={{0,4},{4,0},{8,12},{12,8},{1,5},{5,1},{9,13},{13,9},{2,6},{6,2},{1... | collective-permute-start | bytes 98312 | tf_op jit(solution)/shard_map/ppermute | solution.py:35
  26.2 5.5 %collective-permute-start.11 = (bf16[2,2048]{1,0:T(2,128)(2,1)S(1)}, bf16[2,2048]{1,0:T(2,128)(2,1)S(1)}, u32[]{:S(2)}, u32[]{:S(2)}) collective-permute-start(bf16[2,2048]{1,0:T(2,128)(2,1)S(1)} %get-tuple-element.38.a0), channel_id=1, source_target_pairs={{0,12},{4,8},{8,4},{12,0},{1,13},{5,9},{9,5},{13,1},{2,14},{6,10},... | collective-permute-start | bytes 24584 | tf_op jit(solution)/shard_map/ppermute | solution.py:35
  27.8 4.6 %collective-permute-start.10 = (bf16[2,2048]{1,0:T(2,128)(2,1)S(1)}, bf16[2,2048]{1,0:T(2,128)(2,1)S(1)}, u32[]{:S(2)}, u32[]{:S(2)}) collective-permute-start(bf16[2,2048]{1,0:T(2,128)(2,1)S(1)} %get-tuple-element.38.a0), channel_id=1, source_target_pairs={{0,8},{4,12},{8,0},{12,4},{1,9},{5,13},{9,1},{13,5},{2,10},{6,14},... | collective-permute-start | bytes 24584 | tf_op jit(solution)/shard_map/ppermute | solution.py:35
  28.4 4.0 %collective-permute-start.9 = (bf16[2,2048]{1,0:T(2,128)(2,1)S(1)}, bf16[2,2048]{1,0:T(2,128)(2,1)S(1)}, u32[]{:S(2)}, u32[]{:S(2)}) collective-permute-start(bf16[2,2048]{1,0:T(2,128)(2,1)S(1)} %get-tuple-element.38.a0), channel_id=1, source_target_pairs={{0,4},{4,0},{8,12},{12,8},{1,5},{5,1},{9,13},{13,9},{2,6},{6,2},{1... | collective-permute-start | bytes 24584 | tf_op jit(solution)/shard_map/ppermute | solution.py:35
  34.7 3.3 %collective-permute-start.12 = (bf16[2,4096]{1,0:T(2,128)(2,1)S(1)}, bf16[2,4096]{1,0:T(2,128)(2,1)S(1)}, u32[]{:S(2)}, u32[]{:S(2)}) collective-permute-start(bf16[2,4096]{1,0:T(2,128)(2,1)S(1)} %get-tuple-element.42), channel_id=1, source_target_pairs={{0,3},{1,2},{2,1},{3,0},{4,7},{5,6},{6,5},{7,4},{8,11},{9,10},{10,... | collective-permute-start | bytes 49160 | tf_op jit(solution)/shard_map/ppermute | solution.py:35
  34.7 3.8 %collective-permute-start.13 = (bf16[2,4096]{1,0:T(2,128)(2,1)S(1)}, bf16[2,4096]{1,0:T(2,128)(2,1)S(1)}, u32[]{:S(2)}, u32[]{:S(2)}) collective-permute-start(bf16[2,4096]{1,0:T(2,128)(2,1)S(1)} %get-tuple-element.43), channel_id=1, source_target_pairs={{0,2},{1,3},{2,0},{3,1},{4,6},{5,7},{6,4},{7,5},{8,10},{9,11},{10,... | collective-permute-start | bytes 49160 | tf_op jit(solution)/shard_map/ppermute | solution.py:35
  36.1 2.4 %collective-permute-start.14 = (bf16[2,4096]{1,0:T(2,128)(2,1)S(1)}, bf16[2,4096]{1,0:T(2,128)(2,1)S(1)}, u32[]{:S(2)}, u32[]{:S(2)}) collective-permute-start(bf16[2,4096]{1,0:T(2,128)(2,1)S(1)} %get-tuple-element.44), channel_id=1, source_target_pairs={{0,1},{1,0},{2,3},{3,2},{4,5},{5,4},{6,7},{7,6},{8,9},{9,8},{10,11... | collective-permute-start | bytes 49160 | tf_op jit(solution)/shard_map/ppermute | solution.py:35

commit v8 on v7

--- a/solution.py
+++ b/solution.py
@@ -147,7 +147,6 @@
     return (mixed.astype(jnp.bfloat16), rebuilt_key[None], rebuilt_value[None])
 
 
-CHUNK = 512
 ROW_TILE = 48
 PAY = 128
 VALUES = 48
@@ -195,14 +194,6 @@
     return copies
 
 
-def project_rows(x, wkv):
-    both = jnp.zeros((x.shape[0], wkv.shape[1]), F32)
-    for c in range(x.shape[1] // CHUNK):
-        part = slice(c * CHUNK, (c + 1) * CHUNK)
-        both += jnp.dot(x[:, part], wkv[part, :], preferred_element_type=F32)
-    return both
-
-
 def load_kernel(
     len_hbm, wo_hbm, wk_hbm, wv_hbm, cos_ref, sin_ref, wo, wkv, len_ref, sems
 ):
@@ -218,7 +209,7 @@
 
 
 def own_kernel(s, wkv, out):
-    out[...] = project_rows(s, wkv)
+    out[...] = jnp.dot(s[...], wkv[...], preferred_element_type=F32)
 
 
 def query_kernel(first, far, b0, b1, b2, b3, w, wo_hbm, out_ref, wo, acc, sems):
@@ -243,7 +234,7 @@
     fresh.append(jnp.zeros((8, x.shape[1]), F32))
     base = 3 * ROW_TILE
     x[pl.ds(base, 16), :] = jnp.concatenate(fresh, axis=0).astype(BF16)
-    late = project_rows(x, wkv)
+    late = jnp.dot(x[...], wkv[...], preferred_element_type=F32)
     empty = jnp.zeros((8 - ROWS_DEV, HD), F32)
     for k in range(4):
         target = owner_ref[gy ^ k] ^ gx

time: 39.2 us -> 39.2 us (level)
  no operation moved by 1% of the time
where the time goes in v8:
time: 39.2 us; the launch traced here: 39.1 us
  starting transfers between devices  16 us (41%)
  Pallas kernels  13 us (33%)
  waiting for transfers between devices  7.49 us (19%)
  local copies, waits for them, and re-layouts  1.23 us (3%)
  between operations  0.8 us (2%)
  other arithmetic  0.64 us (2%)
    ppermute x15, starting transfers between devices, swap(): return lax.ppermute(x, axis, [(i, i ^ k) for i in range(n)])  16 us
    ppermute x15, waiting for transfers between devices, swap(): return lax.ppermute(x, axis, [(i, i ^ k) for i in range(n)])  7.49 us
    pallas_call x1, Pallas kernels, per_device(): pl.pallas_call(load_kernel, out_shape=[pltpu.VMEM((PAY, HD), F32)] * 2 +...  5.35 us
    pallas_call x1, Pallas kernels, per_device(): pl.pallas_call(functools.partial(query_kernel, query_cols - quarter), out...  2.33 us
    pallas_call x1, Pallas kernels, per_device(): pl.pallas_call(out_kernel, out_shape=[shape((ROWS_DEV, width), F32)] + [s...  2.28 us
    pallas_call x1, Pallas kernels, per_device(): pl.pallas_call(attend_kernel, out_shape=[pltpu.VMEM((LC, HD), BF16)] * 2...  1.43 us
    unnamed x14, local copies, waits for them, and re-layouts  1.23 us
    pallas_call x1, Pallas kernels, per_device(): pl.pallas_call(payload_kernel, out_shape=[shape((PAY, HD), F32)] + [shape...  1.11 us
  transfers between devices with their start and end apart: 15, of which 7 were waited for; matrix products, arithmetic and copies ran while one was open for 3% of the time, Pallas kernels for 21%

profile of v8, /device:TPU:0, one launch (start us, length us, event | category | flops | bytes accessed | tf_op | source)
XLA Modules:
  0.0 39.1 jit_solution(16614028697562727651)
XLA Ops:
  0.7 3.0 %collective-permute-start = (bf16[40,4096]{1,0:T(8,128)(2,1)}, bf16[40,4096]{1,0:T(8,128)(2,1)S(1)}, u32[]{:S(2)}, u32[]{:S(2)}) collective-permute-start(bf16[40,4096]{1,0:T(8,128)(2,1)} %s.1), channel_id=1, source_target_pairs={{0,2},{1,3},{2,0},{3,1},{4,6},{5,7},{6,4},{7,5},{8,10},{9,11},{10,... | collective-permute-start | bytes 983048 | tf_op jit(solution)/shard_map/ppermute | solution.py:35
  3.7 1.2 %collective-permute-start.2 = (bf16[2,4096]{1,0:T(2,128)(2,1)}, bf16[2,4096]{1,0:T(2,128)(2,1)S(1)}, u32[]{:S(2)}, u32[]{:S(2)}) collective-permute-start(bf16[2,4096]{1,0:T(2,128)(2,1)} %b0.3), channel_id=1, source_target_pairs={{0,2},{1,3},{2,0},{3,1},{4,6},{5,7},{6,4},{7,5},{8,10},{9,11},{10,... | collective-permute-start | bytes 49160 | tf_op jit(solution)/shard_map/ppermute | solution.py:35
  4.9 0.7 %collective-permute-start.1 = (bf16[2,4096]{1,0:T(2,128)(2,1)}, bf16[2,4096]{1,0:T(2,128)(2,1)S(1)}, u32[]{:S(2)}, u32[]{:S(2)}) collective-permute-start(bf16[2,4096]{1,0:T(2,128)(2,1)} %b0.3), channel_id=1, source_target_pairs={{0,1},{1,0},{2,3},{3,2},{4,5},{5,4},{6,7},{7,6},{8,9},{9,8},{10,11... | collective-permute-start | bytes 49160 | tf_op jit(solution)/shard_map/ppermute | solution.py:35
  5.5 0.0 collective-permute-start.4
  5.5 5.3 %load.1 = (f32[128,128]{1,0:T(8,128)S(1)}, f32[128,128]{1,0:T(8,128)S(1)}, bf16[1536,4096]{1,0:T(8,128)(2,1)S(1)}, bf16[4096,256]{1,0:T(8,128)(2,1)S(1)}) custom-call(s32[2]{0:T(128)} %len_ref.1, bf16[2048,4096]{1,0:T(8,128)(2,1)} %wo_hbm.3, bf16[4096,128]{1,0:T(8,128)(2,1)} %wk_hbm.1, bf16[4096,128]{1,0:T(8,128)(2,1)} %wv_hbm.1), custom_call_target="tpu_custom_call" | custom-call | flops 1000 | bytes 16777216 | tf_op jit(solution)/shard_map/load/pallas_call | solution.py:324
  10.9 0.5 %own.1 = f32[40,256]{1,0:T(8,128)S(1)} custom-call(bf16[40,4096]{1,0:T(8,128)(2,1)S(1)} %copy-done.2, bf16[4096,256]{1,0:T(8,128)(2,1)S(1)} %get-tuple-element.25.wkv), custom_call_target="tpu_custom_call" | custom-call | flops 83886080 | bytes 2097152 | tf_op jit(solution)/shard_map/own/pallas_call | solution.py:340
  11.4 0.0 copy-start.5
  11.4 0.0 copy-start.1
  11.4 0.0 copy-start.4
  11.4 0.9 %collective-permute-done.2.b2 = bf16[2,4096]{1,0:T(2,128)(2,1)S(1)} collective-permute-done((bf16[2,4096]{1,0:T(2,128)(2,1)}, bf16[2,4096]{1,0:T(2,128)(2,1)S(1)}, u32[]{:S(2)}, u32[]{:S(2)}) %collective-permute-start.2) | collective-permute-done | bytes 16416 | tf_op jit(solution)/shard_map/ppermute | solution.py:35
  12.3 0.0 collective-permute-done.1.b1
  12.3 0.0 collective-permute-done.far.s2
  12.3 2.3 %query.1 = (f32[8,16,128]{2,1,0:T(8,128)S(1)}, bf16[512,4096]{1,0:T(8,128)(2,1)S(1)}) custom-call(bf16[40,4096]{1,0:T(8,128)(2,1)S(1)} %collective-permute-done.far.s2, bf16[2,4096]{1,0:T(2,128)(2,1)S(1)} %copy-done.3, bf16[2,4096]{1,0:T(2,128)(2,1)S(1)} %collective-permute-done.1.b1, bf16[2,4096]{1,0:T(2,128)(2,1)S(1)} %collective-permute-done.2.b2, ...), custom_call_target="tpu_custom_call" | custom-call | flops 134217728 | bytes 2097152 | tf_op jit(solution)/shard_map/query/pallas_call | solution.py:352
  14.7 1.1 %payload.1 = (f32[128,128]{1,0:T(8,128)S(1)}, bf16[128,128]{1,0:T(8,128)(2,1)S(1)}, bf16[128,128]{1,0:T(8,128)(2,1)S(1)}, bf16[128,128]{1,0:T(8,128)(2,1)S(1)}) custom-call(s32[4]{0:T(128)S(1)} %copy-done.5, f32[40,256]{1,0:T(8,128)S(1)} %own.1, bf16[40,4096]{1,0:T(8,128)(2,1)S(1)} %collective-permute-done.4.s1, ...), custom_call_target="tpu_custom_call" | custom-call | flops 436207616 | bytes 2097152 | tf_op jit(solution)/shard_map/payload/pallas_call | solution.py:365
  15.8 4.1 %collective-permute-start.6 = (bf16[128,128]{1,0:T(8,128)(2,1)S(1)}, bf16[128,128]{1,0:T(8,128)(2,1)S(1)}, u32[]{:S(2)}, u32[]{:S(2)}) collective-permute-start(bf16[128,128]{1,0:T(8,128)(2,1)S(1)} %get-tuple-element.33), channel_id=1, source_target_pairs={{0,12},{4,8},{8,4},{12,0},{1,13},{5,9},{9,5},{13,1},{2,14},{6,10},... | collective-permute-start | bytes 98312 | tf_op jit(solution)/shard_map/ppermute | solution.py:35
  19.9 0.6 %collective-permute-start.8 = (bf16[128,128]{1,0:T(8,128)(2,1)S(1)}, bf16[128,128]{1,0:T(8,128)(2,1)S(1)}, u32[]{:S(2)}, u32[]{:S(2)}) collective-permute-start(bf16[128,128]{1,0:T(8,128)(2,1)S(1)} %get-tuple-element.35), channel_id=1, source_target_pairs={{0,4},{4,0},{8,12},{12,8},{1,5},{5,1},{9,13},{13,9},{2,6},{6,2},{1... | collective-permute-start | bytes 98312 | tf_op jit(solution)/shard_map/ppermute | solution.py:35
  20.6 1.3 %collective-permute-done.6.p1 = bf16[128,128]{1,0:T(8,128)(2,1)S(1)} collective-permute-done((bf16[128,128]{1,0:T(8,128)(2,1)S(1)}, bf16[128,128]{1,0:T(8,128)(2,1)S(1)}, u32[]{:S(2)}, u32[]{:S(2)}) %collective-permute-start.6) | collective-permute-done | bytes 32800 | tf_op jit(solution)/shard_map/ppermute | solution.py:35
  21.9 2.9 %collective-permute-done.7.p2 = bf16[128,128]{1,0:T(8,128)(2,1)S(1)} collective-permute-done((bf16[128,128]{1,0:T(8,128)(2,1)S(1)}, bf16[128,128]{1,0:T(8,128)(2,1)S(1)}, u32[]{:S(2)}, u32[]{:S(2)}) %collective-permute-start.7) | collective-permute-done | bytes 32800 | tf_op jit(solution)/shard_map/ppermute | solution.py:35
  24.7 1.4 %attend.1 = (bf16[40,128]{1,0:T(8,128)(2,1)S(1)}, bf16[40,128]{1,0:T(8,128)(2,1)S(1)}, bf16[2,2048]{1,0:T(2,128)(2,1)S(1)}) custom-call(s32[2]{0:T(128)S(1)} %copy-done.4, f32[128,128]{1,0:T(8,128)S(1)} %get-tuple-element.32.p0, bf16[128,128]{1,0:T(8,128)(2,1)S(1)} %collective-permute-done.6.p1, bf16[128,128]{1,0:T(8,128)(2,1)S(1)} %collective-permute-done.7.p2, ...), custom_call_target="tpu_custom_call" | custom-call | flops 10000000 | bytes 1000000 | tf_op jit(solution)/shard_map/attend/pallas_call | solution.py:379
  26.2 1.6 %collective-permute-start.11 = (bf16[2,2048]{1,0:T(2,128)(2,1)S(1)}, bf16[2,2048]{1,0:T(2,128)(2,1)S(1)}, u32[]{:S(2)}, u32[]{:S(2)}) collective-permute-start(bf16[2,2048]{1,0:T(2,128)(2,1)S(1)} %get-tuple-element.38.a0), channel_id=1, source_target_pairs={{0,12},{4,8},{8,4},{12,0},{1,13},{5,9},{9,5},{13,1},{2,14},{6,10},... | collective-permute-start | bytes 24584 | tf_op jit(solution)/shard_map/ppermute | solution.py:35
  27.8 0.6 %collective-permute-start.10 = (bf16[2,2048]{1,0:T(2,128)(2,1)S(1)}, bf16[2,2048]{1,0:T(2,128)(2,1)S(1)}, u32[]{:S(2)}, u32[]{:S(2)}) collective-permute-start(bf16[2,2048]{1,0:T(2,128)(2,1)S(1)} %get-tuple-element.38.a0), channel_id=1, source_target_pairs={{0,8},{4,12},{8,0},{12,4},{1,9},{5,13},{9,1},{13,5},{2,10},{6,14},... | collective-permute-start | bytes 24584 | tf_op jit(solution)/shard_map/ppermute | solution.py:35
  28.3 2.3 %collective-permute-start.9 = (bf16[2,2048]{1,0:T(2,128)(2,1)S(1)}, bf16[2,2048]{1,0:T(2,128)(2,1)S(1)}, u32[]{:S(2)}, u32[]{:S(2)}) collective-permute-start(bf16[2,2048]{1,0:T(2,128)(2,1)S(1)} %get-tuple-element.38.a0), channel_id=1, source_target_pairs={{0,4},{4,0},{8,12},{12,8},{1,5},{5,1},{9,13},{13,9},{2,6},{6,2},{1... | collective-permute-start | bytes 24584 | tf_op jit(solution)/shard_map/ppermute | solution.py:35
  30.6 1.1 %collective-permute-done.11.a3 = bf16[2,2048]{1,0:T(2,128)(2,1)S(1)} collective-permute-done((bf16[2,2048]{1,0:T(2,128)(2,1)S(1)}, bf16[2,2048]{1,0:T(2,128)(2,1)S(1)}, u32[]{:S(2)}, u32[]{:S(2)}) %collective-permute-start.11) | collective-permute-done | bytes 8224 | tf_op jit(solution)/shard_map/ppermute | solution.py:35
  31.7 0.7 %collective-permute-done.10.a2 = bf16[2,2048]{1,0:T(2,128)(2,1)S(1)} collective-permute-done((bf16[2,2048]{1,0:T(2,128)(2,1)S(1)}, bf16[2,2048]{1,0:T(2,128)(2,1)S(1)}, u32[]{:S(2)}, u32[]{:S(2)}) %collective-permute-start.10) | collective-permute-done | bytes 8224 | tf_op jit(solution)/shard_map/ppermute | solution.py:35
  32.4 2.3 %project.1 = (f32[2,4096]{1,0:T(2,128)S(1)}, bf16[2,4096]{1,0:T(2,128)(2,1)S(1)}, bf16[2,4096]{1,0:T(2,128)(2,1)S(1)}, bf16[2,4096]{1,0:T(2,128)(2,1)S(1)}) custom-call(bf16[2,2048]{1,0:T(2,128)(2,1)S(1)} %get-tuple-element.38.a0, bf16[2,2048]{1,0:T(2,128)(2,1)S(1)} %collective-permute-done.9.a1, bf16[2,2048]{1,0:T(2,128)(2,1)S(1)} %collective-permute-done.10.a2, ...), custom_call_target="tpu_custom_call" | custom-call | flops 134217728 | bytes 16777216 | tf_op jit(solution)/shard_map/project/pallas_call | solution.py:390
  34.6 1.4 %collective-permute-start.13 = (bf16[2,4096]{1,0:T(2,128)(2,1)S(1)}, bf16[2,4096]{1,0:T(2,128)(2,1)S(1)}, u32[]{:S(2)}, u32[]{:S(2)}) collective-permute-start(bf16[2,4096]{1,0:T(2,128)(2,1)S(1)} %get-tuple-element.43), channel_id=1, source_target_pairs={{0,2},{1,3},{2,0},{3,1},{4,6},{5,7},{6,4},{7,5},{8,10},{9,11},{10,... | collective-permute-start | bytes 49160 | tf_op jit(solution)/shard_map/ppermute | solution.py:35
  36.1 0.4 %collective-permute-start.14 = (bf16[2,4096]{1,0:T(2,128)(2,1)S(1)}, bf16[2,4096]{1,0:T(2,128)(2,1)S(1)}, u32[]{:S(2)}, u32[]{:S(2)}) collective-permute-start(bf16[2,4096]{1,0:T(2,128)(2,1)S(1)} %get-tuple-element.44), channel_id=1, source_target_pairs={{0,1},{1,0},{2,3},{3,2},{4,5},{5,4},{6,7},{7,6},{8,9},{9,8},{10,11... | collective-permute-start | bytes 49160 | tf_op jit(solution)/shard_map/ppermute | solution.py:35
  36.5 0.6 %copy.12 = bf16[1,40,128]{2,1,0:T(8,128)(2,1)} copy(bf16[1,40,128]{2,1,0:T(8,128)(2,1)S(1)} %bitcast.3) | data formatting | bytes 20480
  37.1 0.6 %copy.13 = bf16[1,40,128]{2,1,0:T(8,128)(2,1)} copy(bf16[1,40,128]{2,1,0:T(8,128)(2,1)S(1)} %bitcast.2) | data formatting | bytes 20480
  37.7 0.2 collective-permute-done.12
  37.9 0.5 %collective-permute-done.13 = bf16[2,4096]{1,0:T(2,128)(2,1)S(1)} collective-permute-done((bf16[2,4096]{1,0:T(2,128)(2,1)S(1)}, bf16[2,4096]{1,0:T(2,128)(2,1)S(1)}, u32[]{:S(2)}, u32[]{:S(2)}) %collective-permute-start.13) | collective-permute-done | bytes 16416 | tf_op jit(solution)/shard_map/ppermute | solution.py:35
  38.4 0.6 %add_convert_fusion = bf16[2,4096]{1,0:T(2,128)(2,1)} fusion(bf16[2,4096]{1,0:T(2,128)(2,1)S(1)} %collective-permute-done.14, bf16[2,4096]{1,0:T(2,128)(2,1)S(1)} %collective-permute-done.13, f32[2,4096]{1,0:T(2,128)S(1)} %get-tuple-element.41, bf16[2,4096]{1,0:T(2,128)(2,1)S(1)} %collective-permute-done.12), kind=kLoop, calls=%fused_computation | loop fusion | flops 57344 | bytes 98304 | tf_op jit(solution)/shard_map/convert_element_type | solution.py:402
  (19 shorter events, 0.0 us)
Async XLA Ops:
  0.6 10.3 %copy-start.2 = (bf16[40,4096]{1,0:T(8,128)(2,1)S(1)}, bf16[40,4096]{1,0:T(8,128)(2,1)}, u32[]{:S(2)}) copy-start(bf16[40,4096]{1,0:T(8,128)(2,1)} %s.1) | copy-start | bytes 983044
  0.6 11.7 %copy-start.3 = (bf16[2,4096]{1,0:T(2,128)(2,1)S(1)}, bf16[2,4096]{1,0:T(2,128)(2,1)}, u32[]{:S(2)}) copy-start(bf16[2,4096]{1,0:T(2,128)(2,1)} %b0.3) | copy-start | bytes 49156
  0.7 11.7 %copy-start = (bf16[4096,2048]{1,0:T(8,128)(2,1)S(1)}, bf16[4096,2048]{1,0:T(8,128)(2,1)}, u32[]{:S(2)}) copy-start(bf16[4096,2048]{1,0:T(8,128)(2,1)} %w.1) | copy-start | bytes 50331652
  0.7 11.6 %collective-permute-start = (bf16[40,4096]{1,0:T(8,128)(2,1)}, bf16[40,4096]{1,0:T(8,128)(2,1)S(1)}, u32[]{:S(2)}, u32[]{:S(2)}) collective-permute-start(bf16[40,4096]{1,0:T(8,128)(2,1)} %s.1), channel_id=1, source_target_pairs={{0,2},{1,3},{2,0},{3,1},{4,6},{5,7},{6,4},{7,5},{8,10},{9,11},{10,... | collective-permute-start | bytes 983048 | tf_op jit(solution)/shard_map/ppermute | solution.py:35
  3.7 7.8 %collective-permute-start.3 = (bf16[2,4096]{1,0:T(2,128)(2,1)}, bf16[2,4096]{1,0:T(2,128)(2,1)S(1)}, u32[]{:S(2)}, u32[]{:S(2)}) collective-permute-start(bf16[2,4096]{1,0:T(2,128)(2,1)} %b0.3), channel_id=1, source_target_pairs={{0,3},{1,2},{2,1},{3,0},{4,7},{5,6},{6,5},{7,4},{8,11},{9,10},{10,... | collective-permute-start | bytes 49160 | tf_op jit(solution)/shard_map/ppermute | solution.py:35
  3.7 8.6 %collective-permute-start.2 = (bf16[2,4096]{1,0:T(2,128)(2,1)}, bf16[2,4096]{1,0:T(2,128)(2,1)S(1)}, u32[]{:S(2)}, u32[]{:S(2)}) collective-permute-start(bf16[2,4096]{1,0:T(2,128)(2,1)} %b0.3), channel_id=1, source_target_pairs={{0,2},{1,3},{2,0},{3,1},{4,6},{5,7},{6,4},{7,5},{8,10},{9,11},{10,... | collective-permute-start | bytes 49160 | tf_op jit(solution)/shard_map/ppermute | solution.py:35
  4.9 7.4 %collective-permute-start.1 = (bf16[2,4096]{1,0:T(2,128)(2,1)}, bf16[2,4096]{1,0:T(2,128)(2,1)S(1)}, u32[]{:S(2)}, u32[]{:S(2)}) collective-permute-start(bf16[2,4096]{1,0:T(2,128)(2,1)} %b0.3), channel_id=1, source_target_pairs={{0,1},{1,0},{2,3},{3,2},{4,5},{5,4},{6,7},{7,6},{8,9},{9,8},{10,11... | collective-permute-start | bytes 49160 | tf_op jit(solution)/shard_map/ppermute | solution.py:35
  5.5 9.1 %collective-permute-start.4 = (bf16[40,4096]{1,0:T(8,128)(2,1)}, bf16[40,4096]{1,0:T(8,128)(2,1)S(1)}, u32[]{:S(2)}, u32[]{:S(2)}) collective-permute-start(bf16[40,4096]{1,0:T(8,128)(2,1)} %s.1), channel_id=1, source_target_pairs={{0,1},{1,0},{2,3},{3,2},{4,5},{5,4},{6,7},{7,6},{8,9},{9,8},{10,11... | collective-permute-start | bytes 983048 | tf_op jit(solution)/shard_map/ppermute | solution.py:35
  11.4 3.3 %copy-start.5 = (s32[4]{0:T(128)S(1)}, s32[4]{0:T(128)}, u32[]{:S(2)}) copy-start(s32[4]{0:T(128)} %owner_ref.1) | copy-start | bytes 52
  11.4 13.3 %copy-start.1 = (bf16[2,2,512,128]{3,2,1,0:T(8,128)(2,1)S(1)}, bf16[2,2,512,128]{3,2,1,0:T(8,128)(2,1)}, u32[]{:S(2)}) copy-start(bf16[2,2,512,128]{3,2,1,0:T(8,128)(2,1)} %kv.1) | copy-start | bytes 1572868
  11.4 13.3 %copy-start.4 = (s32[2]{0:T(128)S(1)}, s32[2]{0:T(128)}, u32[]{:S(2)}) copy-start(s32[2]{0:T(128)} %len_ref.1) | copy-start | bytes 28
  12.3 2.4 %collective-permute-start.5 = (bf16[40,4096]{1,0:T(8,128)(2,1)S(1)}, bf16[40,4096]{1,0:T(8,128)(2,1)S(1)}, u32[]{:S(2)}, u32[]{:S(2)}) collective-permute-start(bf16[40,4096]{1,0:T(8,128)(2,1)S(1)} %collective-permute-done.far.s2), channel_id=1, source_target_pairs={{0,1},{1,0},{2,3},{3,2},{4,5},{5,4},{6,7},{7,6},{8,9},{9,8},{10,11... | collective-permute-start | bytes 983048 | tf_op jit(solution)/shard_map/ppermute | solution.py:35
  15.8 6.1 %collective-permute-start.6 = (bf16[128,128]{1,0:T(8,128)(2,1)S(1)}, bf16[128,128]{1,0:T(8,128)(2,1)S(1)}, u32[]{:S(2)}, u32[]{:S(2)}) collective-permute-start(bf16[128,128]{1,0:T(8,128)(2,1)S(1)} %get-tuple-element.33), channel_id=1, source_target_pairs={{0,12},{4,8},{8,4},{12,0},{1,13},{5,9},{9,5},{13,1},{2,14},{6,10},... | collective-permute-start | bytes 98312 | tf_op jit(solution)/shard_map/ppermute | solution.py:35
  19.9 4.8 %collective-permute-start.7 = (bf16[128,128]{1,0:T(8,128)(2,1)S(1)}, bf16[128,128]{1,0:T(8,128)(2,1)S(1)}, u32[]{:S(2)}, u32[]{:S(2)}) collective-permute-start(bf16[128,128]{1,0:T(8,128)(2,1)S(1)} %get-tuple-element.34), channel_id=1, source_target_pairs={{0,8},{4,12},{8,0},{12,4},{1,9},{5,13},{9,1},{13,5},{2,10},{6,14},... | collective-permute-start | bytes 98312 | tf_op jit(solution)/shard_map/ppermute | solution.py:35
  19.9 4.8 %collective-permute-start.8 = (bf16[128,128]{1,0:T(8,128)(2,1)S(1)}, bf16[128,128]{1,0:T(8,128)(2,1)S(1)}, u32[]{:S(2)}, u32[]{:S(2)}) collective-permute-start(bf16[128,128]{1,0:T(8,128)(2,1)S(1)} %get-tuple-element.35), channel_id=1, source_target_pairs={{0,4},{4,0},{8,12},{12,8},{1,5},{5,1},{9,13},{13,9},{2,6},{6,2},{1... | collective-permute-start | bytes 98312 | tf_op jit(solution)/shard_map/ppermute | solution.py:35
  26.2 5.5 %collective-permute-start.11 = (bf16[2,2048]{1,0:T(2,128)(2,1)S(1)}, bf16[2,2048]{1,0:T(2,128)(2,1)S(1)}, u32[]{:S(2)}, u32[]{:S(2)}) collective-permute-start(bf16[2,2048]{1,0:T(2,128)(2,1)S(1)} %get-tuple-element.38.a0), channel_id=1, source_target_pairs={{0,12},{4,8},{8,4},{12,0},{1,13},{5,9},{9,5},{13,1},{2,14},{6,10},... | collective-permute-start | bytes 24584 | tf_op jit(solution)/shard_map/ppermute | solution.py:35
  27.8 4.6 %collective-permute-start.10 = (bf16[2,2048]{1,0:T(2,128)(2,1)S(1)}, bf16[2,2048]{1,0:T(2,128)(2,1)S(1)}, u32[]{:S(2)}, u32[]{:S(2)}) collective-permute-start(bf16[2,2048]{1,0:T(2,128)(2,1)S(1)} %get-tuple-element.38.a0), channel_id=1, source_target_pairs={{0,8},{4,12},{8,0},{12,4},{1,9},{5,13},{9,1},{13,5},{2,10},{6,14},... | collective-permute-start | bytes 24584 | tf_op jit(solution)/shard_map/ppermute | solution.py:35
  28.3 4.0 %collective-permute-start.9 = (bf16[2,2048]{1,0:T(2,128)(2,1)S(1)}, bf16[2,2048]{1,0:T(2,128)(2,1)S(1)}, u32[]{:S(2)}, u32[]{:S(2)}) collective-permute-start(bf16[2,2048]{1,0:T(2,128)(2,1)S(1)} %get-tuple-element.38.a0), channel_id=1, source_target_pairs={{0,4},{4,0},{8,12},{12,8},{1,5},{5,1},{9,13},{13,9},{2,6},{6,2},{1... | collective-permute-start | bytes 24584 | tf_op jit(solution)/shard_map/ppermute | solution.py:35
  34.6 3.3 %collective-permute-start.12 = (bf16[2,4096]{1,0:T(2,128)(2,1)S(1)}, bf16[2,4096]{1,0:T(2,128)(2,1)S(1)}, u32[]{:S(2)}, u32[]{:S(2)}) collective-permute-start(bf16[2,4096]{1,0:T(2,128)(2,1)S(1)} %get-tuple-element.42), channel_id=1, source_target_pairs={{0,3},{1,2},{2,1},{3,0},{4,7},{5,6},{6,5},{7,4},{8,11},{9,10},{10,... | collective-permute-start | bytes 49160 | tf_op jit(solution)/shard_map/ppermute | solution.py:35
  34.6 3.8 %collective-permute-start.13 = (bf16[2,4096]{1,0:T(2,128)(2,1)S(1)}, bf16[2,4096]{1,0:T(2,128)(2,1)S(1)}, u32[]{:S(2)}, u32[]{:S(2)}) collective-permute-start(bf16[2,4096]{1,0:T(2,128)(2,1)S(1)} %get-tuple-element.43), channel_id=1, source_target_pairs={{0,2},{1,3},{2,0},{3,1},{4,6},{5,7},{6,4},{7,5},{8,10},{9,11},{10,... | collective-permute-start | bytes 49160 | tf_op jit(solution)/shard_map/ppermute | solution.py:35
  36.1 2.4 %collective-permute-start.14 = (bf16[2,4096]{1,0:T(2,128)(2,1)S(1)}, bf16[2,4096]{1,0:T(2,128)(2,1)S(1)}, u32[]{:S(2)}, u32[]{:S(2)}) collective-permute-start(bf16[2,4096]{1,0:T(2,128)(2,1)S(1)} %get-tuple-element.44), channel_id=1, source_target_pairs={{0,1},{1,0},{2,3},{3,2},{4,5},{5,4},{6,7},{7,6},{8,9},{9,8},{10,11... | collective-permute-start | bytes 49160 | tf_op jit(solution)/shard_map/ppermute | solution.py:35

commit v9 on v8

--- a/solution.py
+++ b/solution.py
@@ -194,6 +194,16 @@
     return copies
 
 
+def start_column_load(source, target, sems, first):
+    copies = []
+    for c in range(target.shape[0]):
+        block = source.at[:, pl.ds(c * HD, HD)]
+        copy = pltpu.make_async_copy(block, target.at[c], sems.at[first + c])
+        copy.start()
+        copies.append(copy)
+    return copies
+
+
 def load_kernel(
     len_hbm, wo_hbm, wk_hbm, wv_hbm, cos_ref, sin_ref, wo, wkv, len_ref, sems
 ):
@@ -201,7 +211,7 @@
     lengths.start()
     copies = start_load(wk_hbm, wkv.at[:, pl.ds(0, HD)], sems, 1, 1)
     copies += start_load(wv_hbm, wkv.at[:, pl.ds(HD, HD)], sems, 2, 1)
-    copies += start_load(wo_hbm.at[pl.ds(0, wo.shape[0])], wo, sems, 3, 6)
+    copies += start_column_load(wo_hbm.at[pl.ds(0, wo.shape[1])], wo, sems, 3)
     lengths.wait()
     angles(len_ref, cos_ref, sin_ref)
     for copy in copies:
@@ -213,8 +223,7 @@
 
 
 def query_kernel(first, far, b0, b1, b2, b3, w, wo_hbm, out_ref, wo, acc, sems):
-    rows = wo.shape[0]
-    copies = start_load(wo_hbm.at[pl.ds(first, rows)], wo, sems, 0, 2)
+    copies = start_column_load(wo_hbm.at[pl.ds(first, wo.shape[1])], wo, sems, 0)
     lhs = jnp.concatenate([b[...].astype(F32) for b in (b0, b1, b2, b3)], axis=0).astype(BF16)
     acc[...] = jnp.dot(lhs, w[...], preferred_element_type=F32)
     for r in range(acc.shape[0]):
@@ -293,11 +302,13 @@
     for s, a in enumerate((a0, a1, a2, a3)):
         blocks[s ^ tag] = a[...].astype(F32)
     lhs = jnp.concatenate([blocks[k] for k in range(4)], axis=0).astype(BF16)
+    acc = None
     first = 0
-    acc = jnp.zeros((lhs.shape[0], w0.shape[1]), F32)
     for w in (w0, w1):
-        last = first + w.shape[0]
-        acc += jnp.dot(lhs[:, first:last], w[...], preferred_element_type=F32)
+        last = first + w.shape[1]
+        columns = jnp.concatenate([w[c] for c in range(w.shape[0])], axis=1)
+        part = jnp.dot(lhs[:, first:last], columns, preferred_element_type=F32)
+        acc = part if acc is None else acc + part
         first = last
     o0[...] = acc[0:2]
     o1[...] = acc[2:4].astype(BF16)
@@ -325,12 +336,12 @@
         load_kernel,
         out_shape=[pltpu.VMEM((PAY, HD), F32)] * 2
         + [
-            pltpu.VMEM((query_cols - quarter, width), BF16),
+            pltpu.VMEM((width // HD, query_cols - quarter, HD), BF16),
             pltpu.VMEM((depth, 2 * HD), BF16),
         ],
         in_specs=[whole(pltpu.HBM)] * 4,
         out_specs=[whole()] * 4,
-        scratch_shapes=[pltpu.SMEM(cache_len.shape, jnp.int32), semaphores((9,))],
+        scratch_shapes=[pltpu.SMEM(cache_len.shape, jnp.int32), semaphores((3 + width // HD,))],
         compiler_params=params(4),
         cost_estimate=cost(1000, 2 * depth * query_cols),
         name="load",
@@ -353,11 +364,11 @@
         functools.partial(query_kernel, query_cols - quarter),
         out_shape=[
             pltpu.VMEM((4 * ROWS_DEV, heads, HD), F32),
-            pltpu.VMEM((quarter, width), BF16),
+            pltpu.VMEM((width // HD, quarter, HD), BF16),
         ],
         in_specs=[whole(pl.ANY)] + [whole()] * 5 + [whole(pltpu.HBM)],
         out_specs=[whole()] * 2,
-        scratch_shapes=[pltpu.VMEM((4 * ROWS_DEV, query_cols), F32), semaphores((2,))],
+        scratch_shapes=[pltpu.VMEM((4 * ROWS_DEV, query_cols), F32), semaphores((width // HD,))],
         compiler_params=params(4),
         cost_estimate=cost(2 * 8 * depth * query_cols, 4 * depth * HD),
         name="query",

time: 39.2 us -> 40.6 us (1.036)
  Pallas kernels: 13 us -> 14.2 us
  starting transfers between devices: 16 us -> 16.5 us
    pallas_call x1, Pallas kernels: 2.33 us -> 3.04 us  [per_device(): pl.pallas_call(functools.partial(query_kernel, query_cols - quarter), out...]
    ppermute x15, starting transfers between devices: 16 us -> 16.5 us  [swap(): return lax.ppermute(x, axis, [(i, i ^ k) for i in range(n)])]
    pallas_call x1, Pallas kernels: 5.35 us -> 5.84 us  [per_device(): pl.pallas_call(load_kernel, out_shape=[pltpu.VMEM((PAY, HD), F32)] * 2 +...]
  transfers between devices with their start and end apart: 15 -> 15, of which waited for: 7 -> 8; matrix products, arithmetic and copies ran while one was open for 3% -> 3% of each run, Pallas kernels for 21% -> 23%
where the time goes in v9:
time: 40.6 us; the launch traced here: 40.5 us
  starting transfers between devices  16.5 us (41%)
  Pallas kernels  14.2 us (35%)
  waiting for transfers between devices  7.14 us (18%)
  local copies, waits for them, and re-layouts  1.23 us (3%)
  between operations  0.78 us (2%)
  other arithmetic  0.64 us (2%)
    ppermute x15, starting transfers between devices, swap(): return lax.ppermute(x, axis, [(i, i ^ k) for i in range(n)])  16.5 us
    ppermute x15, waiting for transfers between devices, swap(): return lax.ppermute(x, axis, [(i, i ^ k) for i in range(n)])  7.14 us
    pallas_call x1, Pallas kernels, per_device(): pl.pallas_call(load_kernel, out_shape=[pltpu.VMEM((PAY, HD), F32)] * 2 +...  5.84 us
    pallas_call x1, Pallas kernels, per_device(): pl.pallas_call(functools.partial(query_kernel, query_cols - quarter), out...  3.04 us
    pallas_call x1, Pallas kernels, per_device(): pl.pallas_call(out_kernel, out_shape=[shape((ROWS_DEV, width), F32)] + [s...  2.28 us
    pallas_call x1, Pallas kernels, per_device(): pl.pallas_call(attend_kernel, out_shape=[pltpu.VMEM((LC, HD), BF16)] * 2...  1.43 us
    unnamed x14, local copies, waits for them, and re-layouts  1.23 us
    pallas_call x1, Pallas kernels, per_device(): pl.pallas_call(payload_kernel, out_shape=[shape((PAY, HD), F32)] + [shape...  1.11 us
  transfers between devices with their start and end apart: 15, of which 8 were waited for; matrix products, arithmetic and copies ran while one was open for 3% of the time, Pallas kernels for 23%

profile of v9, /device:TPU:0, one launch (start us, length us, event | category | flops | bytes accessed | tf_op | source)
XLA Modules:
  0.0 40.5 jit_solution(10193372229890390260)
XLA Ops:
  0.7 3.0 %collective-permute-start = (bf16[40,4096]{1,0:T(8,128)(2,1)}, bf16[40,4096]{1,0:T(8,128)(2,1)S(1)}, u32[]{:S(2)}, u32[]{:S(2)}) collective-permute-start(bf16[40,4096]{1,0:T(8,128)(2,1)} %s.1), channel_id=1, source_target_pairs={{0,2},{1,3},{2,0},{3,1},{4,6},{5,7},{6,4},{7,5},{8,10},{9,11},{10,... | collective-permute-start | bytes 983048 | tf_op jit(solution)/shard_map/ppermute | solution.py:35
  3.7 1.2 %collective-permute-start.2 = (bf16[2,4096]{1,0:T(2,128)(2,1)}, bf16[2,4096]{1,0:T(2,128)(2,1)S(1)}, u32[]{:S(2)}, u32[]{:S(2)}) collective-permute-start(bf16[2,4096]{1,0:T(2,128)(2,1)} %b0.3), channel_id=1, source_target_pairs={{0,2},{1,3},{2,0},{3,1},{4,6},{5,7},{6,4},{7,5},{8,10},{9,11},{10,... | collective-permute-start | bytes 49160 | tf_op jit(solution)/shard_map/ppermute | solution.py:35
  4.9 0.7 %collective-permute-start.1 = (bf16[2,4096]{1,0:T(2,128)(2,1)}, bf16[2,4096]{1,0:T(2,128)(2,1)S(1)}, u32[]{:S(2)}, u32[]{:S(2)}) collective-permute-start(bf16[2,4096]{1,0:T(2,128)(2,1)} %b0.3), channel_id=1, source_target_pairs={{0,1},{1,0},{2,3},{3,2},{4,5},{5,4},{6,7},{7,6},{8,9},{9,8},{10,11... | collective-permute-start | bytes 49160 | tf_op jit(solution)/shard_map/ppermute | solution.py:35
  5.5 0.0 collective-permute-start.4
  5.5 5.8 %load.1 = (f32[128,128]{1,0:T(8,128)S(1)}, f32[128,128]{1,0:T(8,128)S(1)}, bf16[32,1536,128]{2,1,0:T(8,128)(2,1)S(1)}, bf16[4096,256]{1,0:T(8,128)(2,1)S(1)}) custom-call(s32[2]{0:T(128)} %len_ref.1, bf16[2048,4096]{1,0:T(8,128)(2,1)} %wo_hbm.3, bf16[4096,128]{1,0:T(8,128)(2,1)} %wk_hbm.1, bf16[4096,128]{1,0:T(8,128)(2,1)} %wv_hbm.1), custom_call_target="tpu_custom_call" | custom-call | flops 1000 | bytes 16777216 | tf_op jit(solution)/shard_map/load/pallas_call | solution.py:335
  11.4 0.5 %own.1 = f32[40,256]{1,0:T(8,128)S(1)} custom-call(bf16[40,4096]{1,0:T(8,128)(2,1)S(1)} %copy-done.2, bf16[4096,256]{1,0:T(8,128)(2,1)S(1)} %get-tuple-element.25.wkv), custom_call_target="tpu_custom_call" | custom-call | flops 83886080 | bytes 2097152 | tf_op jit(solution)/shard_map/own/pallas_call | solution.py:351
  11.9 0.0 copy-start.5
  11.9 0.0 copy-start.1
  11.9 0.0 copy-start.4
  11.9 0.4 collective-permute-done.2.b2
  12.3 0.2 collective-permute-start.5
  12.5 3.0 %query.1 = (f32[8,16,128]{2,1,0:T(8,128)S(1)}, bf16[32,512,128]{2,1,0:T(8,128)(2,1)S(1)}) custom-call(bf16[40,4096]{1,0:T(8,128)(2,1)S(1)} %collective-permute-done.far.s2, bf16[2,4096]{1,0:T(2,128)(2,1)S(1)} %copy-done.3, bf16[2,4096]{1,0:T(2,128)(2,1)S(1)} %collective-permute-done.1.b1, bf16[2,4096]{1,0:T(2,128)(2,1)S(1)} %collective-permute-done.2.b2, ...), custom_call_target="tpu_custom_call" | custom-call | flops 134217728 | bytes 2097152 | tf_op jit(solution)/shard_map/query/pallas_call | solution.py:363
  15.6 1.1 %payload.1 = (f32[128,128]{1,0:T(8,128)S(1)}, bf16[128,128]{1,0:T(8,128)(2,1)S(1)}, bf16[128,128]{1,0:T(8,128)(2,1)S(1)}, bf16[128,128]{1,0:T(8,128)(2,1)S(1)}) custom-call(s32[4]{0:T(128)S(1)} %copy-done.5, f32[40,256]{1,0:T(8,128)S(1)} %own.1, bf16[40,4096]{1,0:T(8,128)(2,1)S(1)} %collective-permute-done.4.s1, ...), custom_call_target="tpu_custom_call" | custom-call | flops 436207616 | bytes 2097152 | tf_op jit(solution)/shard_map/payload/pallas_call | solution.py:376
  16.7 4.4 %collective-permute-start.6 = (bf16[128,128]{1,0:T(8,128)(2,1)S(1)}, bf16[128,128]{1,0:T(8,128)(2,1)S(1)}, u32[]{:S(2)}, u32[]{:S(2)}) collective-permute-start(bf16[128,128]{1,0:T(8,128)(2,1)S(1)} %get-tuple-element.33), channel_id=1, source_target_pairs={{0,12},{4,8},{8,4},{12,0},{1,13},{5,9},{9,5},{13,1},{2,14},{6,10},... | collective-permute-start | bytes 98312 | tf_op jit(solution)/shard_map/ppermute | solution.py:35
  21.2 0.6 %collective-permute-start.8 = (bf16[128,128]{1,0:T(8,128)(2,1)S(1)}, bf16[128,128]{1,0:T(8,128)(2,1)S(1)}, u32[]{:S(2)}, u32[]{:S(2)}) collective-permute-start(bf16[128,128]{1,0:T(8,128)(2,1)S(1)} %get-tuple-element.35), channel_id=1, source_target_pairs={{0,4},{4,0},{8,12},{12,8},{1,5},{5,1},{9,13},{13,9},{2,6},{6,2},{1... | collective-permute-start | bytes 98312 | tf_op jit(solution)/shard_map/ppermute | solution.py:35
  21.8 1.3 %collective-permute-done.6.p1 = bf16[128,128]{1,0:T(8,128)(2,1)S(1)} collective-permute-done((bf16[128,128]{1,0:T(8,128)(2,1)S(1)}, bf16[128,128]{1,0:T(8,128)(2,1)S(1)}, u32[]{:S(2)}, u32[]{:S(2)}) %collective-permute-start.6) | collective-permute-done | bytes 32800 | tf_op jit(solution)/shard_map/ppermute | solution.py:35
  23.1 2.9 %collective-permute-done.7.p2 = bf16[128,128]{1,0:T(8,128)(2,1)S(1)} collective-permute-done((bf16[128,128]{1,0:T(8,128)(2,1)S(1)}, bf16[128,128]{1,0:T(8,128)(2,1)S(1)}, u32[]{:S(2)}, u32[]{:S(2)}) %collective-permute-start.7) | collective-permute-done | bytes 32800 | tf_op jit(solution)/shard_map/ppermute | solution.py:35
  26.0 1.4 %attend.1 = (bf16[40,128]{1,0:T(8,128)(2,1)S(1)}, bf16[40,128]{1,0:T(8,128)(2,1)S(1)}, bf16[2,2048]{1,0:T(2,128)(2,1)S(1)}) custom-call(s32[2]{0:T(128)S(1)} %copy-done.4, f32[128,128]{1,0:T(8,128)S(1)} %get-tuple-element.32.p0, bf16[128,128]{1,0:T(8,128)(2,1)S(1)} %collective-permute-done.6.p1, bf16[128,128]{1,0:T(8,128)(2,1)S(1)} %collective-permute-done.7.p2, ...), custom_call_target="tpu_custom_call" | custom-call | flops 10000000 | bytes 1000000 | tf_op jit(solution)/shard_map/attend/pallas_call | solution.py:390
  27.4 1.5 %collective-permute-start.11 = (bf16[2,2048]{1,0:T(2,128)(2,1)S(1)}, bf16[2,2048]{1,0:T(2,128)(2,1)S(1)}, u32[]{:S(2)}, u32[]{:S(2)}) collective-permute-start(bf16[2,2048]{1,0:T(2,128)(2,1)S(1)} %get-tuple-element.38.a0), channel_id=1, source_target_pairs={{0,12},{4,8},{8,4},{12,0},{1,13},{5,9},{9,5},{13,1},{2,14},{6,10},... | collective-permute-start | bytes 24584 | tf_op jit(solution)/shard_map/ppermute | solution.py:35
  28.9 0.6 %collective-permute-start.10 = (bf16[2,2048]{1,0:T(2,128)(2,1)S(1)}, bf16[2,2048]{1,0:T(2,128)(2,1)S(1)}, u32[]{:S(2)}, u32[]{:S(2)}) collective-permute-start(bf16[2,2048]{1,0:T(2,128)(2,1)S(1)} %get-tuple-element.38.a0), channel_id=1, source_target_pairs={{0,8},{4,12},{8,0},{12,4},{1,9},{5,13},{9,1},{13,5},{2,10},{6,14},... | collective-permute-start | bytes 24584 | tf_op jit(solution)/shard_map/ppermute | solution.py:35
  29.6 2.3 %collective-permute-start.9 = (bf16[2,2048]{1,0:T(2,128)(2,1)S(1)}, bf16[2,2048]{1,0:T(2,128)(2,1)S(1)}, u32[]{:S(2)}, u32[]{:S(2)}) collective-permute-start(bf16[2,2048]{1,0:T(2,128)(2,1)S(1)} %get-tuple-element.38.a0), channel_id=1, source_target_pairs={{0,4},{4,0},{8,12},{12,8},{1,5},{5,1},{9,13},{13,9},{2,6},{6,2},{1... | collective-permute-start | bytes 24584 | tf_op jit(solution)/shard_map/ppermute | solution.py:35
  31.9 1.1 %collective-permute-done.11.a3 = bf16[2,2048]{1,0:T(2,128)(2,1)S(1)} collective-permute-done((bf16[2,2048]{1,0:T(2,128)(2,1)S(1)}, bf16[2,2048]{1,0:T(2,128)(2,1)S(1)}, u32[]{:S(2)}, u32[]{:S(2)}) %collective-permute-start.11) | collective-permute-done | bytes 8224 | tf_op jit(solution)/shard_map/ppermute | solution.py:35
  32.9 0.6 %collective-permute-done.10.a2 = bf16[2,2048]{1,0:T(2,128)(2,1)S(1)} collective-permute-done((bf16[2,2048]{1,0:T(2,128)(2,1)S(1)}, bf16[2,2048]{1,0:T(2,128)(2,1)S(1)}, u32[]{:S(2)}, u32[]{:S(2)}) %collective-permute-start.10) | collective-permute-done | bytes 8224 | tf_op jit(solution)/shard_map/ppermute | solution.py:35
  33.5 0.1 collective-permute-done.9.a1
  33.6 2.3 %project.1 = (f32[2,4096]{1,0:T(2,128)S(1)}, bf16[2,4096]{1,0:T(2,128)(2,1)S(1)}, bf16[2,4096]{1,0:T(2,128)(2,1)S(1)}, bf16[2,4096]{1,0:T(2,128)(2,1)S(1)}) custom-call(bf16[2,2048]{1,0:T(2,128)(2,1)S(1)} %get-tuple-element.38.a0, bf16[2,2048]{1,0:T(2,128)(2,1)S(1)} %collective-permute-done.9.a1, bf16[2,2048]{1,0:T(2,128)(2,1)S(1)} %collective-permute-done.10.a2, ...), custom_call_target="tpu_custom_call" | custom-call | flops 134217728 | bytes 16777216 | tf_op jit(solution)/shard_map/project/pallas_call | solution.py:401
  35.9 1.0 %collective-permute-start.13 = (bf16[2,4096]{1,0:T(2,128)(2,1)S(1)}, bf16[2,4096]{1,0:T(2,128)(2,1)S(1)}, u32[]{:S(2)}, u32[]{:S(2)}) collective-permute-start(bf16[2,4096]{1,0:T(2,128)(2,1)S(1)} %get-tuple-element.43), channel_id=1, source_target_pairs={{0,2},{1,3},{2,0},{3,1},{4,6},{5,7},{6,4},{7,5},{8,10},{9,11},{10,... | collective-permute-start | bytes 49160 | tf_op jit(solution)/shard_map/ppermute | solution.py:35
  36.8 0.9 %collective-permute-start.14 = (bf16[2,4096]{1,0:T(2,128)(2,1)S(1)}, bf16[2,4096]{1,0:T(2,128)(2,1)S(1)}, u32[]{:S(2)}, u32[]{:S(2)}) collective-permute-start(bf16[2,4096]{1,0:T(2,128)(2,1)S(1)} %get-tuple-element.44), channel_id=1, source_target_pairs={{0,1},{1,0},{2,3},{3,2},{4,5},{5,4},{6,7},{7,6},{8,9},{9,8},{10,11... | collective-permute-start | bytes 49160 | tf_op jit(solution)/shard_map/ppermute | solution.py:35
  37.7 0.6 %copy.12 = bf16[1,40,128]{2,1,0:T(8,128)(2,1)} copy(bf16[1,40,128]{2,1,0:T(8,128)(2,1)S(1)} %bitcast.3) | data formatting | bytes 20480
  38.3 0.6 %copy.13 = bf16[1,40,128]{2,1,0:T(8,128)(2,1)} copy(bf16[1,40,128]{2,1,0:T(8,128)(2,1)S(1)} %bitcast.2) | data formatting | bytes 20480
  38.9 0.1 collective-permute-done.12
  39.0 0.8 %collective-permute-done.13 = bf16[2,4096]{1,0:T(2,128)(2,1)S(1)} collective-permute-done((bf16[2,4096]{1,0:T(2,128)(2,1)S(1)}, bf16[2,4096]{1,0:T(2,128)(2,1)S(1)}, u32[]{:S(2)}, u32[]{:S(2)}) %collective-permute-start.13) | collective-permute-done | bytes 16416 | tf_op jit(solution)/shard_map/ppermute | solution.py:35
  39.8 0.6 %add_convert_fusion = bf16[2,4096]{1,0:T(2,128)(2,1)} fusion(bf16[2,4096]{1,0:T(2,128)(2,1)S(1)} %collective-permute-done.14, bf16[2,4096]{1,0:T(2,128)(2,1)S(1)} %collective-permute-done.13, f32[2,4096]{1,0:T(2,128)S(1)} %get-tuple-element.41, bf16[2,4096]{1,0:T(2,128)(2,1)S(1)} %collective-permute-done.12), kind=kLoop, calls=%fused_computation | loop fusion | flops 57344 | bytes 98304 | tf_op jit(solution)/shard_map/convert_element_type | solution.py:413
  (19 shorter events, 0.0 us)
Async XLA Ops:
  0.6 10.8 %copy-start.2 = (bf16[40,4096]{1,0:T(8,128)(2,1)S(1)}, bf16[40,4096]{1,0:T(8,128)(2,1)}, u32[]{:S(2)}) copy-start(bf16[40,4096]{1,0:T(8,128)(2,1)} %s.1) | copy-start | bytes 983044
  0.6 11.9 %copy-start.3 = (bf16[2,4096]{1,0:T(2,128)(2,1)S(1)}, bf16[2,4096]{1,0:T(2,128)(2,1)}, u32[]{:S(2)}) copy-start(bf16[2,4096]{1,0:T(2,128)(2,1)} %b0.3) | copy-start | bytes 49156
  0.7 11.9 %copy-start = (bf16[4096,2048]{1,0:T(8,128)(2,1)S(1)}, bf16[4096,2048]{1,0:T(8,128)(2,1)}, u32[]{:S(2)}) copy-start(bf16[4096,2048]{1,0:T(8,128)(2,1)} %w.1) | copy-start | bytes 50331652
  0.7 11.6 %collective-permute-start = (bf16[40,4096]{1,0:T(8,128)(2,1)}, bf16[40,4096]{1,0:T(8,128)(2,1)S(1)}, u32[]{:S(2)}, u32[]{:S(2)}) collective-permute-start(bf16[40,4096]{1,0:T(8,128)(2,1)} %s.1), channel_id=1, source_target_pairs={{0,2},{1,3},{2,0},{3,1},{4,6},{5,7},{6,4},{7,5},{8,10},{9,11},{10,... | collective-permute-start | bytes 983048 | tf_op jit(solution)/shard_map/ppermute | solution.py:35
  3.7 8.3 %collective-permute-start.3 = (bf16[2,4096]{1,0:T(2,128)(2,1)}, bf16[2,4096]{1,0:T(2,128)(2,1)S(1)}, u32[]{:S(2)}, u32[]{:S(2)}) collective-permute-start(bf16[2,4096]{1,0:T(2,128)(2,1)} %b0.3), channel_id=1, source_target_pairs={{0,3},{1,2},{2,1},{3,0},{4,7},{5,6},{6,5},{7,4},{8,11},{9,10},{10,... | collective-permute-start | bytes 49160 | tf_op jit(solution)/shard_map/ppermute | solution.py:35
  3.7 8.6 %collective-permute-start.2 = (bf16[2,4096]{1,0:T(2,128)(2,1)}, bf16[2,4096]{1,0:T(2,128)(2,1)S(1)}, u32[]{:S(2)}, u32[]{:S(2)}) collective-permute-start(bf16[2,4096]{1,0:T(2,128)(2,1)} %b0.3), channel_id=1, source_target_pairs={{0,2},{1,3},{2,0},{3,1},{4,6},{5,7},{6,4},{7,5},{8,10},{9,11},{10,... | collective-permute-start | bytes 49160 | tf_op jit(solution)/shard_map/ppermute | solution.py:35
  4.9 7.4 %collective-permute-start.1 = (bf16[2,4096]{1,0:T(2,128)(2,1)}, bf16[2,4096]{1,0:T(2,128)(2,1)S(1)}, u32[]{:S(2)}, u32[]{:S(2)}) collective-permute-start(bf16[2,4096]{1,0:T(2,128)(2,1)} %b0.3), channel_id=1, source_target_pairs={{0,1},{1,0},{2,3},{3,2},{4,5},{5,4},{6,7},{7,6},{8,9},{9,8},{10,11... | collective-permute-start | bytes 49160 | tf_op jit(solution)/shard_map/ppermute | solution.py:35
  5.5 10.1 %collective-permute-start.4 = (bf16[40,4096]{1,0:T(8,128)(2,1)}, bf16[40,4096]{1,0:T(8,128)(2,1)S(1)}, u32[]{:S(2)}, u32[]{:S(2)}) collective-permute-start(bf16[40,4096]{1,0:T(8,128)(2,1)} %s.1), channel_id=1, source_target_pairs={{0,1},{1,0},{2,3},{3,2},{4,5},{5,4},{6,7},{7,6},{8,9},{9,8},{10,11... | collective-permute-start | bytes 983048 | tf_op jit(solution)/shard_map/ppermute | solution.py:35
  11.9 3.7 %copy-start.5 = (s32[4]{0:T(128)S(1)}, s32[4]{0:T(128)}, u32[]{:S(2)}) copy-start(s32[4]{0:T(128)} %owner_ref.1) | copy-start | bytes 52
  11.9 14.1 %copy-start.1 = (bf16[2,2,512,128]{3,2,1,0:T(8,128)(2,1)S(1)}, bf16[2,2,512,128]{3,2,1,0:T(8,128)(2,1)}, u32[]{:S(2)}) copy-start(bf16[2,2,512,128]{3,2,1,0:T(8,128)(2,1)} %kv.1) | copy-start | bytes 1572868
  11.9 14.1 %copy-start.4 = (s32[2]{0:T(128)S(1)}, s32[2]{0:T(128)}, u32[]{:S(2)}) copy-start(s32[2]{0:T(128)} %len_ref.1) | copy-start | bytes 28
  12.3 3.3 %collective-permute-start.5 = (bf16[40,4096]{1,0:T(8,128)(2,1)S(1)}, bf16[40,4096]{1,0:T(8,128)(2,1)S(1)}, u32[]{:S(2)}, u32[]{:S(2)}) collective-permute-start(bf16[40,4096]{1,0:T(8,128)(2,1)S(1)} %collective-permute-done.far.s2), channel_id=1, source_target_pairs={{0,1},{1,0},{2,3},{3,2},{4,5},{5,4},{6,7},{7,6},{8,9},{9,8},{10,11... | collective-permute-start | bytes 983048 | tf_op jit(solution)/shard_map/ppermute | solution.py:35
  16.7 6.4 %collective-permute-start.6 = (bf16[128,128]{1,0:T(8,128)(2,1)S(1)}, bf16[128,128]{1,0:T(8,128)(2,1)S(1)}, u32[]{:S(2)}, u32[]{:S(2)}) collective-permute-start(bf16[128,128]{1,0:T(8,128)(2,1)S(1)} %get-tuple-element.33), channel_id=1, source_target_pairs={{0,12},{4,8},{8,4},{12,0},{1,13},{5,9},{9,5},{13,1},{2,14},{6,10},... | collective-permute-start | bytes 98312 | tf_op jit(solution)/shard_map/ppermute | solution.py:35
  21.2 4.8 %collective-permute-start.7 = (bf16[128,128]{1,0:T(8,128)(2,1)S(1)}, bf16[128,128]{1,0:T(8,128)(2,1)S(1)}, u32[]{:S(2)}, u32[]{:S(2)}) collective-permute-start(bf16[128,128]{1,0:T(8,128)(2,1)S(1)} %get-tuple-element.34), channel_id=1, source_target_pairs={{0,8},{4,12},{8,0},{12,4},{1,9},{5,13},{9,1},{13,5},{2,10},{6,14},... | collective-permute-start | bytes 98312 | tf_op jit(solution)/shard_map/ppermute | solution.py:35
  21.2 4.8 %collective-permute-start.8 = (bf16[128,128]{1,0:T(8,128)(2,1)S(1)}, bf16[128,128]{1,0:T(8,128)(2,1)S(1)}, u32[]{:S(2)}, u32[]{:S(2)}) collective-permute-start(bf16[128,128]{1,0:T(8,128)(2,1)S(1)} %get-tuple-element.35), channel_id=1, source_target_pairs={{0,4},{4,0},{8,12},{12,8},{1,5},{5,1},{9,13},{13,9},{2,6},{6,2},{1... | collective-permute-start | bytes 98312 | tf_op jit(solution)/shard_map/ppermute | solution.py:35
  27.4 5.5 %collective-permute-start.11 = (bf16[2,2048]{1,0:T(2,128)(2,1)S(1)}, bf16[2,2048]{1,0:T(2,128)(2,1)S(1)}, u32[]{:S(2)}, u32[]{:S(2)}) collective-permute-start(bf16[2,2048]{1,0:T(2,128)(2,1)S(1)} %get-tuple-element.38.a0), channel_id=1, source_target_pairs={{0,12},{4,8},{8,4},{12,0},{1,13},{5,9},{9,5},{13,1},{2,14},{6,10},... | collective-permute-start | bytes 24584 | tf_op jit(solution)/shard_map/ppermute | solution.py:35
  28.9 4.6 %collective-permute-start.10 = (bf16[2,2048]{1,0:T(2,128)(2,1)S(1)}, bf16[2,2048]{1,0:T(2,128)(2,1)S(1)}, u32[]{:S(2)}, u32[]{:S(2)}) collective-permute-start(bf16[2,2048]{1,0:T(2,128)(2,1)S(1)} %get-tuple-element.38.a0), channel_id=1, source_target_pairs={{0,8},{4,12},{8,0},{12,4},{1,9},{5,13},{9,1},{13,5},{2,10},{6,14},... | collective-permute-start | bytes 24584 | tf_op jit(solution)/shard_map/ppermute | solution.py:35
  29.6 4.0 %collective-permute-start.9 = (bf16[2,2048]{1,0:T(2,128)(2,1)S(1)}, bf16[2,2048]{1,0:T(2,128)(2,1)S(1)}, u32[]{:S(2)}, u32[]{:S(2)}) collective-permute-start(bf16[2,2048]{1,0:T(2,128)(2,1)S(1)} %get-tuple-element.38.a0), channel_id=1, source_target_pairs={{0,4},{4,0},{8,12},{12,8},{1,5},{5,1},{9,13},{13,9},{2,6},{6,2},{1... | collective-permute-start | bytes 24584 | tf_op jit(solution)/shard_map/ppermute | solution.py:35
  35.9 3.2 %collective-permute-start.12 = (bf16[2,4096]{1,0:T(2,128)(2,1)S(1)}, bf16[2,4096]{1,0:T(2,128)(2,1)S(1)}, u32[]{:S(2)}, u32[]{:S(2)}) collective-permute-start(bf16[2,4096]{1,0:T(2,128)(2,1)S(1)} %get-tuple-element.42), channel_id=1, source_target_pairs={{0,3},{1,2},{2,1},{3,0},{4,7},{5,6},{6,5},{7,4},{8,11},{9,10},{10,... | collective-permute-start | bytes 49160 | tf_op jit(solution)/shard_map/ppermute | solution.py:35
  35.9 4.0 %collective-permute-start.13 = (bf16[2,4096]{1,0:T(2,128)(2,1)S(1)}, bf16[2,4096]{1,0:T(2,128)(2,1)S(1)}, u32[]{:S(2)}, u32[]{:S(2)}) collective-permute-start(bf16[2,4096]{1,0:T(2,128)(2,1)S(1)} %get-tuple-element.43), channel_id=1, source_target_pairs={{0,2},{1,3},{2,0},{3,1},{4,6},{5,7},{6,4},{7,5},{8,10},{9,11},{10,... | collective-permute-start | bytes 49160 | tf_op jit(solution)/shard_map/ppermute | solution.py:35
  36.8 3.0 %collective-permute-start.14 = (bf16[2,4096]{1,0:T(2,128)(2,1)S(1)}, bf16[2,4096]{1,0:T(2,128)(2,1)S(1)}, u32[]{:S(2)}, u32[]{:S(2)}) collective-permute-start(bf16[2,4096]{1,0:T(2,128)(2,1)S(1)} %get-tuple-element.44), channel_id=1, source_target_pairs={{0,1},{1,0},{2,3},{3,2},{4,5},{5,4},{6,7},{7,6},{8,9},{9,8},{10,11... | collective-permute-start | bytes 49160 | tf_op jit(solution)/shard_map/ppermute | solution.py:35

commit v10 on v8

--- a/solution.py
+++ b/solution.py
@@ -225,7 +225,7 @@
 
 
 def payload_kernel(
-    owner_ref, own, s1, s2, s3, b0, b1, b2, b3, wkv, q_ref, o0, o3, o2, o1, x, pay
+    owner_ref, own, s1, s2, s3, b0, b1, b2, b3, wkv, q_ref, o0, o2, o3, o1, x, pay
 ):
     gx, gy = lax.axis_index("gx"), lax.axis_index("gy")
     for k, s in enumerate((s1, s2, s3)):
@@ -305,8 +305,8 @@
     o3[...] = acc[6:8].astype(BF16)
 
 
-def others(blocks, axis):
-    return [swap(b, axis, 3 - k) for k, b in enumerate(blocks)]
+def others(blocks, axis, order):
+    return [swap(b, axis, k) for k, b in zip(order, blocks)]
 
 
 def per_device(stored_rows, new_rows, w_query, w_key, w_value, w_out, kv_cache, cache_len, owner):
@@ -375,7 +375,7 @@
         cost_estimate=cost(2 * 208 * depth * 256, 4 * depth * HD),
         name="payload",
     )(owner, own, near, far, far_near, *fresh, wkv, query)
-    sums = [payload[0]] + others(payload[1:], "gx")
+    sums = [payload[0]] + others(payload[1:], "gx", (2, 3, 1))
     rebuilt_key, rebuilt_value, attn = pl.pallas_call(
         attend_kernel,
         out_shape=[pltpu.VMEM((LC, HD), BF16)] * 2 + [pltpu.VMEM((ROWS_DEV, query_cols), BF16)],
@@ -397,7 +397,7 @@
         cost_estimate=cost(2 * 8 * width * query_cols, 2 * width * query_cols),
         name="project",
     )(*attn_all, wo_first, wo_second)
-    arrived = others(parts[1:], "gy")
+    arrived = others(parts[1:], "gy", (3, 2, 1))
     mixed = parts[0] + arrived[0].astype(F32) + arrived[1].astype(F32) + arrived[2].astype(F32)
     return (mixed.astype(BF16), rebuilt_key[None], rebuilt_value[None])
 

time: 39.2 us -> 39.6 us (1.010)
  waiting for transfers between devices: 7.49 us -> 7.92 us
    ppermute x15, waiting for transfers between devices: 7.49 us -> 7.92 us  [swap(): return lax.ppermute(x, axis, [(i, i ^ k) for i in range(n)])]
where the time goes in v10:
time: 39.6 us; the launch traced here: 39.4 us
  starting transfers between devices  15.9 us (40%)
  Pallas kernels  13 us (33%)
  waiting for transfers between devices  7.92 us (20%)
  local copies, waits for them, and re-layouts  1.23 us (3%)
  between operations  0.8 us (2%)
  other arithmetic  0.64 us (2%)
    ppermute x15, starting transfers between devices, swap(): return lax.ppermute(x, axis, [(i, i ^ k) for i in range(n)])  15.9 us
    ppermute x15, waiting for transfers between devices, swap(): return lax.ppermute(x, axis, [(i, i ^ k) for i in range(n)])  7.92 us
    pallas_call x1, Pallas kernels, per_device(): pl.pallas_call(load_kernel, out_shape=[pltpu.VMEM((PAY, HD), F32)] * 2 +...  5.35 us
    pallas_call x1, Pallas kernels, per_device(): pl.pallas_call(functools.partial(query_kernel, query_cols - quarter), out...  2.33 us
    pallas_call x1, Pallas kernels, per_device(): pl.pallas_call(out_kernel, out_shape=[shape((ROWS_DEV, width), F32)] + [s...  2.28 us
    pallas_call x1, Pallas kernels, per_device(): pl.pallas_call(attend_kernel, out_shape=[pltpu.VMEM((LC, HD), BF16)] * 2...  1.43 us
    unnamed x14, local copies, waits for them, and re-layouts  1.23 us
    pallas_call x1, Pallas kernels, per_device(): pl.pallas_call(payload_kernel, out_shape=[shape((PAY, HD), F32)] + [shape...  1.11 us
  transfers between devices with their start and end apart: 15, of which 7 were waited for; matrix products, arithmetic and copies ran while one was open for 3% of the time, Pallas kernels for 21%

profile of v10, /device:TPU:0, one launch (start us, length us, event | category | flops | bytes accessed | tf_op | source)
XLA Modules:
  0.0 39.4 jit_solution(5869052593306238741)
XLA Ops:
  0.7 3.0 %collective-permute-start = (bf16[40,4096]{1,0:T(8,128)(2,1)}, bf16[40,4096]{1,0:T(8,128)(2,1)S(1)}, u32[]{:S(2)}, u32[]{:S(2)}) collective-permute-start(bf16[40,4096]{1,0:T(8,128)(2,1)} %s.1), channel_id=1, source_target_pairs={{0,2},{1,3},{2,0},{3,1},{4,6},{5,7},{6,4},{7,5},{8,10},{9,11},{10,... | collective-permute-start | bytes 983048 | tf_op jit(solution)/shard_map/ppermute | solution.py:35
  3.7 0.0 collective-permute-start.3
  3.7 1.2 %collective-permute-start.2 = (bf16[2,4096]{1,0:T(2,128)(2,1)}, bf16[2,4096]{1,0:T(2,128)(2,1)S(1)}, u32[]{:S(2)}, u32[]{:S(2)}) collective-permute-start(bf16[2,4096]{1,0:T(2,128)(2,1)} %b0.3), channel_id=1, source_target_pairs={{0,2},{1,3},{2,0},{3,1},{4,6},{5,7},{6,4},{7,5},{8,10},{9,11},{10,... | collective-permute-start | bytes 49160 | tf_op jit(solution)/shard_map/ppermute | solution.py:35
  4.9 0.7 %collective-permute-start.1 = (bf16[2,4096]{1,0:T(2,128)(2,1)}, bf16[2,4096]{1,0:T(2,128)(2,1)S(1)}, u32[]{:S(2)}, u32[]{:S(2)}) collective-permute-start(bf16[2,4096]{1,0:T(2,128)(2,1)} %b0.3), channel_id=1, source_target_pairs={{0,1},{1,0},{2,3},{3,2},{4,5},{5,4},{6,7},{7,6},{8,9},{9,8},{10,11... | collective-permute-start | bytes 49160 | tf_op jit(solution)/shard_map/ppermute | solution.py:35
  5.5 0.0 collective-permute-start.4
  5.5 5.3 %load.1 = (f32[128,128]{1,0:T(8,128)S(1)}, f32[128,128]{1,0:T(8,128)S(1)}, bf16[1536,4096]{1,0:T(8,128)(2,1)S(1)}, bf16[4096,256]{1,0:T(8,128)(2,1)S(1)}) custom-call(s32[2]{0:T(128)} %len_ref.1, bf16[2048,4096]{1,0:T(8,128)(2,1)} %wo_hbm.3, bf16[4096,128]{1,0:T(8,128)(2,1)} %wk_hbm.1, bf16[4096,128]{1,0:T(8,128)(2,1)} %wv_hbm.1), custom_call_target="tpu_custom_call" | custom-call | flops 1000 | bytes 16777216 | tf_op jit(solution)/shard_map/load/pallas_call | solution.py:324
  10.9 0.5 %own.1 = f32[40,256]{1,0:T(8,128)S(1)} custom-call(bf16[40,4096]{1,0:T(8,128)(2,1)S(1)} %copy-done.2, bf16[4096,256]{1,0:T(8,128)(2,1)S(1)} %get-tuple-element.25.wkv), custom_call_target="tpu_custom_call" | custom-call | flops 83886080 | bytes 2097152 | tf_op jit(solution)/shard_map/own/pallas_call | solution.py:340
  11.4 0.0 copy-start.5
  11.4 0.0 copy-start.1
  11.4 0.0 copy-start.4
  11.4 0.0 collective-permute-done.3.b3
  11.4 0.9 %collective-permute-done.2.b2 = bf16[2,4096]{1,0:T(2,128)(2,1)S(1)} collective-permute-done((bf16[2,4096]{1,0:T(2,128)(2,1)}, bf16[2,4096]{1,0:T(2,128)(2,1)S(1)}, u32[]{:S(2)}, u32[]{:S(2)}) %collective-permute-start.2) | collective-permute-done | bytes 16416 | tf_op jit(solution)/shard_map/ppermute | solution.py:35
  12.3 2.3 %query.1 = (f32[8,16,128]{2,1,0:T(8,128)S(1)}, bf16[512,4096]{1,0:T(8,128)(2,1)S(1)}) custom-call(bf16[40,4096]{1,0:T(8,128)(2,1)S(1)} %collective-permute-done.far.s2, bf16[2,4096]{1,0:T(2,128)(2,1)S(1)} %copy-done.3, bf16[2,4096]{1,0:T(2,128)(2,1)S(1)} %collective-permute-done.1.b1, bf16[2,4096]{1,0:T(2,128)(2,1)S(1)} %collective-permute-done.2.b2, ...), custom_call_target="tpu_custom_call" | custom-call | flops 134217728 | bytes 2097152 | tf_op jit(solution)/shard_map/query/pallas_call | solution.py:352
  14.7 1.1 %payload.1 = (f32[128,128]{1,0:T(8,128)S(1)}, bf16[128,128]{1,0:T(8,128)(2,1)S(1)}, bf16[128,128]{1,0:T(8,128)(2,1)S(1)}, bf16[128,128]{1,0:T(8,128)(2,1)S(1)}) custom-call(s32[4]{0:T(128)S(1)} %copy-done.5, f32[40,256]{1,0:T(8,128)S(1)} %own.1, bf16[40,4096]{1,0:T(8,128)(2,1)S(1)} %collective-permute-done.4.s1, ...), custom_call_target="tpu_custom_call" | custom-call | flops 436207616 | bytes 2097152 | tf_op jit(solution)/shard_map/payload/pallas_call | solution.py:365
  15.8 3.1 %collective-permute-start.6 = (bf16[128,128]{1,0:T(8,128)(2,1)S(1)}, bf16[128,128]{1,0:T(8,128)(2,1)S(1)}, u32[]{:S(2)}, u32[]{:S(2)}) collective-permute-start(bf16[128,128]{1,0:T(8,128)(2,1)S(1)} %get-tuple-element.33), channel_id=1, source_target_pairs={{0,8},{4,12},{8,0},{12,4},{1,9},{5,13},{9,1},{13,5},{2,10},{6,14},... | collective-permute-start | bytes 98312 | tf_op jit(solution)/shard_map/ppermute | solution.py:35
  18.9 1.3 %collective-permute-start.7 = (bf16[128,128]{1,0:T(8,128)(2,1)S(1)}, bf16[128,128]{1,0:T(8,128)(2,1)S(1)}, u32[]{:S(2)}, u32[]{:S(2)}) collective-permute-start(bf16[128,128]{1,0:T(8,128)(2,1)S(1)} %get-tuple-element.34), channel_id=1, source_target_pairs={{0,12},{4,8},{8,4},{12,0},{1,13},{5,9},{9,5},{13,1},{2,14},{6,10},... | collective-permute-start | bytes 98312 | tf_op jit(solution)/shard_map/ppermute | solution.py:35
  20.3 0.2 collective-permute-start.8
  20.5 0.3 collective-permute-done.6.p1
  20.8 3.8 %collective-permute-done.7.p2 = bf16[128,128]{1,0:T(8,128)(2,1)S(1)} collective-permute-done((bf16[128,128]{1,0:T(8,128)(2,1)S(1)}, bf16[128,128]{1,0:T(8,128)(2,1)S(1)}, u32[]{:S(2)}, u32[]{:S(2)}) %collective-permute-start.7) | collective-permute-done | bytes 32800 | tf_op jit(solution)/shard_map/ppermute | solution.py:35
  24.6 1.4 %attend.1 = (bf16[40,128]{1,0:T(8,128)(2,1)S(1)}, bf16[40,128]{1,0:T(8,128)(2,1)S(1)}, bf16[2,2048]{1,0:T(2,128)(2,1)S(1)}) custom-call(s32[2]{0:T(128)S(1)} %copy-done.4, f32[128,128]{1,0:T(8,128)S(1)} %get-tuple-element.32.p0, bf16[128,128]{1,0:T(8,128)(2,1)S(1)} %collective-permute-done.6.p1, bf16[128,128]{1,0:T(8,128)(2,1)S(1)} %collective-permute-done.7.p2, ...), custom_call_target="tpu_custom_call" | custom-call | flops 10000000 | bytes 1000000 | tf_op jit(solution)/shard_map/attend/pallas_call | solution.py:379
  26.1 2.1 %collective-permute-start.11 = (bf16[2,2048]{1,0:T(2,128)(2,1)S(1)}, bf16[2,2048]{1,0:T(2,128)(2,1)S(1)}, u32[]{:S(2)}, u32[]{:S(2)}) collective-permute-start(bf16[2,2048]{1,0:T(2,128)(2,1)S(1)} %get-tuple-element.38.a0), channel_id=1, source_target_pairs={{0,12},{4,8},{8,4},{12,0},{1,13},{5,9},{9,5},{13,1},{2,14},{6,10},... | collective-permute-start | bytes 24584 | tf_op jit(solution)/shard_map/ppermute | solution.py:35
  28.2 2.4 %collective-permute-start.9 = (bf16[2,2048]{1,0:T(2,128)(2,1)S(1)}, bf16[2,2048]{1,0:T(2,128)(2,1)S(1)}, u32[]{:S(2)}, u32[]{:S(2)}) collective-permute-start(bf16[2,2048]{1,0:T(2,128)(2,1)S(1)} %get-tuple-element.38.a0), channel_id=1, source_target_pairs={{0,4},{4,0},{8,12},{12,8},{1,5},{5,1},{9,13},{13,9},{2,6},{6,2},{1... | collective-permute-start | bytes 24584 | tf_op jit(solution)/shard_map/ppermute | solution.py:35
  30.5 1.1 %collective-permute-done.11.a3 = bf16[2,2048]{1,0:T(2,128)(2,1)S(1)} collective-permute-done((bf16[2,2048]{1,0:T(2,128)(2,1)S(1)}, bf16[2,2048]{1,0:T(2,128)(2,1)S(1)}, u32[]{:S(2)}, u32[]{:S(2)}) %collective-permute-start.11) | collective-permute-done | bytes 8224 | tf_op jit(solution)/shard_map/ppermute | solution.py:35
  31.6 1.1 %collective-permute-done.10.a2 = bf16[2,2048]{1,0:T(2,128)(2,1)S(1)} collective-permute-done((bf16[2,2048]{1,0:T(2,128)(2,1)S(1)}, bf16[2,2048]{1,0:T(2,128)(2,1)S(1)}, u32[]{:S(2)}, u32[]{:S(2)}) %collective-permute-start.10) | collective-permute-done | bytes 8224 | tf_op jit(solution)/shard_map/ppermute | solution.py:35
  32.7 2.3 %project.1 = (f32[2,4096]{1,0:T(2,128)S(1)}, bf16[2,4096]{1,0:T(2,128)(2,1)S(1)}, bf16[2,4096]{1,0:T(2,128)(2,1)S(1)}, bf16[2,4096]{1,0:T(2,128)(2,1)S(1)}) custom-call(bf16[2,2048]{1,0:T(2,128)(2,1)S(1)} %get-tuple-element.38.a0, bf16[2,2048]{1,0:T(2,128)(2,1)S(1)} %collective-permute-done.9.a1, bf16[2,2048]{1,0:T(2,128)(2,1)S(1)} %collective-permute-done.10.a2, ...), custom_call_target="tpu_custom_call" | custom-call | flops 134217728 | bytes 16777216 | tf_op jit(solution)/shard_map/project/pallas_call | solution.py:390
  35.0 1.4 %collective-permute-start.13 = (bf16[2,4096]{1,0:T(2,128)(2,1)S(1)}, bf16[2,4096]{1,0:T(2,128)(2,1)S(1)}, u32[]{:S(2)}, u32[]{:S(2)}) collective-permute-start(bf16[2,4096]{1,0:T(2,128)(2,1)S(1)} %get-tuple-element.43), channel_id=1, source_target_pairs={{0,2},{1,3},{2,0},{3,1},{4,6},{5,7},{6,4},{7,5},{8,10},{9,11},{10,... | collective-permute-start | bytes 49160 | tf_op jit(solution)/shard_map/ppermute | solution.py:35
  36.4 0.5 %collective-permute-start.14 = (bf16[2,4096]{1,0:T(2,128)(2,1)S(1)}, bf16[2,4096]{1,0:T(2,128)(2,1)S(1)}, u32[]{:S(2)}, u32[]{:S(2)}) collective-permute-start(bf16[2,4096]{1,0:T(2,128)(2,1)S(1)} %get-tuple-element.44), channel_id=1, source_target_pairs={{0,1},{1,0},{2,3},{3,2},{4,5},{5,4},{6,7},{7,6},{8,9},{9,8},{10,11... | collective-permute-start | bytes 49160 | tf_op jit(solution)/shard_map/ppermute | solution.py:35
  36.9 0.6 %copy.12 = bf16[1,40,128]{2,1,0:T(8,128)(2,1)} copy(bf16[1,40,128]{2,1,0:T(8,128)(2,1)S(1)} %bitcast.3) | data formatting | bytes 20480
  37.5 0.6 %copy.13 = bf16[1,40,128]{2,1,0:T(8,128)(2,1)} copy(bf16[1,40,128]{2,1,0:T(8,128)(2,1)S(1)} %bitcast.2) | data formatting | bytes 20480
  38.1 0.1 collective-permute-done.12
  38.2 0.6 %collective-permute-done.13 = bf16[2,4096]{1,0:T(2,128)(2,1)S(1)} collective-permute-done((bf16[2,4096]{1,0:T(2,128)(2,1)S(1)}, bf16[2,4096]{1,0:T(2,128)(2,1)S(1)}, u32[]{:S(2)}, u32[]{:S(2)}) %collective-permute-start.13) | collective-permute-done | bytes 16416 | tf_op jit(solution)/shard_map/ppermute | solution.py:35
  38.8 0.6 %add_convert_fusion = bf16[2,4096]{1,0:T(2,128)(2,1)} fusion(bf16[2,4096]{1,0:T(2,128)(2,1)S(1)} %collective-permute-done.14, bf16[2,4096]{1,0:T(2,128)(2,1)S(1)} %collective-permute-done.13, f32[2,4096]{1,0:T(2,128)S(1)} %get-tuple-element.41, bf16[2,4096]{1,0:T(2,128)(2,1)S(1)} %collective-permute-done.12), kind=kLoop, calls=%fused_computation | loop fusion | flops 57344 | bytes 98304 | tf_op jit(solution)/shard_map/convert_element_type | solution.py:402
  (19 shorter events, 0.0 us)
Async XLA Ops:
  0.6 10.3 %copy-start.2 = (bf16[40,4096]{1,0:T(8,128)(2,1)S(1)}, bf16[40,4096]{1,0:T(8,128)(2,1)}, u32[]{:S(2)}) copy-start(bf16[40,4096]{1,0:T(8,128)(2,1)} %s.1) | copy-start | bytes 983044
  0.6 11.7 %copy-start.3 = (bf16[2,4096]{1,0:T(2,128)(2,1)S(1)}, bf16[2,4096]{1,0:T(2,128)(2,1)}, u32[]{:S(2)}) copy-start(bf16[2,4096]{1,0:T(2,128)(2,1)} %b0.3) | copy-start | bytes 49156
  0.7 11.7 %copy-start = (bf16[4096,2048]{1,0:T(8,128)(2,1)S(1)}, bf16[4096,2048]{1,0:T(8,128)(2,1)}, u32[]{:S(2)}) copy-start(bf16[4096,2048]{1,0:T(8,128)(2,1)} %w.1) | copy-start | bytes 50331652
  0.7 11.6 %collective-permute-start = (bf16[40,4096]{1,0:T(8,128)(2,1)}, bf16[40,4096]{1,0:T(8,128)(2,1)S(1)}, u32[]{:S(2)}, u32[]{:S(2)}) collective-permute-start(bf16[40,4096]{1,0:T(8,128)(2,1)} %s.1), channel_id=1, source_target_pairs={{0,2},{1,3},{2,0},{3,1},{4,6},{5,7},{6,4},{7,5},{8,10},{9,11},{10,... | collective-permute-start | bytes 983048 | tf_op jit(solution)/shard_map/ppermute | solution.py:35
  3.7 7.8 %collective-permute-start.3 = (bf16[2,4096]{1,0:T(2,128)(2,1)}, bf16[2,4096]{1,0:T(2,128)(2,1)S(1)}, u32[]{:S(2)}, u32[]{:S(2)}) collective-permute-start(bf16[2,4096]{1,0:T(2,128)(2,1)} %b0.3), channel_id=1, source_target_pairs={{0,3},{1,2},{2,1},{3,0},{4,7},{5,6},{6,5},{7,4},{8,11},{9,10},{10,... | collective-permute-start | bytes 49160 | tf_op jit(solution)/shard_map/ppermute | solution.py:35
  3.7 8.6 %collective-permute-start.2 = (bf16[2,4096]{1,0:T(2,128)(2,1)}, bf16[2,4096]{1,0:T(2,128)(2,1)S(1)}, u32[]{:S(2)}, u32[]{:S(2)}) collective-permute-start(bf16[2,4096]{1,0:T(2,128)(2,1)} %b0.3), channel_id=1, source_target_pairs={{0,2},{1,3},{2,0},{3,1},{4,6},{5,7},{6,4},{7,5},{8,10},{9,11},{10,... | collective-permute-start | bytes 49160 | tf_op jit(solution)/shard_map/ppermute | solution.py:35
  4.9 7.4 %collective-permute-start.1 = (bf16[2,4096]{1,0:T(2,128)(2,1)}, bf16[2,4096]{1,0:T(2,128)(2,1)S(1)}, u32[]{:S(2)}, u32[]{:S(2)}) collective-permute-start(bf16[2,4096]{1,0:T(2,128)(2,1)} %b0.3), channel_id=1, source_target_pairs={{0,1},{1,0},{2,3},{3,2},{4,5},{5,4},{6,7},{7,6},{8,9},{9,8},{10,11... | collective-permute-start | bytes 49160 | tf_op jit(solution)/shard_map/ppermute | solution.py:35
  5.5 9.1 %collective-permute-start.4 = (bf16[40,4096]{1,0:T(8,128)(2,1)}, bf16[40,4096]{1,0:T(8,128)(2,1)S(1)}, u32[]{:S(2)}, u32[]{:S(2)}) collective-permute-start(bf16[40,4096]{1,0:T(8,128)(2,1)} %s.1), channel_id=1, source_target_pairs={{0,1},{1,0},{2,3},{3,2},{4,5},{5,4},{6,7},{7,6},{8,9},{9,8},{10,11... | collective-permute-start | bytes 983048 | tf_op jit(solution)/shard_map/ppermute | solution.py:35
  11.4 3.3 %copy-start.5 = (s32[4]{0:T(128)S(1)}, s32[4]{0:T(128)}, u32[]{:S(2)}) copy-start(s32[4]{0:T(128)} %owner_ref.1) | copy-start | bytes 52
  11.4 13.2 %copy-start.1 = (bf16[2,2,512,128]{3,2,1,0:T(8,128)(2,1)S(1)}, bf16[2,2,512,128]{3,2,1,0:T(8,128)(2,1)}, u32[]{:S(2)}) copy-start(bf16[2,2,512,128]{3,2,1,0:T(8,128)(2,1)} %kv.1) | copy-start | bytes 1572868
  11.4 13.2 %copy-start.4 = (s32[2]{0:T(128)S(1)}, s32[2]{0:T(128)}, u32[]{:S(2)}) copy-start(s32[2]{0:T(128)} %len_ref.1) | copy-start | bytes 28
  12.3 2.4 %collective-permute-start.5 = (bf16[40,4096]{1,0:T(8,128)(2,1)S(1)}, bf16[40,4096]{1,0:T(8,128)(2,1)S(1)}, u32[]{:S(2)}, u32[]{:S(2)}) collective-permute-start(bf16[40,4096]{1,0:T(8,128)(2,1)S(1)} %collective-permute-done.far.s2), channel_id=1, source_target_pairs={{0,1},{1,0},{2,3},{3,2},{4,5},{5,4},{6,7},{7,6},{8,9},{9,8},{10,11... | collective-permute-start | bytes 983048 | tf_op jit(solution)/shard_map/ppermute | solution.py:35
  15.8 5.0 %collective-permute-start.6 = (bf16[128,128]{1,0:T(8,128)(2,1)S(1)}, bf16[128,128]{1,0:T(8,128)(2,1)S(1)}, u32[]{:S(2)}, u32[]{:S(2)}) collective-permute-start(bf16[128,128]{1,0:T(8,128)(2,1)S(1)} %get-tuple-element.33), channel_id=1, source_target_pairs={{0,8},{4,12},{8,0},{12,4},{1,9},{5,13},{9,1},{13,5},{2,10},{6,14},... | collective-permute-start | bytes 98312 | tf_op jit(solution)/shard_map/ppermute | solution.py:35
  18.9 5.7 %collective-permute-start.7 = (bf16[128,128]{1,0:T(8,128)(2,1)S(1)}, bf16[128,128]{1,0:T(8,128)(2,1)S(1)}, u32[]{:S(2)}, u32[]{:S(2)}) collective-permute-start(bf16[128,128]{1,0:T(8,128)(2,1)S(1)} %get-tuple-element.34), channel_id=1, source_target_pairs={{0,12},{4,8},{8,4},{12,0},{1,13},{5,9},{9,5},{13,1},{2,14},{6,10},... | collective-permute-start | bytes 98312 | tf_op jit(solution)/shard_map/ppermute | solution.py:35
  20.3 4.4 %collective-permute-start.8 = (bf16[128,128]{1,0:T(8,128)(2,1)S(1)}, bf16[128,128]{1,0:T(8,128)(2,1)S(1)}, u32[]{:S(2)}, u32[]{:S(2)}) collective-permute-start(bf16[128,128]{1,0:T(8,128)(2,1)S(1)} %get-tuple-element.35), channel_id=1, source_target_pairs={{0,4},{4,0},{8,12},{12,8},{1,5},{5,1},{9,13},{13,9},{2,6},{6,2},{1... | collective-permute-start | bytes 98312 | tf_op jit(solution)/shard_map/ppermute | solution.py:35
  26.1 5.5 %collective-permute-start.11 = (bf16[2,2048]{1,0:T(2,128)(2,1)S(1)}, bf16[2,2048]{1,0:T(2,128)(2,1)S(1)}, u32[]{:S(2)}, u32[]{:S(2)}) collective-permute-start(bf16[2,2048]{1,0:T(2,128)(2,1)S(1)} %get-tuple-element.38.a0), channel_id=1, source_target_pairs={{0,12},{4,8},{8,4},{12,0},{1,13},{5,9},{9,5},{13,1},{2,14},{6,10},... | collective-permute-start | bytes 24584 | tf_op jit(solution)/shard_map/ppermute | solution.py:35
  28.2 4.5 %collective-permute-start.10 = (bf16[2,2048]{1,0:T(2,128)(2,1)S(1)}, bf16[2,2048]{1,0:T(2,128)(2,1)S(1)}, u32[]{:S(2)}, u32[]{:S(2)}) collective-permute-start(bf16[2,2048]{1,0:T(2,128)(2,1)S(1)} %get-tuple-element.38.a0), channel_id=1, source_target_pairs={{0,8},{4,12},{8,0},{12,4},{1,9},{5,13},{9,1},{13,5},{2,10},{6,14},... | collective-permute-start | bytes 24584 | tf_op jit(solution)/shard_map/ppermute | solution.py:35
  28.2 4.5 %collective-permute-start.9 = (bf16[2,2048]{1,0:T(2,128)(2,1)S(1)}, bf16[2,2048]{1,0:T(2,128)(2,1)S(1)}, u32[]{:S(2)}, u32[]{:S(2)}) collective-permute-start(bf16[2,2048]{1,0:T(2,128)(2,1)S(1)} %get-tuple-element.38.a0), channel_id=1, source_target_pairs={{0,4},{4,0},{8,12},{12,8},{1,5},{5,1},{9,13},{13,9},{2,6},{6,2},{1... | collective-permute-start | bytes 24584 | tf_op jit(solution)/shard_map/ppermute | solution.py:35
  35.0 3.2 %collective-permute-start.12 = (bf16[2,4096]{1,0:T(2,128)(2,1)S(1)}, bf16[2,4096]{1,0:T(2,128)(2,1)S(1)}, u32[]{:S(2)}, u32[]{:S(2)}) collective-permute-start(bf16[2,4096]{1,0:T(2,128)(2,1)S(1)} %get-tuple-element.42), channel_id=1, source_target_pairs={{0,3},{1,2},{2,1},{3,0},{4,7},{5,6},{6,5},{7,4},{8,11},{9,10},{10,... | collective-permute-start | bytes 49160 | tf_op jit(solution)/shard_map/ppermute | solution.py:35
  35.0 3.8 %collective-permute-start.13 = (bf16[2,4096]{1,0:T(2,128)(2,1)S(1)}, bf16[2,4096]{1,0:T(2,128)(2,1)S(1)}, u32[]{:S(2)}, u32[]{:S(2)}) collective-permute-start(bf16[2,4096]{1,0:T(2,128)(2,1)S(1)} %get-tuple-element.43), channel_id=1, source_target_pairs={{0,2},{1,3},{2,0},{3,1},{4,6},{5,7},{6,4},{7,5},{8,10},{9,11},{10,... | collective-permute-start | bytes 49160 | tf_op jit(solution)/shard_map/ppermute | solution.py:35
  36.4 2.4 %collective-permute-start.14 = (bf16[2,4096]{1,0:T(2,128)(2,1)S(1)}, bf16[2,4096]{1,0:T(2,128)(2,1)S(1)}, u32[]{:S(2)}, u32[]{:S(2)}) collective-permute-start(bf16[2,4096]{1,0:T(2,128)(2,1)S(1)} %get-tuple-element.44), channel_id=1, source_target_pairs={{0,1},{1,0},{2,3},{3,2},{4,5},{5,4},{6,7},{7,6},{8,9},{9,8},{10,11... | collective-permute-start | bytes 49160 | tf_op jit(solution)/shard_map/ppermute | solution.py:35

commit v11 on v7

--- a/solution.py
+++ b/solution.py
@@ -149,9 +149,10 @@
 
 CHUNK = 512
 ROW_TILE = 48
-PAY = 128
-VALUES = 48
-QUERY = 96
+PAY = 120
+VALUES = 40
+FRESH = 80
+QUERY = 88
 F32 = jnp.float32
 BF16 = jnp.bfloat16
 
@@ -172,8 +173,8 @@
     first, second = len_ref[0], len_ref[1]
     row = lax.broadcasted_iota(jnp.int32, (PAY, HD), 0)
     lane = lax.broadcasted_iota(jnp.int32, (PAY, HD), 1)
-    resumed = (row == LC) | ((row >= QUERY) & (row < QUERY + 16))
-    other = (row == LC + 1) | (row >= QUERY + 16)
+    resumed = (row == FRESH) | ((row >= QUERY) & (row < QUERY + 16))
+    other = (row == FRESH + 1) | (row >= QUERY + 16)
     position = jnp.where(row < LC, first + row, 0)
     position = jnp.where(resumed, first + LC, jnp.where(other, second, position))
     half = lax.rem(lane, HD // 2).astype(F32)
@@ -244,7 +245,7 @@
     base = 3 * ROW_TILE
     x[pl.ds(base, 16), :] = jnp.concatenate(fresh, axis=0).astype(BF16)
     late = project_rows(x, wkv)
-    empty = jnp.zeros((8 - ROWS_DEV, HD), F32)
+    empty = jnp.zeros((8 - 2 * ROWS_DEV, HD), F32)
     for k in range(4):
         target = owner_ref[gy ^ k] ^ gx
         both = late[(k - 1) * ROW_TILE : (k - 1) * ROW_TILE + LC] if k else own[...]
@@ -252,8 +253,9 @@
         pay[target, pl.ds(VALUES, LC), :] = both[:, HD:]
         both = late[base + k * ROWS_DEV : base + (k + 1) * ROWS_DEV]
         target = k ^ gx ^ gy
-        pay[target, pl.ds(LC, 8), :] = jnp.concatenate([both[:, :HD], empty], axis=0)
-        pay[target, pl.ds(VALUES + LC, 8), :] = jnp.concatenate([both[:, HD:], empty], axis=0)
+        pay[target, pl.ds(FRESH, 8), :] = jnp.concatenate(
+            [both[:, :HD], both[:, HD:], empty], axis=0
+        )
         for r in range(ROWS_DEV):
             pay[target, pl.ds(QUERY + 16 * r, 16), :] = q_ref[k * ROWS_DEV + r]
     o0[...] = pay[0]
@@ -267,16 +269,18 @@
 ):
     total = p0[...] + p1[...].astype(F32) + p2[...].astype(F32) + p3[...].astype(F32)
     turned = total * cos_ref[...] + pltpu.roll(total, HD // 2, 1) * sin_ref[...]
-    turned = turned.astype(BF16)
-    key_out[...] = turned[:LC]
-    value_out[...] = turned[VALUES : VALUES + LC]
+    tail_value = turned[VALUES : VALUES + LC]
+    key_out[...] = turned[:LC].astype(BF16)
+    value_out[...] = tail_value.astype(BF16)
     scale = 1.0 / math.sqrt(HD)
-    more_key = turned[:VALUES]
-    more_value = turned[VALUES:QUERY]
+    more_key = jnp.concatenate([turned[:LC], turned[FRESH:QUERY]], axis=0).astype(BF16)
+    fresh_value = turned[FRESH + ROWS_DEV : FRESH + 2 * ROWS_DEV]
+    empty = jnp.zeros((8 - ROWS_DEV, HD), F32)
+    more_value = jnp.concatenate([tail_value, fresh_value, empty], axis=0).astype(BF16)
     slots = kv.shape[2]
     contract = (((1,), (1,)), ((), ()))
     for r in range(ROWS_DEV):
-        q = turned[QUERY + 16 * r : QUERY + 16 * (r + 1)]
+        q = turned[QUERY + 16 * r : QUERY + 16 * (r + 1)].astype(BF16)
         s = lax.dot_general(q, kv[0, r], contract, preferred_element_type=F32) * scale
         live = lax.broadcasted_iota(jnp.int32, s.shape, 1) < len_ref[r]
         s = jnp.where(live, s, -jnp.inf)

time: 39.2 us -> 39.2 us (level)
  no operation moved by 1% of the time
where the time goes in v11:
time: 39.2 us; the launch traced here: 39.1 us
  starting transfers between devices  15.9 us (41%)
  Pallas kernels  13 us (33%)
  waiting for transfers between devices  7.48 us (19%)
  local copies, waits for them, and re-layouts  1.23 us (3%)
  between operations  0.8 us (2%)
  other arithmetic  0.64 us (2%)
    ppermute x15, starting transfers between devices, swap(): return lax.ppermute(x, axis, [(i, i ^ k) for i in range(n)])  15.9 us
    ppermute x15, waiting for transfers between devices, swap(): return lax.ppermute(x, axis, [(i, i ^ k) for i in range(n)])  7.48 us
    pallas_call x1, Pallas kernels, per_device(): pl.pallas_call(load_kernel, out_shape=[pltpu.VMEM((PAY, HD), F32)] * 2 +...  5.35 us
    pallas_call x1, Pallas kernels, per_device(): pl.pallas_call(functools.partial(query_kernel, query_cols - quarter), out...  2.33 us
    pallas_call x1, Pallas kernels, per_device(): pl.pallas_call(out_kernel, out_shape=[shape((ROWS_DEV, width), F32)] + [s...  2.28 us
    pallas_call x1, Pallas kernels, per_device(): pl.pallas_call(attend_kernel, out_shape=[pltpu.VMEM((LC, HD), BF16)] * 2...  1.43 us
    unnamed x14, local copies, waits for them, and re-layouts  1.23 us
    pallas_call x1, Pallas kernels, per_device(): pl.pallas_call(payload_kernel, out_shape=[shape((PAY, HD), F32)] + [shape...  1.12 us
  transfers between devices with their start and end apart: 15, of which 7 were waited for; matrix products, arithmetic and copies ran while one was open for 3% of the time, Pallas kernels for 21%

profile of v11, /device:TPU:0, one launch (start us, length us, event | category | flops | bytes accessed | tf_op | source)
XLA Modules:
  0.0 39.1 jit_solution(2254878202391862156)
XLA Ops:
  0.7 3.0 %collective-permute-start = (bf16[40,4096]{1,0:T(8,128)(2,1)}, bf16[40,4096]{1,0:T(8,128)(2,1)S(1)}, u32[]{:S(2)}, u32[]{:S(2)}) collective-permute-start(bf16[40,4096]{1,0:T(8,128)(2,1)} %s.1), channel_id=1, source_target_pairs={{0,2},{1,3},{2,0},{3,1},{4,6},{5,7},{6,4},{7,5},{8,10},{9,11},{10,... | collective-permute-start | bytes 983048 | tf_op jit(solution)/shard_map/ppermute | solution.py:35
  3.7 0.0 collective-permute-start.3
  3.7 1.2 %collective-permute-start.2 = (bf16[2,4096]{1,0:T(2,128)(2,1)}, bf16[2,4096]{1,0:T(2,128)(2,1)S(1)}, u32[]{:S(2)}, u32[]{:S(2)}) collective-permute-start(bf16[2,4096]{1,0:T(2,128)(2,1)} %b0.3), channel_id=1, source_target_pairs={{0,2},{1,3},{2,0},{3,1},{4,6},{5,7},{6,4},{7,5},{8,10},{9,11},{10,... | collective-permute-start | bytes 49160 | tf_op jit(solution)/shard_map/ppermute | solution.py:35
  4.9 0.7 %collective-permute-start.1 = (bf16[2,4096]{1,0:T(2,128)(2,1)}, bf16[2,4096]{1,0:T(2,128)(2,1)S(1)}, u32[]{:S(2)}, u32[]{:S(2)}) collective-permute-start(bf16[2,4096]{1,0:T(2,128)(2,1)} %b0.3), channel_id=1, source_target_pairs={{0,1},{1,0},{2,3},{3,2},{4,5},{5,4},{6,7},{7,6},{8,9},{9,8},{10,11... | collective-permute-start | bytes 49160 | tf_op jit(solution)/shard_map/ppermute | solution.py:35
  5.5 0.0 collective-permute-start.4
  5.5 5.3 %load.1 = (f32[120,128]{1,0:T(8,128)S(1)}, f32[120,128]{1,0:T(8,128)S(1)}, bf16[1536,4096]{1,0:T(8,128)(2,1)S(1)}, bf16[4096,256]{1,0:T(8,128)(2,1)S(1)}) custom-call(s32[2]{0:T(128)} %len_ref.1, bf16[2048,4096]{1,0:T(8,128)(2,1)} %wo_hbm.3, bf16[4096,128]{1,0:T(8,128)(2,1)} %wk_hbm.1, bf16[4096,128]{1,0:T(8,128)(2,1)} %wv_hbm.1), custom_call_target="tpu_custom_call" | custom-call | flops 1000 | bytes 16777216 | tf_op jit(solution)/shard_map/load/pallas_call | solution.py:337
  10.9 0.5 %own.1 = f32[40,256]{1,0:T(8,128)S(1)} custom-call(bf16[40,4096]{1,0:T(8,128)(2,1)S(1)} %copy-done.2, bf16[4096,256]{1,0:T(8,128)(2,1)S(1)} %get-tuple-element.25.wkv), custom_call_target="tpu_custom_call" | custom-call | flops 83886080 | bytes 2097152 | tf_op jit(solution)/shard_map/own/pallas_call | solution.py:353
  11.4 0.0 copy-start.5
  11.4 0.0 copy-start.1
  11.4 0.0 copy-start.4
  11.4 0.0 collective-permute-done.3.b3
  11.4 0.9 %collective-permute-done.2.b2 = bf16[2,4096]{1,0:T(2,128)(2,1)S(1)} collective-permute-done((bf16[2,4096]{1,0:T(2,128)(2,1)}, bf16[2,4096]{1,0:T(2,128)(2,1)S(1)}, u32[]{:S(2)}, u32[]{:S(2)}) %collective-permute-start.2) | collective-permute-done | bytes 16416 | tf_op jit(solution)/shard_map/ppermute | solution.py:35
  12.3 2.3 %query.1 = (f32[8,16,128]{2,1,0:T(8,128)S(1)}, bf16[512,4096]{1,0:T(8,128)(2,1)S(1)}) custom-call(bf16[40,4096]{1,0:T(8,128)(2,1)S(1)} %collective-permute-done.far.s2, bf16[2,4096]{1,0:T(2,128)(2,1)S(1)} %copy-done.3, bf16[2,4096]{1,0:T(2,128)(2,1)S(1)} %collective-permute-done.1.b1, bf16[2,4096]{1,0:T(2,128)(2,1)S(1)} %collective-permute-done.2.b2, ...), custom_call_target="tpu_custom_call" | custom-call | flops 134217728 | bytes 2097152 | tf_op jit(solution)/shard_map/query/pallas_call | solution.py:365
  14.7 1.1 %payload.1 = (f32[120,128]{1,0:T(8,128)S(1)}, bf16[120,128]{1,0:T(8,128)(2,1)S(1)}, bf16[120,128]{1,0:T(8,128)(2,1)S(1)}, bf16[120,128]{1,0:T(8,128)(2,1)S(1)}) custom-call(s32[4]{0:T(128)S(1)} %copy-done.5, f32[40,256]{1,0:T(8,128)S(1)} %own.1, bf16[40,4096]{1,0:T(8,128)(2,1)S(1)} %collective-permute-done.4.s1, ...), custom_call_target="tpu_custom_call" | custom-call | flops 436207616 | bytes 2097152 | tf_op jit(solution)/shard_map/payload/pallas_call | solution.py:378
  15.8 4.1 %collective-permute-start.6 = (bf16[120,128]{1,0:T(8,128)(2,1)S(1)}, bf16[120,128]{1,0:T(8,128)(2,1)S(1)}, u32[]{:S(2)}, u32[]{:S(2)}) collective-permute-start(bf16[120,128]{1,0:T(8,128)(2,1)S(1)} %get-tuple-element.33), channel_id=1, source_target_pairs={{0,12},{4,8},{8,4},{12,0},{1,13},{5,9},{9,5},{13,1},{2,14},{6,10},... | collective-permute-start | bytes 92168 | tf_op jit(solution)/shard_map/ppermute | solution.py:35
  19.9 0.6 %collective-permute-start.8 = (bf16[120,128]{1,0:T(8,128)(2,1)S(1)}, bf16[120,128]{1,0:T(8,128)(2,1)S(1)}, u32[]{:S(2)}, u32[]{:S(2)}) collective-permute-start(bf16[120,128]{1,0:T(8,128)(2,1)S(1)} %get-tuple-element.35), channel_id=1, source_target_pairs={{0,4},{4,0},{8,12},{12,8},{1,5},{5,1},{9,13},{13,9},{2,6},{6,2},{1... | collective-permute-start | bytes 92168 | tf_op jit(solution)/shard_map/ppermute | solution.py:35
  20.6 1.3 %collective-permute-done.6.p1 = bf16[120,128]{1,0:T(8,128)(2,1)S(1)} collective-permute-done((bf16[120,128]{1,0:T(8,128)(2,1)S(1)}, bf16[120,128]{1,0:T(8,128)(2,1)S(1)}, u32[]{:S(2)}, u32[]{:S(2)}) %collective-permute-start.6) | collective-permute-done | bytes 30752 | tf_op jit(solution)/shard_map/ppermute | solution.py:35
  21.8 2.9 %collective-permute-done.7.p2 = bf16[120,128]{1,0:T(8,128)(2,1)S(1)} collective-permute-done((bf16[120,128]{1,0:T(8,128)(2,1)S(1)}, bf16[120,128]{1,0:T(8,128)(2,1)S(1)}, u32[]{:S(2)}, u32[]{:S(2)}) %collective-permute-start.7) | collective-permute-done | bytes 30752 | tf_op jit(solution)/shard_map/ppermute | solution.py:35
  24.7 1.4 %attend.1 = (bf16[40,128]{1,0:T(8,128)(2,1)S(1)}, bf16[40,128]{1,0:T(8,128)(2,1)S(1)}, bf16[2,2048]{1,0:T(2,128)(2,1)S(1)}) custom-call(s32[2]{0:T(128)S(1)} %copy-done.4, f32[120,128]{1,0:T(8,128)S(1)} %get-tuple-element.32.p0, bf16[120,128]{1,0:T(8,128)(2,1)S(1)} %collective-permute-done.6.p1, bf16[120,128]{1,0:T(8,128)(2,1)S(1)} %collective-permute-done.7.p2, ...), custom_call_target="tpu_custom_call" | custom-call | flops 10000000 | bytes 1000000 | tf_op jit(solution)/shard_map/attend/pallas_call | solution.py:392
  26.2 1.5 %collective-permute-start.11 = (bf16[2,2048]{1,0:T(2,128)(2,1)S(1)}, bf16[2,2048]{1,0:T(2,128)(2,1)S(1)}, u32[]{:S(2)}, u32[]{:S(2)}) collective-permute-start(bf16[2,2048]{1,0:T(2,128)(2,1)S(1)} %get-tuple-element.38.a0), channel_id=1, source_target_pairs={{0,12},{4,8},{8,4},{12,0},{1,13},{5,9},{9,5},{13,1},{2,14},{6,10},... | collective-permute-start | bytes 24584 | tf_op jit(solution)/shard_map/ppermute | solution.py:35
  27.7 0.6 %collective-permute-start.10 = (bf16[2,2048]{1,0:T(2,128)(2,1)S(1)}, bf16[2,2048]{1,0:T(2,128)(2,1)S(1)}, u32[]{:S(2)}, u32[]{:S(2)}) collective-permute-start(bf16[2,2048]{1,0:T(2,128)(2,1)S(1)} %get-tuple-element.38.a0), channel_id=1, source_target_pairs={{0,8},{4,12},{8,0},{12,4},{1,9},{5,13},{9,1},{13,5},{2,10},{6,14},... | collective-permute-start | bytes 24584 | tf_op jit(solution)/shard_map/ppermute | solution.py:35
  28.3 2.3 %collective-permute-start.9 = (bf16[2,2048]{1,0:T(2,128)(2,1)S(1)}, bf16[2,2048]{1,0:T(2,128)(2,1)S(1)}, u32[]{:S(2)}, u32[]{:S(2)}) collective-permute-start(bf16[2,2048]{1,0:T(2,128)(2,1)S(1)} %get-tuple-element.38.a0), channel_id=1, source_target_pairs={{0,4},{4,0},{8,12},{12,8},{1,5},{5,1},{9,13},{13,9},{2,6},{6,2},{1... | collective-permute-start | bytes 24584 | tf_op jit(solution)/shard_map/ppermute | solution.py:35
  30.6 1.1 %collective-permute-done.11.a3 = bf16[2,2048]{1,0:T(2,128)(2,1)S(1)} collective-permute-done((bf16[2,2048]{1,0:T(2,128)(2,1)S(1)}, bf16[2,2048]{1,0:T(2,128)(2,1)S(1)}, u32[]{:S(2)}, u32[]{:S(2)}) %collective-permute-start.11) | collective-permute-done | bytes 8224 | tf_op jit(solution)/shard_map/ppermute | solution.py:35
  31.7 0.7 %collective-permute-done.10.a2 = bf16[2,2048]{1,0:T(2,128)(2,1)S(1)} collective-permute-done((bf16[2,2048]{1,0:T(2,128)(2,1)S(1)}, bf16[2,2048]{1,0:T(2,128)(2,1)S(1)}, u32[]{:S(2)}, u32[]{:S(2)}) %collective-permute-start.10) | collective-permute-done | bytes 8224 | tf_op jit(solution)/shard_map/ppermute | solution.py:35
  32.3 2.3 %project.1 = (f32[2,4096]{1,0:T(2,128)S(1)}, bf16[2,4096]{1,0:T(2,128)(2,1)S(1)}, bf16[2,4096]{1,0:T(2,128)(2,1)S(1)}, bf16[2,4096]{1,0:T(2,128)(2,1)S(1)}) custom-call(bf16[2,2048]{1,0:T(2,128)(2,1)S(1)} %get-tuple-element.38.a0, bf16[2,2048]{1,0:T(2,128)(2,1)S(1)} %collective-permute-done.9.a1, bf16[2,2048]{1,0:T(2,128)(2,1)S(1)} %collective-permute-done.10.a2, ...), custom_call_target="tpu_custom_call" | custom-call | flops 134217728 | bytes 16777216 | tf_op jit(solution)/shard_map/project/pallas_call | solution.py:403
  34.6 1.4 %collective-permute-start.13 = (bf16[2,4096]{1,0:T(2,128)(2,1)S(1)}, bf16[2,4096]{1,0:T(2,128)(2,1)S(1)}, u32[]{:S(2)}, u32[]{:S(2)}) collective-permute-start(bf16[2,4096]{1,0:T(2,128)(2,1)S(1)} %get-tuple-element.43), channel_id=1, source_target_pairs={{0,2},{1,3},{2,0},{3,1},{4,6},{5,7},{6,4},{7,5},{8,10},{9,11},{10,... | collective-permute-start | bytes 49160 | tf_op jit(solution)/shard_map/ppermute | solution.py:35
  36.0 0.5 %collective-permute-start.14 = (bf16[2,4096]{1,0:T(2,128)(2,1)S(1)}, bf16[2,4096]{1,0:T(2,128)(2,1)S(1)}, u32[]{:S(2)}, u32[]{:S(2)}) collective-permute-start(bf16[2,4096]{1,0:T(2,128)(2,1)S(1)} %get-tuple-element.44), channel_id=1, source_target_pairs={{0,1},{1,0},{2,3},{3,2},{4,5},{5,4},{6,7},{7,6},{8,9},{9,8},{10,11... | collective-permute-start | bytes 49160 | tf_op jit(solution)/shard_map/ppermute | solution.py:35
  36.5 0.6 %copy.12 = bf16[1,40,128]{2,1,0:T(8,128)(2,1)} copy(bf16[1,40,128]{2,1,0:T(8,128)(2,1)S(1)} %bitcast.3) | data formatting | bytes 20480
  37.1 0.6 %copy.13 = bf16[1,40,128]{2,1,0:T(8,128)(2,1)} copy(bf16[1,40,128]{2,1,0:T(8,128)(2,1)S(1)} %bitcast.2) | data formatting | bytes 20480
  37.7 0.1 collective-permute-done.12
  37.8 0.6 %collective-permute-done.13 = bf16[2,4096]{1,0:T(2,128)(2,1)S(1)} collective-permute-done((bf16[2,4096]{1,0:T(2,128)(2,1)S(1)}, bf16[2,4096]{1,0:T(2,128)(2,1)S(1)}, u32[]{:S(2)}, u32[]{:S(2)}) %collective-permute-start.13) | collective-permute-done | bytes 16416 | tf_op jit(solution)/shard_map/ppermute | solution.py:35
  38.4 0.6 %add_convert_fusion = bf16[2,4096]{1,0:T(2,128)(2,1)} fusion(bf16[2,4096]{1,0:T(2,128)(2,1)S(1)} %collective-permute-done.14, bf16[2,4096]{1,0:T(2,128)(2,1)S(1)} %collective-permute-done.13, f32[2,4096]{1,0:T(2,128)S(1)} %get-tuple-element.41, bf16[2,4096]{1,0:T(2,128)(2,1)S(1)} %collective-permute-done.12), kind=kLoop, calls=%fused_computation | loop fusion | flops 57344 | bytes 98304 | tf_op jit(solution)/shard_map/convert_element_type | solution.py:415
  (19 shorter events, 0.0 us)
Async XLA Ops:
  0.6 10.3 %copy-start.2 = (bf16[40,4096]{1,0:T(8,128)(2,1)S(1)}, bf16[40,4096]{1,0:T(8,128)(2,1)}, u32[]{:S(2)}) copy-start(bf16[40,4096]{1,0:T(8,128)(2,1)} %s.1) | copy-start | bytes 983044
  0.6 11.7 %copy-start.3 = (bf16[2,4096]{1,0:T(2,128)(2,1)S(1)}, bf16[2,4096]{1,0:T(2,128)(2,1)}, u32[]{:S(2)}) copy-start(bf16[2,4096]{1,0:T(2,128)(2,1)} %b0.3) | copy-start | bytes 49156
  0.7 11.7 %copy-start = (bf16[4096,2048]{1,0:T(8,128)(2,1)S(1)}, bf16[4096,2048]{1,0:T(8,128)(2,1)}, u32[]{:S(2)}) copy-start(bf16[4096,2048]{1,0:T(8,128)(2,1)} %w.1) | copy-start | bytes 50331652
  0.7 11.6 %collective-permute-start = (bf16[40,4096]{1,0:T(8,128)(2,1)}, bf16[40,4096]{1,0:T(8,128)(2,1)S(1)}, u32[]{:S(2)}, u32[]{:S(2)}) collective-permute-start(bf16[40,4096]{1,0:T(8,128)(2,1)} %s.1), channel_id=1, source_target_pairs={{0,2},{1,3},{2,0},{3,1},{4,6},{5,7},{6,4},{7,5},{8,10},{9,11},{10,... | collective-permute-start | bytes 983048 | tf_op jit(solution)/shard_map/ppermute | solution.py:35
  3.7 7.8 %collective-permute-start.3 = (bf16[2,4096]{1,0:T(2,128)(2,1)}, bf16[2,4096]{1,0:T(2,128)(2,1)S(1)}, u32[]{:S(2)}, u32[]{:S(2)}) collective-permute-start(bf16[2,4096]{1,0:T(2,128)(2,1)} %b0.3), channel_id=1, source_target_pairs={{0,3},{1,2},{2,1},{3,0},{4,7},{5,6},{6,5},{7,4},{8,11},{9,10},{10,... | collective-permute-start | bytes 49160 | tf_op jit(solution)/shard_map/ppermute | solution.py:35
  3.7 8.6 %collective-permute-start.2 = (bf16[2,4096]{1,0:T(2,128)(2,1)}, bf16[2,4096]{1,0:T(2,128)(2,1)S(1)}, u32[]{:S(2)}, u32[]{:S(2)}) collective-permute-start(bf16[2,4096]{1,0:T(2,128)(2,1)} %b0.3), channel_id=1, source_target_pairs={{0,2},{1,3},{2,0},{3,1},{4,6},{5,7},{6,4},{7,5},{8,10},{9,11},{10,... | collective-permute-start | bytes 49160 | tf_op jit(solution)/shard_map/ppermute | solution.py:35
  4.9 7.4 %collective-permute-start.1 = (bf16[2,4096]{1,0:T(2,128)(2,1)}, bf16[2,4096]{1,0:T(2,128)(2,1)S(1)}, u32[]{:S(2)}, u32[]{:S(2)}) collective-permute-start(bf16[2,4096]{1,0:T(2,128)(2,1)} %b0.3), channel_id=1, source_target_pairs={{0,1},{1,0},{2,3},{3,2},{4,5},{5,4},{6,7},{7,6},{8,9},{9,8},{10,11... | collective-permute-start | bytes 49160 | tf_op jit(solution)/shard_map/ppermute | solution.py:35
  5.5 9.1 %collective-permute-start.4 = (bf16[40,4096]{1,0:T(8,128)(2,1)}, bf16[40,4096]{1,0:T(8,128)(2,1)S(1)}, u32[]{:S(2)}, u32[]{:S(2)}) collective-permute-start(bf16[40,4096]{1,0:T(8,128)(2,1)} %s.1), channel_id=1, source_target_pairs={{0,1},{1,0},{2,3},{3,2},{4,5},{5,4},{6,7},{7,6},{8,9},{9,8},{10,11... | collective-permute-start | bytes 983048 | tf_op jit(solution)/shard_map/ppermute | solution.py:35
  11.4 3.3 %copy-start.5 = (s32[4]{0:T(128)S(1)}, s32[4]{0:T(128)}, u32[]{:S(2)}) copy-start(s32[4]{0:T(128)} %owner_ref.1) | copy-start | bytes 52
  11.4 13.3 %copy-start.1 = (bf16[2,2,512,128]{3,2,1,0:T(8,128)(2,1)S(1)}, bf16[2,2,512,128]{3,2,1,0:T(8,128)(2,1)}, u32[]{:S(2)}) copy-start(bf16[2,2,512,128]{3,2,1,0:T(8,128)(2,1)} %kv.1) | copy-start | bytes 1572868
  11.4 13.3 %copy-start.4 = (s32[2]{0:T(128)S(1)}, s32[2]{0:T(128)}, u32[]{:S(2)}) copy-start(s32[2]{0:T(128)} %len_ref.1) | copy-start | bytes 28
  12.3 2.4 %collective-permute-start.5 = (bf16[40,4096]{1,0:T(8,128)(2,1)S(1)}, bf16[40,4096]{1,0:T(8,128)(2,1)S(1)}, u32[]{:S(2)}, u32[]{:S(2)}) collective-permute-start(bf16[40,4096]{1,0:T(8,128)(2,1)S(1)} %collective-permute-done.far.s2), channel_id=1, source_target_pairs={{0,1},{1,0},{2,3},{3,2},{4,5},{5,4},{6,7},{7,6},{8,9},{9,8},{10,11... | collective-permute-start | bytes 983048 | tf_op jit(solution)/shard_map/ppermute | solution.py:35
  15.8 6.0 %collective-permute-start.6 = (bf16[120,128]{1,0:T(8,128)(2,1)S(1)}, bf16[120,128]{1,0:T(8,128)(2,1)S(1)}, u32[]{:S(2)}, u32[]{:S(2)}) collective-permute-start(bf16[120,128]{1,0:T(8,128)(2,1)S(1)} %get-tuple-element.33), channel_id=1, source_target_pairs={{0,12},{4,8},{8,4},{12,0},{1,13},{5,9},{9,5},{13,1},{2,14},{6,10},... | collective-permute-start | bytes 92168 | tf_op jit(solution)/shard_map/ppermute | solution.py:35
  19.9 4.8 %collective-permute-start.7 = (bf16[120,128]{1,0:T(8,128)(2,1)S(1)}, bf16[120,128]{1,0:T(8,128)(2,1)S(1)}, u32[]{:S(2)}, u32[]{:S(2)}) collective-permute-start(bf16[120,128]{1,0:T(8,128)(2,1)S(1)} %get-tuple-element.34), channel_id=1, source_target_pairs={{0,8},{4,12},{8,0},{12,4},{1,9},{5,13},{9,1},{13,5},{2,10},{6,14},... | collective-permute-start | bytes 92168 | tf_op jit(solution)/shard_map/ppermute | solution.py:35
  19.9 4.8 %collective-permute-start.8 = (bf16[120,128]{1,0:T(8,128)(2,1)S(1)}, bf16[120,128]{1,0:T(8,128)(2,1)S(1)}, u32[]{:S(2)}, u32[]{:S(2)}) collective-permute-start(bf16[120,128]{1,0:T(8,128)(2,1)S(1)} %get-tuple-element.35), channel_id=1, source_target_pairs={{0,4},{4,0},{8,12},{12,8},{1,5},{5,1},{9,13},{13,9},{2,6},{6,2},{1... | collective-permute-start | bytes 92168 | tf_op jit(solution)/shard_map/ppermute | solution.py:35
  26.2 5.5 %collective-permute-start.11 = (bf16[2,2048]{1,0:T(2,128)(2,1)S(1)}, bf16[2,2048]{1,0:T(2,128)(2,1)S(1)}, u32[]{:S(2)}, u32[]{:S(2)}) collective-permute-start(bf16[2,2048]{1,0:T(2,128)(2,1)S(1)} %get-tuple-element.38.a0), channel_id=1, source_target_pairs={{0,12},{4,8},{8,4},{12,0},{1,13},{5,9},{9,5},{13,1},{2,14},{6,10},... | collective-permute-start | bytes 24584 | tf_op jit(solution)/shard_map/ppermute | solution.py:35
  27.7 4.6 %collective-permute-start.10 = (bf16[2,2048]{1,0:T(2,128)(2,1)S(1)}, bf16[2,2048]{1,0:T(2,128)(2,1)S(1)}, u32[]{:S(2)}, u32[]{:S(2)}) collective-permute-start(bf16[2,2048]{1,0:T(2,128)(2,1)S(1)} %get-tuple-element.38.a0), channel_id=1, source_target_pairs={{0,8},{4,12},{8,0},{12,4},{1,9},{5,13},{9,1},{13,5},{2,10},{6,14},... | collective-permute-start | bytes 24584 | tf_op jit(solution)/shard_map/ppermute | solution.py:35
  28.3 4.0 %collective-permute-start.9 = (bf16[2,2048]{1,0:T(2,128)(2,1)S(1)}, bf16[2,2048]{1,0:T(2,128)(2,1)S(1)}, u32[]{:S(2)}, u32[]{:S(2)}) collective-permute-start(bf16[2,2048]{1,0:T(2,128)(2,1)S(1)} %get-tuple-element.38.a0), channel_id=1, source_target_pairs={{0,4},{4,0},{8,12},{12,8},{1,5},{5,1},{9,13},{13,9},{2,6},{6,2},{1... | collective-permute-start | bytes 24584 | tf_op jit(solution)/shard_map/ppermute | solution.py:35
  34.6 3.2 %collective-permute-start.12 = (bf16[2,4096]{1,0:T(2,128)(2,1)S(1)}, bf16[2,4096]{1,0:T(2,128)(2,1)S(1)}, u32[]{:S(2)}, u32[]{:S(2)}) collective-permute-start(bf16[2,4096]{1,0:T(2,128)(2,1)S(1)} %get-tuple-element.42), channel_id=1, source_target_pairs={{0,3},{1,2},{2,1},{3,0},{4,7},{5,6},{6,5},{7,4},{8,11},{9,10},{10,... | collective-permute-start | bytes 49160 | tf_op jit(solution)/shard_map/ppermute | solution.py:35
  34.6 3.8 %collective-permute-start.13 = (bf16[2,4096]{1,0:T(2,128)(2,1)S(1)}, bf16[2,4096]{1,0:T(2,128)(2,1)S(1)}, u32[]{:S(2)}, u32[]{:S(2)}) collective-permute-start(bf16[2,4096]{1,0:T(2,128)(2,1)S(1)} %get-tuple-element.43), channel_id=1, source_target_pairs={{0,2},{1,3},{2,0},{3,1},{4,6},{5,7},{6,4},{7,5},{8,10},{9,11},{10,... | collective-permute-start | bytes 49160 | tf_op jit(solution)/shard_map/ppermute | solution.py:35
  36.0 2.4 %collective-permute-start.14 = (bf16[2,4096]{1,0:T(2,128)(2,1)S(1)}, bf16[2,4096]{1,0:T(2,128)(2,1)S(1)}, u32[]{:S(2)}, u32[]{:S(2)}) collective-permute-start(bf16[2,4096]{1,0:T(2,128)(2,1)S(1)} %get-tuple-element.44), channel_id=1, source_target_pairs={{0,1},{1,0},{2,3},{3,2},{4,5},{5,4},{6,7},{7,6},{8,9},{9,8},{10,11... | collective-permute-start | bytes 49160 | tf_op jit(solution)/shard_map/ppermute | solution.py:35

commit v12 on v11

--- a/solution.py
+++ b/solution.py
@@ -147,7 +147,6 @@
     return (mixed.astype(jnp.bfloat16), rebuilt_key[None], rebuilt_value[None])
 
 
-CHUNK = 512
 ROW_TILE = 48
 PAY = 120
 VALUES = 40
@@ -196,14 +195,6 @@
     return copies
 
 
-def project_rows(x, wkv):
-    both = jnp.zeros((x.shape[0], wkv.shape[1]), F32)
-    for c in range(x.shape[1] // CHUNK):
-        part = slice(c * CHUNK, (c + 1) * CHUNK)
-        both += jnp.dot(x[:, part], wkv[part, :], preferred_element_type=F32)
-    return both
-
-
 def load_kernel(
     len_hbm, wo_hbm, wk_hbm, wv_hbm, cos_ref, sin_ref, wo, wkv, len_ref, sems
 ):
@@ -219,7 +210,7 @@
 
 
 def own_kernel(s, wkv, out):
-    out[...] = project_rows(s, wkv)
+    out[...] = jnp.dot(s[...], wkv[...], preferred_element_type=F32)
 
 
 def query_kernel(first, far, b0, b1, b2, b3, w, wo_hbm, out_ref, wo, acc, sems):
@@ -244,7 +235,7 @@
     fresh.append(jnp.zeros((8, x.shape[1]), F32))
     base = 3 * ROW_TILE
     x[pl.ds(base, 16), :] = jnp.concatenate(fresh, axis=0).astype(BF16)
-    late = project_rows(x, wkv)
+    late = jnp.dot(x[...], wkv[...], preferred_element_type=F32)
     empty = jnp.zeros((8 - 2 * ROWS_DEV, HD), F32)
     for k in range(4):
         target = owner_ref[gy ^ k] ^ gx

time: 39.2 us -> 39.2 us (level)
  no operation moved by 1% of the time
where the time goes in v12:
time: 39.2 us; the launch traced here: 39.1 us
  starting transfers between devices  15.9 us (41%)
  Pallas kernels  13 us (33%)
  waiting for transfers between devices  7.48 us (19%)
  local copies, waits for them, and re-layouts  1.23 us (3%)
  between operations  0.8 us (2%)
  other arithmetic  0.64 us (2%)
    ppermute x15, starting transfers between devices, swap(): return lax.ppermute(x, axis, [(i, i ^ k) for i in range(n)])  15.9 us
    ppermute x15, waiting for transfers between devices, swap(): return lax.ppermute(x, axis, [(i, i ^ k) for i in range(n)])  7.48 us
    pallas_call x1, Pallas kernels, per_device(): pl.pallas_call(load_kernel, out_shape=[pltpu.VMEM((PAY, HD), F32)] * 2 +...  5.35 us
    pallas_call x1, Pallas kernels, per_device(): pl.pallas_call(functools.partial(query_kernel, query_cols - quarter), out...  2.33 us
    pallas_call x1, Pallas kernels, per_device(): pl.pallas_call(out_kernel, out_shape=[shape((ROWS_DEV, width), F32)] + [s...  2.28 us
    pallas_call x1, Pallas kernels, per_device(): pl.pallas_call(attend_kernel, out_shape=[pltpu.VMEM((LC, HD), BF16)] * 2...  1.43 us
    unnamed x14, local copies, waits for them, and re-layouts  1.23 us
    pallas_call x1, Pallas kernels, per_device(): pl.pallas_call(payload_kernel, out_shape=[shape((PAY, HD), F32)] + [shape...  1.12 us
  transfers between devices with their start and end apart: 15, of which 7 were waited for; matrix products, arithmetic and copies ran while one was open for 3% of the time, Pallas kernels for 21%

profile of v12, /device:TPU:0, one launch (start us, length us, event | category | flops | bytes accessed | tf_op | source)
XLA Modules:
  0.0 39.1 jit_solution(8284603754685442078)
XLA Ops:
  0.7 3.0 %collective-permute-start = (bf16[40,4096]{1,0:T(8,128)(2,1)}, bf16[40,4096]{1,0:T(8,128)(2,1)S(1)}, u32[]{:S(2)}, u32[]{:S(2)}) collective-permute-start(bf16[40,4096]{1,0:T(8,128)(2,1)} %s.1), channel_id=1, source_target_pairs={{0,2},{1,3},{2,0},{3,1},{4,6},{5,7},{6,4},{7,5},{8,10},{9,11},{10,... | collective-permute-start | bytes 983048 | tf_op jit(solution)/shard_map/ppermute | solution.py:35
  3.7 0.0 collective-permute-start.3
  3.7 1.2 %collective-permute-start.2 = (bf16[2,4096]{1,0:T(2,128)(2,1)}, bf16[2,4096]{1,0:T(2,128)(2,1)S(1)}, u32[]{:S(2)}, u32[]{:S(2)}) collective-permute-start(bf16[2,4096]{1,0:T(2,128)(2,1)} %b0.3), channel_id=1, source_target_pairs={{0,2},{1,3},{2,0},{3,1},{4,6},{5,7},{6,4},{7,5},{8,10},{9,11},{10,... | collective-permute-start | bytes 49160 | tf_op jit(solution)/shard_map/ppermute | solution.py:35
  4.9 0.7 %collective-permute-start.1 = (bf16[2,4096]{1,0:T(2,128)(2,1)}, bf16[2,4096]{1,0:T(2,128)(2,1)S(1)}, u32[]{:S(2)}, u32[]{:S(2)}) collective-permute-start(bf16[2,4096]{1,0:T(2,128)(2,1)} %b0.3), channel_id=1, source_target_pairs={{0,1},{1,0},{2,3},{3,2},{4,5},{5,4},{6,7},{7,6},{8,9},{9,8},{10,11... | collective-permute-start | bytes 49160 | tf_op jit(solution)/shard_map/ppermute | solution.py:35
  5.5 0.0 collective-permute-start.4
  5.5 5.3 %load.1 = (f32[120,128]{1,0:T(8,128)S(1)}, f32[120,128]{1,0:T(8,128)S(1)}, bf16[1536,4096]{1,0:T(8,128)(2,1)S(1)}, bf16[4096,256]{1,0:T(8,128)(2,1)S(1)}) custom-call(s32[2]{0:T(128)} %len_ref.1, bf16[2048,4096]{1,0:T(8,128)(2,1)} %wo_hbm.3, bf16[4096,128]{1,0:T(8,128)(2,1)} %wk_hbm.1, bf16[4096,128]{1,0:T(8,128)(2,1)} %wv_hbm.1), custom_call_target="tpu_custom_call" | custom-call | flops 1000 | bytes 16777216 | tf_op jit(solution)/shard_map/load/pallas_call | solution.py:328
  10.9 0.5 %own.1 = f32[40,256]{1,0:T(8,128)S(1)} custom-call(bf16[40,4096]{1,0:T(8,128)(2,1)S(1)} %copy-done.2, bf16[4096,256]{1,0:T(8,128)(2,1)S(1)} %get-tuple-element.25.wkv), custom_call_target="tpu_custom_call" | custom-call | flops 83886080 | bytes 2097152 | tf_op jit(solution)/shard_map/own/pallas_call | solution.py:344
  11.4 0.0 copy-start.5
  11.4 0.0 copy-start.1
  11.4 0.0 copy-start.4
  11.4 0.9 %collective-permute-done.2.b2 = bf16[2,4096]{1,0:T(2,128)(2,1)S(1)} collective-permute-done((bf16[2,4096]{1,0:T(2,128)(2,1)}, bf16[2,4096]{1,0:T(2,128)(2,1)S(1)}, u32[]{:S(2)}, u32[]{:S(2)}) %collective-permute-start.2) | collective-permute-done | bytes 16416 | tf_op jit(solution)/shard_map/ppermute | solution.py:35
  12.3 0.0 collective-permute-done.1.b1
  12.3 2.3 %query.1 = (f32[8,16,128]{2,1,0:T(8,128)S(1)}, bf16[512,4096]{1,0:T(8,128)(2,1)S(1)}) custom-call(bf16[40,4096]{1,0:T(8,128)(2,1)S(1)} %collective-permute-done.far.s2, bf16[2,4096]{1,0:T(2,128)(2,1)S(1)} %copy-done.3, bf16[2,4096]{1,0:T(2,128)(2,1)S(1)} %collective-permute-done.1.b1, bf16[2,4096]{1,0:T(2,128)(2,1)S(1)} %collective-permute-done.2.b2, ...), custom_call_target="tpu_custom_call" | custom-call | flops 134217728 | bytes 2097152 | tf_op jit(solution)/shard_map/query/pallas_call | solution.py:356
  14.7 1.1 %payload.1 = (f32[120,128]{1,0:T(8,128)S(1)}, bf16[120,128]{1,0:T(8,128)(2,1)S(1)}, bf16[120,128]{1,0:T(8,128)(2,1)S(1)}, bf16[120,128]{1,0:T(8,128)(2,1)S(1)}) custom-call(s32[4]{0:T(128)S(1)} %copy-done.5, f32[40,256]{1,0:T(8,128)S(1)} %own.1, bf16[40,4096]{1,0:T(8,128)(2,1)S(1)} %collective-permute-done.4.s1, ...), custom_call_target="tpu_custom_call" | custom-call | flops 436207616 | bytes 2097152 | tf_op jit(solution)/shard_map/payload/pallas_call | solution.py:369
  15.8 4.1 %collective-permute-start.6 = (bf16[120,128]{1,0:T(8,128)(2,1)S(1)}, bf16[120,128]{1,0:T(8,128)(2,1)S(1)}, u32[]{:S(2)}, u32[]{:S(2)}) collective-permute-start(bf16[120,128]{1,0:T(8,128)(2,1)S(1)} %get-tuple-element.33), channel_id=1, source_target_pairs={{0,12},{4,8},{8,4},{12,0},{1,13},{5,9},{9,5},{13,1},{2,14},{6,10},... | collective-permute-start | bytes 92168 | tf_op jit(solution)/shard_map/ppermute | solution.py:35
  19.9 0.6 %collective-permute-start.8 = (bf16[120,128]{1,0:T(8,128)(2,1)S(1)}, bf16[120,128]{1,0:T(8,128)(2,1)S(1)}, u32[]{:S(2)}, u32[]{:S(2)}) collective-permute-start(bf16[120,128]{1,0:T(8,128)(2,1)S(1)} %get-tuple-element.35), channel_id=1, source_target_pairs={{0,4},{4,0},{8,12},{12,8},{1,5},{5,1},{9,13},{13,9},{2,6},{6,2},{1... | collective-permute-start | bytes 92168 | tf_op jit(solution)/shard_map/ppermute | solution.py:35
  20.6 1.3 %collective-permute-done.6.p1 = bf16[120,128]{1,0:T(8,128)(2,1)S(1)} collective-permute-done((bf16[120,128]{1,0:T(8,128)(2,1)S(1)}, bf16[120,128]{1,0:T(8,128)(2,1)S(1)}, u32[]{:S(2)}, u32[]{:S(2)}) %collective-permute-start.6) | collective-permute-done | bytes 30752 | tf_op jit(solution)/shard_map/ppermute | solution.py:35
  21.8 2.9 %collective-permute-done.7.p2 = bf16[120,128]{1,0:T(8,128)(2,1)S(1)} collective-permute-done((bf16[120,128]{1,0:T(8,128)(2,1)S(1)}, bf16[120,128]{1,0:T(8,128)(2,1)S(1)}, u32[]{:S(2)}, u32[]{:S(2)}) %collective-permute-start.7) | collective-permute-done | bytes 30752 | tf_op jit(solution)/shard_map/ppermute | solution.py:35
  24.7 1.4 %attend.1 = (bf16[40,128]{1,0:T(8,128)(2,1)S(1)}, bf16[40,128]{1,0:T(8,128)(2,1)S(1)}, bf16[2,2048]{1,0:T(2,128)(2,1)S(1)}) custom-call(s32[2]{0:T(128)S(1)} %copy-done.4, f32[120,128]{1,0:T(8,128)S(1)} %get-tuple-element.32.p0, bf16[120,128]{1,0:T(8,128)(2,1)S(1)} %collective-permute-done.6.p1, bf16[120,128]{1,0:T(8,128)(2,1)S(1)} %collective-permute-done.7.p2, ...), custom_call_target="tpu_custom_call" | custom-call | flops 10000000 | bytes 1000000 | tf_op jit(solution)/shard_map/attend/pallas_call | solution.py:383
  26.2 1.5 %collective-permute-start.11 = (bf16[2,2048]{1,0:T(2,128)(2,1)S(1)}, bf16[2,2048]{1,0:T(2,128)(2,1)S(1)}, u32[]{:S(2)}, u32[]{:S(2)}) collective-permute-start(bf16[2,2048]{1,0:T(2,128)(2,1)S(1)} %get-tuple-element.38.a0), channel_id=1, source_target_pairs={{0,12},{4,8},{8,4},{12,0},{1,13},{5,9},{9,5},{13,1},{2,14},{6,10},... | collective-permute-start | bytes 24584 | tf_op jit(solution)/shard_map/ppermute | solution.py:35
  27.7 0.6 %collective-permute-start.10 = (bf16[2,2048]{1,0:T(2,128)(2,1)S(1)}, bf16[2,2048]{1,0:T(2,128)(2,1)S(1)}, u32[]{:S(2)}, u32[]{:S(2)}) collective-permute-start(bf16[2,2048]{1,0:T(2,128)(2,1)S(1)} %get-tuple-element.38.a0), channel_id=1, source_target_pairs={{0,8},{4,12},{8,0},{12,4},{1,9},{5,13},{9,1},{13,5},{2,10},{6,14},... | collective-permute-start | bytes 24584 | tf_op jit(solution)/shard_map/ppermute | solution.py:35
  28.3 2.3 %collective-permute-start.9 = (bf16[2,2048]{1,0:T(2,128)(2,1)S(1)}, bf16[2,2048]{1,0:T(2,128)(2,1)S(1)}, u32[]{:S(2)}, u32[]{:S(2)}) collective-permute-start(bf16[2,2048]{1,0:T(2,128)(2,1)S(1)} %get-tuple-element.38.a0), channel_id=1, source_target_pairs={{0,4},{4,0},{8,12},{12,8},{1,5},{5,1},{9,13},{13,9},{2,6},{6,2},{1... | collective-permute-start | bytes 24584 | tf_op jit(solution)/shard_map/ppermute | solution.py:35
  30.6 1.1 %collective-permute-done.11.a3 = bf16[2,2048]{1,0:T(2,128)(2,1)S(1)} collective-permute-done((bf16[2,2048]{1,0:T(2,128)(2,1)S(1)}, bf16[2,2048]{1,0:T(2,128)(2,1)S(1)}, u32[]{:S(2)}, u32[]{:S(2)}) %collective-permute-start.11) | collective-permute-done | bytes 8224 | tf_op jit(solution)/shard_map/ppermute | solution.py:35
  31.7 0.7 %collective-permute-done.10.a2 = bf16[2,2048]{1,0:T(2,128)(2,1)S(1)} collective-permute-done((bf16[2,2048]{1,0:T(2,128)(2,1)S(1)}, bf16[2,2048]{1,0:T(2,128)(2,1)S(1)}, u32[]{:S(2)}, u32[]{:S(2)}) %collective-permute-start.10) | collective-permute-done | bytes 8224 | tf_op jit(solution)/shard_map/ppermute | solution.py:35
  32.3 2.3 %project.1 = (f32[2,4096]{1,0:T(2,128)S(1)}, bf16[2,4096]{1,0:T(2,128)(2,1)S(1)}, bf16[2,4096]{1,0:T(2,128)(2,1)S(1)}, bf16[2,4096]{1,0:T(2,128)(2,1)S(1)}) custom-call(bf16[2,2048]{1,0:T(2,128)(2,1)S(1)} %get-tuple-element.38.a0, bf16[2,2048]{1,0:T(2,128)(2,1)S(1)} %collective-permute-done.9.a1, bf16[2,2048]{1,0:T(2,128)(2,1)S(1)} %collective-permute-done.10.a2, ...), custom_call_target="tpu_custom_call" | custom-call | flops 134217728 | bytes 16777216 | tf_op jit(solution)/shard_map/project/pallas_call | solution.py:394
  34.6 1.4 %collective-permute-start.13 = (bf16[2,4096]{1,0:T(2,128)(2,1)S(1)}, bf16[2,4096]{1,0:T(2,128)(2,1)S(1)}, u32[]{:S(2)}, u32[]{:S(2)}) collective-permute-start(bf16[2,4096]{1,0:T(2,128)(2,1)S(1)} %get-tuple-element.43), channel_id=1, source_target_pairs={{0,2},{1,3},{2,0},{3,1},{4,6},{5,7},{6,4},{7,5},{8,10},{9,11},{10,... | collective-permute-start | bytes 49160 | tf_op jit(solution)/shard_map/ppermute | solution.py:35
  36.0 0.5 %collective-permute-start.14 = (bf16[2,4096]{1,0:T(2,128)(2,1)S(1)}, bf16[2,4096]{1,0:T(2,128)(2,1)S(1)}, u32[]{:S(2)}, u32[]{:S(2)}) collective-permute-start(bf16[2,4096]{1,0:T(2,128)(2,1)S(1)} %get-tuple-element.44), channel_id=1, source_target_pairs={{0,1},{1,0},{2,3},{3,2},{4,5},{5,4},{6,7},{7,6},{8,9},{9,8},{10,11... | collective-permute-start | bytes 49160 | tf_op jit(solution)/shard_map/ppermute | solution.py:35
  36.5 0.6 %copy.12 = bf16[1,40,128]{2,1,0:T(8,128)(2,1)} copy(bf16[1,40,128]{2,1,0:T(8,128)(2,1)S(1)} %bitcast.3) | data formatting | bytes 20480
  37.1 0.6 %copy.13 = bf16[1,40,128]{2,1,0:T(8,128)(2,1)} copy(bf16[1,40,128]{2,1,0:T(8,128)(2,1)S(1)} %bitcast.2) | data formatting | bytes 20480
  37.7 0.1 collective-permute-done.12
  37.8 0.6 %collective-permute-done.13 = bf16[2,4096]{1,0:T(2,128)(2,1)S(1)} collective-permute-done((bf16[2,4096]{1,0:T(2,128)(2,1)S(1)}, bf16[2,4096]{1,0:T(2,128)(2,1)S(1)}, u32[]{:S(2)}, u32[]{:S(2)}) %collective-permute-start.13) | collective-permute-done | bytes 16416 | tf_op jit(solution)/shard_map/ppermute | solution.py:35
  38.4 0.6 %add_convert_fusion = bf16[2,4096]{1,0:T(2,128)(2,1)} fusion(bf16[2,4096]{1,0:T(2,128)(2,1)S(1)} %collective-permute-done.14, bf16[2,4096]{1,0:T(2,128)(2,1)S(1)} %collective-permute-done.13, f32[2,4096]{1,0:T(2,128)S(1)} %get-tuple-element.41, bf16[2,4096]{1,0:T(2,128)(2,1)S(1)} %collective-permute-done.12), kind=kLoop, calls=%fused_computation | loop fusion | flops 57344 | bytes 98304 | tf_op jit(solution)/shard_map/convert_element_type | solution.py:406
  (19 shorter events, 0.0 us)
Async XLA Ops:
  0.6 10.3 %copy-start.2 = (bf16[40,4096]{1,0:T(8,128)(2,1)S(1)}, bf16[40,4096]{1,0:T(8,128)(2,1)}, u32[]{:S(2)}) copy-start(bf16[40,4096]{1,0:T(8,128)(2,1)} %s.1) | copy-start | bytes 983044
  0.6 11.7 %copy-start.3 = (bf16[2,4096]{1,0:T(2,128)(2,1)S(1)}, bf16[2,4096]{1,0:T(2,128)(2,1)}, u32[]{:S(2)}) copy-start(bf16[2,4096]{1,0:T(2,128)(2,1)} %b0.3) | copy-start | bytes 49156
  0.7 11.7 %copy-start = (bf16[4096,2048]{1,0:T(8,128)(2,1)S(1)}, bf16[4096,2048]{1,0:T(8,128)(2,1)}, u32[]{:S(2)}) copy-start(bf16[4096,2048]{1,0:T(8,128)(2,1)} %w.1) | copy-start | bytes 50331652
  0.7 11.6 %collective-permute-start = (bf16[40,4096]{1,0:T(8,128)(2,1)}, bf16[40,4096]{1,0:T(8,128)(2,1)S(1)}, u32[]{:S(2)}, u32[]{:S(2)}) collective-permute-start(bf16[40,4096]{1,0:T(8,128)(2,1)} %s.1), channel_id=1, source_target_pairs={{0,2},{1,3},{2,0},{3,1},{4,6},{5,7},{6,4},{7,5},{8,10},{9,11},{10,... | collective-permute-start | bytes 983048 | tf_op jit(solution)/shard_map/ppermute | solution.py:35
  3.7 7.8 %collective-permute-start.3 = (bf16[2,4096]{1,0:T(2,128)(2,1)}, bf16[2,4096]{1,0:T(2,128)(2,1)S(1)}, u32[]{:S(2)}, u32[]{:S(2)}) collective-permute-start(bf16[2,4096]{1,0:T(2,128)(2,1)} %b0.3), channel_id=1, source_target_pairs={{0,3},{1,2},{2,1},{3,0},{4,7},{5,6},{6,5},{7,4},{8,11},{9,10},{10,... | collective-permute-start | bytes 49160 | tf_op jit(solution)/shard_map/ppermute | solution.py:35
  3.7 8.6 %collective-permute-start.2 = (bf16[2,4096]{1,0:T(2,128)(2,1)}, bf16[2,4096]{1,0:T(2,128)(2,1)S(1)}, u32[]{:S(2)}, u32[]{:S(2)}) collective-permute-start(bf16[2,4096]{1,0:T(2,128)(2,1)} %b0.3), channel_id=1, source_target_pairs={{0,2},{1,3},{2,0},{3,1},{4,6},{5,7},{6,4},{7,5},{8,10},{9,11},{10,... | collective-permute-start | bytes 49160 | tf_op jit(solution)/shard_map/ppermute | solution.py:35
  4.9 7.4 %collective-permute-start.1 = (bf16[2,4096]{1,0:T(2,128)(2,1)}, bf16[2,4096]{1,0:T(2,128)(2,1)S(1)}, u32[]{:S(2)}, u32[]{:S(2)}) collective-permute-start(bf16[2,4096]{1,0:T(2,128)(2,1)} %b0.3), channel_id=1, source_target_pairs={{0,1},{1,0},{2,3},{3,2},{4,5},{5,4},{6,7},{7,6},{8,9},{9,8},{10,11... | collective-permute-start | bytes 49160 | tf_op jit(solution)/shard_map/ppermute | solution.py:35
  5.5 9.1 %collective-permute-start.4 = (bf16[40,4096]{1,0:T(8,128)(2,1)}, bf16[40,4096]{1,0:T(8,128)(2,1)S(1)}, u32[]{:S(2)}, u32[]{:S(2)}) collective-permute-start(bf16[40,4096]{1,0:T(8,128)(2,1)} %s.1), channel_id=1, source_target_pairs={{0,1},{1,0},{2,3},{3,2},{4,5},{5,4},{6,7},{7,6},{8,9},{9,8},{10,11... | collective-permute-start | bytes 983048 | tf_op jit(solution)/shard_map/ppermute | solution.py:35
  11.4 3.3 %copy-start.5 = (s32[4]{0:T(128)S(1)}, s32[4]{0:T(128)}, u32[]{:S(2)}) copy-start(s32[4]{0:T(128)} %owner_ref.1) | copy-start | bytes 52
  11.4 13.3 %copy-start.1 = (bf16[2,2,512,128]{3,2,1,0:T(8,128)(2,1)S(1)}, bf16[2,2,512,128]{3,2,1,0:T(8,128)(2,1)}, u32[]{:S(2)}) copy-start(bf16[2,2,512,128]{3,2,1,0:T(8,128)(2,1)} %kv.1) | copy-start | bytes 1572868
  11.4 13.3 %copy-start.4 = (s32[2]{0:T(128)S(1)}, s32[2]{0:T(128)}, u32[]{:S(2)}) copy-start(s32[2]{0:T(128)} %len_ref.1) | copy-start | bytes 28
  12.3 2.4 %collective-permute-start.5 = (bf16[40,4096]{1,0:T(8,128)(2,1)S(1)}, bf16[40,4096]{1,0:T(8,128)(2,1)S(1)}, u32[]{:S(2)}, u32[]{:S(2)}) collective-permute-start(bf16[40,4096]{1,0:T(8,128)(2,1)S(1)} %collective-permute-done.far.s2), channel_id=1, source_target_pairs={{0,1},{1,0},{2,3},{3,2},{4,5},{5,4},{6,7},{7,6},{8,9},{9,8},{10,11... | collective-permute-start | bytes 983048 | tf_op jit(solution)/shard_map/ppermute | solution.py:35
  15.8 6.0 %collective-permute-start.6 = (bf16[120,128]{1,0:T(8,128)(2,1)S(1)}, bf16[120,128]{1,0:T(8,128)(2,1)S(1)}, u32[]{:S(2)}, u32[]{:S(2)}) collective-permute-start(bf16[120,128]{1,0:T(8,128)(2,1)S(1)} %get-tuple-element.33), channel_id=1, source_target_pairs={{0,12},{4,8},{8,4},{12,0},{1,13},{5,9},{9,5},{13,1},{2,14},{6,10},... | collective-permute-start | bytes 92168 | tf_op jit(solution)/shard_map/ppermute | solution.py:35
  19.9 4.8 %collective-permute-start.7 = (bf16[120,128]{1,0:T(8,128)(2,1)S(1)}, bf16[120,128]{1,0:T(8,128)(2,1)S(1)}, u32[]{:S(2)}, u32[]{:S(2)}) collective-permute-start(bf16[120,128]{1,0:T(8,128)(2,1)S(1)} %get-tuple-element.34), channel_id=1, source_target_pairs={{0,8},{4,12},{8,0},{12,4},{1,9},{5,13},{9,1},{13,5},{2,10},{6,14},... | collective-permute-start | bytes 92168 | tf_op jit(solution)/shard_map/ppermute | solution.py:35
  19.9 4.8 %collective-permute-start.8 = (bf16[120,128]{1,0:T(8,128)(2,1)S(1)}, bf16[120,128]{1,0:T(8,128)(2,1)S(1)}, u32[]{:S(2)}, u32[]{:S(2)}) collective-permute-start(bf16[120,128]{1,0:T(8,128)(2,1)S(1)} %get-tuple-element.35), channel_id=1, source_target_pairs={{0,4},{4,0},{8,12},{12,8},{1,5},{5,1},{9,13},{13,9},{2,6},{6,2},{1... | collective-permute-start | bytes 92168 | tf_op jit(solution)/shard_map/ppermute | solution.py:35
  26.2 5.5 %collective-permute-start.11 = (bf16[2,2048]{1,0:T(2,128)(2,1)S(1)}, bf16[2,2048]{1,0:T(2,128)(2,1)S(1)}, u32[]{:S(2)}, u32[]{:S(2)}) collective-permute-start(bf16[2,2048]{1,0:T(2,128)(2,1)S(1)} %get-tuple-element.38.a0), channel_id=1, source_target_pairs={{0,12},{4,8},{8,4},{12,0},{1,13},{5,9},{9,5},{13,1},{2,14},{6,10},... | collective-permute-start | bytes 24584 | tf_op jit(solution)/shard_map/ppermute | solution.py:35
  27.7 4.6 %collective-permute-start.10 = (bf16[2,2048]{1,0:T(2,128)(2,1)S(1)}, bf16[2,2048]{1,0:T(2,128)(2,1)S(1)}, u32[]{:S(2)}, u32[]{:S(2)}) collective-permute-start(bf16[2,2048]{1,0:T(2,128)(2,1)S(1)} %get-tuple-element.38.a0), channel_id=1, source_target_pairs={{0,8},{4,12},{8,0},{12,4},{1,9},{5,13},{9,1},{13,5},{2,10},{6,14},... | collective-permute-start | bytes 24584 | tf_op jit(solution)/shard_map/ppermute | solution.py:35
  28.3 4.0 %collective-permute-start.9 = (bf16[2,2048]{1,0:T(2,128)(2,1)S(1)}, bf16[2,2048]{1,0:T(2,128)(2,1)S(1)}, u32[]{:S(2)}, u32[]{:S(2)}) collective-permute-start(bf16[2,2048]{1,0:T(2,128)(2,1)S(1)} %get-tuple-element.38.a0), channel_id=1, source_target_pairs={{0,4},{4,0},{8,12},{12,8},{1,5},{5,1},{9,13},{13,9},{2,6},{6,2},{1... | collective-permute-start | bytes 24584 | tf_op jit(solution)/shard_map/ppermute | solution.py:35
  34.6 3.2 %collective-permute-start.12 = (bf16[2,4096]{1,0:T(2,128)(2,1)S(1)}, bf16[2,4096]{1,0:T(2,128)(2,1)S(1)}, u32[]{:S(2)}, u32[]{:S(2)}) collective-permute-start(bf16[2,4096]{1,0:T(2,128)(2,1)S(1)} %get-tuple-element.42), channel_id=1, source_target_pairs={{0,3},{1,2},{2,1},{3,0},{4,7},{5,6},{6,5},{7,4},{8,11},{9,10},{10,... | collective-permute-start | bytes 49160 | tf_op jit(solution)/shard_map/ppermute | solution.py:35
  34.6 3.8 %collective-permute-start.13 = (bf16[2,4096]{1,0:T(2,128)(2,1)S(1)}, bf16[2,4096]{1,0:T(2,128)(2,1)S(1)}, u32[]{:S(2)}, u32[]{:S(2)}) collective-permute-start(bf16[2,4096]{1,0:T(2,128)(2,1)S(1)} %get-tuple-element.43), channel_id=1, source_target_pairs={{0,2},{1,3},{2,0},{3,1},{4,6},{5,7},{6,4},{7,5},{8,10},{9,11},{10,... | collective-permute-start | bytes 49160 | tf_op jit(solution)/shard_map/ppermute | solution.py:35
  36.0 2.4 %collective-permute-start.14 = (bf16[2,4096]{1,0:T(2,128)(2,1)S(1)}, bf16[2,4096]{1,0:T(2,128)(2,1)S(1)}, u32[]{:S(2)}, u32[]{:S(2)}) collective-permute-start(bf16[2,4096]{1,0:T(2,128)(2,1)S(1)} %get-tuple-element.44), channel_id=1, source_target_pairs={{0,1},{1,0},{2,3},{3,2},{4,5},{5,4},{6,7},{7,6},{8,9},{9,8},{10,11... | collective-permute-start | bytes 49160 | tf_op jit(solution)/shard_map/ppermute | solution.py:35
